TPU v7x, 32 devices: a whole 2x2x4 slice. The times are simulated.
32 devices in a mesh: section: 2 (over core), node: 4 (over y, x), dev: 4 (over z).
Axes of the slice: x: 2, y: 2, z: 4, core: 2. Of those that a mesh axis runs over, the one named last changes fastest.
Arguments:
- inputs_forward: bfloat16 [2, 512, 3584], P('section', 'dev', 'node'), may hold values from -6 to 6
- routes_forward: int32 [2, 512, 2], P('section', 'dev'), may hold values from 0 to 3, all different within a row; in each aligned block of 128 rows (0 to 127, 128 to 255, ..., all dimensions but the last counted through in order) at most 128 rows name the same one
- gates_forward: float32 [2, 512, 2], P('section', 'dev'), may hold values from 0.2 to 1.2
- grads_backward: bfloat16 [2, 512, 3584], P('section', 'dev', 'node'), may hold values from -6 to 6
- routes_backward: int32 [2, 512, 2], P('section', 'dev'), may hold values from 0 to 3, all different within a row; in each aligned block of 128 rows (0 to 127, 128 to 255, ..., all dimensions but the last counted through in order) at most 128 rows name the same one
- gates_backward: float32 [2, 512, 2], P('section', 'dev'), may hold values from 0.2 to 1.2
- w_gate: bfloat16 [2, 4, 3584, 1024], P('section', 'dev', 'node'), may hold values from -0.09375 to 0.09375
- w_up: bfloat16 [2, 4, 3584, 1024], P('section', 'dev', 'node'), may hold values from -0.09375 to 0.09375
- w_down: bfloat16 [2, 4, 1024, 3584], P('section', 'dev', None, 'node'), may hold values from -0.1875 to 0.1875
- saved_gate: bfloat16 [2, 4, 512, 1024], P('section', 'dev'), may hold values from -5 to 5
- saved_up: bfloat16 [2, 4, 512, 1024], P('section', 'dev'), may hold values from -5 to 5
Outputs:
- forward_next: bfloat16 [2, 512, 3584], P('section', 'dev', 'node')
- backward_next: bfloat16 [2, 512, 3584], P('section', 'dev', 'node')
Inputs may be any that keep to these rules, and one draw needn't show every extreme that they name: `routes_forward`: each row names 2 different experts. Among the rows of one device no expert is named more than 128 times, a bound that some block reaches. `routes_backward`: each row names 2 different experts. Among the rows of one device no expert is named more than 128 times, a bound that some block reaches.
All inputs are finite; a program needn't handle non-finite values.
Results may differ from a plain program's by a relative error of at most 0.014.
Values may be sent and summed in bfloat16 or wider, within the bound.
No kernel may reach another device: no remote copies, remote signals or barrier semaphores. Data moves between devices by JAX's collectives and lax.ppermute only.
A program may use at most 64 MiB of HBM per device.

v0:
```python
import jax
import jax.numpy as jnp
from jax import lax
from jax.sharding import PartitionSpec as P


def from_behind(value, axis, steps):
    count = lax.axis_size(axis)
    pairs = [(source, (source + steps) % count) for source in range(count)]
    return lax.ppermute(value, axis, pairs)


def slot_targets(routing, experts, capacity):
    flat = routing.reshape(-1)
    onehot = (flat[:, None] == jnp.arange(experts, dtype=jnp.int32)[None, :]).astype(jnp.int32)
    earlier = jnp.cumsum(onehot, axis=0) - onehot
    return flat * capacity + jnp.sum(earlier * onehot, axis=1)


def pack_rows(token_rows, targets, slot_count, chosen):
    match = (jnp.arange(slot_count, dtype=jnp.int32)[:, None] == targets[None, :]).astype(
        jnp.bfloat16
    )
    select = jnp.sum(match.reshape(slot_count, token_rows.shape[0], chosen), axis=2)
    return jnp.dot(select, token_rows, preferred_element_type=jnp.float32).astype(jnp.bfloat16)


def combine_rows(token_rows, weights_of, returned_rows, targets):
    width = token_rows.shape[1]
    picked = returned_rows.reshape(-1, width)[targets]
    picked = picked.reshape(token_rows.shape[0], weights_of.shape[1], width).astype(jnp.float32)
    mixed = token_rows.astype(jnp.float32) + jnp.sum(weights_of[:, :, None] * picked, axis=1)
    return mixed.astype(jnp.bfloat16)


def backward_act(grad_hidden, stored_gate, stored_up):
    act_gate = stored_gate.astype(jnp.float32)
    act_up = stored_up.astype(jnp.float32)
    squash = jax.nn.sigmoid(act_gate)
    grad_gate = (grad_hidden * act_up * squash * (1.0 + act_gate * (1.0 - squash))).astype(
        jnp.bfloat16
    )
    grad_up = (grad_hidden * act_gate * squash).astype(jnp.bfloat16)
    return (grad_gate, grad_up)


def shards(
    inputs_forward,
    routes_forward,
    gates_forward,
    grads_backward,
    routes_backward,
    gates_backward,
    w_gate,
    w_up,
    w_down,
    saved_gate,
    saved_up,
):
    experts = lax.axis_size("dev")
    chosen = routes_forward.shape[2]
    token_rows = inputs_forward[0]
    grad_rows = grads_backward[0]
    slot_total = saved_gate.shape[2]
    capacity = slot_total // experts
    width = token_rows.shape[1]
    targets_forward = slot_targets(routes_forward[0], experts, capacity)
    targets_backward = slot_targets(routes_backward[0], experts, capacity)
    sent_forward = pack_rows(token_rows, targets_forward, slot_total, chosen).reshape(
        experts, capacity, width
    )
    sent_backward = pack_rows(grad_rows, targets_backward, slot_total, chosen).reshape(
        experts, capacity, width
    )
    arrived_forward, arrived_backward = (
        lax.all_to_all(sent_forward, "dev", split_axis=0, concat_axis=0, tiled=True),
        lax.all_to_all(sent_backward, "dev", split_axis=0, concat_axis=0, tiled=True),
    )
    arrived_forward = arrived_forward.reshape(slot_total, width)
    arrived_backward = arrived_backward.reshape(slot_total, width)
    gate_local = w_gate[0, 0]
    up_local = w_up[0, 0]
    down_local = w_down[0, 0]
    stored_gate = saved_gate[0, 0]
    stored_up = saved_up[0, 0]
    contract_last = (((1,), (1,)), ((), ()))
    part_gate = jnp.dot(arrived_forward, gate_local, preferred_element_type=jnp.float32)
    part_up = jnp.dot(arrived_forward, up_local, preferred_element_type=jnp.float32)
    part_grad = lax.dot_general(
        arrived_backward, down_local, contract_last, preferred_element_type=jnp.float32
    )
    gate_share, up_share = (
        lax.psum_scatter(
            part_gate.astype(jnp.bfloat16), "node", scatter_dimension=1, tiled=True
        ).astype(jnp.float32),
        lax.psum_scatter(
            part_up.astype(jnp.bfloat16), "node", scatter_dimension=1, tiled=True
        ).astype(jnp.float32),
    )
    hidden_share = (jax.nn.silu(gate_share) * up_share).astype(jnp.bfloat16)
    hidden = lax.all_gather(hidden_share, "node", axis=1, tiled=True)
    grad_hidden = lax.psum(part_grad.astype(jnp.bfloat16), "node").astype(jnp.float32)
    grad_gate, grad_up = backward_act(grad_hidden, stored_gate, stored_up)
    result_forward = jnp.dot(hidden, down_local, preferred_element_type=jnp.float32).astype(
        jnp.bfloat16
    )
    result_backward = lax.dot_general(
        grad_gate, gate_local, contract_last, preferred_element_type=jnp.float32
    )
    result_backward = result_backward + lax.dot_general(
        grad_up, up_local, contract_last, preferred_element_type=jnp.float32
    )
    result_backward = result_backward.astype(jnp.bfloat16)
    back_forward, back_backward = (
        lax.all_to_all(
            result_forward.reshape(experts, capacity, width),
            "dev",
            split_axis=0,
            concat_axis=0,
            tiled=True,
        ),
        lax.all_to_all(
            result_backward.reshape(experts, capacity, width),
            "dev",
            split_axis=0,
            concat_axis=0,
            tiled=True,
        ),
    )
    mixed_forward = combine_rows(token_rows, gates_forward[0], back_forward, targets_forward)
    mixed_backward = combine_rows(grad_rows, gates_backward[0], back_backward, targets_backward)
    next_forward = from_behind(mixed_forward[None], "section", 1)
    next_backward = from_behind(mixed_backward[None], "section", -1)
    return (next_forward, next_backward)


def solution(mesh):
    return jax.shard_map(
        shards,
        mesh=mesh,
        in_specs=(
            P("section", "dev", "node"),
            P("section", "dev", None),
            P("section", "dev", None),
            P("section", "dev", "node"),
            P("section", "dev", None),
            P("section", "dev", None),
            P("section", "dev", "node", None),
            P("section", "dev", "node", None),
            P("section", "dev", None, "node"),
            P("section", "dev", None, None),
            P("section", "dev", None, None),
        ),
        out_specs=(P("section", "dev", "node"), P("section", "dev", "node")),
        check_vma=False,
    )
```

profile of v0, /device:TPU:0, one launch (start us, length us, event | category | flops | bytes accessed | tf_op | source)
XLA Modules:
  0.0 240.8 jit_solution(6459605222488941071)
XLA Ops:
  7.2 0.9 copy.41
  8.4 1.2 reduce-window.16
  10.4 2.3 convolution_convert_fusion
  12.7 6.3 %all-to-all-start.2 = ((bf16[4,128,896]{2,1,0:T(8,128)(2,1)}), bf16[4,128,896]{2,1,0:T(8,128)(2,1)}, u32[]{:S(2)}, u32[]{:S(2)}) async-start(bf16[4,128,896]{2,1,0:T(8,128)(2,1)} %bitcast.20), calls=%async_computation.4 | async-start | bytes 1835008 | tf_op jit(solution)/shard_map/all_to_all | solution.py:77
  19.4 1.2 reduce-window.14
  21.4 1.3 convolution_convert_fusion.1
  22.7 19.3 %all-to-all-done.2 = bf16[4,128,896]{2,1,0:T(8,128)(2,1)} async-done(((bf16[4,128,896]{2,1,0:T(8,128)(2,1)}), bf16[4,128,896]{2,1,0:T(8,128)(2,1)}, u32[]{:S(2)}, u32[]{:S(2)}) %all-to-all-start.2) | async-done | bytes 917536 | tf_op jit(solution)/shard_map/all_to_all | solution.py:77
  42.0 3.5 %all-to-all-start = ((bf16[4,128,896]{2,1,0:T(8,128)(2,1)}), bf16[4,128,896]{2,1,0:T(8,128)(2,1)S(1)}, u32[]{:S(2)}, u32[]{:S(2)}) async-start(bf16[4,128,896]{2,1,0:T(8,128)(2,1)} %bitcast.5), calls=%async_computation | async-start | bytes 1835008 | tf_op jit(solution)/shard_map/all_to_all | solution.py:76
  45.6 4.1 %fusion.27 = bf16[512,1024]{1,0:T(8,128)(2,1)} fusion(bf16[512,896]{1,0:T(8,128)(2,1)} %bitcast.21, bf16[1,1,1024,896]{3,2,1,0:T(8,128)(2,1)} %param.19), kind=kOutput, calls=%fused_computation.30 | convolution fusion | flops 940048384 | bytes 3801088 | tf_op jit(solution)/shard_map/dot_general | solution.py:89
  49.8 18.2 %all-to-all-done = bf16[4,128,896]{2,1,0:T(8,128)(2,1)S(1)} async-done(((bf16[4,128,896]{2,1,0:T(8,128)(2,1)}), bf16[4,128,896]{2,1,0:T(8,128)(2,1)S(1)}, u32[]{:S(2)}, u32[]{:S(2)}) %all-to-all-start) | async-done | bytes 917536 | tf_op jit(solution)/shard_map/all_to_all | solution.py:76
  68.0 3.8 %fusion.21 = bf16[512,1024]{1,0:T(8,128)(2,1)} fusion(bf16[512,896]{1,0:T(8,128)(2,1)S(1)} %bitcast.116, bf16[1,1,896,1024]{3,2,1,0:T(8,128)(2,1)} %param.17), kind=kOutput, calls=%fused_computation.28 | convolution fusion | flops 940048384 | bytes 3801088 | tf_op jit(solution)/shard_map/dot_general | solution.py:87
  71.8 2.2 fusion.24
  74.1 29.8 %all-reduce.2.cloned.1.call-done = bf16[512,1024]{1,0:T(8,128)(2,1)} async-done(((bf16[512,1024]{1,0:T(8,128)(2,1)}), bf16[512,1024]{1,0:T(8,128)(2,1)}) %all-reduce.2.cloned.1.call-update) | async-done | bytes 1048592 | tf_op jit(solution)/shard_map/psum | solution.py:102
  103.8 4.2 %fusion.13 = f32[512,896]{1,0:T(8,128)} fusion(bf16[1,1,896,1024]{3,2,1,0:T(8,128)(2,1)S(1)} %copy-done, bf16[512,1024]{1,0:T(8,128)(2,1)} %all-reduce.2.cloned.1.call-done, bf16[1,1,512,1024]{3,2,1,0:T(8,128)(2,1)} %param.20), kind=kOutput, calls=%fused_computation.19 | convolution fusion | flops 943718400 | bytes 5767168 | tf_op jit(solution)/shard_map/dot_general | solution.py:110
  108.1 26.4 %reduce-scatter.3.cloned.1.call-done = bf16[512,256]{1,0:T(8,128)(2,1)} async-done(((bf16[512,1024]{1,0:T(8,128)(2,1)}), bf16[512,256]{1,0:T(8,128)(2,1)}) %reduce-scatter.3.cloned.1.call-update) | async-done | bytes 262160 | tf_op jit(solution)/shard_map/reduce_scatter | solution.py:93
  134.5 30.9 %reduce-scatter.5.cloned.1.call-done = bf16[512,256]{1,0:T(8,128)(2,1)} async-done(((bf16[512,1024]{1,0:T(8,128)(2,1)}), bf16[512,256]{1,0:T(8,128)(2,1)}) %reduce-scatter.5.cloned.1.call-update) | async-done | bytes 262160 | tf_op jit(solution)/shard_map/reduce_scatter | solution.py:96
  165.4 1.9 fusion.44
  167.3 5.7 %add_convert_fusion = bf16[512,896]{1,0:T(8,128)(2,1)} fusion(f32[512,896]{1,0:T(8,128)} %fusion.13, bf16[1,1,896,1024]{3,2,1,0:T(8,128)(2,1)} %param.17, bf16[512,1024]{1,0:T(8,128)(2,1)} %all-reduce.2.cloned.1.call-done, bf16[1,1,512,1024]{3,2,1,0:T(8,128)(2,1)} %param.21, bf16[1,1,512,1024]{3,2,1,0:T(8,128)(2,1)} %param.20), kind=kOutput, calls=%fused_computation.27 | convolution fusion | flops 947257344 | bytes 7733248 | tf_op jit(solution)/shard_map/dot_general | solution.py:107
  173.1 4.6 %all-to-all-start.3 = ((bf16[4,128,896]{2,1,0:T(8,128)(2,1)}), bf16[4,128,896]{2,1,0:T(8,128)(2,1)S(1)}, u32[]{:S(2)}, u32[]{:S(2)}) async-start(bf16[4,128,896]{2,1,0:T(8,128)(2,1)} %bitcast.118), calls=%async_computation.5 | async-start | bytes 1835008 | tf_op jit(solution)/shard_map/all_to_all | solution.py:122
  177.7 16.3 %all-gather.2.cloned.1.call-done = bf16[512,1024]{1,0:T(8,128)(2,1)} async-done(((bf16[512,256]{1,0:T(8,128)(2,1)}), bf16[512,1024]{1,0:T(8,128)(2,1)}) %all-gather.2.cloned.1.call-update) | async-done | bytes 1048592 | tf_op jit(solution)/shard_map/all_gather | solution.py:101
  194.0 4.0 %fusion.32 = bf16[512,896]{1,0:T(8,128)(2,1)} fusion(bf16[512,1024]{1,0:T(8,128)(2,1)} %all-gather.2.cloned.1.call-done, bf16[1,1,1024,896]{3,2,1,0:T(8,128)(2,1)} %param.19), kind=kOutput, calls=%fused_computation.33 | convolution fusion | flops 939982848 | bytes 3801088 | tf_op jit(solution)/shard_map/dot_general | solution.py:104
  198.0 2.6 %all-to-all-done.3 = bf16[4,128,896]{2,1,0:T(8,128)(2,1)S(1)} async-done(((bf16[4,128,896]{2,1,0:T(8,128)(2,1)}), bf16[4,128,896]{2,1,0:T(8,128)(2,1)S(1)}, u32[]{:S(2)}, u32[]{:S(2)}) %all-to-all-start.3) | async-done | bytes 917536 | tf_op jit(solution)/shard_map/all_to_all | solution.py:122
  200.6 1.0 copy-done.1
  201.6 3.7 %all-to-all-start.1 = ((bf16[4,128,896]{2,1,0:T(8,128)(2,1)}), bf16[4,128,896]{2,1,0:T(8,128)(2,1)S(1)}, u32[]{:S(2)}, u32[]{:S(2)}) async-start(bf16[4,128,896]{2,1,0:T(8,128)(2,1)} %bitcast.115), calls=%async_computation.3 | async-start | bytes 1835008 | tf_op jit(solution)/shard_map/all_to_all | solution.py:115
  206.5 2.8 %gather_fusion.1 = bf16[256,896]{1,0:T(8,128)(2,1)S(1)} fusion(bf16[512,896]{1,0:T(8,128)(2,1)} %bitcast.114, s32[1024]{0:T(1024)S(1)} %pad_clamp_fusion), kind=kCustom, calls=%fused_computation.1 | custom fusion | bytes 918528 | tf_op jit(solution)/shard_map/gather | solution.py:30
  209.3 1.4 reshape.185
  210.7 2.4 multiply_reduce_fusion
  213.8 13.6 %all-to-all-done.1 = bf16[4,128,896]{2,1,0:T(8,128)(2,1)S(1)} async-done(((bf16[4,128,896]{2,1,0:T(8,128)(2,1)}), bf16[4,128,896]{2,1,0:T(8,128)(2,1)S(1)}, u32[]{:S(2)}, u32[]{:S(2)}) %all-to-all-start.1) | async-done | bytes 917536 | tf_op jit(solution)/shard_map/all_to_all | solution.py:115
  227.5 1.2 gather_fusion
  229.1 1.1 multiply_reduce_fusion.1
  230.4 1.5 collective-permute-done
  232.6 1.6 copy.55
  (69 shorter events, 5.5 us)
Async XLA Ops:
  7.2 64.6 %copy-start = (bf16[1,1,896,1024]{3,2,1,0:T(8,128)(2,1)S(1)}, bf16[1,1,896,1024]{3,2,1,0:T(8,128)(2,1)}, u32[]{:S(2)}) copy-start(bf16[1,1,896,1024]{3,2,1,0:T(8,128)(2,1)} %param.18) | copy-start | bytes 5505028
  8.2 10.8 %copy-start.5 = (s32[1,128,2]{1,2,0:T(2,128)S(1)}, s32[1,128,2]{1,2,0:T(2,128)}, u32[]{:S(2)}) copy-start(s32[1,128,2]{1,2,0:T(2,128)} %param.12) | copy-start | bytes 3076
  10.4 11.0 %copy-start.3 = (bf16[1,128,896]{2,1,0:T(8,128)(2,1)S(1)}, bf16[1,128,896]{2,1,0:T(8,128)(2,1)}, u32[]{:S(2)}) copy-start(bf16[1,128,896]{2,1,0:T(8,128)(2,1)} %param.11) | copy-start | bytes 688132
  12.7 29.3 %all-to-all-start.2 = ((bf16[4,128,896]{2,1,0:T(8,128)(2,1)}), bf16[4,128,896]{2,1,0:T(8,128)(2,1)}, u32[]{:S(2)}, u32[]{:S(2)}) async-start(bf16[4,128,896]{2,1,0:T(8,128)(2,1)} %bitcast.20), calls=%async_computation.4 | async-start | bytes 1835008 | tf_op jit(solution)/shard_map/all_to_all | solution.py:77
  42.0 25.9 %all-to-all-start = ((bf16[4,128,896]{2,1,0:T(8,128)(2,1)}), bf16[4,128,896]{2,1,0:T(8,128)(2,1)S(1)}, u32[]{:S(2)}, u32[]{:S(2)}) async-start(bf16[4,128,896]{2,1,0:T(8,128)(2,1)} %bitcast.5), calls=%async_computation | async-start | bytes 1835008 | tf_op jit(solution)/shard_map/all_to_all | solution.py:76
  45.6 58.3 %all-reduce.2.cloned.1.call-start = ((), (), s32[]{:S(2)}) async-start(), calls=%async_computation.9 | async-start | bytes 2097152 | tf_op jit(solution)/shard_map/psum | solution.py:102
  49.7 84.8 %reduce-scatter.3.cloned.1.call-start = ((), (), s32[]{:S(2)}) async-start(), calls=%async_computation.6 | async-start | bytes 1310720 | tf_op jit(solution)/shard_map/reduce_scatter | solution.py:93
  71.7 93.7 %reduce-scatter.5.cloned.1.call-start = ((), (), s32[]{:S(2)}) async-start(), calls=%async_computation.7 | async-start | bytes 1310720 | tf_op jit(solution)/shard_map/reduce_scatter | solution.py:96
  74.0 119.9 %all-gather.2.cloned.1.call-start = ((), (), s32[]{:S(2)}) async-start(), calls=%async_computation.8 | async-start | bytes 1310720 | tf_op jit(solution)/shard_map/all_gather | solution.py:101
  173.1 27.5 %all-to-all-start.3 = ((bf16[4,128,896]{2,1,0:T(8,128)(2,1)}), bf16[4,128,896]{2,1,0:T(8,128)(2,1)S(1)}, u32[]{:S(2)}, u32[]{:S(2)}) async-start(bf16[4,128,896]{2,1,0:T(8,128)(2,1)} %bitcast.118), calls=%async_computation.5 | async-start | bytes 1835008 | tf_op jit(solution)/shard_map/all_to_all | solution.py:122
  198.0 7.4 %copy-start.6 = (f32[1,128,2]{1,2,0:T(2,128)S(1)}, f32[1,128,2]{1,2,0:T(2,128)}, u32[]{:S(2)}) copy-start(f32[1,128,2]{1,2,0:T(2,128)} %param.16) | copy-start | bytes 3076
  198.0 8.3 %copy-start.7 = (f32[1,128,2]{1,2,0:T(2,128)S(1)}, f32[1,128,2]{1,2,0:T(2,128)}, u32[]{:S(2)}) copy-start(f32[1,128,2]{1,2,0:T(2,128)} %param.13) | copy-start | bytes 3076
  200.6 1.0 copy-start.1
  201.6 25.9 %all-to-all-start.1 = ((bf16[4,128,896]{2,1,0:T(8,128)(2,1)}), bf16[4,128,896]{2,1,0:T(8,128)(2,1)S(1)}, u32[]{:S(2)}, u32[]{:S(2)}) async-start(bf16[4,128,896]{2,1,0:T(8,128)(2,1)} %bitcast.115), calls=%async_computation.3 | async-start | bytes 1835008 | tf_op jit(solution)/shard_map/all_to_all | solution.py:115
  209.3 3.8 %copy-start.2 = (bf16[1,128,896]{2,1,0:T(8,128)(2,1)S(1)}, bf16[1,128,896]{2,1,0:T(8,128)(2,1)}, u32[]{:S(2)}) copy-start(bf16[1,128,896]{2,1,0:T(8,128)(2,1)} %param.14) | copy-start | bytes 688132
  213.8 16.6 %collective-permute-start.1 = (bf16[1,128,896]{2,1,0:T(8,128)(2,1)}, bf16[1,128,896]{2,1,0:T(8,128)(2,1)}, u32[]{:S(2)}, u32[]{:S(2)}) collective-permute-start(bf16[1,128,896]{2,1,0:T(8,128)(2,1)} %fusion.47), channel_id=1, source_target_pairs={{0,16},{16,0},{1,17},{17,1},{2,18},{18,2},{3,19},{19,3},{4,20},{20... | collective-permute-start | bytes 688136 | tf_op jit(solution)/shard_map/ppermute | solution.py:10
  228.7 1.6 copy-start.4
  230.3 1.6 collective-permute-start
Sparse Core Ops, SparseCore 0:
  49.9 53.9 all-reduce.1
  106.7 27.7 reduce-scatter.2
  137.6 27.7 reduce-scatter.4
  167.5 26.4 all-gather.1
where the time goes:
time: 241 us
  waiting for transfers between devices  159 us (66%)
  matrix products  27.7 us (11%)
  starting transfers between devices  18.4 us (8%)
  between operations  14 us (6%)
  local copies, waits for them, and re-layouts  12.9 us (5%)
  other arithmetic  9.16 us (4%)
    reduce_scatter x1, waiting for transfers between devices, shards(): lax.psum_scatter(part_up.astype(jnp.bfloat16), 'node', scatter_dimension=...  30.9 us
    psum x1, waiting for transfers between devices, shards(): lax.psum(part_grad.astype(jnp.bfloat16), 'node').astype(jnp.float32)  29.8 us
    reduce_scatter x1, waiting for transfers between devices, shards(): lax.psum_scatter(part_gate.astype(jnp.bfloat16), 'node', scatter_dimensio...  26.4 us
    all_to_all x1, waiting for transfers between devices, shards(): lax.all_to_all(sent_backward, 'dev', split_axis=0, concat_axis=0, tiled=T...  19.3 us
    all_to_all x1, waiting for transfers between devices, shards(): lax.all_to_all(sent_forward, 'dev', split_axis=0, concat_axis=0, tiled=True)  18.2 us
    all_gather x1, waiting for transfers between devices, shards(): hidden = lax.all_gather(hidden_share, 'node', axis=1, tiled=True)  16.3 us
    all_to_all x1, waiting for transfers between devices, shards(): lax.all_to_all(result_forward.reshape(experts, capacity, width), 'dev', s...  13.6 us
    all_to_all x1, starting transfers between devices, shards(): lax.all_to_all(sent_backward, 'dev', split_axis=0, concat_axis=0, tiled=T...  6.32 us
  transfers between devices with their start and end apart: 10, of which 9 were waited for; matrix products, arithmetic and copies ran while one was open for 16% of the time, Pallas kernels for 0%

commit v1 on v0

--- a/solution.py
+++ b/solution.py
@@ -1,6 +1,10 @@
+import functools
+
 import jax
 import jax.numpy as jnp
 from jax import lax
+from jax.experimental import pallas as pl
+from jax.experimental.pallas import tpu as pltpu
 from jax.sharding import PartitionSpec as P
 
 
@@ -44,7 +48,7 @@
     return (grad_gate, grad_up)
 
 
-def shards(
+def shards_by_slots(
     inputs_forward,
     routes_forward,
     gates_forward,
@@ -134,6 +138,393 @@
     return (next_forward, next_backward)
 
 
+CONTRACT_LAST = (((1,), (1,)), ((), ()))
+CONTRACT_FIRST = (((0,), (0,)), ((), ()))
+
+
+def across(value, axis, mask):
+    count = lax.axis_size(axis)
+    return lax.ppermute(value, axis, [(source, source ^ mask) for source in range(count)])
+
+
+def call(body, grid, in_specs, out_specs, out_shape, scratch, flops, touched, args):
+    return pl.pallas_call(
+        body,
+        grid_spec=pltpu.PrefetchScalarGridSpec(
+            num_scalar_prefetch=1,
+            grid=(grid,),
+            in_specs=in_specs,
+            out_specs=out_specs,
+            scratch_shapes=scratch,
+        ),
+        out_shape=out_shape,
+        cost_estimate=pl.CostEstimate(flops=flops, bytes_accessed=touched, transcendentals=0),
+        compiler_params=pltpu.CompilerParams(
+            dimension_semantics=("arbitrary",), vmem_limit_bytes=32 << 20
+        ),
+    )(*args)
+
+
+def whole(shape):
+    return pl.BlockSpec(shape, lambda step, place: (0,) * len(shape))
+
+
+def size_of(arrays):
+    return sum(array.size * array.dtype.itemsize for array in arrays)
+
+
+def by_owner(place, row_refs, sorted_rows, nodes):
+    rows = row_refs[0].shape[0] // nodes
+    group = len(row_refs)
+    for mask in range(nodes):
+        first = pl.multiple_of((place[0] ^ mask) * rows, rows)
+        for index, ref in enumerate(row_refs):
+            at = (mask * group + index) * rows
+            sorted_rows[at : at + rows, :] = ref[pl.ds(first, rows), :]
+
+
+def from_owners(place, piece_refs, joined):
+    nodes, group = len(piece_refs), joined.shape[0]
+    rows = joined.shape[1] // nodes
+    for mask, ref in enumerate(piece_refs):
+        first = pl.multiple_of((place[0] ^ mask) * rows, rows)
+        for index in range(group):
+            joined[index, pl.ds(first, rows), :] = ref[index * rows : (index + 1) * rows, :]
+
+
+def gate_up_parts(place, rows, w_gate, w_up, nodes, tiles):
+    group, (count, width), hidden = len(rows), rows[0].shape, w_gate.shape[1]
+    tile, share = hidden // tiles, group * count // nodes
+
+    def body(place_ref, *refs):
+        row_refs, gate_ref, up_ref = refs[:group], refs[group], refs[group + 1]
+        outs, sorted_rows = refs[group + 2 : -1], refs[-1]
+
+        @pl.when(pl.program_id(0) == 0)
+        def _():
+            by_owner(place_ref, row_refs, sorted_rows, nodes)
+
+        for half, weight_ref in enumerate((gate_ref, up_ref)):
+            part = jnp.dot(sorted_rows[...], weight_ref[...], preferred_element_type=jnp.float32)
+            part = part.astype(jnp.bfloat16)
+            for mask in range(nodes):
+                outs[mask][half] = part[mask * share : (mask + 1) * share]
+
+    return call(
+        body,
+        tiles,
+        [whole((count, width))] * group
+        + [pl.BlockSpec((width, tile), lambda step, place: (0, step))] * 2,
+        [pl.BlockSpec((2, share, tile), lambda step, place: (0, 0, step))] * nodes,
+        [jax.ShapeDtypeStruct((2, share, hidden), jnp.bfloat16)] * nodes,
+        [pltpu.VMEM((group * count, width), jnp.bfloat16)],
+        4 * group * count * width * hidden,
+        size_of(rows) + size_of((w_gate, w_up)) + 4 * group * count * hidden,
+        (place, *rows, w_gate, w_up),
+    )
+
+
+def down_rows(place, pieces, w_down, group, tiles):
+    nodes, (share, hidden), width = len(pieces), pieces[0].shape, w_down.shape[1]
+    count, tile = share * nodes // group, hidden // tiles
+
+    def body(place_ref, *refs):
+        piece_refs, down_ref = refs[:nodes], refs[nodes]
+        outs, (joined, total) = refs[nodes + 1 : -2], refs[-2:]
+        step = pl.program_id(0)
+        from_owners(place_ref, piece_refs, joined)
+        part = jnp.dot(
+            joined[...].reshape(group * count, tile),
+            down_ref[...],
+            preferred_element_type=jnp.float32,
+        )
+
+        @pl.when(step == 0)
+        def _():
+            total[...] = part
+
+        @pl.when(step > 0)
+        def _():
+            total[...] += part
+
+        @pl.when(step == tiles - 1)
+        def _():
+            for index, out in enumerate(outs):
+                out[...] = total[index * count : (index + 1) * count].astype(jnp.bfloat16)
+
+    return call(
+        body,
+        tiles,
+        [pl.BlockSpec((share, tile), lambda step, place: (0, step))] * nodes
+        + [pl.BlockSpec((tile, width), lambda step, place: (step, 0))],
+        [whole((count, width))] * group,
+        [jax.ShapeDtypeStruct((count, width), jnp.bfloat16)] * group,
+        [
+            pltpu.VMEM((group, count, tile), jnp.bfloat16),
+            pltpu.VMEM((group * count, width), jnp.float32),
+        ],
+        2 * group * count * width * hidden,
+        size_of(pieces) + size_of((w_down,)) + 2 * group * count * width,
+        (place, *pieces, w_down),
+    )
+
+
+def grad_hidden_parts(place, rows, w_down, nodes, tiles):
+    group, (count, width), hidden = len(rows), rows[0].shape, w_down.shape[0]
+    tile, share = hidden // tiles, group * count // nodes
+
+    def body(place_ref, *refs):
+        row_refs, down_ref = refs[:group], refs[group]
+        outs, sorted_rows = refs[group + 1 : -1], refs[-1]
+
+        @pl.when(pl.program_id(0) == 0)
+        def _():
+            by_owner(place_ref, row_refs, sorted_rows, nodes)
+
+        part = lax.dot_general(
+            sorted_rows[...], down_ref[...], CONTRACT_LAST, preferred_element_type=jnp.float32
+        ).astype(jnp.bfloat16)
+        for mask in range(nodes):
+            outs[mask][...] = part[mask * share : (mask + 1) * share]
+
+    return call(
+        body,
+        tiles,
+        [whole((count, width))] * group
+        + [pl.BlockSpec((tile, width), lambda step, place: (step, 0))],
+        [pl.BlockSpec((share, tile), lambda step, place: (0, step))] * nodes,
+        [jax.ShapeDtypeStruct((share, hidden), jnp.bfloat16)] * nodes,
+        [pltpu.VMEM((group * count, width), jnp.bfloat16)],
+        2 * group * count * width * hidden,
+        size_of(rows) + size_of((w_down,)) + 2 * group * count * hidden,
+        (place, *rows, w_down),
+    )
+
+
+def input_grad_rows(place, pieces, w_gate, w_up, saved_gate, saved_up, masks, tiles):
+    nodes, (share, hidden), width = len(pieces), pieces[0].shape, w_gate.shape[0]
+    group = len(masks)
+    count, tile = share * nodes // group, hidden // tiles
+
+    def body(place_ref, *refs):
+        piece_refs, (gate_ref, up_ref) = refs[:nodes], refs[nodes : nodes + 2]
+        stored = refs[nodes + 2 : nodes + 2 + 2 * group]
+        outs, (joined, total) = refs[nodes + 2 + 2 * group : -2], refs[-2:]
+        step = pl.program_id(0)
+        from_owners(place_ref, piece_refs, joined)
+        grads_gate, grads_up = [], []
+        for index in range(group):
+            grad_gate, grad_up = backward_act(
+                joined[index].astype(jnp.float32), stored[index][...], stored[group + index][...]
+            )
+            grads_gate.append(grad_gate)
+            grads_up.append(grad_up)
+        part = lax.dot_general(
+            jnp.concatenate(grads_gate, axis=0),
+            gate_ref[...],
+            CONTRACT_LAST,
+            preferred_element_type=jnp.float32,
+        ) + lax.dot_general(
+            jnp.concatenate(grads_up, axis=0),
+            up_ref[...],
+            CONTRACT_LAST,
+            preferred_element_type=jnp.float32,
+        )
+
+        @pl.when(step == 0)
+        def _():
+            total[...] = part
+
+        @pl.when(step > 0)
+        def _():
+            total[...] += part
+
+        @pl.when(step == tiles - 1)
+        def _():
+            for index, out in enumerate(outs):
+                out[...] = total[index * count : (index + 1) * count].astype(jnp.bfloat16)
+
+    stored_specs = [
+        pl.BlockSpec((count, tile), functools.partial(lambda mask, step, place: (place[1] ^ mask, step), mask))
+        for mask in masks
+    ]
+    return call(
+        body,
+        tiles,
+        [pl.BlockSpec((share, tile), lambda step, place: (0, step))] * nodes
+        + [pl.BlockSpec((width, tile), lambda step, place: (0, step))] * 2
+        + stored_specs * 2,
+        [whole((count, width))] * group,
+        [jax.ShapeDtypeStruct((count, width), jnp.bfloat16)] * group,
+        [
+            pltpu.VMEM((group, count, tile), jnp.bfloat16),
+            pltpu.VMEM((group * count, width), jnp.float32),
+        ],
+        4 * group * count * width * hidden,
+        size_of(pieces) + size_of((w_gate, w_up)) + 6 * group * count * hidden,
+        (place, *pieces, w_gate, w_up) + (saved_gate,) * group + (saved_up,) * group,
+    )
+
+
+def selections(place_ref, routes_ref, experts, capacity):
+    chosen, count = routes_ref.shape
+    routes = routes_ref[...]
+    line = lax.broadcasted_iota(jnp.int32, (experts, count), 0) ^ place_ref[1]
+    named = jnp.zeros((experts, count), jnp.float32)
+    for choice in range(chosen):
+        named += (routes[choice : choice + 1] == line).astype(jnp.float32)
+    earlier = lax.broadcasted_iota(jnp.int32, (count, count), 0) < lax.broadcasted_iota(
+        jnp.int32, (count, count), 1
+    )
+    rank = jnp.dot(
+        named.astype(jnp.bfloat16),
+        earlier.astype(jnp.bfloat16),
+        preferred_element_type=jnp.float32,
+    )
+    slot = jnp.where(named > 0, rank, -1.0)
+    slots = lax.broadcasted_iota(jnp.int32, (capacity, count), 0).astype(jnp.float32)
+    return [
+        (slots == slot[mask : mask + 1]).astype(jnp.float32).astype(jnp.bfloat16)
+        for mask in range(experts)
+    ]
+
+
+def slot_rows(place, routes, rows, experts, capacity):
+    count, width = rows.shape
+
+    def body(place_ref, routes_ref, rows_ref, *outs):
+        for select, out in zip(selections(place_ref, routes_ref, experts, capacity), outs):
+            out[...] = jnp.dot(
+                select, rows_ref[...], preferred_element_type=jnp.float32
+            ).astype(jnp.bfloat16)
+
+    return call(
+        body,
+        1,
+        [whole(routes.shape), whole(rows.shape)],
+        [whole((capacity, width))] * experts,
+        [jax.ShapeDtypeStruct((capacity, width), jnp.bfloat16)] * experts,
+        [],
+        2 * experts * capacity * count * width,
+        (experts + 1) * size_of((rows,)),
+        (place, routes, rows),
+    )
+
+
+def mix_slots(place, routes, routes_by_token, weights, rows, returned):
+    experts, (capacity, width) = len(returned), returned[0].shape
+
+    def body(place_ref, routes_ref, named_ref, weights_ref, rows_ref, *refs):
+        returned_refs, out = refs[:-1], refs[-1]
+        total = rows_ref[...].astype(jnp.float32)
+        chosen = selections(place_ref, routes_ref, experts, capacity)
+        for mask, (select, ref) in enumerate(zip(chosen, returned_refs)):
+            weight = jnp.sum(
+                jnp.where(named_ref[...] == (place_ref[1] ^ mask), weights_ref[...], 0.0),
+                axis=1,
+                keepdims=True,
+            )
+            total += weight * lax.dot_general(
+                select, ref[...], CONTRACT_FIRST, preferred_element_type=jnp.float32
+            )
+        out[...] = total.astype(jnp.bfloat16)
+
+    return call(
+        body,
+        1,
+        [whole(routes.shape), whole(routes_by_token.shape), whole(weights.shape), whole(rows.shape)]
+        + [whole((capacity, width))] * experts,
+        whole(rows.shape),
+        jax.ShapeDtypeStruct(rows.shape, jnp.bfloat16),
+        [],
+        2 * experts * capacity * rows.size,
+        (experts + 2) * size_of((rows,)),
+        (place, routes, routes_by_token, weights, rows, *returned),
+    )
+
+
+def mix_tokens(expert, routes, weights, rows, returned):
+    total = rows.astype(jnp.float32)
+    for mask, value in enumerate(returned):
+        weight = jnp.sum(jnp.where(routes == (expert ^ mask), weights, 0.0), axis=1, keepdims=True)
+        total = total + weight * value.astype(jnp.float32)
+    return total.astype(jnp.bfloat16)
+
+
+def sum_pieces(pieces):
+    return sum(piece.astype(jnp.float32) for piece in pieces)
+
+
+def sections_shards(
+    inputs_forward,
+    routes_forward,
+    gates_forward,
+    grads_backward,
+    routes_backward,
+    gates_backward,
+    w_gate,
+    w_up,
+    w_down,
+    saved_gate,
+    saved_up,
+):
+    experts, nodes = lax.axis_size("dev"), lax.axis_size("node")
+    expert = lax.axis_index("dev")
+    place = jnp.stack([lax.axis_index("node"), expert]).astype(jnp.int32)
+    capacity = saved_gate.shape[2] // experts
+    token_rows, grad_rows = inputs_forward[0], grads_backward[0]
+    gate_local, up_local, down_local = w_gate[0, 0], w_up[0, 0], w_down[0, 0]
+    stored_gate, stored_up = saved_gate[0, 0], saved_up[0, 0]
+    routes_lines = routes_backward[0].T
+
+    arrived_forward = [token_rows] + [across(token_rows, "dev", m) for m in range(1, experts)]
+    packed = slot_rows(place, routes_lines, grad_rows, experts, capacity)
+    arrived_backward = [packed[0]] + [across(packed[m], "dev", m) for m in range(1, experts)]
+
+    back_forward, back_backward = [None] * experts, [None] * experts
+    for masks in GROUPS:
+        parts = gate_up_parts(place, [arrived_forward[m] for m in masks], gate_local, up_local, nodes, 4)
+        pieces = [parts[0]] + [across(parts[q], "node", q) for q in range(1, nodes)]
+        gate_share, up_share = sum_pieces(pieces)
+        hidden = (jax.nn.silu(gate_share) * up_share).astype(jnp.bfloat16)
+        hidden_pieces = [hidden] + [across(hidden, "node", q) for q in range(1, nodes)]
+        for m, value in zip(masks, down_rows(place, hidden_pieces, down_local, len(masks), 4)):
+            back_forward[m] = across(value, "dev", m) if m else value
+
+        parts = grad_hidden_parts(place, [arrived_backward[m] for m in masks], down_local, nodes, 4)
+        pieces = [parts[0]] + [across(parts[q], "node", q) for q in range(1, nodes)]
+        grad_hidden = sum_pieces(pieces).astype(jnp.bfloat16)
+        grad_pieces = [grad_hidden] + [across(grad_hidden, "node", q) for q in range(1, nodes)]
+        rows = input_grad_rows(
+            place, grad_pieces, gate_local, up_local, stored_gate, stored_up, masks, 4
+        )
+        for m, value in zip(masks, rows):
+            back_backward[m] = across(value, "dev", m) if m else value
+
+    mixed_forward = mix_tokens(expert, routes_forward[0], gates_forward[0], token_rows, back_forward)
+    next_forward = from_behind(mixed_forward[None], "section", 1)
+    mixed_backward = mix_slots(
+        place, routes_lines, routes_backward[0], gates_backward[0], grad_rows, back_backward
+    )
+    next_backward = from_behind(mixed_backward[None], "section", -1)
+    return (next_forward, next_backward)
+
+
+GROUPS = ((0, 1), (2, 3))
+
+
+def power_of_two(number):
+    return number & (number - 1) == 0
+
+
+def shards(*args):
+    experts, nodes = lax.axis_size("dev"), lax.axis_size("node")
+    tokens, capacity = args[0].shape[1], args[9].shape[2] // experts
+    if capacity == tokens and power_of_two(experts) and power_of_two(nodes) and tokens % (16 * nodes) == 0:
+        return sections_shards(*args)
+    return shards_by_slots(*args)
+
+
 def solution(mesh):
     return jax.shard_map(
         shards,

time: 241 us -> 149 us (0.62)
  waiting for transfers between devices: 159 us -> 66.4 us
  starting transfers between devices: 18.4 us -> 49.6 us
  matrix products: 27.7 us -> 0 us
  Pallas kernels: 0 us -> 24.6 us
  between operations: 14 us -> 0.94 us
  local copies, waits for them, and re-layouts: 12.9 us -> 4.84 us
  other arithmetic: 9.16 us -> 1.96 us
    ppermute x0 -> x36, waiting for transfers between devices: none -> 64.9 us  [across(): lax.ppermute(value, axis, [(source, source ^ mask) for source in range(co...]
    reduce_scatter x2 -> x0, waiting for transfers between devices: 57.3 us -> none  [the longest x1 30.9 us: shards(): lax.psum_scatter(part_up.astype(jnp.bfloat16), 'node', scatter_dimension=...]
    all_to_all x4 -> x0, waiting for transfers between devices: 53.7 us -> none  [the longest x1 19.3 us: shards(): lax.all_to_all(sent_backward, 'dev', split_axis=0, concat_axis=0, tiled=T...]
    ppermute x0 -> x36, starting transfers between devices: none -> 49.5 us  [across(): lax.ppermute(value, axis, [(source, source ^ mask) for source in range(co...]
    psum x1 -> x0, waiting for transfers between devices: 29.8 us -> none  [shards(): lax.psum(part_grad.astype(jnp.bfloat16), 'node').astype(jnp.float32)]
    dot_general x8 -> x0, matrix products: 27.7 us -> none  [the longest x1 5.74 us: shards(): lax.dot_general(grad_gate, gate_local, contract_last, preferred_element_t...]
    pallas_call x0 -> x10, Pallas kernels: none -> 24.6 us  [call(): pl.pallas_call(body, grid_spec=pltpu.PrefetchScalarGridSpec(num_scalar_pr...]
    all_to_all x4 -> x0, starting transfers between devices: 18.1 us -> none  [the longest x1 6.32 us: shards(): lax.all_to_all(sent_backward, 'dev', split_axis=0, concat_axis=0, tiled=T...]
  transfers between devices with their start and end apart: 10 -> 38, of which waited for: 9 -> 12; matrix products, arithmetic and copies ran while one was open for 16% -> 1% of each run, Pallas kernels for 0% -> 16%
where the time goes in v1:
time: 149 us; the launch traced here: 148 us
  waiting for transfers between devices  66.4 us (45%)
  starting transfers between devices  49.6 us (33%)
  Pallas kernels  24.6 us (17%)
  local copies, waits for them, and re-layouts  4.84 us (3%)
  other arithmetic  1.96 us (1%)
    ppermute x36, waiting for transfers between devices, across(): lax.ppermute(value, axis, [(source, source ^ mask) for source in range(co...  64.9 us
    ppermute x36, starting transfers between devices, across(): lax.ppermute(value, axis, [(source, source ^ mask) for source in range(co...  49.5 us
    pallas_call x10, Pallas kernels, call(): pl.pallas_call(body, grid_spec=pltpu.PrefetchScalarGridSpec(num_scalar_pr...  24.6 us
    unnamed x28, local copies, waits for them, and re-layouts  4.78 us
  transfers between devices with their start and end apart: 38, of which 12 were waited for; matrix products, arithmetic and copies ran while one was open for 1% of the time, Pallas kernels for 16%

profile of v1, /device:TPU:0, one launch (start us, length us, event | category | flops | bytes accessed | tf_op | source)
XLA Modules:
  0.0 148.4 jit_solution(13021632542650142795)
XLA Ops:
  3.6 3.1 %collective-permute-start.19 = (bf16[128,896]{1,0:T(8,128)(2,1)S(1)}, bf16[128,896]{1,0:T(8,128)(2,1)S(1)}, u32[]{:S(2)}, u32[]{:S(2)}) collective-permute-start(bf16[128,896]{1,0:T(8,128)(2,1)S(1)} %get-tuple-element.43), channel_id=1, source_target_pairs={{0,1},{1,0},{2,3},{3,2},{4,5},{5,4},{6,7},{7,6},{8,9},{9,8},{10,11... | collective-permute-start | bytes 688136 | tf_op jit(solution)/shard_map/ppermute | solution.py:147
  6.7 2.6 %collective-permute-start.27 = (bf16[128,896]{1,0:T(8,128)(2,1)S(1)}, bf16[128,896]{1,0:T(8,128)(2,1)S(1)}, u32[]{:S(2)}, u32[]{:S(2)}) collective-permute-start(bf16[128,896]{1,0:T(8,128)(2,1)S(1)} %get-tuple-element.50), channel_id=1, source_target_pairs={{0,2},{1,3},{2,0},{3,1},{4,6},{5,7},{6,4},{7,5},{8,10},{9,11},{10,... | collective-permute-start | bytes 688136 | tf_op jit(solution)/shard_map/ppermute | solution.py:147
  9.3 1.9 %collective-permute-start.8 = (bf16[128,896]{1,0:T(8,128)(2,1)}, bf16[128,896]{1,0:T(8,128)(2,1)S(1)}, u32[]{:S(2)}, u32[]{:S(2)}) collective-permute-start(bf16[128,896]{1,0:T(8,128)(2,1)} %bitcast.57), channel_id=1, source_target_pairs={{0,2},{1,3},{2,0},{3,1},{4,6},{5,7},{6,4},{7,5},{8,10},{9,11},{10,... | collective-permute-start | bytes 688136 | tf_op jit(solution)/shard_map/ppermute | solution.py:147
  11.2 1.9 %collective-permute-start.9 = (bf16[128,896]{1,0:T(8,128)(2,1)}, bf16[128,896]{1,0:T(8,128)(2,1)S(1)}, u32[]{:S(2)}, u32[]{:S(2)}) collective-permute-start(bf16[128,896]{1,0:T(8,128)(2,1)} %bitcast.58), channel_id=1, source_target_pairs={{0,3},{1,2},{2,1},{3,0},{4,7},{5,6},{6,5},{7,4},{8,11},{9,10},{10,... | collective-permute-start | bytes 688136 | tf_op jit(solution)/shard_map/ppermute | solution.py:147
  13.1 3.3 %collective-permute-done.19.refs_1_ = bf16[128,896]{1,0:T(8,128)(2,1)S(1)} collective-permute-done((bf16[128,896]{1,0:T(8,128)(2,1)S(1)}, bf16[128,896]{1,0:T(8,128)(2,1)S(1)}, u32[]{:S(2)}, u32[]{:S(2)}) %collective-permute-start.19) | collective-permute-done | bytes 229408 | tf_op jit(solution)/shard_map/ppermute | solution.py:147
  16.4 1.5 %copy-done.2 = bf16[1,1,1024,896]{3,2,1,0:T(8,128)(2,1)S(1)} copy-done((bf16[1,1,1024,896]{3,2,1,0:T(8,128)(2,1)S(1)}, bf16[1,1,1024,896]{3,2,1,0:T(8,128)(2,1)}, u32[]{:S(2)}) %copy-start.2) | copy-done | bytes 1835032
  17.9 2.1 %shard_map.127 = (bf16[64,1024]{1,0:T(8,128)(2,1)S(1)}, bf16[64,1024]{1,0:T(8,128)(2,1)S(1)}, bf16[64,1024]{1,0:T(8,128)(2,1)S(1)}, bf16[64,1024]{1,0:T(8,128)(2,1)S(1)}) custom-call(s32[2]{0:T(128)S(1)} %pad_add_fusion.place_ref, bf16[128,896]{1,0:T(8,128)(2,1)S(1)} %get-tuple-element.42.refs_0_, bf16[128,896]{1,0:T(8,128)(2,1)S(1)} %collective-permute-done.19.refs_1_, ...), custom_call_target="tpu_custom_call" | custom-call | flops 469762048 | bytes 2818048 | tf_op jit(solution)/shard_map/pallas_call | solution.py:151
  20.0 15.8 %collective-permute-done.27.refs_0_ = bf16[128,896]{1,0:T(8,128)(2,1)S(1)} collective-permute-done((bf16[128,896]{1,0:T(8,128)(2,1)S(1)}, bf16[128,896]{1,0:T(8,128)(2,1)S(1)}, u32[]{:S(2)}, u32[]{:S(2)}) %collective-permute-start.27) | collective-permute-done | bytes 229408 | tf_op jit(solution)/shard_map/ppermute | solution.py:147
  35.8 2.4 %collective-permute-start.22 = (bf16[64,1024]{1,0:T(8,128)(2,1)S(1)}, bf16[64,1024]{1,0:T(8,128)(2,1)S(1)}, u32[]{:S(2)}, u32[]{:S(2)}) collective-permute-start(bf16[64,1024]{1,0:T(8,128)(2,1)S(1)} %get-tuple-element.47), channel_id=1, source_target_pairs={{0,12},{4,8},{8,4},{12,0},{1,13},{5,9},{9,5},{13,1},{2,14},{6,10},... | collective-permute-start | bytes 393224 | tf_op jit(solution)/shard_map/ppermute | solution.py:147
  38.8 2.1 %shard_map.129 = (bf16[64,1024]{1,0:T(8,128)(2,1)S(1)}, bf16[64,1024]{1,0:T(8,128)(2,1)S(1)}, bf16[64,1024]{1,0:T(8,128)(2,1)S(1)}, bf16[64,1024]{1,0:T(8,128)(2,1)S(1)}) custom-call(s32[2]{0:T(128)S(1)} %pad_add_fusion.place_ref, bf16[128,896]{1,0:T(8,128)(2,1)S(1)} %collective-permute-done.27.refs_0_, ...), custom_call_target="tpu_custom_call" | custom-call | flops 469762048 | bytes 2818048 | tf_op jit(solution)/shard_map/pallas_call | solution.py:151
  40.8 4.8 %collective-permute-done.8.refs_0_ = bf16[128,896]{1,0:T(8,128)(2,1)S(1)} collective-permute-done((bf16[128,896]{1,0:T(8,128)(2,1)}, bf16[128,896]{1,0:T(8,128)(2,1)S(1)}, u32[]{:S(2)}, u32[]{:S(2)}) %collective-permute-start.8) | collective-permute-done | bytes 229408 | tf_op jit(solution)/shard_map/ppermute | solution.py:147
  45.6 1.5 %collective-permute-start.20 = (bf16[64,1024]{1,0:T(8,128)(2,1)S(1)}, bf16[64,1024]{1,0:T(8,128)(2,1)S(1)}, u32[]{:S(2)}, u32[]{:S(2)}) collective-permute-start(bf16[64,1024]{1,0:T(8,128)(2,1)S(1)} %get-tuple-element.45), channel_id=1, source_target_pairs={{0,4},{4,0},{8,12},{12,8},{1,5},{5,1},{9,13},{13,9},{2,6},{6,2},{1... | collective-permute-start | bytes 393224 | tf_op jit(solution)/shard_map/ppermute | solution.py:147
  48.6 3.0 %shard_map.124 = (bf16[2,64,1024]{2,1,0:T(8,128)(2,1)S(1)}, bf16[2,64,1024]{2,1,0:T(8,128)(2,1)S(1)}, bf16[2,64,1024]{2,1,0:T(8,128)(2,1)S(1)}, bf16[2,64,1024]{2,1,0:T(8,128)(2,1)S(1)}) custom-call(s32[2]{0:T(128)S(1)} %pad_add_fusion.place_ref, bf16[128,896]{1,0:T(8,128)(2,1)S(1)} %collective-permute-done.8.refs_0_, ...), custom_call_target="tpu_custom_call" | custom-call | flops 939524096 | bytes 5177344 | tf_op jit(solution)/shard_map/pallas_call | solution.py:151
  51.6 1.5 %collective-permute-start.12 = (bf16[2,64,1024]{2,1,0:T(8,128)(2,1)S(1)}, bf16[2,64,1024]{2,1,0:T(8,128)(2,1)S(1)}, u32[]{:S(2)}, u32[]{:S(2)}) collective-permute-start(bf16[2,64,1024]{2,1,0:T(8,128)(2,1)S(1)} %get-tuple-element.39), channel_id=1, source_target_pairs={{0,12},{4,8},{8,4},{12,0},{1,13},{5,9},{9,5},{13,1},{2,14},{6,10},... | collective-permute-start | bytes 786440 | tf_op jit(solution)/shard_map/ppermute | solution.py:147
  53.1 3.0 %shard_map.122 = (bf16[2,64,1024]{2,1,0:T(8,128)(2,1)S(1)}, bf16[2,64,1024]{2,1,0:T(8,128)(2,1)S(1)}, bf16[2,64,1024]{2,1,0:T(8,128)(2,1)S(1)}, bf16[2,64,1024]{2,1,0:T(8,128)(2,1)S(1)}) custom-call(s32[2]{0:T(128)S(1)} %pad_add_fusion.place_ref, bf16[128,896]{1,0:T(8,128)(2,1)S(1)} %bitcast.60, bf16[128,896]{1,0:T(8,128)(2,1)S(1)} %collective-permute-done.refs_1_, ...), custom_call_target="tpu_custom_call" | custom-call | flops 939524096 | bytes 5177344 | tf_op jit(solution)/shard_map/pallas_call | solution.py:151
  56.2 1.6 %collective-permute-start.11 = (bf16[2,64,1024]{2,1,0:T(8,128)(2,1)S(1)}, bf16[2,64,1024]{2,1,0:T(8,128)(2,1)S(1)}, u32[]{:S(2)}, u32[]{:S(2)}) collective-permute-start(bf16[2,64,1024]{2,1,0:T(8,128)(2,1)S(1)} %get-tuple-element.38), channel_id=1, source_target_pairs={{0,8},{4,12},{8,0},{12,4},{1,9},{5,13},{9,1},{13,5},{2,10},{6,14},... | collective-permute-start | bytes 786440 | tf_op jit(solution)/shard_map/ppermute | solution.py:147
  60.4 6.7 %collective-permute-done.30 = bf16[64,1024]{1,0:T(8,128)(2,1)S(1)} collective-permute-done((bf16[64,1024]{1,0:T(8,128)(2,1)S(1)}, bf16[64,1024]{1,0:T(8,128)(2,1)S(1)}, u32[]{:S(2)}, u32[]{:S(2)}) %collective-permute-start.30) | collective-permute-done | bytes 131104 | tf_op jit(solution)/shard_map/ppermute | solution.py:147
  72.9 4.3 %collective-permute-done.3 = bf16[2,64,1024]{2,1,0:T(8,128)(2,1)S(1)} collective-permute-done((bf16[2,64,1024]{2,1,0:T(8,128)(2,1)S(1)}, bf16[2,64,1024]{2,1,0:T(8,128)(2,1)S(1)}, u32[]{:S(2)}, u32[]{:S(2)}) %collective-permute-start.3) | collective-permute-done | bytes 262176 | tf_op jit(solution)/shard_map/ppermute | solution.py:147
  78.7 2.3 %collective-permute-done.2 = bf16[2,64,1024]{2,1,0:T(8,128)(2,1)S(1)} collective-permute-done((bf16[2,64,1024]{2,1,0:T(8,128)(2,1)S(1)}, bf16[2,64,1024]{2,1,0:T(8,128)(2,1)S(1)}, u32[]{:S(2)}, u32[]{:S(2)}) %collective-permute-start.2) | collective-permute-done | bytes 262176 | tf_op jit(solution)/shard_map/ppermute | solution.py:147
  85.0 2.0 %collective-permute-start.34 = (bf16[64,1024]{1,0:T(8,128)(2,1)S(1)}, bf16[64,1024]{1,0:T(8,128)(2,1)S(1)}, u32[]{:S(2)}, u32[]{:S(2)}) collective-permute-start(bf16[64,1024]{1,0:T(8,128)(2,1)S(1)} %add_convert_fusion.1.refs_0_), channel_id=1, source_target_pairs={{0,12},{4,8},{8,4},{12,0},{1,13},{5,9},{9,5},{13,1},{2,14},{6,10},... | collective-permute-start | bytes 393224 | tf_op jit(solution)/shard_map/ppermute | solution.py:147
  89.4 3.8 %shard_map.128 = (bf16[128,896]{1,0:T(8,128)(2,1)S(1)}, bf16[128,896]{1,0:T(8,128)(2,1)S(1)}) custom-call(s32[2]{0:T(128)S(1)} %pad_add_fusion.place_ref, bf16[64,1024]{1,0:T(8,128)(2,1)S(1)} %add_convert_fusion.2.refs_0_, bf16[64,1024]{1,0:T(8,128)(2,1)S(1)} %collective-permute-done.23.refs_1_, bf16[64,1024]{1,0:T(8,128)(2,1)S(1)} %collective-permute-done.24.refs_2_, ...), custom_call_target="tpu_custom_call" | custom-call | flops 939524096 | bytes 5767168 | tf_op jit(solution)/shard_map/pallas_call | solution.py:151
  93.3 2.1 %collective-permute-start.15 = (bf16[64,1024]{1,0:T(8,128)(2,1)S(1)}, bf16[64,1024]{1,0:T(8,128)(2,1)S(1)}, u32[]{:S(2)}, u32[]{:S(2)}) collective-permute-start(bf16[64,1024]{1,0:T(8,128)(2,1)S(1)} %fusion.1.refs_0_), channel_id=1, source_target_pairs={{0,12},{4,8},{8,4},{12,0},{1,13},{5,9},{9,5},{13,1},{2,14},{6,10},... | collective-permute-start | bytes 393224 | tf_op jit(solution)/shard_map/ppermute | solution.py:147
  95.4 3.2 %collective-permute-start.26 = (bf16[128,896]{1,0:T(8,128)(2,1)S(1)}, bf16[128,896]{1,0:T(8,128)(2,1)S(1)}, u32[]{:S(2)}, u32[]{:S(2)}) collective-permute-start(bf16[128,896]{1,0:T(8,128)(2,1)S(1)} %get-tuple-element.49), channel_id=1, source_target_pairs={{0,1},{1,0},{2,3},{3,2},{4,5},{5,4},{6,7},{7,6},{8,9},{9,8},{10,11... | collective-permute-start | bytes 688136 | tf_op jit(solution)/shard_map/ppermute | solution.py:147
  98.7 1.5 %collective-permute-start.4 = (bf16[64,1024]{1,0:T(8,128)(2,1)S(1)}, bf16[64,1024]{1,0:T(8,128)(2,1)S(1)}, u32[]{:S(2)}, u32[]{:S(2)}) collective-permute-start(bf16[64,1024]{1,0:T(8,128)(2,1)S(1)} %fusion.3.refs_0_), channel_id=1, source_target_pairs={{0,4},{4,0},{8,12},{12,8},{1,5},{5,1},{9,13},{13,9},{2,6},{6,2},{1... | collective-permute-start | bytes 393224 | tf_op jit(solution)/shard_map/ppermute | solution.py:147
  102.3 3.9 %shard_map.130 = (bf16[128,896]{1,0:T(8,128)(2,1)S(1)}, bf16[128,896]{1,0:T(8,128)(2,1)S(1)}) custom-call(s32[2]{0:T(128)S(1)} %pad_add_fusion.place_ref, bf16[64,1024]{1,0:T(8,128)(2,1)S(1)} %add_convert_fusion.1.refs_0_, bf16[64,1024]{1,0:T(8,128)(2,1)S(1)} %collective-permute-done.32.refs_1_, bf16[64,1024]{1,0:T(8,128)(2,1)S(1)} %collective-permute-done.33.refs_2_, ...), custom_call_target="tpu_custom_call" | custom-call | flops 939524096 | bytes 5767168 | tf_op jit(solution)/shard_map/pallas_call | solution.py:151
  107.3 2.3 %shard_map.125 = (bf16[128,896]{1,0:T(8,128)(2,1)S(1)}, bf16[128,896]{1,0:T(8,128)(2,1)S(1)}) custom-call(s32[2]{0:T(128)S(1)} %pad_add_fusion.place_ref, bf16[64,1024]{1,0:T(8,128)(2,1)S(1)} %fusion.1.refs_0_, bf16[64,1024]{1,0:T(8,128)(2,1)S(1)} %collective-permute-done.13.refs_1_, bf16[64,1024]{1,0:T(8,128)(2,1)S(1)} %collective-permute-done.14.refs_2_, ...), custom_call_target="tpu_custom_call" | custom-call | flops 469762048 | bytes 2818048 | tf_op jit(solution)/shard_map/pallas_call | solution.py:151
  109.6 1.5 %collective-permute-start.36 = (bf16[128,896]{1,0:T(8,128)(2,1)S(1)}, bf16[128,896]{1,0:T(8,128)(2,1)S(1)}, u32[]{:S(2)}, u32[]{:S(2)}) collective-permute-start(bf16[128,896]{1,0:T(8,128)(2,1)S(1)} %get-tuple-element.57), channel_id=1, source_target_pairs={{0,3},{1,2},{2,1},{3,0},{4,7},{5,6},{6,5},{7,4},{8,11},{9,10},{10,... | collective-permute-start | bytes 688136 | tf_op jit(solution)/shard_map/ppermute | solution.py:147
  111.2 2.4 %collective-permute-start.17 = (bf16[128,896]{1,0:T(8,128)(2,1)S(1)}, bf16[128,896]{1,0:T(8,128)(2,1)S(1)}, u32[]{:S(2)}, u32[]{:S(2)}) collective-permute-start(bf16[128,896]{1,0:T(8,128)(2,1)S(1)} %get-tuple-element.41), channel_id=1, source_target_pairs={{0,3},{1,2},{2,1},{3,0},{4,7},{5,6},{6,5},{7,4},{8,11},{9,10},{10,... | collective-permute-start | bytes 688136 | tf_op jit(solution)/shard_map/ppermute | solution.py:147
  113.6 2.3 %shard_map.123 = (bf16[128,896]{1,0:T(8,128)(2,1)S(1)}, bf16[128,896]{1,0:T(8,128)(2,1)S(1)}) custom-call(s32[2]{0:T(128)S(1)} %pad_add_fusion.place_ref, bf16[64,1024]{1,0:T(8,128)(2,1)S(1)} %fusion.3.refs_0_, bf16[64,1024]{1,0:T(8,128)(2,1)S(1)} %collective-permute-done.4.refs_1_, bf16[64,1024]{1,0:T(8,128)(2,1)S(1)} %collective-permute-done.5.refs_2_, ...), custom_call_target="tpu_custom_call" | custom-call | flops 469762048 | bytes 2818048 | tf_op jit(solution)/shard_map/pallas_call | solution.py:151
  116.0 2.0 %collective-permute-start.7 = (bf16[128,896]{1,0:T(8,128)(2,1)S(1)}, bf16[128,896]{1,0:T(8,128)(2,1)}, u32[]{:S(2)}, u32[]{:S(2)}) collective-permute-start(bf16[128,896]{1,0:T(8,128)(2,1)S(1)} %get-tuple-element.35), channel_id=1, source_target_pairs={{0,1},{1,0},{2,3},{3,2},{4,5},{5,4},{6,7},{7,6},{8,9},{9,8},{10,11... | collective-permute-start | bytes 688136 | tf_op jit(solution)/shard_map/ppermute | solution.py:147
  118.1 14.0 %collective-permute-done.35.refs_2_ = bf16[128,896]{1,0:T(8,128)(2,1)S(1)} collective-permute-done((bf16[128,896]{1,0:T(8,128)(2,1)S(1)}, bf16[128,896]{1,0:T(8,128)(2,1)S(1)}, u32[]{:S(2)}, u32[]{:S(2)}) %collective-permute-start.35) | collective-permute-done | bytes 229408 | tf_op jit(solution)/shard_map/ppermute | solution.py:147
  133.3 10.8 %collective-permute-done.16 = bf16[128,896]{1,0:T(8,128)(2,1)S(1)} collective-permute-done((bf16[128,896]{1,0:T(8,128)(2,1)S(1)}, bf16[128,896]{1,0:T(8,128)(2,1)S(1)}, u32[]{:S(2)}, u32[]{:S(2)}) %collective-permute-start.16) | collective-permute-done | bytes 229408 | tf_op jit(solution)/shard_map/ppermute | solution.py:147
  (92 shorter events, 30.1 us)
Async XLA Ops:
  3.6 12.8 %collective-permute-start.19 = (bf16[128,896]{1,0:T(8,128)(2,1)S(1)}, bf16[128,896]{1,0:T(8,128)(2,1)S(1)}, u32[]{:S(2)}, u32[]{:S(2)}) collective-permute-start(bf16[128,896]{1,0:T(8,128)(2,1)S(1)} %get-tuple-element.43), channel_id=1, source_target_pairs={{0,1},{1,0},{2,3},{3,2},{4,5},{5,4},{6,7},{7,6},{8,9},{9,8},{10,11... | collective-permute-start | bytes 688136 | tf_op jit(solution)/shard_map/ppermute | solution.py:147
  6.7 29.1 %collective-permute-start.27 = (bf16[128,896]{1,0:T(8,128)(2,1)S(1)}, bf16[128,896]{1,0:T(8,128)(2,1)S(1)}, u32[]{:S(2)}, u32[]{:S(2)}) collective-permute-start(bf16[128,896]{1,0:T(8,128)(2,1)S(1)} %get-tuple-element.50), channel_id=1, source_target_pairs={{0,2},{1,3},{2,0},{3,1},{4,6},{5,7},{6,4},{7,5},{8,10},{9,11},{10,... | collective-permute-start | bytes 688136 | tf_op jit(solution)/shard_map/ppermute | solution.py:147
  9.2 29.0 %collective-permute-start.28 = (bf16[128,896]{1,0:T(8,128)(2,1)S(1)}, bf16[128,896]{1,0:T(8,128)(2,1)S(1)}, u32[]{:S(2)}, u32[]{:S(2)}) collective-permute-start(bf16[128,896]{1,0:T(8,128)(2,1)S(1)} %get-tuple-element.51), channel_id=1, source_target_pairs={{0,3},{1,2},{2,1},{3,0},{4,7},{5,6},{6,5},{7,4},{8,11},{9,10},{10,... | collective-permute-start | bytes 688136 | tf_op jit(solution)/shard_map/ppermute | solution.py:147
  9.3 36.4 %collective-permute-start.8 = (bf16[128,896]{1,0:T(8,128)(2,1)}, bf16[128,896]{1,0:T(8,128)(2,1)S(1)}, u32[]{:S(2)}, u32[]{:S(2)}) collective-permute-start(bf16[128,896]{1,0:T(8,128)(2,1)} %bitcast.57), channel_id=1, source_target_pairs={{0,2},{1,3},{2,0},{3,1},{4,6},{5,7},{6,4},{7,5},{8,10},{9,11},{10,... | collective-permute-start | bytes 688136 | tf_op jit(solution)/shard_map/ppermute | solution.py:147
  11.2 36.0 %collective-permute-start.9 = (bf16[128,896]{1,0:T(8,128)(2,1)}, bf16[128,896]{1,0:T(8,128)(2,1)S(1)}, u32[]{:S(2)}, u32[]{:S(2)}) collective-permute-start(bf16[128,896]{1,0:T(8,128)(2,1)} %bitcast.58), channel_id=1, source_target_pairs={{0,3},{1,2},{2,1},{3,0},{4,7},{5,6},{6,5},{7,4},{8,11},{9,10},{10,... | collective-permute-start | bytes 688136 | tf_op jit(solution)/shard_map/ppermute | solution.py:147
  16.4 35.2 %collective-permute-start = (bf16[128,896]{1,0:T(8,128)(2,1)}, bf16[128,896]{1,0:T(8,128)(2,1)S(1)}, u32[]{:S(2)}, u32[]{:S(2)}) collective-permute-start(bf16[128,896]{1,0:T(8,128)(2,1)} %bitcast.59), channel_id=1, source_target_pairs={{0,1},{1,0},{2,3},{3,2},{4,5},{5,4},{6,7},{7,6},{8,9},{9,8},{10,11... | collective-permute-start | bytes 688136 | tf_op jit(solution)/shard_map/ppermute | solution.py:147
  35.8 20.4 %collective-permute-start.22 = (bf16[64,1024]{1,0:T(8,128)(2,1)S(1)}, bf16[64,1024]{1,0:T(8,128)(2,1)S(1)}, u32[]{:S(2)}, u32[]{:S(2)}) collective-permute-start(bf16[64,1024]{1,0:T(8,128)(2,1)S(1)} %get-tuple-element.47), channel_id=1, source_target_pairs={{0,12},{4,8},{8,4},{12,0},{1,13},{5,9},{9,5},{13,1},{2,14},{6,10},... | collective-permute-start | bytes 393224 | tf_op jit(solution)/shard_map/ppermute | solution.py:147
  38.2 19.5 %collective-permute-start.21 = (bf16[64,1024]{1,0:T(8,128)(2,1)S(1)}, bf16[64,1024]{1,0:T(8,128)(2,1)S(1)}, u32[]{:S(2)}, u32[]{:S(2)}) collective-permute-start(bf16[64,1024]{1,0:T(8,128)(2,1)S(1)} %get-tuple-element.46), channel_id=1, source_target_pairs={{0,8},{4,12},{8,0},{12,4},{1,9},{5,13},{9,1},{13,5},{2,10},{6,14},... | collective-permute-start | bytes 393224 | tf_op jit(solution)/shard_map/ppermute | solution.py:147
  45.6 12.7 %collective-permute-start.20 = (bf16[64,1024]{1,0:T(8,128)(2,1)S(1)}, bf16[64,1024]{1,0:T(8,128)(2,1)S(1)}, u32[]{:S(2)}, u32[]{:S(2)}) collective-permute-start(bf16[64,1024]{1,0:T(8,128)(2,1)S(1)} %get-tuple-element.45), channel_id=1, source_target_pairs={{0,4},{4,0},{8,12},{12,8},{1,5},{5,1},{9,13},{13,9},{2,6},{6,2},{1... | collective-permute-start | bytes 393224 | tf_op jit(solution)/shard_map/ppermute | solution.py:147
  47.1 11.7 %collective-permute-start.31 = (bf16[64,1024]{1,0:T(8,128)(2,1)S(1)}, bf16[64,1024]{1,0:T(8,128)(2,1)S(1)}, u32[]{:S(2)}, u32[]{:S(2)}) collective-permute-start(bf16[64,1024]{1,0:T(8,128)(2,1)S(1)} %get-tuple-element.55), channel_id=1, source_target_pairs={{0,12},{4,8},{8,4},{12,0},{1,13},{5,9},{9,5},{13,1},{2,14},{6,10},... | collective-permute-start | bytes 393224 | tf_op jit(solution)/shard_map/ppermute | solution.py:147
  51.6 18.4 %collective-permute-start.12 = (bf16[2,64,1024]{2,1,0:T(8,128)(2,1)S(1)}, bf16[2,64,1024]{2,1,0:T(8,128)(2,1)S(1)}, u32[]{:S(2)}, u32[]{:S(2)}) collective-permute-start(bf16[2,64,1024]{2,1,0:T(8,128)(2,1)S(1)} %get-tuple-element.39), channel_id=1, source_target_pairs={{0,12},{4,8},{8,4},{12,0},{1,13},{5,9},{9,5},{13,1},{2,14},{6,10},... | collective-permute-start | bytes 786440 | tf_op jit(solution)/shard_map/ppermute | solution.py:147
  56.2 14.5 %collective-permute-start.11 = (bf16[2,64,1024]{2,1,0:T(8,128)(2,1)S(1)}, bf16[2,64,1024]{2,1,0:T(8,128)(2,1)S(1)}, u32[]{:S(2)}, u32[]{:S(2)}) collective-permute-start(bf16[2,64,1024]{2,1,0:T(8,128)(2,1)S(1)} %get-tuple-element.38), channel_id=1, source_target_pairs={{0,8},{4,12},{8,0},{12,4},{1,9},{5,13},{9,1},{13,5},{2,10},{6,14},... | collective-permute-start | bytes 786440 | tf_op jit(solution)/shard_map/ppermute | solution.py:147
  57.7 14.4 %collective-permute-start.10 = (bf16[2,64,1024]{2,1,0:T(8,128)(2,1)S(1)}, bf16[2,64,1024]{2,1,0:T(8,128)(2,1)S(1)}, u32[]{:S(2)}, u32[]{:S(2)}) collective-permute-start(bf16[2,64,1024]{2,1,0:T(8,128)(2,1)S(1)} %get-tuple-element.37), channel_id=1, source_target_pairs={{0,4},{4,0},{8,12},{12,8},{1,5},{5,1},{9,13},{13,9},{2,6},{6,2},{1... | collective-permute-start | bytes 786440 | tf_op jit(solution)/shard_map/ppermute | solution.py:147
  68.5 12.5 %collective-permute-start.2 = (bf16[2,64,1024]{2,1,0:T(8,128)(2,1)S(1)}, bf16[2,64,1024]{2,1,0:T(8,128)(2,1)S(1)}, u32[]{:S(2)}, u32[]{:S(2)}) collective-permute-start(bf16[2,64,1024]{2,1,0:T(8,128)(2,1)S(1)} %get-tuple-element.32), channel_id=1, source_target_pairs={{0,8},{4,12},{8,0},{12,4},{1,9},{5,13},{9,1},{13,5},{2,10},{6,14},... | collective-permute-start | bytes 786440 | tf_op jit(solution)/shard_map/ppermute | solution.py:147
  70.0 12.2 %collective-permute-start.1 = (bf16[2,64,1024]{2,1,0:T(8,128)(2,1)S(1)}, bf16[2,64,1024]{2,1,0:T(8,128)(2,1)S(1)}, u32[]{:S(2)}, u32[]{:S(2)}) collective-permute-start(bf16[2,64,1024]{2,1,0:T(8,128)(2,1)S(1)} %get-tuple-element.31), channel_id=1, source_target_pairs={{0,4},{4,0},{8,12},{12,8},{1,5},{5,1},{9,13},{13,9},{2,6},{6,2},{1... | collective-permute-start | bytes 786440 | tf_op jit(solution)/shard_map/ppermute | solution.py:147
  70.7 14.3 %collective-permute-start.23 = (bf16[64,1024]{1,0:T(8,128)(2,1)S(1)}, bf16[64,1024]{1,0:T(8,128)(2,1)S(1)}, u32[]{:S(2)}, u32[]{:S(2)}) collective-permute-start(bf16[64,1024]{1,0:T(8,128)(2,1)S(1)} %add_convert_fusion.2.refs_0_), channel_id=1, source_target_pairs={{0,4},{4,0},{8,12},{12,8},{1,5},{5,1},{9,13},{13,9},{2,6},{6,2},{1... | collective-permute-start | bytes 393224 | tf_op jit(solution)/shard_map/ppermute | solution.py:147
  72.1 14.9 %collective-permute-start.24 = (bf16[64,1024]{1,0:T(8,128)(2,1)S(1)}, bf16[64,1024]{1,0:T(8,128)(2,1)S(1)}, u32[]{:S(2)}, u32[]{:S(2)}) collective-permute-start(bf16[64,1024]{1,0:T(8,128)(2,1)S(1)} %add_convert_fusion.2.refs_0_), channel_id=1, source_target_pairs={{0,8},{4,12},{8,0},{12,4},{1,9},{5,13},{9,1},{13,5},{2,10},{6,14},... | collective-permute-start | bytes 393224 | tf_op jit(solution)/shard_map/ppermute | solution.py:147
  77.2 11.3 %collective-permute-start.25 = (bf16[64,1024]{1,0:T(8,128)(2,1)S(1)}, bf16[64,1024]{1,0:T(8,128)(2,1)S(1)}, u32[]{:S(2)}, u32[]{:S(2)}) collective-permute-start(bf16[64,1024]{1,0:T(8,128)(2,1)S(1)} %add_convert_fusion.2.refs_0_), channel_id=1, source_target_pairs={{0,12},{4,8},{8,4},{12,0},{1,13},{5,9},{9,5},{13,1},{2,14},{6,10},... | collective-permute-start | bytes 393224 | tf_op jit(solution)/shard_map/ppermute | solution.py:147
  81.0 12.2 %collective-permute-start.32 = (bf16[64,1024]{1,0:T(8,128)(2,1)S(1)}, bf16[64,1024]{1,0:T(8,128)(2,1)S(1)}, u32[]{:S(2)}, u32[]{:S(2)}) collective-permute-start(bf16[64,1024]{1,0:T(8,128)(2,1)S(1)} %add_convert_fusion.1.refs_0_), channel_id=1, source_target_pairs={{0,4},{4,0},{8,12},{12,8},{1,5},{5,1},{9,13},{13,9},{2,6},{6,2},{1... | collective-permute-start | bytes 393224 | tf_op jit(solution)/shard_map/ppermute | solution.py:147
  82.2 13.1 %collective-permute-start.33 = (bf16[64,1024]{1,0:T(8,128)(2,1)S(1)}, bf16[64,1024]{1,0:T(8,128)(2,1)S(1)}, u32[]{:S(2)}, u32[]{:S(2)}) collective-permute-start(bf16[64,1024]{1,0:T(8,128)(2,1)S(1)} %add_convert_fusion.1.refs_0_), channel_id=1, source_target_pairs={{0,8},{4,12},{8,0},{12,4},{1,9},{5,13},{9,1},{13,5},{2,10},{6,14},... | collective-permute-start | bytes 393224 | tf_op jit(solution)/shard_map/ppermute | solution.py:147
  85.0 13.7 %collective-permute-start.34 = (bf16[64,1024]{1,0:T(8,128)(2,1)S(1)}, bf16[64,1024]{1,0:T(8,128)(2,1)S(1)}, u32[]{:S(2)}, u32[]{:S(2)}) collective-permute-start(bf16[64,1024]{1,0:T(8,128)(2,1)S(1)} %add_convert_fusion.1.refs_0_), channel_id=1, source_target_pairs={{0,12},{4,8},{8,4},{12,0},{1,13},{5,9},{9,5},{13,1},{2,14},{6,10},... | collective-permute-start | bytes 393224 | tf_op jit(solution)/shard_map/ppermute | solution.py:147
  87.1 13.2 %collective-permute-start.13 = (bf16[64,1024]{1,0:T(8,128)(2,1)S(1)}, bf16[64,1024]{1,0:T(8,128)(2,1)S(1)}, u32[]{:S(2)}, u32[]{:S(2)}) collective-permute-start(bf16[64,1024]{1,0:T(8,128)(2,1)S(1)} %fusion.1.refs_0_), channel_id=1, source_target_pairs={{0,4},{4,0},{8,12},{12,8},{1,5},{5,1},{9,13},{13,9},{2,6},{6,2},{1... | collective-permute-start | bytes 393224 | tf_op jit(solution)/shard_map/ppermute | solution.py:147
  88.5 12.3 %collective-permute-start.14 = (bf16[64,1024]{1,0:T(8,128)(2,1)S(1)}, bf16[64,1024]{1,0:T(8,128)(2,1)S(1)}, u32[]{:S(2)}, u32[]{:S(2)}) collective-permute-start(bf16[64,1024]{1,0:T(8,128)(2,1)S(1)} %fusion.1.refs_0_), channel_id=1, source_target_pairs={{0,8},{4,12},{8,0},{12,4},{1,9},{5,13},{9,1},{13,5},{2,10},{6,14},... | collective-permute-start | bytes 393224 | tf_op jit(solution)/shard_map/ppermute | solution.py:147
  93.3 12.9 %collective-permute-start.15 = (bf16[64,1024]{1,0:T(8,128)(2,1)S(1)}, bf16[64,1024]{1,0:T(8,128)(2,1)S(1)}, u32[]{:S(2)}, u32[]{:S(2)}) collective-permute-start(bf16[64,1024]{1,0:T(8,128)(2,1)S(1)} %fusion.1.refs_0_), channel_id=1, source_target_pairs={{0,12},{4,8},{8,4},{12,0},{1,13},{5,9},{9,5},{13,1},{2,14},{6,10},... | collective-permute-start | bytes 393224 | tf_op jit(solution)/shard_map/ppermute | solution.py:147
  95.4 20.6 %collective-permute-start.26 = (bf16[128,896]{1,0:T(8,128)(2,1)S(1)}, bf16[128,896]{1,0:T(8,128)(2,1)S(1)}, u32[]{:S(2)}, u32[]{:S(2)}) collective-permute-start(bf16[128,896]{1,0:T(8,128)(2,1)S(1)} %get-tuple-element.49), channel_id=1, source_target_pairs={{0,1},{1,0},{2,3},{3,2},{4,5},{5,4},{6,7},{7,6},{8,9},{9,8},{10,11... | collective-permute-start | bytes 688136 | tf_op jit(solution)/shard_map/ppermute | solution.py:147
  100.8 12.7 %collective-permute-start.6 = (bf16[64,1024]{1,0:T(8,128)(2,1)S(1)}, bf16[64,1024]{1,0:T(8,128)(2,1)S(1)}, u32[]{:S(2)}, u32[]{:S(2)}) collective-permute-start(bf16[64,1024]{1,0:T(8,128)(2,1)S(1)} %fusion.3.refs_0_), channel_id=1, source_target_pairs={{0,12},{4,8},{8,4},{12,0},{1,13},{5,9},{9,5},{13,1},{2,14},{6,10},... | collective-permute-start | bytes 393224 | tf_op jit(solution)/shard_map/ppermute | solution.py:147
  106.2 25.9 %collective-permute-start.35 = (bf16[128,896]{1,0:T(8,128)(2,1)S(1)}, bf16[128,896]{1,0:T(8,128)(2,1)S(1)}, u32[]{:S(2)}, u32[]{:S(2)}) collective-permute-start(bf16[128,896]{1,0:T(8,128)(2,1)S(1)} %get-tuple-element.56), channel_id=1, source_target_pairs={{0,2},{1,3},{2,0},{3,1},{4,6},{5,7},{6,4},{7,5},{8,10},{9,11},{10,... | collective-permute-start | bytes 688136 | tf_op jit(solution)/shard_map/ppermute | solution.py:147
  109.6 22.5 %collective-permute-start.36 = (bf16[128,896]{1,0:T(8,128)(2,1)S(1)}, bf16[128,896]{1,0:T(8,128)(2,1)S(1)}, u32[]{:S(2)}, u32[]{:S(2)}) collective-permute-start(bf16[128,896]{1,0:T(8,128)(2,1)S(1)} %get-tuple-element.57), channel_id=1, source_target_pairs={{0,3},{1,2},{2,1},{3,0},{4,7},{5,6},{6,5},{7,4},{8,11},{9,10},{10,... | collective-permute-start | bytes 688136 | tf_op jit(solution)/shard_map/ppermute | solution.py:147
  111.2 22.2 %collective-permute-start.17 = (bf16[128,896]{1,0:T(8,128)(2,1)S(1)}, bf16[128,896]{1,0:T(8,128)(2,1)S(1)}, u32[]{:S(2)}, u32[]{:S(2)}) collective-permute-start(bf16[128,896]{1,0:T(8,128)(2,1)S(1)} %get-tuple-element.41), channel_id=1, source_target_pairs={{0,3},{1,2},{2,1},{3,0},{4,7},{5,6},{6,5},{7,4},{8,11},{9,10},{10,... | collective-permute-start | bytes 688136 | tf_op jit(solution)/shard_map/ppermute | solution.py:147
  113.5 30.7 %collective-permute-start.16 = (bf16[128,896]{1,0:T(8,128)(2,1)S(1)}, bf16[128,896]{1,0:T(8,128)(2,1)S(1)}, u32[]{:S(2)}, u32[]{:S(2)}) collective-permute-start(bf16[128,896]{1,0:T(8,128)(2,1)S(1)} %get-tuple-element.40), channel_id=1, source_target_pairs={{0,2},{1,3},{2,0},{3,1},{4,6},{5,7},{6,4},{7,5},{8,10},{9,11},{10,... | collective-permute-start | bytes 688136 | tf_op jit(solution)/shard_map/ppermute | solution.py:147
  116.0 28.2 %collective-permute-start.7 = (bf16[128,896]{1,0:T(8,128)(2,1)S(1)}, bf16[128,896]{1,0:T(8,128)(2,1)}, u32[]{:S(2)}, u32[]{:S(2)}) collective-permute-start(bf16[128,896]{1,0:T(8,128)(2,1)S(1)} %get-tuple-element.35), channel_id=1, source_target_pairs={{0,1},{1,0},{2,3},{3,2},{4,5},{5,4},{6,7},{7,6},{8,9},{9,8},{10,11... | collective-permute-start | bytes 688136 | tf_op jit(solution)/shard_map/ppermute | solution.py:147
  133.2 12.3 %collective-permute-start.37 = (bf16[1,128,896]{2,1,0:T(8,128)(2,1)S(1)}, bf16[1,128,896]{2,1,0:T(8,128)(2,1)S(1)}, u32[]{:S(2)}, u32[]{:S(2)}) collective-permute-start(bf16[1,128,896]{2,1,0:T(8,128)(2,1)S(1)} %bitcast.66), channel_id=1, source_target_pairs={{0,16},{16,0},{1,17},{17,1},{2,18},{18,2},{3,19},{19,3},{4,20},{20... | collective-permute-start | bytes 688136 | tf_op jit(solution)/shard_map/ppermute | solution.py:14
  (18 other events, 223.8 us)

commit v2 on v0

--- a/solution.py
+++ b/solution.py
@@ -1,6 +1,10 @@
+import functools
+
 import jax
 import jax.numpy as jnp
 from jax import lax
+from jax.experimental import pallas as pl
+from jax.experimental.pallas import tpu as pltpu
 from jax.sharding import PartitionSpec as P
 
 
@@ -44,7 +48,7 @@
     return (grad_gate, grad_up)
 
 
-def shards(
+def shards_by_slots(
     inputs_forward,
     routes_forward,
     gates_forward,
@@ -134,6 +138,309 @@
     return (next_forward, next_backward)
 
 
+CONTRACT_LAST = (((1,), (1,)), ((), ()))
+CONTRACT_FIRST = (((0,), (0,)), ((), ()))
+VMEM = pl.BlockSpec(memory_space=pltpu.VMEM)
+SMEM = pl.BlockSpec(memory_space=pltpu.SMEM)
+VMEM_BYTES = 14 << 20
+ANY = pl.BlockSpec(memory_space=pl.ANY)
+
+
+def across(value, axis, mask):
+    count = lax.axis_size(axis)
+    return lax.ppermute(value, axis, [(source, source ^ mask) for source in range(count)])
+
+
+def ring_order(count):
+    return [0] + list(range(1, count, 2)) + list(range(2, count, 2))[::-1]
+
+
+def ring_pairs(count, steps):
+    order = ring_order(count)
+    return [(order[i], order[(i + steps) % count]) for i in range(count)]
+
+
+def along_ring(value, steps):
+    return lax.ppermute(value, "dev", ring_pairs(lax.axis_size("dev"), steps))
+
+
+def along_ring_and_sections(value, shift):
+    count, sections = lax.axis_size("dev"), lax.axis_size("section")
+    pairs = [
+        (section * count + source, (section + shift) % sections * count + target)
+        for section in range(sections)
+        for source, target in ring_pairs(count, 1)
+    ]
+    return lax.ppermute(value, ("section", "dev"), pairs)
+
+
+def block_behind(expert, count, steps):
+    block = 0
+    for target, source in ring_pairs(count, -steps):
+        block = block + jnp.where(expert == target, source, 0)
+    return block
+
+
+def call(body, place, operands, after, out_shape, scratch, flops):
+    def with_after(place_ref, *refs):
+        body(place_ref, *refs[: len(operands)], *refs[len(operands) + len(after) :])
+
+    touched = sum(array.size * array.dtype.itemsize for array in operands)
+    return pl.pallas_call(
+        with_after,
+        in_specs=[SMEM] + [VMEM] * len(operands) + [ANY] * len(after),
+        out_specs=jax.tree.map(lambda _: VMEM, out_shape),
+        scratch_shapes=scratch,
+        out_shape=out_shape,
+        cost_estimate=pl.CostEstimate(flops=flops, bytes_accessed=touched, transcendentals=0),
+        compiler_params=pltpu.CompilerParams(vmem_limit_bytes=VMEM_BYTES),
+    )(place, *operands, *after)
+
+
+def matmul(left, right, dims=(((1,), (0,)), ((), ()))):
+    return lax.dot_general(left, right, dims, preferred_element_type=jnp.float32)
+
+
+def by_owner(place_ref, rows_ref, sorted_rows, nodes):
+    rows = rows_ref.shape[0] // nodes
+    for mask in range(nodes):
+        first = pl.multiple_of((place_ref[0] ^ mask) * rows, rows)
+        sorted_rows[mask * rows : (mask + 1) * rows, :] = rows_ref[pl.ds(first, rows), :]
+
+
+def first_products(place, token_rows, grad_rows, weights, nodes, after):
+    (count, width), hidden = token_rows.shape, weights[0].shape[1]
+    share = count // nodes
+
+    def body(place_ref, token_ref, grad_ref, gate_ref, up_ref, down_ref, *refs):
+        outs, (sorted_tokens, sorted_grads) = refs[:nodes], refs[nodes:]
+        by_owner(place_ref, token_ref, sorted_tokens, nodes)
+        by_owner(place_ref, grad_ref, sorted_grads, nodes)
+        parts = (
+            matmul(sorted_tokens[...], gate_ref[...]),
+            matmul(sorted_tokens[...], up_ref[...]),
+            matmul(sorted_grads[...], down_ref[...], CONTRACT_LAST),
+        )
+        for index, part in enumerate(parts):
+            for mask in range(nodes):
+                outs[mask][index] = part[mask * share : (mask + 1) * share].astype(jnp.bfloat16)
+
+    return call(
+        body,
+        place,
+        (token_rows, grad_rows, *weights),
+        after,
+        [jax.ShapeDtypeStruct((3, share, hidden), jnp.bfloat16)] * nodes,
+        [pltpu.VMEM((count, width), jnp.bfloat16)] * 2,
+        6 * count * width * hidden,
+    )
+
+
+def activations(place, pieces, after):
+    _, share, hidden = pieces[0].shape
+
+    def body(place_ref, *refs):
+        piece_refs, out = refs[:-1], refs[-1]
+        gate, up, grad = (
+            sum(ref[index].astype(jnp.float32) for ref in piece_refs) for index in range(3)
+        )
+        out[0] = (gate / (1.0 + jnp.exp(-gate)) * up).astype(jnp.bfloat16)
+        out[1] = grad.astype(jnp.bfloat16)
+
+    return call(
+        body,
+        place,
+        pieces,
+        after,
+        jax.ShapeDtypeStruct((2, share, hidden), jnp.bfloat16),
+        [],
+        16 * share * hidden,
+    )
+
+
+def join(place_ref, piece_refs, index, joined):
+    rows = piece_refs[0].shape[1]
+    for mask, ref in enumerate(piece_refs):
+        first = pl.multiple_of((place_ref[0] ^ mask) * rows, rows)
+        joined[pl.ds(first, rows), :] = ref[index]
+
+
+def weight_column(expert, routes, gates):
+    chosen, count = routes.shape
+    line = jnp.zeros((1, count), jnp.float32)
+    for choice in range(chosen):
+        line += jnp.where(routes[choice : choice + 1] == expert, gates[choice : choice + 1], 0.0)
+    diagonal = lax.broadcasted_iota(jnp.int32, (count, count), 0) == lax.broadcasted_iota(
+        jnp.int32, (count, count), 1
+    )
+    return jnp.sum(jnp.where(diagonal, line, 0.0), axis=1, keepdims=True)
+
+
+def slot_selection(expert, routes, capacity):
+    chosen, count = routes.shape
+    named = jnp.zeros((1, count), jnp.float32)
+    for choice in range(chosen):
+        named += (routes[choice : choice + 1] == expert).astype(jnp.float32)
+    earlier = lax.broadcasted_iota(jnp.int32, (count, count), 0) < lax.broadcasted_iota(
+        jnp.int32, (count, count), 1
+    )
+    rank = matmul(
+        jnp.broadcast_to(named, (16, count)).astype(jnp.bfloat16),
+        earlier.astype(jnp.float32).astype(jnp.bfloat16),
+    )[0:1]
+    slot = jnp.where(named > 0, rank, -1.0)
+    slots = lax.broadcasted_iota(jnp.int32, (capacity, count), 0).astype(jnp.float32)
+    return (slots == slot).astype(jnp.float32).astype(jnp.bfloat16)
+
+
+def forward_results(place, pieces, w_down, info, added, after):
+    nodes, (_, share, hidden), width = len(pieces), pieces[0].shape, w_down.shape[1]
+    count, chosen = share * nodes, info.shape[0] // 4
+
+    def body(place_ref, *refs):
+        piece_refs, (down_ref, info_ref, added_ref, out, joined) = refs[:nodes], refs[nodes:]
+        join(place_ref, piece_refs, 0, joined)
+        routes = info_ref[0:chosen].astype(jnp.int32)
+        weight = weight_column(place_ref[1], routes, info_ref[chosen : 2 * chosen])
+        result = matmul(joined[...], down_ref[...]).astype(jnp.bfloat16).astype(jnp.float32)
+        out[...] = (added_ref[...].astype(jnp.float32) + weight * result).astype(jnp.bfloat16)
+
+    return call(
+        body,
+        place,
+        (*pieces, w_down, info, added),
+        after,
+        jax.ShapeDtypeStruct((count, width), jnp.bfloat16),
+        [pltpu.VMEM((count, hidden), jnp.bfloat16)],
+        2 * count * width * hidden,
+    )
+
+
+def backward_results(place, pieces, w_gate, w_up, saved_gate, saved_up, info, added, block, after):
+    nodes, (_, share, hidden), width = len(pieces), pieces[0].shape, w_gate.shape[0]
+    count, chosen = share * nodes, info.shape[0] // 4
+    experts = saved_gate.shape[0] // count
+
+    def body(place_ref, *refs):
+        piece_refs, refs = refs[:nodes], refs[nodes:]
+        gate_ref, up_ref, saved_gate_ref, saved_up_ref, info_ref, added_ref, out, joined = refs
+        join(place_ref, piece_refs, 1, joined)
+        expert = place_ref[1]
+        routes = info_ref[2 * chosen : 3 * chosen].astype(jnp.int32)
+        weight = weight_column(expert, routes, info_ref[3 * chosen :])
+        select = slot_selection(expert, routes, count)
+        first = pl.multiple_of(block_behind(expert, experts, block) * count, count)
+        grad_gate, grad_up = backward_act(
+            joined[...].astype(jnp.float32),
+            matmul(select, saved_gate_ref[pl.ds(first, count), :], CONTRACT_FIRST),
+            matmul(select, saved_up_ref[pl.ds(first, count), :], CONTRACT_FIRST),
+        )
+        result = matmul(grad_gate, gate_ref[...], CONTRACT_LAST)
+        result += matmul(grad_up, up_ref[...], CONTRACT_LAST)
+        result = result.astype(jnp.bfloat16).astype(jnp.float32)
+        out[...] = (added_ref[...].astype(jnp.float32) + weight * result).astype(jnp.bfloat16)
+
+    return call(
+        body,
+        place,
+        (*pieces, w_gate, w_up, saved_gate, saved_up, info, added),
+        after,
+        jax.ShapeDtypeStruct((count, width), jnp.bfloat16),
+        [pltpu.VMEM((count, hidden), jnp.bfloat16)],
+        4 * count * width * hidden,
+    )
+
+
+def ring_shards(
+    inputs_forward,
+    routes_forward,
+    gates_forward,
+    grads_backward,
+    routes_backward,
+    gates_backward,
+    w_gate,
+    w_up,
+    w_down,
+    saved_gate,
+    saved_up,
+):
+    experts, nodes = lax.axis_size("dev"), lax.axis_size("node")
+    place = jnp.stack([lax.axis_index("node"), lax.axis_index("dev")]).astype(jnp.int32)
+    weights = (w_gate[0, 0], w_up[0, 0], w_down[0, 0])
+    stored_gate, stored_up = saved_gate[0, 0], saved_up[0, 0]
+
+    tokens, grads = [inputs_forward[0]], [grads_backward[0]]
+    info = jnp.concatenate(
+        [
+            routes_forward[0].T.astype(jnp.float32),
+            gates_forward[0].T,
+            routes_backward[0].T.astype(jnp.float32),
+            gates_backward[0].T,
+        ]
+    )
+    for _ in range(1, experts):
+        tokens.append(along_ring(tokens[-1], 1))
+        grads.append(along_ring(grads[-1], 1))
+    infos = [info] + [along_ring(info, step) for step in range(1, experts)]
+
+    pieces, shares = [None] * experts, [None] * experts
+    order = []
+
+    def exchange(own):
+        return [own[mask] if mask == 0 else across(own[mask], "node", mask) for mask in range(nodes)]
+
+    def first(step):
+        own = first_products(place, tokens[step], grads[step], weights, nodes, order[-1:])
+        order.append(own[0])
+        pieces[step] = exchange(own)
+
+    def middle(step):
+        own = activations(place, pieces[step], order[-1:])
+        order.append(own)
+        shares[step] = exchange([own] * nodes)
+
+    hops = [inputs_forward[0], grads_backward[0]]
+    base = [None, None]
+
+    def last(step):
+        added = hops
+        if step == 1:
+            added = [jnp.zeros_like(hops[0]), jnp.zeros_like(hops[1])]
+        forward = forward_results(place, shares[step], weights[2], infos[step], added[0], order[-1:])
+        order.append(forward)
+        backward = backward_results(
+            place, shares[step], *weights[:2], stored_gate, stored_up, infos[step], added[1], step, order[-1:]
+        )
+        order.append(backward)
+        if step == 0:
+            base[:] = [from_behind(forward, "section", 1), from_behind(backward, "section", -1)]
+        elif step < experts - 1:
+            hops[:] = [along_ring(forward, 1), along_ring(backward, 1)]
+        else:
+            hops[:] = [along_ring_and_sections(forward, 1), along_ring_and_sections(backward, -1)]
+
+    for turn in range(experts + 2):
+        for act, step in ((first, turn), (last, turn - 2), (middle, turn - 1)):
+            if 0 <= step < experts:
+                act(step)
+    return tuple(
+        (own.astype(jnp.float32) + others.astype(jnp.float32)).astype(jnp.bfloat16)[None]
+        for own, others in zip(base, hops)
+    )
+
+
+def power_of_two(number):
+    return number & (number - 1) == 0
+
+
+def shards(*args):
+    experts, nodes = lax.axis_size("dev"), lax.axis_size("node")
+    tokens, capacity = args[0].shape[1], args[9].shape[2] // experts
+    if capacity == tokens and experts > 1 and power_of_two(nodes) and tokens % (16 * nodes) == 0:
+        return ring_shards(*args)
+    return shards_by_slots(*args)
+
+
 def solution(mesh):
     return jax.shard_map(
         shards,

time: 241 us -> 117 us (0.49)
  waiting for transfers between devices: 159 us -> 47.4 us
  matrix products: 27.7 us -> 0 us
  Pallas kernels: 0 us -> 23.3 us
  starting transfers between devices: 18.4 us -> 36.7 us
  between operations: 14 us -> 1 us
  other arithmetic: 9.16 us -> 1.58 us
  local copies, waits for them, and re-layouts: 12.9 us -> 7.16 us
    reduce_scatter x2 -> x0, waiting for transfers between devices: 57.3 us -> none  [the longest x1 30.9 us: shards(): lax.psum_scatter(part_up.astype(jnp.bfloat16), 'node', scatter_dimension=...]
    all_to_all x4 -> x0, waiting for transfers between devices: 53.7 us -> none  [the longest x1 19.3 us: shards(): lax.all_to_all(sent_backward, 'dev', split_axis=0, concat_axis=0, tiled=T...]
    ppermute x0 -> x39, waiting for transfers between devices: none -> 47.4 us  [the longest x13 27.4 us: along_ring(): return lax.ppermute(value, 'dev', ring_pairs(lax.axis_size('dev'), steps))]
    ppermute x0 -> x39, starting transfers between devices: none -> 36.7 us  [the longest x24 26.2 us: across(): lax.ppermute(value, axis, [(source, source ^ mask) for source in range(co...]
    psum x1 -> x0, waiting for transfers between devices: 29.8 us -> none  [shards(): lax.psum(part_grad.astype(jnp.bfloat16), 'node').astype(jnp.float32)]
    dot_general x8 -> x0, matrix products: 27.7 us -> none  [the longest x1 5.74 us: shards(): lax.dot_general(grad_gate, gate_local, contract_last, preferred_element_t...]
    pallas_call x0 -> x16, Pallas kernels: none -> 23.3 us  [call(): pl.pallas_call(with_after, in_specs=[SMEM] + [VMEM] * len(operands) + [AN...]
    all_to_all x4 -> x0, starting transfers between devices: 18.1 us -> none  [the longest x1 6.32 us: shards(): lax.all_to_all(sent_backward, 'dev', split_axis=0, concat_axis=0, tiled=T...]
  transfers between devices with their start and end apart: 10 -> 41, of which waited for: 9 -> 15; matrix products, arithmetic and copies ran while one was open for 16% -> 1% of each run, Pallas kernels for 0% -> 19%
where the time goes in v2:
time: 117 us
  waiting for transfers between devices  47.4 us (41%)
  starting transfers between devices  36.7 us (31%)
  Pallas kernels  23.3 us (20%)
  local copies, waits for them, and re-layouts  7.16 us (6%)
  other arithmetic  1.58 us (1%)
    ppermute x13, waiting for transfers between devices, along_ring(): return lax.ppermute(value, 'dev', ring_pairs(lax.axis_size('dev'), steps))  27.4 us
    ppermute x24, starting transfers between devices, across(): lax.ppermute(value, axis, [(source, source ^ mask) for source in range(co...  26.2 us
    pallas_call x16, Pallas kernels, call(): pl.pallas_call(with_after, in_specs=[SMEM] + [VMEM] * len(operands) + [AN...  23.3 us
    ppermute x24, waiting for transfers between devices, across(): lax.ppermute(value, axis, [(source, source ^ mask) for source in range(co...  14.4 us
    ppermute x13, starting transfers between devices, along_ring(): return lax.ppermute(value, 'dev', ring_pairs(lax.axis_size('dev'), steps))  9.17 us
    unnamed x32, local copies, waits for them, and re-layouts  7.14 us
    ppermute x2, waiting for transfers between devices, along_ring_and_sections(): return lax.ppermute(value, ('section', 'dev'), pairs)  5.56 us
  transfers between devices with their start and end apart: 41, of which 15 were waited for; matrix products, arithmetic and copies ran while one was open for 1% of the time, Pallas kernels for 19%

profile of v2, /device:TPU:0, one launch (start us, length us, event | category | flops | bytes accessed | tf_op | source)
XLA Modules:
  0.0 117.2 jit_solution(13040130417789548465)
XLA Ops:
  0.6 3.1 %collective-permute-start.3 = (bf16[128,896]{1,0:T(8,128)(2,1)}, bf16[128,896]{1,0:T(8,128)(2,1)S(1)}, u32[]{:S(2)}, u32[]{:S(2)}) collective-permute-start(bf16[128,896]{1,0:T(8,128)(2,1)} %bitcast.59), channel_id=1, source_target_pairs={{0,1},{1,3},{3,2},{2,0},{4,5},{5,7},{7,6},{6,4},{8,9},{9,11},{11,1... | collective-permute-start | bytes 688136 | tf_op jit(solution)/shard_map/ppermute | solution.py:164
  3.7 2.6 %collective-permute-start.4 = (bf16[128,896]{1,0:T(8,128)(2,1)}, bf16[128,896]{1,0:T(8,128)(2,1)S(1)}, u32[]{:S(2)}, u32[]{:S(2)}) collective-permute-start(bf16[128,896]{1,0:T(8,128)(2,1)} %bitcast.62), channel_id=1, source_target_pairs={{0,1},{1,3},{3,2},{2,0},{4,5},{5,7},{7,6},{6,4},{8,9},{9,11},{11,1... | collective-permute-start | bytes 688136 | tf_op jit(solution)/shard_map/ppermute | solution.py:164
  6.4 1.5 %copy-done = bf16[1,1,1024,896]{3,2,1,0:T(8,128)(2,1)S(1)} copy-done((bf16[1,1,1024,896]{3,2,1,0:T(8,128)(2,1)S(1)}, bf16[1,1,1024,896]{3,2,1,0:T(8,128)(2,1)}, u32[]{:S(2)}) %copy-start) | copy-done | bytes 1835032
  7.9 1.5 %copy-done.2 = bf16[1,1,896,1024]{3,2,1,0:T(8,128)(2,1)S(1)} copy-done((bf16[1,1,896,1024]{3,2,1,0:T(8,128)(2,1)S(1)}, bf16[1,1,896,1024]{3,2,1,0:T(8,128)(2,1)}, u32[]{:S(2)}) %copy-start.2) | copy-done | bytes 1835032
  9.4 1.5 %copy-done.4 = bf16[1,1,896,1024]{3,2,1,0:T(8,128)(2,1)S(1)} copy-done((bf16[1,1,896,1024]{3,2,1,0:T(8,128)(2,1)S(1)}, bf16[1,1,896,1024]{3,2,1,0:T(8,128)(2,1)}, u32[]{:S(2)}) %copy-start.4) | copy-done | bytes 1835032
  12.8 1.8 %shard_map.122 = (bf16[3,32,1024]{2,1,0:T(8,128)(2,1)S(1)}, bf16[3,32,1024]{2,1,0:T(8,128)(2,1)S(1)}, bf16[3,32,1024]{2,1,0:T(8,128)(2,1)S(1)}, bf16[3,32,1024]{2,1,0:T(8,128)(2,1)S(1)}) custom-call(s32[2]{0:T(128)S(1)} %pad_add_fusion.place_ref, bf16[128,896]{1,0:T(8,128)(2,1)S(1)} %bitcast.60, bf16[128,896]{1,0:T(8,128)(2,1)S(1)} %bitcast.63, ...), custom_call_target="tpu_custom_call" | custom-call | flops 704643072 | bytes 5963776 | tf_op jit(solution)/shard_map/pallas_call | solution.py:189
  14.6 1.6 %collective-permute-start = (bf16[3,32,1024]{2,1,0:T(8,128)(2,1)S(1)}, bf16[3,32,1024]{2,1,0:T(8,128)(2,1)S(1)}, u32[]{:S(2)}, u32[]{:S(2)}) collective-permute-start(bf16[3,32,1024]{2,1,0:T(8,128)(2,1)S(1)} %get-tuple-element.19), channel_id=1, source_target_pairs={{0,4},{4,0},{8,12},{12,8},{1,5},{5,1},{9,13},{13,9},{2,6},{6,2},{1... | collective-permute-start | bytes 589832 | tf_op jit(solution)/shard_map/ppermute | solution.py:151
  16.1 1.5 %collective-permute-start.1 = (bf16[3,32,1024]{2,1,0:T(8,128)(2,1)S(1)}, bf16[3,32,1024]{2,1,0:T(8,128)(2,1)S(1)}, u32[]{:S(2)}, u32[]{:S(2)}) collective-permute-start(bf16[3,32,1024]{2,1,0:T(8,128)(2,1)S(1)} %get-tuple-element.20), channel_id=1, source_target_pairs={{0,8},{4,12},{8,0},{12,4},{1,9},{5,13},{9,1},{13,5},{2,10},{6,14},... | collective-permute-start | bytes 589832 | tf_op jit(solution)/shard_map/ppermute | solution.py:151
  18.2 1.8 %shard_map.123 = (bf16[3,32,1024]{2,1,0:T(8,128)(2,1)S(1)}, bf16[3,32,1024]{2,1,0:T(8,128)(2,1)S(1)}, bf16[3,32,1024]{2,1,0:T(8,128)(2,1)S(1)}, bf16[3,32,1024]{2,1,0:T(8,128)(2,1)S(1)}) custom-call(s32[2]{0:T(128)S(1)} %pad_add_fusion.place_ref, bf16[128,896]{1,0:T(8,128)(2,1)S(1)} %collective-permute-done.3.refs_0_, ...), custom_call_target="tpu_custom_call" | custom-call | flops 704643072 | bytes 5963776 | tf_op jit(solution)/shard_map/pallas_call | solution.py:189
  20.1 2.4 %collective-permute-done.refs_1_ = bf16[3,32,1024]{2,1,0:T(8,128)(2,1)S(1)} collective-permute-done((bf16[3,32,1024]{2,1,0:T(8,128)(2,1)S(1)}, bf16[3,32,1024]{2,1,0:T(8,128)(2,1)S(1)}, u32[]{:S(2)}, u32[]{:S(2)}) %collective-permute-start) | collective-permute-done | bytes 196640 | tf_op jit(solution)/shard_map/ppermute | solution.py:151
  22.5 3.7 %collective-permute-done.1.refs_2_ = bf16[3,32,1024]{2,1,0:T(8,128)(2,1)S(1)} collective-permute-done((bf16[3,32,1024]{2,1,0:T(8,128)(2,1)S(1)}, bf16[3,32,1024]{2,1,0:T(8,128)(2,1)S(1)}, u32[]{:S(2)}, u32[]{:S(2)}) %collective-permute-start.1) | collective-permute-done | bytes 196640 | tf_op jit(solution)/shard_map/ppermute | solution.py:151
  29.0 1.4 %collective-permute-start.7 = (bf16[2,32,1024]{2,1,0:T(8,128)(2,1)S(1)}, bf16[2,32,1024]{2,1,0:T(8,128)(2,1)S(1)}, u32[]{:S(2)}, u32[]{:S(2)}) collective-permute-start(bf16[2,32,1024]{2,1,0:T(8,128)(2,1)S(1)} %shard_map.124.refs_5_.refs_0_), channel_id=1, source_target_pairs={{0,12},{4,8},{8,4},{12,0},{1,13},{5,9},{9,5},{13,1},{2,14},{6,10},... | collective-permute-start | bytes 393224 | tf_op jit(solution)/shard_map/ppermute | solution.py:151
  31.2 2.0 %collective-permute-done.5.refs_1_ = bf16[2,32,1024]{2,1,0:T(8,128)(2,1)S(1)} collective-permute-done((bf16[2,32,1024]{2,1,0:T(8,128)(2,1)S(1)}, bf16[2,32,1024]{2,1,0:T(8,128)(2,1)S(1)}, u32[]{:S(2)}, u32[]{:S(2)}) %collective-permute-start.5) | collective-permute-done | bytes 131104 | tf_op jit(solution)/shard_map/ppermute | solution.py:151
  34.9 2.3 %collective-permute-done.7.refs_3_ = bf16[2,32,1024]{2,1,0:T(8,128)(2,1)S(1)} collective-permute-done((bf16[2,32,1024]{2,1,0:T(8,128)(2,1)S(1)}, bf16[2,32,1024]{2,1,0:T(8,128)(2,1)S(1)}, u32[]{:S(2)}, u32[]{:S(2)}) %collective-permute-start.7) | collective-permute-done | bytes 131104 | tf_op jit(solution)/shard_map/ppermute | solution.py:151
  37.7 2.1 %collective-permute-done.8.refs_0_ = bf16[128,896]{1,0:T(8,128)(2,1)S(1)} collective-permute-done((bf16[128,896]{1,0:T(8,128)(2,1)S(1)}, bf16[128,896]{1,0:T(8,128)(2,1)S(1)}, u32[]{:S(2)}, u32[]{:S(2)}) %collective-permute-start.8) | collective-permute-done | bytes 229408 | tf_op jit(solution)/shard_map/ppermute | solution.py:164
  39.8 4.9 %collective-permute-done.9.refs_1_ = bf16[128,896]{1,0:T(8,128)(2,1)S(1)} collective-permute-done((bf16[128,896]{1,0:T(8,128)(2,1)S(1)}, bf16[128,896]{1,0:T(8,128)(2,1)S(1)}, u32[]{:S(2)}, u32[]{:S(2)}) %collective-permute-start.9) | collective-permute-done | bytes 229408 | tf_op jit(solution)/shard_map/ppermute | solution.py:164
  44.8 1.8 %shard_map.125 = (bf16[3,32,1024]{2,1,0:T(8,128)(2,1)S(1)}, bf16[3,32,1024]{2,1,0:T(8,128)(2,1)S(1)}, bf16[3,32,1024]{2,1,0:T(8,128)(2,1)S(1)}, bf16[3,32,1024]{2,1,0:T(8,128)(2,1)S(1)}) custom-call(s32[2]{0:T(128)S(1)} %pad_add_fusion.place_ref, bf16[128,896]{1,0:T(8,128)(2,1)S(1)} %collective-permute-done.8.refs_0_, ...), custom_call_target="tpu_custom_call" | custom-call | flops 704643072 | bytes 5963776 | tf_op jit(solution)/shard_map/pallas_call | solution.py:189
  48.4 2.3 %shard_map.127.refs_4_ = bf16[128,896]{1,0:T(8,128)(2,1)S(1)} custom-call(s32[2]{0:T(128)S(1)} %pad_add_fusion.place_ref, bf16[2,32,1024]{2,1,0:T(8,128)(2,1)S(1)} %shard_map.124.refs_5_.refs_0_, bf16[2,32,1024]{2,1,0:T(8,128)(2,1)S(1)} %collective-permute-done.5.refs_1_, bf16[2,32,1024]{2,1,0:T(8,128)(2,1)S(1)} %collective-permute-done.6.refs_2_, ...), custom_call_target="tpu_custom_call" | custom-call | flops 469762048 | bytes 6524928 | tf_op jit(solution)/shard_map/pallas_call | solution.py:189
  53.9 3.4 %collective-permute-done.25.refs_5_.refs_8_ = f32[8,128]{1,0:T(8,128)S(1)} collective-permute-done((f32[8,128]{1,0:T(8,128)S(1)}, f32[8,128]{1,0:T(8,128)S(1)}, u32[]{:S(2)}, u32[]{:S(2)}) %collective-permute-start.25) | collective-permute-done | bytes 4128 | tf_op jit(solution)/shard_map/ppermute | solution.py:164
  61.7 1.9 %shard_map.129 = (bf16[3,32,1024]{2,1,0:T(8,128)(2,1)S(1)}, bf16[3,32,1024]{2,1,0:T(8,128)(2,1)S(1)}, bf16[3,32,1024]{2,1,0:T(8,128)(2,1)S(1)}, bf16[3,32,1024]{2,1,0:T(8,128)(2,1)S(1)}) custom-call(s32[2]{0:T(128)S(1)} %pad_add_fusion.place_ref, bf16[128,896]{1,0:T(8,128)(2,1)S(1)} %collective-permute-done.11.refs_0_, ...), custom_call_target="tpu_custom_call" | custom-call | flops 704643072 | bytes 5963776 | tf_op jit(solution)/shard_map/pallas_call | solution.py:189
  65.2 2.3 %shard_map.131.refs_4_ = bf16[128,896]{1,0:T(8,128)(2,1)S(1)} custom-call(s32[2]{0:T(128)S(1)} %pad_add_fusion.place_ref, bf16[2,32,1024]{2,1,0:T(8,128)(2,1)S(1)} %shard_map.128.refs_5_.refs_0_, bf16[2,32,1024]{2,1,0:T(8,128)(2,1)S(1)} %collective-permute-done.22.refs_1_, bf16[2,32,1024]{2,1,0:T(8,128)(2,1)S(1)} %collective-permute-done.23.refs_2_, ...), custom_call_target="tpu_custom_call" | custom-call | flops 469762048 | bytes 6524928 | tf_op jit(solution)/shard_map/pallas_call | solution.py:189
  67.5 2.6 %collective-permute-done.20.refs_2_ = bf16[3,32,1024]{2,1,0:T(8,128)(2,1)S(1)} collective-permute-done((bf16[3,32,1024]{2,1,0:T(8,128)(2,1)S(1)}, bf16[3,32,1024]{2,1,0:T(8,128)(2,1)S(1)}, u32[]{:S(2)}, u32[]{:S(2)}) %collective-permute-start.20) | collective-permute-done | bytes 196640 | tf_op jit(solution)/shard_map/ppermute | solution.py:151
  72.5 2.7 %collective-permute-start.28 = (bf16[2,32,1024]{2,1,0:T(8,128)(2,1)S(1)}, bf16[2,32,1024]{2,1,0:T(8,128)(2,1)S(1)}, u32[]{:S(2)}, u32[]{:S(2)}) collective-permute-start(bf16[2,32,1024]{2,1,0:T(8,128)(2,1)S(1)} %shard_map.132.refs_0_.refs_7_), channel_id=1, source_target_pairs={{0,12},{4,8},{8,4},{12,0},{1,13},{5,9},{9,5},{13,1},{2,14},{6,10},... | collective-permute-start | bytes 393224 | tf_op jit(solution)/shard_map/ppermute | solution.py:151
  75.5 5.1 %collective-permute-done.29.refs_5_.refs_8_ = f32[8,128]{1,0:T(8,128)S(1)} collective-permute-done((f32[8,128]{1,0:T(8,128)S(1)}, f32[8,128]{1,0:T(8,128)S(1)}, u32[]{:S(2)}, u32[]{:S(2)}) %collective-permute-start.29) | collective-permute-done | bytes 4128 | tf_op jit(solution)/shard_map/ppermute | solution.py:164
  81.4 2.7 %collective-permute-start.18 = (bf16[3,32,1024]{2,1,0:T(8,128)(2,1)S(1)}, bf16[3,32,1024]{2,1,0:T(8,128)(2,1)S(1)}, u32[]{:S(2)}, u32[]{:S(2)}) collective-permute-start(bf16[3,32,1024]{2,1,0:T(8,128)(2,1)S(1)} %get-tuple-element.30), channel_id=1, source_target_pairs={{0,12},{4,8},{8,4},{12,0},{1,13},{5,9},{9,5},{13,1},{2,14},{6,10},... | collective-permute-start | bytes 589832 | tf_op jit(solution)/shard_map/ppermute | solution.py:151
  86.1 2.9 %collective-permute-done.30.refs_9_ = bf16[128,896]{1,0:T(8,128)(2,1)S(1)} collective-permute-done((bf16[128,896]{1,0:T(8,128)(2,1)S(1)}, bf16[128,896]{1,0:T(8,128)(2,1)S(1)}, u32[]{:S(2)}, u32[]{:S(2)}) %collective-permute-start.30) | collective-permute-done | bytes 229408 | tf_op jit(solution)/shard_map/ppermute | solution.py:164
  89.0 2.3 %shard_map.134.refs_4_ = bf16[128,896]{1,0:T(8,128)(2,1)S(1)} custom-call(s32[2]{0:T(128)S(1)} %pad_add_fusion.place_ref, bf16[2,32,1024]{2,1,0:T(8,128)(2,1)S(1)} %shard_map.132.refs_0_.refs_7_, bf16[2,32,1024]{2,1,0:T(8,128)(2,1)S(1)} %collective-permute-done.26.refs_1_, bf16[2,32,1024]{2,1,0:T(8,128)(2,1)S(1)} %collective-permute-done.27.refs_2_, ...), custom_call_target="tpu_custom_call" | custom-call | flops 469762048 | bytes 6524928 | tf_op jit(solution)/shard_map/pallas_call | solution.py:189
  92.8 2.8 %collective-permute-start.34 = (bf16[2,32,1024]{2,1,0:T(8,128)(2,1)S(1)}, bf16[2,32,1024]{2,1,0:T(8,128)(2,1)S(1)}, u32[]{:S(2)}, u32[]{:S(2)}) collective-permute-start(bf16[2,32,1024]{2,1,0:T(8,128)(2,1)S(1)} %shard_map.135.refs_0_.refs_7_), channel_id=1, source_target_pairs={{0,12},{4,8},{8,4},{12,0},{1,13},{5,9},{9,5},{13,1},{2,14},{6,10},... | collective-permute-start | bytes 393224 | tf_op jit(solution)/shard_map/ppermute | solution.py:151
  96.4 2.8 %collective-permute-done.35.refs_5_.refs_8_ = f32[8,128]{1,0:T(8,128)S(1)} collective-permute-done((f32[8,128]{1,0:T(8,128)S(1)}, f32[8,128]{1,0:T(8,128)S(1)}, u32[]{:S(2)}, u32[]{:S(2)}) %collective-permute-start.35) | collective-permute-done | bytes 4128 | tf_op jit(solution)/shard_map/ppermute | solution.py:164
  101.6 6.1 %collective-permute-done.39.refs_9_ = bf16[128,896]{1,0:T(8,128)(2,1)S(1)} collective-permute-done((bf16[128,896]{1,0:T(8,128)(2,1)S(1)}, bf16[128,896]{1,0:T(8,128)(2,1)S(1)}, u32[]{:S(2)}, u32[]{:S(2)}) %collective-permute-start.39) | collective-permute-done | bytes 229408 | tf_op jit(solution)/shard_map/ppermute | solution.py:164
  107.7 2.3 %shard_map.137 = bf16[128,896]{1,0:T(8,128)(2,1)S(1)} custom-call(s32[2]{0:T(128)S(1)} %pad_add_fusion.place_ref, bf16[2,32,1024]{2,1,0:T(8,128)(2,1)S(1)} %shard_map.135.refs_0_.refs_7_, bf16[2,32,1024]{2,1,0:T(8,128)(2,1)S(1)} %collective-permute-done.32.refs_1_, bf16[2,32,1024]{2,1,0:T(8,128)(2,1)S(1)} %collective-permute-done.33.refs_2_, ...), custom_call_target="tpu_custom_call" | custom-call | flops 469762048 | bytes 6524928 | tf_op jit(solution)/shard_map/pallas_call | solution.py:189
  110.9 5.6 %collective-permute-done.40 = bf16[128,896]{1,0:T(8,128)(2,1)S(1)} collective-permute-done((bf16[128,896]{1,0:T(8,128)(2,1)S(1)}, bf16[128,896]{1,0:T(8,128)(2,1)S(1)}, u32[]{:S(2)}, u32[]{:S(2)}) %collective-permute-start.40) | collective-permute-done | bytes 229408 | tf_op jit(solution)/shard_map/ppermute | solution.py:174
  (104 shorter events, 30.8 us)
Async XLA Ops:
  0.6 17.5 %collective-permute-start.3 = (bf16[128,896]{1,0:T(8,128)(2,1)}, bf16[128,896]{1,0:T(8,128)(2,1)S(1)}, u32[]{:S(2)}, u32[]{:S(2)}) collective-permute-start(bf16[128,896]{1,0:T(8,128)(2,1)} %bitcast.59), channel_id=1, source_target_pairs={{0,1},{1,3},{3,2},{2,0},{4,5},{5,7},{7,6},{6,4},{8,9},{9,11},{11,1... | collective-permute-start | bytes 688136 | tf_op jit(solution)/shard_map/ppermute | solution.py:164
  3.7 14.5 %collective-permute-start.4 = (bf16[128,896]{1,0:T(8,128)(2,1)}, bf16[128,896]{1,0:T(8,128)(2,1)S(1)}, u32[]{:S(2)}, u32[]{:S(2)}) collective-permute-start(bf16[128,896]{1,0:T(8,128)(2,1)} %bitcast.62), channel_id=1, source_target_pairs={{0,1},{1,3},{3,2},{2,0},{4,5},{5,7},{7,6},{6,4},{8,9},{9,11},{11,1... | collective-permute-start | bytes 688136 | tf_op jit(solution)/shard_map/ppermute | solution.py:164
  14.6 7.9 %collective-permute-start = (bf16[3,32,1024]{2,1,0:T(8,128)(2,1)S(1)}, bf16[3,32,1024]{2,1,0:T(8,128)(2,1)S(1)}, u32[]{:S(2)}, u32[]{:S(2)}) collective-permute-start(bf16[3,32,1024]{2,1,0:T(8,128)(2,1)S(1)} %get-tuple-element.19), channel_id=1, source_target_pairs={{0,4},{4,0},{8,12},{12,8},{1,5},{5,1},{9,13},{13,9},{2,6},{6,2},{1... | collective-permute-start | bytes 589832 | tf_op jit(solution)/shard_map/ppermute | solution.py:151
  16.1 10.0 %collective-permute-start.1 = (bf16[3,32,1024]{2,1,0:T(8,128)(2,1)S(1)}, bf16[3,32,1024]{2,1,0:T(8,128)(2,1)S(1)}, u32[]{:S(2)}, u32[]{:S(2)}) collective-permute-start(bf16[3,32,1024]{2,1,0:T(8,128)(2,1)S(1)} %get-tuple-element.20), channel_id=1, source_target_pairs={{0,8},{4,12},{8,0},{12,4},{1,9},{5,13},{9,1},{13,5},{2,10},{6,14},... | collective-permute-start | bytes 589832 | tf_op jit(solution)/shard_map/ppermute | solution.py:151
  17.7 8.5 %collective-permute-start.2 = (bf16[3,32,1024]{2,1,0:T(8,128)(2,1)S(1)}, bf16[3,32,1024]{2,1,0:T(8,128)(2,1)S(1)}, u32[]{:S(2)}, u32[]{:S(2)}) collective-permute-start(bf16[3,32,1024]{2,1,0:T(8,128)(2,1)S(1)} %get-tuple-element.21), channel_id=1, source_target_pairs={{0,12},{4,8},{8,4},{12,0},{1,13},{5,9},{9,5},{13,1},{2,14},{6,10},... | collective-permute-start | bytes 589832 | tf_op jit(solution)/shard_map/ppermute | solution.py:151
  29.0 8.2 %collective-permute-start.7 = (bf16[2,32,1024]{2,1,0:T(8,128)(2,1)S(1)}, bf16[2,32,1024]{2,1,0:T(8,128)(2,1)S(1)}, u32[]{:S(2)}, u32[]{:S(2)}) collective-permute-start(bf16[2,32,1024]{2,1,0:T(8,128)(2,1)S(1)} %shard_map.124.refs_5_.refs_0_), channel_id=1, source_target_pairs={{0,12},{4,8},{8,4},{12,0},{1,13},{5,9},{9,5},{13,1},{2,14},{6,10},... | collective-permute-start | bytes 393224 | tf_op jit(solution)/shard_map/ppermute | solution.py:151
  30.4 9.4 %collective-permute-start.8 = (bf16[128,896]{1,0:T(8,128)(2,1)S(1)}, bf16[128,896]{1,0:T(8,128)(2,1)S(1)}, u32[]{:S(2)}, u32[]{:S(2)}) collective-permute-start(bf16[128,896]{1,0:T(8,128)(2,1)S(1)} %collective-permute-done.3.refs_0_), channel_id=1, source_target_pairs={{0,1},{1,3},{3,2},{2,0},{4,5},{5,7},{7,6},{6,4},{8,9},{9,11},{11,1... | collective-permute-start | bytes 688136 | tf_op jit(solution)/shard_map/ppermute | solution.py:164
  30.8 13.9 %collective-permute-start.9 = (bf16[128,896]{1,0:T(8,128)(2,1)S(1)}, bf16[128,896]{1,0:T(8,128)(2,1)S(1)}, u32[]{:S(2)}, u32[]{:S(2)}) collective-permute-start(bf16[128,896]{1,0:T(8,128)(2,1)S(1)} %collective-permute-done.4.refs_1_), channel_id=1, source_target_pairs={{0,1},{1,3},{3,2},{2,0},{4,5},{5,7},{7,6},{6,4},{8,9},{9,11},{11,1... | collective-permute-start | bytes 688136 | tf_op jit(solution)/shard_map/ppermute | solution.py:164
  33.2 17.5 %collective-permute-start.13 = (bf16[3,32,1024]{2,1,0:T(8,128)(2,1)S(1)}, bf16[3,32,1024]{2,1,0:T(8,128)(2,1)S(1)}, u32[]{:S(2)}, u32[]{:S(2)}) collective-permute-start(bf16[3,32,1024]{2,1,0:T(8,128)(2,1)S(1)} %get-tuple-element.24), channel_id=1, source_target_pairs={{0,4},{4,0},{8,12},{12,8},{1,5},{5,1},{9,13},{13,9},{2,6},{6,2},{1... | collective-permute-start | bytes 589832 | tf_op jit(solution)/shard_map/ppermute | solution.py:151
  33.8 16.9 %collective-permute-start.14 = (bf16[3,32,1024]{2,1,0:T(8,128)(2,1)S(1)}, bf16[3,32,1024]{2,1,0:T(8,128)(2,1)S(1)}, u32[]{:S(2)}, u32[]{:S(2)}) collective-permute-start(bf16[3,32,1024]{2,1,0:T(8,128)(2,1)S(1)} %get-tuple-element.25), channel_id=1, source_target_pairs={{0,8},{4,12},{8,0},{12,4},{1,9},{5,13},{9,1},{13,5},{2,10},{6,14},... | collective-permute-start | bytes 589832 | tf_op jit(solution)/shard_map/ppermute | solution.py:151
  37.2 13.5 %collective-permute-start.15 = (bf16[3,32,1024]{2,1,0:T(8,128)(2,1)S(1)}, bf16[3,32,1024]{2,1,0:T(8,128)(2,1)S(1)}, u32[]{:S(2)}, u32[]{:S(2)}) collective-permute-start(bf16[3,32,1024]{2,1,0:T(8,128)(2,1)S(1)} %get-tuple-element.26), channel_id=1, source_target_pairs={{0,12},{4,8},{8,4},{12,0},{1,13},{5,9},{9,5},{13,1},{2,14},{6,10},... | collective-permute-start | bytes 589832 | tf_op jit(solution)/shard_map/ppermute | solution.py:151
  39.8 19.5 %collective-permute-start.11 = (bf16[128,896]{1,0:T(8,128)(2,1)S(1)}, bf16[128,896]{1,0:T(8,128)(2,1)S(1)}, u32[]{:S(2)}, u32[]{:S(2)}) collective-permute-start(bf16[128,896]{1,0:T(8,128)(2,1)S(1)} %collective-permute-done.8.refs_0_), channel_id=1, source_target_pairs={{0,1},{1,3},{3,2},{2,0},{4,5},{5,7},{7,6},{6,4},{8,9},{9,11},{11,1... | collective-permute-start | bytes 688136 | tf_op jit(solution)/shard_map/ppermute | solution.py:164
  44.8 16.0 %collective-permute-start.12 = (bf16[128,896]{1,0:T(8,128)(2,1)S(1)}, bf16[128,896]{1,0:T(8,128)(2,1)S(1)}, u32[]{:S(2)}, u32[]{:S(2)}) collective-permute-start(bf16[128,896]{1,0:T(8,128)(2,1)S(1)} %collective-permute-done.9.refs_1_), channel_id=1, source_target_pairs={{0,1},{1,3},{3,2},{2,0},{4,5},{5,7},{7,6},{6,4},{8,9},{9,11},{11,1... | collective-permute-start | bytes 688136 | tf_op jit(solution)/shard_map/ppermute | solution.py:164
  53.3 10.3 %collective-permute-start.23 = (bf16[2,32,1024]{2,1,0:T(8,128)(2,1)S(1)}, bf16[2,32,1024]{2,1,0:T(8,128)(2,1)S(1)}, u32[]{:S(2)}, u32[]{:S(2)}) collective-permute-start(bf16[2,32,1024]{2,1,0:T(8,128)(2,1)S(1)} %shard_map.128.refs_5_.refs_0_), channel_id=1, source_target_pairs={{0,8},{4,12},{8,0},{12,4},{1,9},{5,13},{9,1},{13,5},{2,10},{6,14},... | collective-permute-start | bytes 393224 | tf_op jit(solution)/shard_map/ppermute | solution.py:151
  57.2 6.9 %collective-permute-start.24 = (bf16[2,32,1024]{2,1,0:T(8,128)(2,1)S(1)}, bf16[2,32,1024]{2,1,0:T(8,128)(2,1)S(1)}, u32[]{:S(2)}, u32[]{:S(2)}) collective-permute-start(bf16[2,32,1024]{2,1,0:T(8,128)(2,1)S(1)} %shard_map.128.refs_5_.refs_0_), channel_id=1, source_target_pairs={{0,12},{4,8},{8,4},{12,0},{1,13},{5,9},{9,5},{13,1},{2,14},{6,10},... | collective-permute-start | bytes 393224 | tf_op jit(solution)/shard_map/ppermute | solution.py:151
  58.2 9.3 %collective-permute-start.19 = (bf16[3,32,1024]{2,1,0:T(8,128)(2,1)S(1)}, bf16[3,32,1024]{2,1,0:T(8,128)(2,1)S(1)}, u32[]{:S(2)}, u32[]{:S(2)}) collective-permute-start(bf16[3,32,1024]{2,1,0:T(8,128)(2,1)S(1)} %get-tuple-element.31), channel_id=1, source_target_pairs={{0,4},{4,0},{8,12},{12,8},{1,5},{5,1},{9,13},{13,9},{2,6},{6,2},{1... | collective-permute-start | bytes 589832 | tf_op jit(solution)/shard_map/ppermute | solution.py:151
  59.4 10.7 %collective-permute-start.20 = (bf16[3,32,1024]{2,1,0:T(8,128)(2,1)S(1)}, bf16[3,32,1024]{2,1,0:T(8,128)(2,1)S(1)}, u32[]{:S(2)}, u32[]{:S(2)}) collective-permute-start(bf16[3,32,1024]{2,1,0:T(8,128)(2,1)S(1)} %get-tuple-element.32), channel_id=1, source_target_pairs={{0,8},{4,12},{8,0},{12,4},{1,9},{5,13},{9,1},{13,5},{2,10},{6,14},... | collective-permute-start | bytes 589832 | tf_op jit(solution)/shard_map/ppermute | solution.py:151
  60.7 10.3 %collective-permute-start.21 = (bf16[3,32,1024]{2,1,0:T(8,128)(2,1)S(1)}, bf16[3,32,1024]{2,1,0:T(8,128)(2,1)S(1)}, u32[]{:S(2)}, u32[]{:S(2)}) collective-permute-start(bf16[3,32,1024]{2,1,0:T(8,128)(2,1)S(1)} %get-tuple-element.33), channel_id=1, source_target_pairs={{0,12},{4,8},{8,4},{12,0},{1,13},{5,9},{9,5},{13,1},{2,14},{6,10},... | collective-permute-start | bytes 589832 | tf_op jit(solution)/shard_map/ppermute | solution.py:151
  65.1 19.0 %collective-permute-start.31 = (bf16[128,896]{1,0:T(8,128)(2,1)S(1)}, bf16[128,896]{1,0:T(8,128)(2,1)S(1)}, u32[]{:S(2)}, u32[]{:S(2)}) collective-permute-start(bf16[128,896]{1,0:T(8,128)(2,1)S(1)} %shard_map.130.refs_10_), channel_id=1, source_target_pairs={{0,1},{1,3},{3,2},{2,0},{4,5},{5,7},{7,6},{6,4},{8,9},{9,11},{11,1... | collective-permute-start | bytes 688136 | tf_op jit(solution)/shard_map/ppermute | solution.py:164
  71.7 9.0 %collective-permute-start.26 = (bf16[2,32,1024]{2,1,0:T(8,128)(2,1)S(1)}, bf16[2,32,1024]{2,1,0:T(8,128)(2,1)S(1)}, u32[]{:S(2)}, u32[]{:S(2)}) collective-permute-start(bf16[2,32,1024]{2,1,0:T(8,128)(2,1)S(1)} %shard_map.132.refs_0_.refs_7_), channel_id=1, source_target_pairs={{0,4},{4,0},{8,12},{12,8},{1,5},{5,1},{9,13},{13,9},{2,6},{6,2},{1... | collective-permute-start | bytes 393224 | tf_op jit(solution)/shard_map/ppermute | solution.py:151
  72.5 8.9 %collective-permute-start.27 = (bf16[2,32,1024]{2,1,0:T(8,128)(2,1)S(1)}, bf16[2,32,1024]{2,1,0:T(8,128)(2,1)S(1)}, u32[]{:S(2)}, u32[]{:S(2)}) collective-permute-start(bf16[2,32,1024]{2,1,0:T(8,128)(2,1)S(1)} %shard_map.132.refs_0_.refs_7_), channel_id=1, source_target_pairs={{0,8},{4,12},{8,0},{12,4},{1,9},{5,13},{9,1},{13,5},{2,10},{6,14},... | collective-permute-start | bytes 393224 | tf_op jit(solution)/shard_map/ppermute | solution.py:151
  72.5 8.9 %collective-permute-start.28 = (bf16[2,32,1024]{2,1,0:T(8,128)(2,1)S(1)}, bf16[2,32,1024]{2,1,0:T(8,128)(2,1)S(1)}, u32[]{:S(2)}, u32[]{:S(2)}) collective-permute-start(bf16[2,32,1024]{2,1,0:T(8,128)(2,1)S(1)} %shard_map.132.refs_0_.refs_7_), channel_id=1, source_target_pairs={{0,12},{4,8},{8,4},{12,0},{1,13},{5,9},{9,5},{13,1},{2,14},{6,10},... | collective-permute-start | bytes 393224 | tf_op jit(solution)/shard_map/ppermute | solution.py:151
  80.6 8.4 %collective-permute-start.30 = (bf16[128,896]{1,0:T(8,128)(2,1)S(1)}, bf16[128,896]{1,0:T(8,128)(2,1)S(1)}, u32[]{:S(2)}, u32[]{:S(2)}) collective-permute-start(bf16[128,896]{1,0:T(8,128)(2,1)S(1)} %shard_map.131.refs_4_), channel_id=1, source_target_pairs={{0,1},{1,3},{3,2},{2,0},{4,5},{5,7},{7,6},{6,4},{8,9},{9,11},{11,1... | collective-permute-start | bytes 688136 | tf_op jit(solution)/shard_map/ppermute | solution.py:164
  80.6 10.7 %collective-permute-start.16 = (bf16[3,32,1024]{2,1,0:T(8,128)(2,1)S(1)}, bf16[3,32,1024]{2,1,0:T(8,128)(2,1)S(1)}, u32[]{:S(2)}, u32[]{:S(2)}) collective-permute-start(bf16[3,32,1024]{2,1,0:T(8,128)(2,1)S(1)} %get-tuple-element.28), channel_id=1, source_target_pairs={{0,4},{4,0},{8,12},{12,8},{1,5},{5,1},{9,13},{13,9},{2,6},{6,2},{1... | collective-permute-start | bytes 589832 | tf_op jit(solution)/shard_map/ppermute | solution.py:151
  81.4 9.9 %collective-permute-start.17 = (bf16[3,32,1024]{2,1,0:T(8,128)(2,1)S(1)}, bf16[3,32,1024]{2,1,0:T(8,128)(2,1)S(1)}, u32[]{:S(2)}, u32[]{:S(2)}) collective-permute-start(bf16[3,32,1024]{2,1,0:T(8,128)(2,1)S(1)} %get-tuple-element.29), channel_id=1, source_target_pairs={{0,8},{4,12},{8,0},{12,4},{1,9},{5,13},{9,1},{13,5},{2,10},{6,14},... | collective-permute-start | bytes 589832 | tf_op jit(solution)/shard_map/ppermute | solution.py:151
  81.4 9.9 %collective-permute-start.18 = (bf16[3,32,1024]{2,1,0:T(8,128)(2,1)S(1)}, bf16[3,32,1024]{2,1,0:T(8,128)(2,1)S(1)}, u32[]{:S(2)}, u32[]{:S(2)}) collective-permute-start(bf16[3,32,1024]{2,1,0:T(8,128)(2,1)S(1)} %get-tuple-element.30), channel_id=1, source_target_pairs={{0,12},{4,8},{8,4},{12,0},{1,13},{5,9},{9,5},{13,1},{2,14},{6,10},... | collective-permute-start | bytes 589832 | tf_op jit(solution)/shard_map/ppermute | solution.py:151
  85.1 14.1 %collective-permute-start.36 = (bf16[128,896]{1,0:T(8,128)(2,1)S(1)}, bf16[128,896]{1,0:T(8,128)(2,1)S(1)}, u32[]{:S(2)}, u32[]{:S(2)}) collective-permute-start(bf16[128,896]{1,0:T(8,128)(2,1)S(1)} %shard_map.133.refs_10_), channel_id=1, source_target_pairs={{0,1},{1,3},{3,2},{2,0},{4,5},{5,7},{7,6},{6,4},{8,9},{9,11},{11,1... | collective-permute-start | bytes 688136 | tf_op jit(solution)/shard_map/ppermute | solution.py:164
  92.0 7.2 %collective-permute-start.32 = (bf16[2,32,1024]{2,1,0:T(8,128)(2,1)S(1)}, bf16[2,32,1024]{2,1,0:T(8,128)(2,1)S(1)}, u32[]{:S(2)}, u32[]{:S(2)}) collective-permute-start(bf16[2,32,1024]{2,1,0:T(8,128)(2,1)S(1)} %shard_map.135.refs_0_.refs_7_), channel_id=1, source_target_pairs={{0,4},{4,0},{8,12},{12,8},{1,5},{5,1},{9,13},{13,9},{2,6},{6,2},{1... | collective-permute-start | bytes 393224 | tf_op jit(solution)/shard_map/ppermute | solution.py:151
  99.2 8.5 %collective-permute-start.39 = (bf16[128,896]{1,0:T(8,128)(2,1)S(1)}, bf16[128,896]{1,0:T(8,128)(2,1)S(1)}, u32[]{:S(2)}, u32[]{:S(2)}) collective-permute-start(bf16[128,896]{1,0:T(8,128)(2,1)S(1)} %shard_map.134.refs_4_), channel_id=1, source_target_pairs={{0,1},{1,3},{3,2},{2,0},{4,5},{5,7},{7,6},{6,4},{8,9},{9,11},{11,1... | collective-permute-start | bytes 688136 | tf_op jit(solution)/shard_map/ppermute | solution.py:164
  99.2 10.9 %collective-permute-start.10 = (bf16[128,896]{1,0:T(8,128)(2,1)S(1)}, bf16[128,896]{1,0:T(8,128)(2,1)S(1)}, u32[]{:S(2)}, u32[]{:S(2)}) collective-permute-start(bf16[128,896]{1,0:T(8,128)(2,1)S(1)} %shard_map.126.refs_10_), channel_id=1, source_target_pairs={{0,16},{16,0},{1,17},{17,1},{2,18},{18,2},{3,19},{19,3},{4,20},{20... | collective-permute-start | bytes 688136 | tf_op jit(solution)/shard_map/ppermute | solution.py:14
  100.3 9.8 %collective-permute-start.37 = (bf16[128,896]{1,0:T(8,128)(2,1)S(1)}, bf16[128,896]{1,0:T(8,128)(2,1)S(1)}, u32[]{:S(2)}, u32[]{:S(2)}) collective-permute-start(bf16[128,896]{1,0:T(8,128)(2,1)S(1)} %shard_map.136.refs_10_), channel_id=1, source_target_pairs={{0,17},{1,19},{3,18},{2,16},{16,1},{17,3},{19,2},{18,0},{4,21},{5,... | collective-permute-start | bytes 688136 | tf_op jit(solution)/shard_map/ppermute | solution.py:174
  101.5 9.3 %collective-permute-start.38 = (bf16[128,896]{1,0:T(8,128)(2,1)S(1)}, bf16[128,896]{1,0:T(8,128)(2,1)S(1)}, u32[]{:S(2)}, u32[]{:S(2)}) collective-permute-start(bf16[128,896]{1,0:T(8,128)(2,1)S(1)} %shard_map.127.refs_4_), channel_id=1, source_target_pairs={{0,16},{16,0},{1,17},{17,1},{2,18},{18,2},{3,19},{19,3},{4,20},{20... | collective-permute-start | bytes 688136 | tf_op jit(solution)/shard_map/ppermute | solution.py:14
  (25 other events, 151.8 us)

commit v3 on v2

--- a/solution.py
+++ b/solution.py
@@ -143,6 +143,7 @@
 VMEM = pl.BlockSpec(memory_space=pltpu.VMEM)
 SMEM = pl.BlockSpec(memory_space=pltpu.SMEM)
 VMEM_BYTES = 14 << 20
+CF = 1.0
 ANY = pl.BlockSpec(memory_space=pl.ANY)
 
 
@@ -181,7 +182,7 @@
     return block
 
 
-def call(body, place, operands, after, out_shape, scratch, flops):
+def call(body, place, operands, after, out_shape, scratch, flops, aliases={}):
     def with_after(place_ref, *refs):
         body(place_ref, *refs[: len(operands)], *refs[len(operands) + len(after) :])
 
@@ -192,7 +193,8 @@
         out_specs=jax.tree.map(lambda _: VMEM, out_shape),
         scratch_shapes=scratch,
         out_shape=out_shape,
-        cost_estimate=pl.CostEstimate(flops=flops, bytes_accessed=touched, transcendentals=0),
+        input_output_aliases={index + 1: out for index, out in aliases.items()},
+        cost_estimate=pl.CostEstimate(flops=int(CF * flops), bytes_accessed=int(CF * touched), transcendentals=0),
         compiler_params=pltpu.CompilerParams(vmem_limit_bytes=VMEM_BYTES),
     )(place, *operands, *after)
 
@@ -202,14 +204,14 @@
 
 
 def by_owner(place_ref, rows_ref, sorted_rows, nodes):
-    rows = rows_ref.shape[0] // nodes
+    rows = sorted_rows.shape[0] // nodes
     for mask in range(nodes):
         first = pl.multiple_of((place_ref[0] ^ mask) * rows, rows)
         sorted_rows[mask * rows : (mask + 1) * rows, :] = rows_ref[pl.ds(first, rows), :]
 
 
-def first_products(place, token_rows, grad_rows, weights, nodes, after):
-    (count, width), hidden = token_rows.shape, weights[0].shape[1]
+def first_products(place, token_rows, grad_rows, weights, nodes, planes, after):
+    (count, width), hidden = grad_rows.shape, weights[0].shape[1]
     share = count // nodes
 
     def body(place_ref, token_ref, grad_ref, gate_ref, up_ref, down_ref, *refs):
@@ -230,39 +232,78 @@
         place,
         (token_rows, grad_rows, *weights),
         after,
-        [jax.ShapeDtypeStruct((3, share, hidden), jnp.bfloat16)] * nodes,
+        [jax.ShapeDtypeStruct((planes, share, hidden), jnp.bfloat16)] * nodes,
         [pltpu.VMEM((count, width), jnp.bfloat16)] * 2,
         6 * count * width * hidden,
     )
 
 
-def activations(place, pieces, after):
-    _, share, hidden = pieces[0].shape
+def activations(place, pieces, filled, after):
+    nodes, (_, share, hidden) = len(pieces), pieces[0].shape
 
     def body(place_ref, *refs):
-        piece_refs, out = refs[:-1], refs[-1]
+        piece_refs, outs = refs[:nodes], refs[nodes + len(filled) :]
         gate, up, grad = (
             sum(ref[index].astype(jnp.float32) for ref in piece_refs) for index in range(3)
         )
-        out[0] = (gate / (1.0 + jnp.exp(-gate)) * up).astype(jnp.bfloat16)
-        out[1] = grad.astype(jnp.bfloat16)
-
+        act = (gate / (1.0 + jnp.exp(-gate)) * up).astype(jnp.bfloat16)
+        grad = grad.astype(jnp.bfloat16)
+        for out in outs:
+            planes = out.shape[0]
+            out[planes - 2] = act
+            out[planes - 1] = grad
+
+    shapes = [jax.ShapeDtypeStruct(array.shape, array.dtype) for array in filled]
     return call(
         body,
         place,
-        pieces,
+        (*pieces, *filled),
         after,
-        jax.ShapeDtypeStruct((2, share, hidden), jnp.bfloat16),
+        shapes or [jax.ShapeDtypeStruct((2, share, hidden), jnp.bfloat16)],
         [],
         16 * share * hidden,
+        {nodes + index: index for index in range(len(filled))},
     )
 
 
 def join(place_ref, piece_refs, index, joined):
-    rows = piece_refs[0].shape[1]
+    planes, rows, _ = piece_refs[0].shape
     for mask, ref in enumerate(piece_refs):
         first = pl.multiple_of((place_ref[0] ^ mask) * rows, rows)
-        joined[pl.ds(first, rows), :] = ref[index]
+        joined[pl.ds(first, rows), :] = ref[planes - 2 + index]
+
+
+def with_info(place, rows, routes, gates):
+    (count, width), chosen = rows.shape, routes[0].shape[0]
+    height = -(-6 * chosen // 16) * 16
+
+    def body(place_ref, rows_ref, *refs):
+        infos, out = refs[:-1], refs[-1]
+        lines = [ref[...].astype(jnp.float32) for ref in infos[:2]]
+        for ref in infos[2:]:
+            coarse = ref[...].astype(jnp.bfloat16).astype(jnp.float32)
+            lines += [coarse, ref[...] - coarse]
+        lines.append(jnp.zeros((height - 6 * chosen, count), jnp.float32))
+        out[0:count, :] = rows_ref[...]
+        out[count : count + height, :] = jnp.zeros((height, width), jnp.bfloat16)
+        out[count : count + height, 0:count] = jnp.concatenate(lines).astype(jnp.bfloat16)
+
+    return call(
+        body,
+        place,
+        (rows, *routes, *gates),
+        (),
+        jax.ShapeDtypeStruct((count + height, width), jnp.bfloat16),
+        [],
+        rows.size,
+    )
+
+
+def info_of(ref, count, chosen, which):
+    lines = ref[count:, 0:count].astype(jnp.float32)
+    routes = lines[which * chosen : (which + 1) * chosen].astype(jnp.int32)
+    first = 2 * (which + 1) * chosen
+    return routes, lines[first : first + chosen] + lines[first + chosen : first + 2 * chosen]
 
 
 def weight_column(expert, routes, gates):
@@ -293,22 +334,28 @@
     return (slots == slot).astype(jnp.float32).astype(jnp.bfloat16)
 
 
-def forward_results(place, pieces, w_down, info, added, after):
+def give(out, weight, result, added_refs):
+    total = weight * result.astype(jnp.bfloat16).astype(jnp.float32)
+    for ref in added_refs:
+        total += ref[0 : out.shape[0], :].astype(jnp.float32)
+    out[...] = total.astype(jnp.bfloat16)
+
+
+def forward_results(place, pieces, w_down, info, chosen, added, after):
     nodes, (_, share, hidden), width = len(pieces), pieces[0].shape, w_down.shape[1]
-    count, chosen = share * nodes, info.shape[0] // 4
+    count = share * nodes
 
     def body(place_ref, *refs):
-        piece_refs, (down_ref, info_ref, added_ref, out, joined) = refs[:nodes], refs[nodes:]
+        piece_refs, refs = refs[:nodes], refs[nodes:]
+        (down_ref, info_ref), added_refs, (out, joined) = refs[:2], refs[2:-2], refs[-2:]
         join(place_ref, piece_refs, 0, joined)
-        routes = info_ref[0:chosen].astype(jnp.int32)
-        weight = weight_column(place_ref[1], routes, info_ref[chosen : 2 * chosen])
-        result = matmul(joined[...], down_ref[...]).astype(jnp.bfloat16).astype(jnp.float32)
-        out[...] = (added_ref[...].astype(jnp.float32) + weight * result).astype(jnp.bfloat16)
+        weight = weight_column(place_ref[1], *info_of(info_ref, count, chosen, 0))
+        give(out, weight, matmul(joined[...], down_ref[...]), added_refs)
 
     return call(
         body,
         place,
-        (*pieces, w_down, info, added),
+        (*pieces, w_down, info, *added),
         after,
         jax.ShapeDtypeStruct((count, width), jnp.bfloat16),
         [pltpu.VMEM((count, hidden), jnp.bfloat16)],
@@ -316,18 +363,19 @@
     )
 
 
-def backward_results(place, pieces, w_gate, w_up, saved_gate, saved_up, info, added, block, after):
+def backward_results(place, pieces, w_gate, w_up, saved_gate, saved_up, info, chosen, added, block, after):
     nodes, (_, share, hidden), width = len(pieces), pieces[0].shape, w_gate.shape[0]
-    count, chosen = share * nodes, info.shape[0] // 4
+    count = share * nodes
     experts = saved_gate.shape[0] // count
 
     def body(place_ref, *refs):
         piece_refs, refs = refs[:nodes], refs[nodes:]
-        gate_ref, up_ref, saved_gate_ref, saved_up_ref, info_ref, added_ref, out, joined = refs
+        gate_ref, up_ref, saved_gate_ref, saved_up_ref, info_ref = refs[:5]
+        added_refs, (out, joined) = refs[5:-2], refs[-2:]
         join(place_ref, piece_refs, 1, joined)
         expert = place_ref[1]
-        routes = info_ref[2 * chosen : 3 * chosen].astype(jnp.int32)
-        weight = weight_column(expert, routes, info_ref[3 * chosen :])
+        routes, gates = info_of(info_ref, count, chosen, 1)
+        weight = weight_column(expert, routes, gates)
         select = slot_selection(expert, routes, count)
         first = pl.multiple_of(block_behind(expert, experts, block) * count, count)
         grad_gate, grad_up = backward_act(
@@ -337,13 +385,12 @@
         )
         result = matmul(grad_gate, gate_ref[...], CONTRACT_LAST)
         result += matmul(grad_up, up_ref[...], CONTRACT_LAST)
-        result = result.astype(jnp.bfloat16).astype(jnp.float32)
-        out[...] = (added_ref[...].astype(jnp.float32) + weight * result).astype(jnp.bfloat16)
+        give(out, weight, result, added_refs)
 
     return call(
         body,
         place,
-        (*pieces, w_gate, w_up, saved_gate, saved_up, info, added),
+        (*pieces, w_gate, w_up, saved_gate, saved_up, info, *added),
         after,
         jax.ShapeDtypeStruct((count, width), jnp.bfloat16),
         [pltpu.VMEM((count, hidden), jnp.bfloat16)],
@@ -369,62 +416,80 @@
     weights = (w_gate[0, 0], w_up[0, 0], w_down[0, 0])
     stored_gate, stored_up = saved_gate[0, 0], saved_up[0, 0]
 
-    tokens, grads = [inputs_forward[0]], [grads_backward[0]]
-    info = jnp.concatenate(
-        [
-            routes_forward[0].T.astype(jnp.float32),
-            gates_forward[0].T,
-            routes_backward[0].T.astype(jnp.float32),
-            gates_backward[0].T,
-        ]
-    )
+    chosen = routes_forward.shape[2]
+    tokens = [
+        with_info(
+            place,
+            inputs_forward[0],
+            (routes_forward[0].T, routes_backward[0].T),
+            (gates_forward[0].T, gates_backward[0].T),
+        )
+    ]
+    grads = [grads_backward[0]]
     for _ in range(1, experts):
         tokens.append(along_ring(tokens[-1], 1))
         grads.append(along_ring(grads[-1], 1))
-    infos = [info] + [along_ring(info, step) for step in range(1, experts)]
-
-    pieces, shares = [None] * experts, [None] * experts
-    order = []
-
-    def exchange(own):
-        return [own[mask] if mask == 0 else across(own[mask], "node", mask) for mask in range(nodes)]
+
+    sent, arrived, done = [None] * (experts + 1), [None] * (experts + 1), []
+
+    def exchange(turn, own):
+        sent[turn] = own
+        arrived[turn] = [own[0]] + [
+            across(own[mask % len(own)], "node", mask) for mask in range(1, nodes)
+        ]
 
     def first(step):
-        own = first_products(place, tokens[step], grads[step], weights, nodes, order[-1:])
-        order.append(own[0])
-        pieces[step] = exchange(own)
+        planes = 3 if step == 0 else 5
+        sent[step] = first_products(
+            place, tokens[step], grads[step], weights, nodes, planes, done[-1:]
+        )
+        done.append(sent[step][0])
+        if step == 0:
+            exchange(0, sent[0])
 
     def middle(step):
-        own = activations(place, pieces[step], order[-1:])
-        order.append(own)
-        shares[step] = exchange([own] * nodes)
-
-    hops = [inputs_forward[0], grads_backward[0]]
-    base = [None, None]
-
-    def last(step):
-        added = hops
-        if step == 1:
-            added = [jnp.zeros_like(hops[0]), jnp.zeros_like(hops[1])]
-        forward = forward_results(place, shares[step], weights[2], infos[step], added[0], order[-1:])
-        order.append(forward)
-        backward = backward_results(
-            place, shares[step], *weights[:2], stored_gate, stored_up, infos[step], added[1], step, order[-1:]
-        )
-        order.append(backward)
-        if step == 0:
-            base[:] = [from_behind(forward, "section", 1), from_behind(backward, "section", -1)]
-        elif step < experts - 1:
-            hops[:] = [along_ring(forward, 1), along_ring(backward, 1)]
-        else:
-            hops[:] = [along_ring_and_sections(forward, 1), along_ring_and_sections(backward, -1)]
-
-    for turn in range(experts + 2):
-        for act, step in ((first, turn), (last, turn - 2), (middle, turn - 1)):
-            if 0 <= step < experts:
-                act(step)
+        filled = sent[step + 1] if step + 1 < experts else ()
+        own = activations(place, arrived[step], filled, done[-1:])
+        done.append(own[0])
+        exchange(step + 1, own)
+
+    base, hops = [None, None], [(inputs_forward[0],), (grads_backward[0],)]
+
+    def last(step, *kinds):
+        for kind in kinds:
+            pieces, added = arrived[step + 1], hops[kind]
+            if kind == 0:
+                value = forward_results(
+                    place, pieces, weights[2], tokens[step], chosen, added, done[-1:]
+                )
+            else:
+                value = backward_results(
+                    place, pieces, *weights[:2], stored_gate, stored_up, tokens[step], chosen, added, step, done[-1:]
+                )
+            done.append(value)
+            if step == 0:
+                base[kind], hops[kind] = from_behind(value, "section", 1 - 2 * kind), ()
+            elif step < experts - 1:
+                hops[kind] = (along_ring(value, 1),)
+            else:
+                hops[kind] = (along_ring_and_sections(value, 1 - 2 * kind),)
+
+    first(0)
+    first(1)
+    middle(0)
+    for turn in range(1, experts - 1):
+        if turn >= 2:
+            last(turn - 2, 0, 1)
+        first(turn + 1)
+        middle(turn)
+    if experts >= 3:
+        last(experts - 3, 0, 1)
+    last(experts - 2, 0)
+    middle(experts - 1)
+    last(experts - 2, 1)
+    last(experts - 1, 0, 1)
     return tuple(
-        (own.astype(jnp.float32) + others.astype(jnp.float32)).astype(jnp.bfloat16)[None]
+        (own.astype(jnp.float32) + others[0].astype(jnp.float32)).astype(jnp.bfloat16)[None]
         for own, others in zip(base, hops)
     )
 

time: 117 us -> 110 us (0.940)
  starting transfers between devices: 36.7 us -> 28.3 us
  local copies, waits for them, and re-layouts: 7.16 us -> 9.72 us
  waiting for transfers between devices: 47.4 us -> 45 us
    ppermute x24 -> x15, starting transfers between devices: 26.2 us -> 18.6 us  [across(): lax.ppermute(value, axis, [(source, source ^ mask) for source in range(co...]
    ppermute x2, waiting for transfers between devices: 5.56 us -> 11.1 us  [along_ring_and_sections(): return lax.ppermute(value, ('section', 'dev'), pairs)]
    ppermute x13 -> x10, waiting for transfers between devices: 27.4 us -> 22.4 us  [along_ring(): return lax.ppermute(value, 'dev', ring_pairs(lax.axis_size('dev'), steps))]
    ppermute x24 -> x15, waiting for transfers between devices: 14.4 us -> 11.6 us  [across(): lax.ppermute(value, axis, [(source, source ^ mask) for source in range(co...]
    unnamed x32 -> x35, local copies, waits for them, and re-layouts: 7.14 us -> 9.72 us
    ppermute x13 -> x10, starting transfers between devices: 9.17 us -> 8.23 us  [along_ring(): return lax.ppermute(value, 'dev', ring_pairs(lax.axis_size('dev'), steps))]
    pallas_call x16 -> x17, Pallas kernels: 23.3 us -> 23.8 us  [call(): pl.pallas_call(with_after, in_specs=[SMEM] + [VMEM] * len(operands) + [AN...]
  transfers between devices with their start and end apart: 41 -> 29, of which waited for: 15 -> 11; matrix products, arithmetic and copies ran while one was open for 1% -> 1% of each run, Pallas kernels for 19% -> 19%
where the time goes in v3:
time: 110 us; the launch traced here: 109 us
  waiting for transfers between devices  45 us (41%)
  starting transfers between devices  28.3 us (26%)
  Pallas kernels  23.8 us (22%)
  local copies, waits for them, and re-layouts  9.72 us (9%)
  other arithmetic  1.58 us (1%)
    pallas_call x17, Pallas kernels, call(): pl.pallas_call(with_after, in_specs=[SMEM] + [VMEM] * len(operands) + [AN...  23.8 us
    ppermute x10, waiting for transfers between devices, along_ring(): return lax.ppermute(value, 'dev', ring_pairs(lax.axis_size('dev'), steps))  22.4 us
    ppermute x15, starting transfers between devices, across(): lax.ppermute(value, axis, [(source, source ^ mask) for source in range(co...  18.6 us
    ppermute x15, waiting for transfers between devices, across(): lax.ppermute(value, axis, [(source, source ^ mask) for source in range(co...  11.6 us
    ppermute x2, waiting for transfers between devices, along_ring_and_sections(): return lax.ppermute(value, ('section', 'dev'), pairs)  11.1 us
    unnamed x35, local copies, waits for them, and re-layouts  9.72 us
    ppermute x10, starting transfers between devices, along_ring(): return lax.ppermute(value, 'dev', ring_pairs(lax.axis_size('dev'), steps))  8.23 us
  transfers between devices with their start and end apart: 29, of which 11 were waited for; matrix products, arithmetic and copies ran while one was open for 1% of the time, Pallas kernels for 19%

profile of v3, /device:TPU:0, one launch (start us, length us, event | category | flops | bytes accessed | tf_op | source)
XLA Modules:
  0.0 109.3 jit_solution(2835925823448065547)
XLA Ops:
  4.9 3.1 %collective-permute-start.3 = (bf16[144,896]{1,0:T(8,128)(2,1)S(1)}, bf16[144,896]{1,0:T(8,128)(2,1)S(1)}, u32[]{:S(2)}, u32[]{:S(2)}) collective-permute-start(bf16[144,896]{1,0:T(8,128)(2,1)S(1)} %shard_map.122.refs_0_.refs_5_.refs_8_), channel_id=1, source_target_pairs={{0,1},{1,3},{3,2},{2,0},{4,5},{5,7},{7,6},{6,4},{8,9},{9,11},{11,1... | collective-permute-start | bytes 774152 | tf_op jit(solution)/shard_map/ppermute | solution.py:165
  8.0 2.6 %collective-permute-start.4 = (bf16[128,896]{1,0:T(8,128)(2,1)}, bf16[128,896]{1,0:T(8,128)(2,1)S(1)}, u32[]{:S(2)}, u32[]{:S(2)}) collective-permute-start(bf16[128,896]{1,0:T(8,128)(2,1)} %bitcast.59), channel_id=1, source_target_pairs={{0,1},{1,3},{3,2},{2,0},{4,5},{5,7},{7,6},{6,4},{8,9},{9,11},{11,1... | collective-permute-start | bytes 688136 | tf_op jit(solution)/shard_map/ppermute | solution.py:165
  10.6 1.5 %copy-done = bf16[1,1,1024,896]{3,2,1,0:T(8,128)(2,1)S(1)} copy-done((bf16[1,1,1024,896]{3,2,1,0:T(8,128)(2,1)S(1)}, bf16[1,1,1024,896]{3,2,1,0:T(8,128)(2,1)}, u32[]{:S(2)}) %copy-start) | copy-done | bytes 1835032
  12.1 1.5 %copy-done.2 = bf16[1,1,896,1024]{3,2,1,0:T(8,128)(2,1)S(1)} copy-done((bf16[1,1,896,1024]{3,2,1,0:T(8,128)(2,1)S(1)}, bf16[1,1,896,1024]{3,2,1,0:T(8,128)(2,1)}, u32[]{:S(2)}) %copy-start.2) | copy-done | bytes 1835032
  13.6 1.5 %copy-done.4 = bf16[1,1,896,1024]{3,2,1,0:T(8,128)(2,1)S(1)} copy-done((bf16[1,1,896,1024]{3,2,1,0:T(8,128)(2,1)S(1)}, bf16[1,1,896,1024]{3,2,1,0:T(8,128)(2,1)}, u32[]{:S(2)}) %copy-start.4) | copy-done | bytes 1835032
  16.0 1.8 %shard_map.123 = (bf16[3,32,1024]{2,1,0:T(8,128)(2,1)S(1)}, bf16[3,32,1024]{2,1,0:T(8,128)(2,1)S(1)}, bf16[3,32,1024]{2,1,0:T(8,128)(2,1)S(1)}, bf16[3,32,1024]{2,1,0:T(8,128)(2,1)S(1)}) custom-call(s32[2]{0:T(128)S(1)} %pad_add_fusion.place_ref, bf16[144,896]{1,0:T(8,128)(2,1)S(1)} %shard_map.122.refs_0_.refs_5_.refs_8_, bf16[128,896]{1,0:T(8,128)(2,1)S(1)} %bitcast.60, ...), custom_call_target="tpu_custom_call" | custom-call | flops 704643072 | bytes 5992448 | tf_op jit(solution)/shard_map/pallas_call | solution.py:190
  17.9 1.5 %collective-permute-start = (bf16[3,32,1024]{2,1,0:T(8,128)(2,1)S(1)}, bf16[3,32,1024]{2,1,0:T(8,128)(2,1)S(1)}, u32[]{:S(2)}, u32[]{:S(2)}) collective-permute-start(bf16[3,32,1024]{2,1,0:T(8,128)(2,1)S(1)} %get-tuple-element.31), channel_id=1, source_target_pairs={{0,4},{4,0},{8,12},{12,8},{1,5},{5,1},{9,13},{13,9},{2,6},{6,2},{1... | collective-permute-start | bytes 589832 | tf_op jit(solution)/shard_map/ppermute | solution.py:152
  19.4 1.5 %collective-permute-start.1 = (bf16[3,32,1024]{2,1,0:T(8,128)(2,1)S(1)}, bf16[3,32,1024]{2,1,0:T(8,128)(2,1)S(1)}, u32[]{:S(2)}, u32[]{:S(2)}) collective-permute-start(bf16[3,32,1024]{2,1,0:T(8,128)(2,1)S(1)} %get-tuple-element.32), channel_id=1, source_target_pairs={{0,8},{4,12},{8,0},{12,4},{1,9},{5,13},{9,1},{13,5},{2,10},{6,14},... | collective-permute-start | bytes 589832 | tf_op jit(solution)/shard_map/ppermute | solution.py:152
  21.5 1.8 %shard_map.124 = (bf16[5,32,1024]{2,1,0:T(8,128)(2,1)S(1)}, bf16[5,32,1024]{2,1,0:T(8,128)(2,1)S(1)}, bf16[5,32,1024]{2,1,0:T(8,128)(2,1)S(1)}, bf16[5,32,1024]{2,1,0:T(8,128)(2,1)S(1)}) custom-call(s32[2]{0:T(128)S(1)} %pad_add_fusion.place_ref, bf16[144,896]{1,0:T(8,128)(2,1)S(1)} %collective-permute-done.3.refs_0_.refs_5_.refs_8_, ...), custom_call_target="tpu_custom_call" | custom-call | flops 704643072 | bytes 5992448 | tf_op jit(solution)/shard_map/pallas_call | solution.py:190
  23.4 2.4 %collective-permute-done.refs_1_ = bf16[3,32,1024]{2,1,0:T(8,128)(2,1)S(1)} collective-permute-done((bf16[3,32,1024]{2,1,0:T(8,128)(2,1)S(1)}, bf16[3,32,1024]{2,1,0:T(8,128)(2,1)S(1)}, u32[]{:S(2)}, u32[]{:S(2)}) %collective-permute-start) | collective-permute-done | bytes 196640 | tf_op jit(solution)/shard_map/ppermute | solution.py:152
  25.8 3.7 %collective-permute-done.1.refs_2_ = bf16[3,32,1024]{2,1,0:T(8,128)(2,1)S(1)} collective-permute-done((bf16[3,32,1024]{2,1,0:T(8,128)(2,1)S(1)}, bf16[3,32,1024]{2,1,0:T(8,128)(2,1)S(1)}, u32[]{:S(2)}, u32[]{:S(2)}) %collective-permute-start.1) | collective-permute-done | bytes 196640 | tf_op jit(solution)/shard_map/ppermute | solution.py:152
  32.3 1.4 %collective-permute-start.7 = (bf16[5,32,1024]{2,1,0:T(8,128)(2,1)S(1)}, bf16[5,32,1024]{2,1,0:T(8,128)(2,1)S(1)}, u32[]{:S(2)}, u32[]{:S(2)}) collective-permute-start(bf16[5,32,1024]{2,1,0:T(8,128)(2,1)S(1)} %get-tuple-element.41), channel_id=1, source_target_pairs={{0,12},{4,8},{8,4},{12,0},{1,13},{5,9},{9,5},{13,1},{2,14},{6,10},... | collective-permute-start | bytes 983048 | tf_op jit(solution)/shard_map/ppermute | solution.py:152
  34.5 10.4 %collective-permute-done.9.refs_1_ = bf16[128,896]{1,0:T(8,128)(2,1)S(1)} collective-permute-done((bf16[128,896]{1,0:T(8,128)(2,1)S(1)}, bf16[128,896]{1,0:T(8,128)(2,1)S(1)}, u32[]{:S(2)}, u32[]{:S(2)}) %collective-permute-start.9) | collective-permute-done | bytes 229408 | tf_op jit(solution)/shard_map/ppermute | solution.py:165
  44.9 1.8 %shard_map.126 = (bf16[5,32,1024]{2,1,0:T(8,128)(2,1)S(1)}, bf16[5,32,1024]{2,1,0:T(8,128)(2,1)S(1)}, bf16[5,32,1024]{2,1,0:T(8,128)(2,1)S(1)}, bf16[5,32,1024]{2,1,0:T(8,128)(2,1)S(1)}) custom-call(s32[2]{0:T(128)S(1)} %pad_add_fusion.place_ref, bf16[144,896]{1,0:T(8,128)(2,1)S(1)} %collective-permute-done.8.refs_0_.refs_5_.refs_8_, ...), custom_call_target="tpu_custom_call" | custom-call | flops 704643072 | bytes 5992448 | tf_op jit(solution)/shard_map/pallas_call | solution.py:190
  47.5 1.5 %collective-permute-start.11 = (bf16[5,32,1024]{2,1,0:T(8,128)(2,1)S(1)}, bf16[5,32,1024]{2,1,0:T(8,128)(2,1)S(1)}, u32[]{:S(2)}, u32[]{:S(2)}) collective-permute-start(bf16[5,32,1024]{2,1,0:T(8,128)(2,1)S(1)} %get-tuple-element.47), channel_id=1, source_target_pairs={{0,4},{4,0},{8,12},{12,8},{1,5},{5,1},{9,13},{13,9},{2,6},{6,2},{1... | collective-permute-start | bytes 983048 | tf_op jit(solution)/shard_map/ppermute | solution.py:152
  49.6 1.5 %collective-permute-start.13 = (bf16[5,32,1024]{2,1,0:T(8,128)(2,1)S(1)}, bf16[5,32,1024]{2,1,0:T(8,128)(2,1)S(1)}, u32[]{:S(2)}, u32[]{:S(2)}) collective-permute-start(bf16[5,32,1024]{2,1,0:T(8,128)(2,1)S(1)} %get-tuple-element.49), channel_id=1, source_target_pairs={{0,12},{4,8},{8,4},{12,0},{1,13},{5,9},{9,5},{13,1},{2,14},{6,10},... | collective-permute-start | bytes 983048 | tf_op jit(solution)/shard_map/ppermute | solution.py:152
  53.4 2.3 %shard_map.129.refs_5_ = bf16[128,896]{1,0:T(8,128)(2,1)S(1)} custom-call(s32[2]{0:T(128)S(1)} %pad_add_fusion.place_ref, bf16[5,32,1024]{2,1,0:T(8,128)(2,1)S(1)} %get-tuple-element.38.refs_5_.refs_0_, bf16[5,32,1024]{2,1,0:T(8,128)(2,1)S(1)} %collective-permute-done.5.refs_1_, bf16[5,32,1024]{2,1,0:T(8,128)(2,1)S(1)} %collective-permute-done.6.refs_2_, ...), custom_call_target="tpu_custom_call" | custom-call | flops 469762048 | bytes 7565312 | tf_op jit(solution)/shard_map/pallas_call | solution.py:190
  55.7 5.1 %collective-permute-done.15.refs_1_ = bf16[128,896]{1,0:T(8,128)(2,1)S(1)} collective-permute-done((bf16[128,896]{1,0:T(8,128)(2,1)S(1)}, bf16[128,896]{1,0:T(8,128)(2,1)S(1)}, u32[]{:S(2)}, u32[]{:S(2)}) %collective-permute-start.15) | collective-permute-done | bytes 229408 | tf_op jit(solution)/shard_map/ppermute | solution.py:165
  60.8 1.8 %shard_map.130 = (bf16[5,32,1024]{2,1,0:T(8,128)(2,1)S(1)}, bf16[5,32,1024]{2,1,0:T(8,128)(2,1)S(1)}, bf16[5,32,1024]{2,1,0:T(8,128)(2,1)S(1)}, bf16[5,32,1024]{2,1,0:T(8,128)(2,1)S(1)}) custom-call(s32[2]{0:T(128)S(1)} %pad_add_fusion.place_ref, bf16[144,896]{1,0:T(8,128)(2,1)S(1)} %collective-permute-done.14.refs_0_.refs_5_.refs_8_, ...), custom_call_target="tpu_custom_call" | custom-call | flops 704643072 | bytes 5992448 | tf_op jit(solution)/shard_map/pallas_call | solution.py:190
  63.4 1.5 %collective-permute-start.16 = (bf16[5,32,1024]{2,1,0:T(8,128)(2,1)S(1)}, bf16[5,32,1024]{2,1,0:T(8,128)(2,1)S(1)}, u32[]{:S(2)}, u32[]{:S(2)}) collective-permute-start(bf16[5,32,1024]{2,1,0:T(8,128)(2,1)S(1)} %get-tuple-element.55), channel_id=1, source_target_pairs={{0,4},{4,0},{8,12},{12,8},{1,5},{5,1},{9,13},{13,9},{2,6},{6,2},{1... | collective-permute-start | bytes 983048 | tf_op jit(solution)/shard_map/ppermute | solution.py:152
  65.4 1.5 %collective-permute-start.18 = (bf16[5,32,1024]{2,1,0:T(8,128)(2,1)S(1)}, bf16[5,32,1024]{2,1,0:T(8,128)(2,1)S(1)}, u32[]{:S(2)}, u32[]{:S(2)}) collective-permute-start(bf16[5,32,1024]{2,1,0:T(8,128)(2,1)S(1)} %get-tuple-element.57), channel_id=1, source_target_pairs={{0,12},{4,8},{8,4},{12,0},{1,13},{5,9},{9,5},{13,1},{2,14},{6,10},... | collective-permute-start | bytes 983048 | tf_op jit(solution)/shard_map/ppermute | solution.py:152
  68.0 2.3 %shard_map.133.refs_7_ = bf16[128,896]{1,0:T(8,128)(2,1)S(1)} custom-call(s32[2]{0:T(128)S(1)} %pad_add_fusion.place_ref, bf16[5,32,1024]{2,1,0:T(8,128)(2,1)S(1)} %get-tuple-element.46.refs_7_.refs_0_, bf16[5,32,1024]{2,1,0:T(8,128)(2,1)S(1)} %collective-permute-done.11.refs_1_, bf16[5,32,1024]{2,1,0:T(8,128)(2,1)S(1)} %collective-permute-done.12.refs_2_, ...), custom_call_target="tpu_custom_call" | custom-call | flops 469762048 | bytes 7335936 | tf_op jit(solution)/shard_map/pallas_call | solution.py:190
  71.1 4.4 %collective-permute-done.19.refs_6_ = bf16[128,896]{1,0:T(8,128)(2,1)S(1)} collective-permute-done((bf16[128,896]{1,0:T(8,128)(2,1)S(1)}, bf16[128,896]{1,0:T(8,128)(2,1)S(1)}, u32[]{:S(2)}, u32[]{:S(2)}) %collective-permute-start.19) | collective-permute-done | bytes 229408 | tf_op jit(solution)/shard_map/ppermute | solution.py:165
  77.8 2.5 %collective-permute-done.24.refs_9_ = bf16[128,896]{1,0:T(8,128)(2,1)S(1)} collective-permute-done((bf16[128,896]{1,0:T(8,128)(2,1)S(1)}, bf16[128,896]{1,0:T(8,128)(2,1)S(1)}, u32[]{:S(2)}, u32[]{:S(2)}) %collective-permute-start.24) | collective-permute-done | bytes 229408 | tf_op jit(solution)/shard_map/ppermute | solution.py:165
  80.4 2.3 %shard_map.136.refs_7_ = bf16[128,896]{1,0:T(8,128)(2,1)S(1)} custom-call(s32[2]{0:T(128)S(1)} %pad_add_fusion.place_ref, bf16[5,32,1024]{2,1,0:T(8,128)(2,1)S(1)} %get-tuple-element.54.refs_6_.refs_0_, bf16[5,32,1024]{2,1,0:T(8,128)(2,1)S(1)} %collective-permute-done.16.refs_1_, bf16[5,32,1024]{2,1,0:T(8,128)(2,1)S(1)} %collective-permute-done.17.refs_2_, ...), custom_call_target="tpu_custom_call" | custom-call | flops 469762048 | bytes 7565312 | tf_op jit(solution)/shard_map/pallas_call | solution.py:190
  82.7 2.8 %collective-permute-start.20 = (bf16[2,32,1024]{2,1,0:T(8,128)(2,1)S(1)}, bf16[2,32,1024]{2,1,0:T(8,128)(2,1)S(1)}, u32[]{:S(2)}, u32[]{:S(2)}) collective-permute-start(bf16[2,32,1024]{2,1,0:T(8,128)(2,1)S(1)} %shard_map.135.refs_10_.refs_0_), channel_id=1, source_target_pairs={{0,4},{4,0},{8,12},{12,8},{1,5},{5,1},{9,13},{13,9},{2,6},{6,2},{1... | collective-permute-start | bytes 393224 | tf_op jit(solution)/shard_map/ppermute | solution.py:152
  85.5 1.5 %collective-permute-start.22 = (bf16[2,32,1024]{2,1,0:T(8,128)(2,1)S(1)}, bf16[2,32,1024]{2,1,0:T(8,128)(2,1)S(1)}, u32[]{:S(2)}, u32[]{:S(2)}) collective-permute-start(bf16[2,32,1024]{2,1,0:T(8,128)(2,1)S(1)} %shard_map.135.refs_10_.refs_0_), channel_id=1, source_target_pairs={{0,12},{4,8},{8,4},{12,0},{1,13},{5,9},{9,5},{13,1},{2,14},{6,10},... | collective-permute-start | bytes 393224 | tf_op jit(solution)/shard_map/ppermute | solution.py:152
  87.1 1.4 %collective-permute-done.20.refs_1_ = bf16[2,32,1024]{2,1,0:T(8,128)(2,1)S(1)} collective-permute-done((bf16[2,32,1024]{2,1,0:T(8,128)(2,1)S(1)}, bf16[2,32,1024]{2,1,0:T(8,128)(2,1)S(1)}, u32[]{:S(2)}, u32[]{:S(2)}) %collective-permute-start.20) | collective-permute-done | bytes 131104 | tf_op jit(solution)/shard_map/ppermute | solution.py:152
  88.5 3.4 %collective-permute-done.21.refs_2_ = bf16[2,32,1024]{2,1,0:T(8,128)(2,1)S(1)} collective-permute-done((bf16[2,32,1024]{2,1,0:T(8,128)(2,1)S(1)}, bf16[2,32,1024]{2,1,0:T(8,128)(2,1)S(1)}, u32[]{:S(2)}, u32[]{:S(2)}) %collective-permute-start.21) | collective-permute-done | bytes 131104 | tf_op jit(solution)/shard_map/ppermute | solution.py:152
  92.9 2.3 %shard_map.138 = bf16[128,896]{1,0:T(8,128)(2,1)S(1)} custom-call(s32[2]{0:T(128)S(1)} %pad_add_fusion.place_ref, bf16[2,32,1024]{2,1,0:T(8,128)(2,1)S(1)} %shard_map.135.refs_10_.refs_0_, bf16[2,32,1024]{2,1,0:T(8,128)(2,1)S(1)} %collective-permute-done.20.refs_1_, bf16[2,32,1024]{2,1,0:T(8,128)(2,1)S(1)} %collective-permute-done.21.refs_2_, ...), custom_call_target="tpu_custom_call" | custom-call | flops 469762048 | bytes 6778880 | tf_op jit(solution)/shard_map/pallas_call | solution.py:190
  96.7 6.9 %collective-permute-done.28 = bf16[128,896]{1,0:T(8,128)(2,1)S(1)} collective-permute-done((bf16[128,896]{1,0:T(8,128)(2,1)S(1)}, bf16[128,896]{1,0:T(8,128)(2,1)S(1)}, u32[]{:S(2)}, u32[]{:S(2)}) %collective-permute-start.28) | collective-permute-done | bytes 229408 | tf_op jit(solution)/shard_map/ppermute | solution.py:175
  104.4 4.2 %collective-permute-done.25 = bf16[128,896]{1,0:T(8,128)(2,1)S(1)} collective-permute-done((bf16[128,896]{1,0:T(8,128)(2,1)S(1)}, bf16[128,896]{1,0:T(8,128)(2,1)S(1)}, u32[]{:S(2)}, u32[]{:S(2)}) %collective-permute-start.25) | collective-permute-done | bytes 229408 | tf_op jit(solution)/shard_map/ppermute | solution.py:175
  (81 shorter events, 22.4 us)
Async XLA Ops:
  4.9 16.5 %collective-permute-start.3 = (bf16[144,896]{1,0:T(8,128)(2,1)S(1)}, bf16[144,896]{1,0:T(8,128)(2,1)S(1)}, u32[]{:S(2)}, u32[]{:S(2)}) collective-permute-start(bf16[144,896]{1,0:T(8,128)(2,1)S(1)} %shard_map.122.refs_0_.refs_5_.refs_8_), channel_id=1, source_target_pairs={{0,1},{1,3},{3,2},{2,0},{4,5},{5,7},{7,6},{6,4},{8,9},{9,11},{11,1... | collective-permute-start | bytes 774152 | tf_op jit(solution)/shard_map/ppermute | solution.py:165
  8.0 13.4 %collective-permute-start.4 = (bf16[128,896]{1,0:T(8,128)(2,1)}, bf16[128,896]{1,0:T(8,128)(2,1)S(1)}, u32[]{:S(2)}, u32[]{:S(2)}) collective-permute-start(bf16[128,896]{1,0:T(8,128)(2,1)} %bitcast.59), channel_id=1, source_target_pairs={{0,1},{1,3},{3,2},{2,0},{4,5},{5,7},{7,6},{6,4},{8,9},{9,11},{11,1... | collective-permute-start | bytes 688136 | tf_op jit(solution)/shard_map/ppermute | solution.py:165
  16.0 5.4 %copy-start.1 = (bf16[1,1,1024,896]{3,2,1,0:T(8,128)(2,1)S(1)}, bf16[1,1,1024,896]{3,2,1,0:T(8,128)(2,1)}, u32[]{:S(2)}) copy-start(bf16[1,1,1024,896]{3,2,1,0:T(8,128)(2,1)} %param.19) | copy-start | bytes 5505028
  16.0 5.4 %copy-start.3 = (bf16[1,1,896,1024]{3,2,1,0:T(8,128)(2,1)S(1)}, bf16[1,1,896,1024]{3,2,1,0:T(8,128)(2,1)}, u32[]{:S(2)}) copy-start(bf16[1,1,896,1024]{3,2,1,0:T(8,128)(2,1)} %param.17) | copy-start | bytes 5505028
  17.9 7.9 %collective-permute-start = (bf16[3,32,1024]{2,1,0:T(8,128)(2,1)S(1)}, bf16[3,32,1024]{2,1,0:T(8,128)(2,1)S(1)}, u32[]{:S(2)}, u32[]{:S(2)}) collective-permute-start(bf16[3,32,1024]{2,1,0:T(8,128)(2,1)S(1)} %get-tuple-element.31), channel_id=1, source_target_pairs={{0,4},{4,0},{8,12},{12,8},{1,5},{5,1},{9,13},{13,9},{2,6},{6,2},{1... | collective-permute-start | bytes 589832 | tf_op jit(solution)/shard_map/ppermute | solution.py:152
  19.4 10.0 %collective-permute-start.1 = (bf16[3,32,1024]{2,1,0:T(8,128)(2,1)S(1)}, bf16[3,32,1024]{2,1,0:T(8,128)(2,1)S(1)}, u32[]{:S(2)}, u32[]{:S(2)}) collective-permute-start(bf16[3,32,1024]{2,1,0:T(8,128)(2,1)S(1)} %get-tuple-element.32), channel_id=1, source_target_pairs={{0,8},{4,12},{8,0},{12,4},{1,9},{5,13},{9,1},{13,5},{2,10},{6,14},... | collective-permute-start | bytes 589832 | tf_op jit(solution)/shard_map/ppermute | solution.py:152
  21.0 8.5 %collective-permute-start.2 = (bf16[3,32,1024]{2,1,0:T(8,128)(2,1)S(1)}, bf16[3,32,1024]{2,1,0:T(8,128)(2,1)S(1)}, u32[]{:S(2)}, u32[]{:S(2)}) collective-permute-start(bf16[3,32,1024]{2,1,0:T(8,128)(2,1)S(1)} %get-tuple-element.33), channel_id=1, source_target_pairs={{0,12},{4,8},{8,4},{12,0},{1,13},{5,9},{9,5},{13,1},{2,14},{6,10},... | collective-permute-start | bytes 589832 | tf_op jit(solution)/shard_map/ppermute | solution.py:152
  23.3 21.6 %copy-start.5 = (bf16[1,1,896,1024]{3,2,1,0:T(8,128)(2,1)S(1)}, bf16[1,1,896,1024]{3,2,1,0:T(8,128)(2,1)}, u32[]{:S(2)}) copy-start(bf16[1,1,896,1024]{3,2,1,0:T(8,128)(2,1)} %param.18) | copy-start | bytes 5505028
  30.1 16.7 %collective-permute-start.5 = (bf16[5,32,1024]{2,1,0:T(8,128)(2,1)S(1)}, bf16[5,32,1024]{2,1,0:T(8,128)(2,1)S(1)}, u32[]{:S(2)}, u32[]{:S(2)}) collective-permute-start(bf16[5,32,1024]{2,1,0:T(8,128)(2,1)S(1)} %get-tuple-element.39), channel_id=1, source_target_pairs={{0,4},{4,0},{8,12},{12,8},{1,5},{5,1},{9,13},{13,9},{2,6},{6,2},{1... | collective-permute-start | bytes 983048 | tf_op jit(solution)/shard_map/ppermute | solution.py:152
  31.4 15.4 %collective-permute-start.6 = (bf16[5,32,1024]{2,1,0:T(8,128)(2,1)S(1)}, bf16[5,32,1024]{2,1,0:T(8,128)(2,1)S(1)}, u32[]{:S(2)}, u32[]{:S(2)}) collective-permute-start(bf16[5,32,1024]{2,1,0:T(8,128)(2,1)S(1)} %get-tuple-element.40), channel_id=1, source_target_pairs={{0,8},{4,12},{8,0},{12,4},{1,9},{5,13},{9,1},{13,5},{2,10},{6,14},... | collective-permute-start | bytes 983048 | tf_op jit(solution)/shard_map/ppermute | solution.py:152
  32.3 14.6 %collective-permute-start.7 = (bf16[5,32,1024]{2,1,0:T(8,128)(2,1)S(1)}, bf16[5,32,1024]{2,1,0:T(8,128)(2,1)S(1)}, u32[]{:S(2)}, u32[]{:S(2)}) collective-permute-start(bf16[5,32,1024]{2,1,0:T(8,128)(2,1)S(1)} %get-tuple-element.41), channel_id=1, source_target_pairs={{0,12},{4,8},{8,4},{12,0},{1,13},{5,9},{9,5},{13,1},{2,14},{6,10},... | collective-permute-start | bytes 983048 | tf_op jit(solution)/shard_map/ppermute | solution.py:152
  33.7 11.2 %collective-permute-start.8 = (bf16[144,896]{1,0:T(8,128)(2,1)S(1)}, bf16[144,896]{1,0:T(8,128)(2,1)S(1)}, u32[]{:S(2)}, u32[]{:S(2)}) collective-permute-start(bf16[144,896]{1,0:T(8,128)(2,1)S(1)} %collective-permute-done.3.refs_0_.refs_5_.refs_8_), channel_id=1, source_target_pairs={{0,1},{1,3},{3,2},{2,0},{4,5},{5,7},{7,6},{6,4},{8,9},{9,11},{11,1... | collective-permute-start | bytes 774152 | tf_op jit(solution)/shard_map/ppermute | solution.py:165
  34.1 10.8 %collective-permute-start.9 = (bf16[128,896]{1,0:T(8,128)(2,1)S(1)}, bf16[128,896]{1,0:T(8,128)(2,1)S(1)}, u32[]{:S(2)}, u32[]{:S(2)}) collective-permute-start(bf16[128,896]{1,0:T(8,128)(2,1)S(1)} %collective-permute-done.4.refs_1_), channel_id=1, source_target_pairs={{0,1},{1,3},{3,2},{2,0},{4,5},{5,7},{7,6},{6,4},{8,9},{9,11},{11,1... | collective-permute-start | bytes 688136 | tf_op jit(solution)/shard_map/ppermute | solution.py:165
  47.5 15.1 %collective-permute-start.11 = (bf16[5,32,1024]{2,1,0:T(8,128)(2,1)S(1)}, bf16[5,32,1024]{2,1,0:T(8,128)(2,1)S(1)}, u32[]{:S(2)}, u32[]{:S(2)}) collective-permute-start(bf16[5,32,1024]{2,1,0:T(8,128)(2,1)S(1)} %get-tuple-element.47), channel_id=1, source_target_pairs={{0,4},{4,0},{8,12},{12,8},{1,5},{5,1},{9,13},{13,9},{2,6},{6,2},{1... | collective-permute-start | bytes 983048 | tf_op jit(solution)/shard_map/ppermute | solution.py:152
  49.0 13.6 %collective-permute-start.12 = (bf16[5,32,1024]{2,1,0:T(8,128)(2,1)S(1)}, bf16[5,32,1024]{2,1,0:T(8,128)(2,1)S(1)}, u32[]{:S(2)}, u32[]{:S(2)}) collective-permute-start(bf16[5,32,1024]{2,1,0:T(8,128)(2,1)S(1)} %get-tuple-element.48), channel_id=1, source_target_pairs={{0,8},{4,12},{8,0},{12,4},{1,9},{5,13},{9,1},{13,5},{2,10},{6,14},... | collective-permute-start | bytes 983048 | tf_op jit(solution)/shard_map/ppermute | solution.py:152
  49.6 13.1 %collective-permute-start.13 = (bf16[5,32,1024]{2,1,0:T(8,128)(2,1)S(1)}, bf16[5,32,1024]{2,1,0:T(8,128)(2,1)S(1)}, u32[]{:S(2)}, u32[]{:S(2)}) collective-permute-start(bf16[5,32,1024]{2,1,0:T(8,128)(2,1)S(1)} %get-tuple-element.49), channel_id=1, source_target_pairs={{0,12},{4,8},{8,4},{12,0},{1,13},{5,9},{9,5},{13,1},{2,14},{6,10},... | collective-permute-start | bytes 983048 | tf_op jit(solution)/shard_map/ppermute | solution.py:152
  51.1 9.7 %collective-permute-start.14 = (bf16[144,896]{1,0:T(8,128)(2,1)S(1)}, bf16[144,896]{1,0:T(8,128)(2,1)S(1)}, u32[]{:S(2)}, u32[]{:S(2)}) collective-permute-start(bf16[144,896]{1,0:T(8,128)(2,1)S(1)} %collective-permute-done.8.refs_0_.refs_5_.refs_8_), channel_id=1, source_target_pairs={{0,1},{1,3},{3,2},{2,0},{4,5},{5,7},{7,6},{6,4},{8,9},{9,11},{11,1... | collective-permute-start | bytes 774152 | tf_op jit(solution)/shard_map/ppermute | solution.py:165
  51.1 9.7 %collective-permute-start.15 = (bf16[128,896]{1,0:T(8,128)(2,1)S(1)}, bf16[128,896]{1,0:T(8,128)(2,1)S(1)}, u32[]{:S(2)}, u32[]{:S(2)}) collective-permute-start(bf16[128,896]{1,0:T(8,128)(2,1)S(1)} %collective-permute-done.9.refs_1_), channel_id=1, source_target_pairs={{0,1},{1,3},{3,2},{2,0},{4,5},{5,7},{7,6},{6,4},{8,9},{9,11},{11,1... | collective-permute-start | bytes 688136 | tf_op jit(solution)/shard_map/ppermute | solution.py:165
  63.4 12.1 %collective-permute-start.16 = (bf16[5,32,1024]{2,1,0:T(8,128)(2,1)S(1)}, bf16[5,32,1024]{2,1,0:T(8,128)(2,1)S(1)}, u32[]{:S(2)}, u32[]{:S(2)}) collective-permute-start(bf16[5,32,1024]{2,1,0:T(8,128)(2,1)S(1)} %get-tuple-element.55), channel_id=1, source_target_pairs={{0,4},{4,0},{8,12},{12,8},{1,5},{5,1},{9,13},{13,9},{2,6},{6,2},{1... | collective-permute-start | bytes 983048 | tf_op jit(solution)/shard_map/ppermute | solution.py:152
  64.9 11.2 %collective-permute-start.17 = (bf16[5,32,1024]{2,1,0:T(8,128)(2,1)S(1)}, bf16[5,32,1024]{2,1,0:T(8,128)(2,1)S(1)}, u32[]{:S(2)}, u32[]{:S(2)}) collective-permute-start(bf16[5,32,1024]{2,1,0:T(8,128)(2,1)S(1)} %get-tuple-element.56), channel_id=1, source_target_pairs={{0,8},{4,12},{8,0},{12,4},{1,9},{5,13},{9,1},{13,5},{2,10},{6,14},... | collective-permute-start | bytes 983048 | tf_op jit(solution)/shard_map/ppermute | solution.py:152
  65.4 10.7 %collective-permute-start.18 = (bf16[5,32,1024]{2,1,0:T(8,128)(2,1)S(1)}, bf16[5,32,1024]{2,1,0:T(8,128)(2,1)S(1)}, u32[]{:S(2)}, u32[]{:S(2)}) collective-permute-start(bf16[5,32,1024]{2,1,0:T(8,128)(2,1)S(1)} %get-tuple-element.57), channel_id=1, source_target_pairs={{0,12},{4,8},{8,4},{12,0},{1,13},{5,9},{9,5},{13,1},{2,14},{6,10},... | collective-permute-start | bytes 983048 | tf_op jit(solution)/shard_map/ppermute | solution.py:152
  67.9 7.5 %collective-permute-start.19 = (bf16[128,896]{1,0:T(8,128)(2,1)S(1)}, bf16[128,896]{1,0:T(8,128)(2,1)S(1)}, u32[]{:S(2)}, u32[]{:S(2)}) collective-permute-start(bf16[128,896]{1,0:T(8,128)(2,1)S(1)} %shard_map.132.refs_9_), channel_id=1, source_target_pairs={{0,1},{1,3},{3,2},{2,0},{4,5},{5,7},{7,6},{6,4},{8,9},{9,11},{11,1... | collective-permute-start | bytes 688136 | tf_op jit(solution)/shard_map/ppermute | solution.py:165
  70.3 10.1 %collective-permute-start.24 = (bf16[128,896]{1,0:T(8,128)(2,1)S(1)}, bf16[128,896]{1,0:T(8,128)(2,1)S(1)}, u32[]{:S(2)}, u32[]{:S(2)}) collective-permute-start(bf16[128,896]{1,0:T(8,128)(2,1)S(1)} %shard_map.133.refs_7_), channel_id=1, source_target_pairs={{0,1},{1,3},{3,2},{2,0},{4,5},{5,7},{7,6},{6,4},{8,9},{9,11},{11,1... | collective-permute-start | bytes 688136 | tf_op jit(solution)/shard_map/ppermute | solution.py:165
  77.1 14.8 %collective-permute-start.23 = (bf16[128,896]{1,0:T(8,128)(2,1)S(1)}, bf16[128,896]{1,0:T(8,128)(2,1)S(1)}, u32[]{:S(2)}, u32[]{:S(2)}) collective-permute-start(bf16[128,896]{1,0:T(8,128)(2,1)S(1)} %shard_map.134.refs_4_), channel_id=1, source_target_pairs={{0,1},{1,3},{3,2},{2,0},{4,5},{5,7},{7,6},{6,4},{8,9},{9,11},{11,1... | collective-permute-start | bytes 688136 | tf_op jit(solution)/shard_map/ppermute | solution.py:165
  82.7 10.3 %collective-permute-start.27 = (bf16[128,896]{1,0:T(8,128)(2,1)S(1)}, bf16[128,896]{1,0:T(8,128)(2,1)S(1)}, u32[]{:S(2)}, u32[]{:S(2)}) collective-permute-start(bf16[128,896]{1,0:T(8,128)(2,1)S(1)} %shard_map.136.refs_7_), channel_id=1, source_target_pairs={{0,1},{1,3},{3,2},{2,0},{4,5},{5,7},{7,6},{6,4},{8,9},{9,11},{11,1... | collective-permute-start | bytes 688136 | tf_op jit(solution)/shard_map/ppermute | solution.py:165
  82.7 5.8 %collective-permute-start.20 = (bf16[2,32,1024]{2,1,0:T(8,128)(2,1)S(1)}, bf16[2,32,1024]{2,1,0:T(8,128)(2,1)S(1)}, u32[]{:S(2)}, u32[]{:S(2)}) collective-permute-start(bf16[2,32,1024]{2,1,0:T(8,128)(2,1)S(1)} %shard_map.135.refs_10_.refs_0_), channel_id=1, source_target_pairs={{0,4},{4,0},{8,12},{12,8},{1,5},{5,1},{9,13},{13,9},{2,6},{6,2},{1... | collective-permute-start | bytes 393224 | tf_op jit(solution)/shard_map/ppermute | solution.py:152
  85.5 6.4 %collective-permute-start.21 = (bf16[2,32,1024]{2,1,0:T(8,128)(2,1)S(1)}, bf16[2,32,1024]{2,1,0:T(8,128)(2,1)S(1)}, u32[]{:S(2)}, u32[]{:S(2)}) collective-permute-start(bf16[2,32,1024]{2,1,0:T(8,128)(2,1)S(1)} %shard_map.135.refs_10_.refs_0_), channel_id=1, source_target_pairs={{0,8},{4,12},{8,0},{12,4},{1,9},{5,13},{9,1},{13,5},{2,10},{6,14},... | collective-permute-start | bytes 393224 | tf_op jit(solution)/shard_map/ppermute | solution.py:152
  85.5 6.4 %collective-permute-start.22 = (bf16[2,32,1024]{2,1,0:T(8,128)(2,1)S(1)}, bf16[2,32,1024]{2,1,0:T(8,128)(2,1)S(1)}, u32[]{:S(2)}, u32[]{:S(2)}) collective-permute-start(bf16[2,32,1024]{2,1,0:T(8,128)(2,1)S(1)} %shard_map.135.refs_10_.refs_0_), channel_id=1, source_target_pairs={{0,12},{4,8},{8,4},{12,0},{1,13},{5,9},{9,5},{13,1},{2,14},{6,10},... | collective-permute-start | bytes 393224 | tf_op jit(solution)/shard_map/ppermute | solution.py:152
  88.5 8.3 %collective-permute-start.26 = (bf16[128,896]{1,0:T(8,128)(2,1)S(1)}, bf16[128,896]{1,0:T(8,128)(2,1)S(1)}, u32[]{:S(2)}, u32[]{:S(2)}) collective-permute-start(bf16[128,896]{1,0:T(8,128)(2,1)S(1)} %shard_map.129.refs_5_), channel_id=1, source_target_pairs={{0,16},{16,0},{1,17},{17,1},{2,18},{18,2},{3,19},{19,3},{4,20},{20... | collective-permute-start | bytes 688136 | tf_op jit(solution)/shard_map/ppermute | solution.py:14
  95.2 8.4 %collective-permute-start.28 = (bf16[128,896]{1,0:T(8,128)(2,1)S(1)}, bf16[128,896]{1,0:T(8,128)(2,1)S(1)}, u32[]{:S(2)}, u32[]{:S(2)}) collective-permute-start(bf16[128,896]{1,0:T(8,128)(2,1)S(1)} %shard_map.138), channel_id=1, source_target_pairs={{0,17},{1,19},{3,18},{2,16},{16,1},{17,3},{19,2},{18,0},{4,21},{5,... | collective-permute-start | bytes 688136 | tf_op jit(solution)/shard_map/ppermute | solution.py:175
  95.3 9.1 %collective-permute-start.10 = (bf16[128,896]{1,0:T(8,128)(2,1)S(1)}, bf16[128,896]{1,0:T(8,128)(2,1)S(1)}, u32[]{:S(2)}, u32[]{:S(2)}) collective-permute-start(bf16[128,896]{1,0:T(8,128)(2,1)S(1)} %shard_map.128.refs_10_), channel_id=1, source_target_pairs={{0,16},{16,0},{1,17},{17,1},{2,18},{18,2},{3,19},{19,3},{4,20},{20... | collective-permute-start | bytes 688136 | tf_op jit(solution)/shard_map/ppermute | solution.py:14
  95.4 13.2 %collective-permute-start.25 = (bf16[128,896]{1,0:T(8,128)(2,1)S(1)}, bf16[128,896]{1,0:T(8,128)(2,1)S(1)}, u32[]{:S(2)}, u32[]{:S(2)}) collective-permute-start(bf16[128,896]{1,0:T(8,128)(2,1)S(1)} %shard_map.137.refs_10_), channel_id=1, source_target_pairs={{0,17},{1,19},{3,18},{2,16},{16,1},{17,3},{19,2},{18,0},{4,21},{5,... | collective-permute-start | bytes 688136 | tf_op jit(solution)/shard_map/ppermute | solution.py:175
  (13 other events, 18.5 us)

commit v4 on v3

--- a/solution.py
+++ b/solution.py
@@ -143,8 +143,10 @@
 VMEM = pl.BlockSpec(memory_space=pltpu.VMEM)
 SMEM = pl.BlockSpec(memory_space=pltpu.SMEM)
 VMEM_BYTES = 14 << 20
-CF = 1.0
+CF = 100.0
+WIDE_BYTES = 56 << 20
 ANY = pl.BlockSpec(memory_space=pl.ANY)
+HBM = pl.BlockSpec(memory_space=pltpu.HBM)
 
 
 def across(value, axis, mask):
@@ -273,30 +275,96 @@
         joined[pl.ds(first, rows), :] = ref[planes - 2 + index]
 
 
-def with_info(place, rows, routes, gates):
+def copied(sources, targets, sems):
+    copies = [
+        pltpu.make_async_copy(source, target, sems.at[index])
+        for index, (source, target) in enumerate(zip(sources, targets))
+    ]
+    for copy in copies:
+        copy.start()
+    return copies
+
+
+def with_info(rows, routes, gates):
     (count, width), chosen = rows.shape, routes[0].shape[0]
     height = -(-6 * chosen // 16) * 16
-
-    def body(place_ref, rows_ref, *refs):
-        infos, out = refs[:-1], refs[-1]
-        lines = [ref[...].astype(jnp.float32) for ref in infos[:2]]
-        for ref in infos[2:]:
+    small = (*routes, *gates)
+
+    def body(*refs):
+        inputs, out, held, sems = refs[:5], refs[5], refs[6:10], refs[10]
+        targets = (out.at[pl.ds(0, count)], *held)
+        for copy in copied(inputs, targets, sems):
+            copy.wait()
+        lines = [ref[...].astype(jnp.float32) for ref in held[:2]]
+        for ref in held[2:]:
             coarse = ref[...].astype(jnp.bfloat16).astype(jnp.float32)
             lines += [coarse, ref[...] - coarse]
         lines.append(jnp.zeros((height - 6 * chosen, count), jnp.float32))
-        out[0:count, :] = rows_ref[...]
-        out[count : count + height, :] = jnp.zeros((height, width), jnp.bfloat16)
-        out[count : count + height, 0:count] = jnp.concatenate(lines).astype(jnp.bfloat16)
-
-    return call(
+        out[count:, :] = jnp.zeros((height, width), jnp.bfloat16)
+        out[count:, 0:count] = jnp.concatenate(lines).astype(jnp.bfloat16)
+
+    return pl.pallas_call(
         body,
-        place,
-        (rows, *routes, *gates),
-        (),
-        jax.ShapeDtypeStruct((count + height, width), jnp.bfloat16),
-        [],
-        rows.size,
-    )
+        in_specs=[HBM] * 5,
+        out_specs=VMEM,
+        out_shape=jax.ShapeDtypeStruct((count + height, width), jnp.bfloat16),
+        scratch_shapes=[pltpu.VMEM(value.shape, value.dtype) for value in small]
+        + [pltpu.SemaphoreType.DMA((5,))],
+        compiler_params=pltpu.CompilerParams(vmem_limit_bytes=WIDE_BYTES),
+    )(rows, *small)
+
+
+def opening_products(place, token_rows, grad_rows, weights, nodes):
+    (count, width), hidden = grad_rows.shape, weights[0].shape[1]
+    share = count // nodes
+    operands = (token_rows, weights[0], weights[1], grad_rows, weights[2])
+    cuts = 4
+
+    def body(place_ref, *refs):
+        inputs, pieces, held = refs[:5], refs[5 : 5 + nodes], refs[5 + nodes : 10 + nodes]
+        sorted_rows, sems = refs[10 + nodes :]
+
+        def pieces_of(ref):
+            rows = ref.shape[0] // cuts
+            return [ref.at[pl.ds(cut * rows, rows)] for cut in range(cuts)]
+
+        parts = [
+            copied(pieces_of(source), pieces_of(target), sems.at[index])
+            for index, (source, target) in enumerate(zip(inputs, held))
+        ]
+
+        def wait(index):
+            for copy in parts[index]:
+                copy.wait()
+
+        def give(index, part):
+            for mask in range(nodes):
+                pieces[mask][index] = part[mask * share : (mask + 1) * share].astype(jnp.bfloat16)
+
+        wait(0)
+        by_owner(place_ref, held[0], sorted_rows, nodes)
+        for index in (0, 1):
+            wait(index + 1)
+            give(index, matmul(sorted_rows[...], held[index + 1][...]))
+        wait(3)
+        by_owner(place_ref, held[3], sorted_rows, nodes)
+        wait(4)
+        give(2, matmul(sorted_rows[...], held[4][...], CONTRACT_LAST))
+
+    return pl.pallas_call(
+        body,
+        in_specs=[SMEM] + [HBM] * 5,
+        out_specs=[VMEM] * nodes,
+        out_shape=[jax.ShapeDtypeStruct((3, share, hidden), jnp.bfloat16)] * nodes,
+        scratch_shapes=[pltpu.VMEM(value.shape, value.dtype) for value in operands]
+        + [pltpu.VMEM((count, width), jnp.bfloat16), pltpu.SemaphoreType.DMA((5, cuts))],
+        cost_estimate=pl.CostEstimate(
+            flops=int(CF * 6 * count * width * hidden),
+            bytes_accessed=int(CF * 6 * width * hidden),
+            transcendentals=0,
+        ),
+        compiler_params=pltpu.CompilerParams(vmem_limit_bytes=WIDE_BYTES),
+    )(place, *operands)
 
 
 def info_of(ref, count, chosen, which):
@@ -419,7 +487,6 @@
     chosen = routes_forward.shape[2]
     tokens = [
         with_info(
-            place,
             inputs_forward[0],
             (routes_forward[0].T, routes_backward[0].T),
             (gates_forward[0].T, gates_backward[0].T),
@@ -439,10 +506,14 @@
         ]
 
     def first(step):
-        planes = 3 if step == 0 else 5
-        sent[step] = first_products(
-            place, tokens[step], grads[step], weights, nodes, planes, done[-1:]
-        )
+        if step == 0:
+            sent[0] = opening_products(
+                place, inputs_forward[0], grads_backward[0], weights, nodes
+            )
+        else:
+            sent[step] = first_products(
+                place, tokens[step], grads[step], weights, nodes, 5, done[-1:]
+            )
         done.append(sent[step][0])
         if step == 0:
             exchange(0, sent[0])

time: 110 us -> 105 us (0.955)
  waiting for transfers between devices: 45 us -> 32.1 us
  starting transfers between devices: 28.3 us -> 37.3 us
  local copies, waits for them, and re-layouts: 9.72 us -> 1.56 us
  Pallas kernels: 23.8 us -> 29.5 us
  other arithmetic: 1.58 us -> 3.07 us
    ppermute x10, waiting for transfers between devices: 22.4 us -> 6.14 us  [along_ring(): return lax.ppermute(value, 'dev', ring_pairs(lax.axis_size('dev'), steps))]
    unnamed x35 -> x29, local copies, waits for them, and re-layouts: 9.72 us -> 1.56 us
    ppermute x10, starting transfers between devices: 8.23 us -> 15.7 us  [along_ring(): return lax.ppermute(value, 'dev', ring_pairs(lax.axis_size('dev'), steps))]
    pallas_call x0 -> x2, Pallas kernels: none -> 7.35 us  [the longest x1 5.64 us: opening_products(): pl.pallas_call(body, in_specs=[SMEM] + [HBM] * 5, out_specs=[VMEM] * node...]
    ppermute x15, waiting for transfers between devices: 11.6 us -> 18.8 us  [across(): lax.ppermute(value, axis, [(source, source ^ mask) for source in range(co...]
    ppermute x2, waiting for transfers between devices: 11.1 us -> 7.19 us  [along_ring_and_sections(): return lax.ppermute(value, ('section', 'dev'), pairs)]
    pallas_call x17 -> x15, Pallas kernels: 23.8 us -> 22.1 us  [call(): pl.pallas_call(with_after, in_specs=[SMEM] + [VMEM] * len(operands) + [AN...]
    ppermute x2, starting transfers between devices: 1.41 us -> 3.04 us  [along_ring_and_sections(): return lax.ppermute(value, ('section', 'dev'), pairs)]
  transfers between devices with their start and end apart: 29 -> 29, of which waited for: 11 -> 12; matrix products, arithmetic and copies ran while one was open for 1% -> 2% of each run, Pallas kernels for 19% -> 27%
where the time goes in v4:
time: 105 us; the launch traced here: 104 us
  starting transfers between devices  37.3 us (36%)
  waiting for transfers between devices  32.1 us (31%)
  Pallas kernels  29.5 us (28%)
  other arithmetic  3.07 us (3%)
  local copies, waits for them, and re-layouts  1.56 us (1%)
    pallas_call x15, Pallas kernels, call(): pl.pallas_call(with_after, in_specs=[SMEM] + [VMEM] * len(operands) + [AN...  22.1 us
    ppermute x15, waiting for transfers between devices, across(): lax.ppermute(value, axis, [(source, source ^ mask) for source in range(co...  18.8 us
    ppermute x15, starting transfers between devices, across(): lax.ppermute(value, axis, [(source, source ^ mask) for source in range(co...  17.7 us
    ppermute x10, starting transfers between devices, along_ring(): return lax.ppermute(value, 'dev', ring_pairs(lax.axis_size('dev'), steps))  15.7 us
    ppermute x2, waiting for transfers between devices, along_ring_and_sections(): return lax.ppermute(value, ('section', 'dev'), pairs)  7.19 us
    ppermute x10, waiting for transfers between devices, along_ring(): return lax.ppermute(value, 'dev', ring_pairs(lax.axis_size('dev'), steps))  6.14 us
    pallas_call x1, Pallas kernels, opening_products(): pl.pallas_call(body, in_specs=[SMEM] + [HBM] * 5, out_specs=[VMEM] * node...  5.64 us
    ppermute x2, starting transfers between devices, along_ring_and_sections(): return lax.ppermute(value, ('section', 'dev'), pairs)  3.04 us
  transfers between devices with their start and end apart: 29, of which 12 were waited for; matrix products, arithmetic and copies ran while one was open for 2% of the time, Pallas kernels for 27%

profile of v4, /device:TPU:0, one launch (start us, length us, event | category | flops | bytes accessed | tf_op | source)
XLA Modules:
  0.0 104.4 jit_solution(3787143678875622998)
XLA Ops:
  0.6 1.7 %shard_map.123.refs_5_.refs_8_ = bf16[144,896]{1,0:T(8,128)(2,1)} custom-call(bf16[128,896]{1,0:T(8,128)(2,1)} %bitcast.25, s32[2,128]{1,0:T(2,128)} %bitcast.63, s32[2,128]{1,0:T(2,128)} %bitcast.64, f32[2,128]{1,0:T(2,128)} %bitcast.65, f32[2,128]{1,0:T(2,128)} %bitcast.66), custom_call_target="tpu_custom_call" | custom-call | tf_op jit(solution)/shard_map/pallas_call | solution.py:306
  2.3 3.1 %collective-permute-start.3 = (bf16[144,896]{1,0:T(8,128)(2,1)}, bf16[144,896]{1,0:T(8,128)(2,1)S(1)}, u32[]{:S(2)}, u32[]{:S(2)}) collective-permute-start(bf16[144,896]{1,0:T(8,128)(2,1)} %shard_map.123.refs_5_.refs_8_), channel_id=1, source_target_pairs={{0,1},{1,3},{3,2},{2,0},{4,5},{5,7},{7,6},{6,4},{8,9},{9,11},{11,1... | collective-permute-start | bytes 774152 | tf_op jit(solution)/shard_map/ppermute | solution.py:167
  5.4 2.6 %collective-permute-start.4 = (bf16[128,896]{1,0:T(8,128)(2,1)}, bf16[128,896]{1,0:T(8,128)(2,1)S(1)}, u32[]{:S(2)}, u32[]{:S(2)}) collective-permute-start(bf16[128,896]{1,0:T(8,128)(2,1)} %bitcast.60), channel_id=1, source_target_pairs={{0,1},{1,3},{3,2},{2,0},{4,5},{5,7},{7,6},{6,4},{8,9},{9,11},{11,1... | collective-permute-start | bytes 688136 | tf_op jit(solution)/shard_map/ppermute | solution.py:167
  8.7 5.6 %shard_map.122 = (bf16[3,32,1024]{2,1,0:T(8,128)(2,1)}, bf16[3,32,1024]{2,1,0:T(8,128)(2,1)}, bf16[3,32,1024]{2,1,0:T(8,128)(2,1)}, bf16[3,32,1024]{2,1,0:T(8,128)(2,1)}) custom-call(s32[2]{0:T(128)} %pad_add_fusion.place_ref, bf16[128,896]{1,0:T(8,128)(2,1)} %bitcast.26, bf16[896,1024]{1,0:T(8,128)(2,1)} %bitcast.36, bf16[896,1024]{1,0:T(8,128)(2,1)} %bitcast.44, ...), custom_call_target="tpu_custom_call" | custom-call | flops 70464307200 | bytes 550502400 | tf_op jit(solution)/shard_map/pallas_call | solution.py:354
  14.3 1.6 %collective-permute-start = (bf16[3,32,1024]{2,1,0:T(8,128)(2,1)}, bf16[3,32,1024]{2,1,0:T(8,128)(2,1)S(1)}, u32[]{:S(2)}, u32[]{:S(2)}) collective-permute-start(bf16[3,32,1024]{2,1,0:T(8,128)(2,1)} %get-tuple-element.31), channel_id=1, source_target_pairs={{0,4},{4,0},{8,12},{12,8},{1,5},{5,1},{9,13},{13,9},{2,6},{6,2},{1... | collective-permute-start | bytes 589832 | tf_op jit(solution)/shard_map/ppermute | solution.py:154
  15.9 1.5 %collective-permute-start.1 = (bf16[3,32,1024]{2,1,0:T(8,128)(2,1)}, bf16[3,32,1024]{2,1,0:T(8,128)(2,1)S(1)}, u32[]{:S(2)}, u32[]{:S(2)}) collective-permute-start(bf16[3,32,1024]{2,1,0:T(8,128)(2,1)} %get-tuple-element.32), channel_id=1, source_target_pairs={{0,8},{4,12},{8,0},{12,4},{1,9},{5,13},{9,1},{13,5},{2,10},{6,14},... | collective-permute-start | bytes 589832 | tf_op jit(solution)/shard_map/ppermute | solution.py:154
  18.7 3.3 %collective-permute-start.8 = (bf16[144,896]{1,0:T(8,128)(2,1)S(1)}, bf16[144,896]{1,0:T(8,128)(2,1)S(1)}, u32[]{:S(2)}, u32[]{:S(2)}) collective-permute-start(bf16[144,896]{1,0:T(8,128)(2,1)S(1)} %collective-permute-done.3.refs_0_.refs_5_.refs_8_), channel_id=1, source_target_pairs={{0,1},{1,3},{3,2},{2,0},{4,5},{5,7},{7,6},{6,4},{8,9},{9,11},{11,1... | collective-permute-start | bytes 774152 | tf_op jit(solution)/shard_map/ppermute | solution.py:167
  22.9 1.8 %shard_map.124 = (bf16[5,32,1024]{2,1,0:T(8,128)(2,1)S(1)}, bf16[5,32,1024]{2,1,0:T(8,128)(2,1)S(1)}, bf16[5,32,1024]{2,1,0:T(8,128)(2,1)S(1)}, bf16[5,32,1024]{2,1,0:T(8,128)(2,1)S(1)}) custom-call(s32[2]{0:T(128)S(1)} %copy-done.4, bf16[144,896]{1,0:T(8,128)(2,1)S(1)} %collective-permute-done.3.refs_0_.refs_5_.refs_8_, ...), custom_call_target="tpu_custom_call" | custom-call | flops 70464307200 | bytes 599244800 | tf_op jit(solution)/shard_map/pallas_call | solution.py:192
  28.9 1.4 %collective-permute-start.7 = (bf16[5,32,1024]{2,1,0:T(8,128)(2,1)S(1)}, bf16[5,32,1024]{2,1,0:T(8,128)(2,1)S(1)}, u32[]{:S(2)}, u32[]{:S(2)}) collective-permute-start(bf16[5,32,1024]{2,1,0:T(8,128)(2,1)S(1)} %get-tuple-element.41), channel_id=1, source_target_pairs={{0,12},{4,8},{8,4},{12,0},{1,13},{5,9},{9,5},{13,1},{2,14},{6,10},... | collective-permute-start | bytes 983048 | tf_op jit(solution)/shard_map/ppermute | solution.py:154
  31.0 1.8 %shard_map.126 = (bf16[5,32,1024]{2,1,0:T(8,128)(2,1)S(1)}, bf16[5,32,1024]{2,1,0:T(8,128)(2,1)S(1)}, bf16[5,32,1024]{2,1,0:T(8,128)(2,1)S(1)}, bf16[5,32,1024]{2,1,0:T(8,128)(2,1)S(1)}) custom-call(s32[2]{0:T(128)S(1)} %copy-done.4, bf16[144,896]{1,0:T(8,128)(2,1)S(1)} %collective-permute-done.8.refs_0_.refs_5_.refs_8_, ...), custom_call_target="tpu_custom_call" | custom-call | flops 70464307200 | bytes 599244800 | tf_op jit(solution)/shard_map/pallas_call | solution.py:192
  32.9 2.6 %collective-permute-start.14 = (bf16[144,896]{1,0:T(8,128)(2,1)S(1)}, bf16[144,896]{1,0:T(8,128)(2,1)S(1)}, u32[]{:S(2)}, u32[]{:S(2)}) collective-permute-start(bf16[144,896]{1,0:T(8,128)(2,1)S(1)} %collective-permute-done.8.refs_0_.refs_5_.refs_8_), channel_id=1, source_target_pairs={{0,1},{1,3},{3,2},{2,0},{4,5},{5,7},{7,6},{6,4},{8,9},{9,11},{11,1... | collective-permute-start | bytes 774152 | tf_op jit(solution)/shard_map/ppermute | solution.py:167
  35.5 2.0 %collective-permute-done.5.refs_1_ = bf16[5,32,1024]{2,1,0:T(8,128)(2,1)S(1)} collective-permute-done((bf16[5,32,1024]{2,1,0:T(8,128)(2,1)S(1)}, bf16[5,32,1024]{2,1,0:T(8,128)(2,1)S(1)}, u32[]{:S(2)}, u32[]{:S(2)}) %collective-permute-start.5) | collective-permute-done | bytes 327712 | tf_op jit(solution)/shard_map/ppermute | solution.py:154
  37.5 5.3 %collective-permute-done.6.refs_2_ = bf16[5,32,1024]{2,1,0:T(8,128)(2,1)S(1)} collective-permute-done((bf16[5,32,1024]{2,1,0:T(8,128)(2,1)S(1)}, bf16[5,32,1024]{2,1,0:T(8,128)(2,1)S(1)}, u32[]{:S(2)}, u32[]{:S(2)}) %collective-permute-start.6) | collective-permute-done | bytes 327712 | tf_op jit(solution)/shard_map/ppermute | solution.py:154
  45.3 1.8 %collective-permute-start.13 = (bf16[5,32,1024]{2,1,0:T(8,128)(2,1)S(1)}, bf16[5,32,1024]{2,1,0:T(8,128)(2,1)S(1)}, u32[]{:S(2)}, u32[]{:S(2)}) collective-permute-start(bf16[5,32,1024]{2,1,0:T(8,128)(2,1)S(1)} %get-tuple-element.49), channel_id=1, source_target_pairs={{0,12},{4,8},{8,4},{12,0},{1,13},{5,9},{9,5},{13,1},{2,14},{6,10},... | collective-permute-start | bytes 983048 | tf_op jit(solution)/shard_map/ppermute | solution.py:154
  48.6 3.0 %shard_map.129.refs_5_ = bf16[128,896]{1,0:T(8,128)(2,1)} custom-call(s32[2]{0:T(128)S(1)} %copy-done.4, bf16[5,32,1024]{2,1,0:T(8,128)(2,1)S(1)} %get-tuple-element.38.refs_5_.refs_0_, bf16[5,32,1024]{2,1,0:T(8,128)(2,1)S(1)} %collective-permute-done.5.refs_1_, bf16[5,32,1024]{2,1,0:T(8,128)(2,1)S(1)} %collective-permute-done.6.refs_2_, ...), custom_call_target="tpu_custom_call" | custom-call | flops 46976204800 | bytes 756531200 | tf_op jit(solution)/shard_map/pallas_call | solution.py:192
  51.6 1.8 %shard_map.130 = (bf16[5,32,1024]{2,1,0:T(8,128)(2,1)S(1)}, bf16[5,32,1024]{2,1,0:T(8,128)(2,1)S(1)}, bf16[5,32,1024]{2,1,0:T(8,128)(2,1)S(1)}, bf16[5,32,1024]{2,1,0:T(8,128)(2,1)S(1)}) custom-call(s32[2]{0:T(128)S(1)} %copy-done.4, bf16[144,896]{1,0:T(8,128)(2,1)S(1)} %collective-permute-done.14.refs_0_.refs_5_.refs_8_, ...), custom_call_target="tpu_custom_call" | custom-call | flops 70464307200 | bytes 599244800 | tf_op jit(solution)/shard_map/pallas_call | solution.py:192
  53.5 3.9 %collective-permute-done.12.refs_2_ = bf16[5,32,1024]{2,1,0:T(8,128)(2,1)S(1)} collective-permute-done((bf16[5,32,1024]{2,1,0:T(8,128)(2,1)S(1)}, bf16[5,32,1024]{2,1,0:T(8,128)(2,1)S(1)}, u32[]{:S(2)}, u32[]{:S(2)}) %collective-permute-start.12) | collective-permute-done | bytes 327712 | tf_op jit(solution)/shard_map/ppermute | solution.py:154
  59.5 1.8 %collective-permute-start.16 = (bf16[5,32,1024]{2,1,0:T(8,128)(2,1)S(1)}, bf16[5,32,1024]{2,1,0:T(8,128)(2,1)S(1)}, u32[]{:S(2)}, u32[]{:S(2)}) collective-permute-start(bf16[5,32,1024]{2,1,0:T(8,128)(2,1)S(1)} %get-tuple-element.55), channel_id=1, source_target_pairs={{0,4},{4,0},{8,12},{12,8},{1,5},{5,1},{9,13},{13,9},{2,6},{6,2},{1... | collective-permute-start | bytes 983048 | tf_op jit(solution)/shard_map/ppermute | solution.py:154
  63.0 2.3 %shard_map.133.refs_7_ = bf16[128,896]{1,0:T(8,128)(2,1)S(1)} custom-call(s32[2]{0:T(128)S(1)} %copy-done.4, bf16[5,32,1024]{2,1,0:T(8,128)(2,1)S(1)} %get-tuple-element.46.refs_7_.refs_0_, bf16[5,32,1024]{2,1,0:T(8,128)(2,1)S(1)} %collective-permute-done.11.refs_1_, bf16[5,32,1024]{2,1,0:T(8,128)(2,1)S(1)} %collective-permute-done.12.refs_2_, ...), custom_call_target="tpu_custom_call" | custom-call | flops 46976204800 | bytes 733593600 | tf_op jit(solution)/shard_map/pallas_call | solution.py:192
  65.3 1.7 %collective-permute-done.19.refs_6_ = bf16[128,896]{1,0:T(8,128)(2,1)S(1)} collective-permute-done((bf16[128,896]{1,0:T(8,128)(2,1)S(1)}, bf16[128,896]{1,0:T(8,128)(2,1)S(1)}, u32[]{:S(2)}, u32[]{:S(2)}) %collective-permute-start.19) | collective-permute-done | bytes 229408 | tf_op jit(solution)/shard_map/ppermute | solution.py:167
  67.0 2.0 %collective-permute-done.16.refs_1_ = bf16[5,32,1024]{2,1,0:T(8,128)(2,1)S(1)} collective-permute-done((bf16[5,32,1024]{2,1,0:T(8,128)(2,1)S(1)}, bf16[5,32,1024]{2,1,0:T(8,128)(2,1)S(1)}, u32[]{:S(2)}, u32[]{:S(2)}) %collective-permute-start.16) | collective-permute-done | bytes 327712 | tf_op jit(solution)/shard_map/ppermute | solution.py:154
  69.1 4.3 %collective-permute-done.17.refs_2_ = bf16[5,32,1024]{2,1,0:T(8,128)(2,1)S(1)} collective-permute-done((bf16[5,32,1024]{2,1,0:T(8,128)(2,1)S(1)}, bf16[5,32,1024]{2,1,0:T(8,128)(2,1)S(1)}, u32[]{:S(2)}, u32[]{:S(2)}) %collective-permute-start.17) | collective-permute-done | bytes 327712 | tf_op jit(solution)/shard_map/ppermute | solution.py:154
  76.9 1.6 %collective-permute-start.22 = (bf16[2,32,1024]{2,1,0:T(8,128)(2,1)S(1)}, bf16[2,32,1024]{2,1,0:T(8,128)(2,1)S(1)}, u32[]{:S(2)}, u32[]{:S(2)}) collective-permute-start(bf16[2,32,1024]{2,1,0:T(8,128)(2,1)S(1)} %shard_map.135.refs_10_.refs_0_), channel_id=1, source_target_pairs={{0,12},{4,8},{8,4},{12,0},{1,13},{5,9},{9,5},{13,1},{2,14},{6,10},... | collective-permute-start | bytes 393224 | tf_op jit(solution)/shard_map/ppermute | solution.py:154
  79.2 2.3 %shard_map.136.refs_7_ = bf16[128,896]{1,0:T(8,128)(2,1)S(1)} custom-call(s32[2]{0:T(128)S(1)} %copy-done.4, bf16[5,32,1024]{2,1,0:T(8,128)(2,1)S(1)} %get-tuple-element.54.refs_6_.refs_0_, bf16[5,32,1024]{2,1,0:T(8,128)(2,1)S(1)} %collective-permute-done.16.refs_1_, bf16[5,32,1024]{2,1,0:T(8,128)(2,1)S(1)} %collective-permute-done.17.refs_2_, ...), custom_call_target="tpu_custom_call" | custom-call | flops 46976204800 | bytes 756531200 | tf_op jit(solution)/shard_map/pallas_call | solution.py:192
  81.6 1.7 %collective-permute-start.27 = (bf16[128,896]{1,0:T(8,128)(2,1)S(1)}, bf16[128,896]{1,0:T(8,128)(2,1)S(1)}, u32[]{:S(2)}, u32[]{:S(2)}) collective-permute-start(bf16[128,896]{1,0:T(8,128)(2,1)S(1)} %shard_map.136.refs_7_), channel_id=1, source_target_pairs={{0,1},{1,3},{3,2},{2,0},{4,5},{5,7},{7,6},{6,4},{8,9},{9,11},{11,1... | collective-permute-start | bytes 688136 | tf_op jit(solution)/shard_map/ppermute | solution.py:167
  83.3 2.2 %collective-permute-done.23.refs_6_ = bf16[128,896]{1,0:T(8,128)(2,1)S(1)} collective-permute-done((bf16[128,896]{1,0:T(8,128)(2,1)S(1)}, bf16[128,896]{1,0:T(8,128)(2,1)S(1)}, u32[]{:S(2)}, u32[]{:S(2)}) %collective-permute-start.23) | collective-permute-done | bytes 229408 | tf_op jit(solution)/shard_map/ppermute | solution.py:167
  86.5 2.0 %collective-permute-done.27.refs_9_ = bf16[128,896]{1,0:T(8,128)(2,1)S(1)} collective-permute-done((bf16[128,896]{1,0:T(8,128)(2,1)S(1)}, bf16[128,896]{1,0:T(8,128)(2,1)S(1)}, u32[]{:S(2)}, u32[]{:S(2)}) %collective-permute-start.27) | collective-permute-done | bytes 229408 | tf_op jit(solution)/shard_map/ppermute | solution.py:167
  88.5 2.3 %shard_map.138 = bf16[128,896]{1,0:T(8,128)(2,1)S(1)} custom-call(s32[2]{0:T(128)S(1)} %copy-done.4, bf16[2,32,1024]{2,1,0:T(8,128)(2,1)S(1)} %shard_map.135.refs_10_.refs_0_, bf16[2,32,1024]{2,1,0:T(8,128)(2,1)S(1)} %collective-permute-done.20.refs_1_, bf16[2,32,1024]{2,1,0:T(8,128)(2,1)S(1)} %collective-permute-done.21.refs_2_, ...), custom_call_target="tpu_custom_call" | custom-call | flops 46976204800 | bytes 677888000 | tf_op jit(solution)/shard_map/pallas_call | solution.py:192
  91.8 3.0 %collective-permute-start.25 = (bf16[128,896]{1,0:T(8,128)(2,1)S(1)}, bf16[128,896]{1,0:T(8,128)(2,1)S(1)}, u32[]{:S(2)}, u32[]{:S(2)}) collective-permute-start(bf16[128,896]{1,0:T(8,128)(2,1)S(1)} %shard_map.137.refs_10_), channel_id=1, source_target_pairs={{0,17},{1,19},{3,18},{2,16},{16,1},{17,3},{19,2},{18,0},{4,21},{5,... | collective-permute-start | bytes 688136 | tf_op jit(solution)/shard_map/ppermute | solution.py:177
  94.8 4.9 %collective-permute-done.28 = bf16[128,896]{1,0:T(8,128)(2,1)S(1)} collective-permute-done((bf16[128,896]{1,0:T(8,128)(2,1)S(1)}, bf16[128,896]{1,0:T(8,128)(2,1)S(1)}, u32[]{:S(2)}, u32[]{:S(2)}) %collective-permute-start.28) | collective-permute-done | bytes 229408 | tf_op jit(solution)/shard_map/ppermute | solution.py:177
  99.7 1.7 %fusion.1 = bf16[1,128,896]{2,1,0:T(8,128)(2,1)} fusion(bf16[128,896]{1,0:T(8,128)(2,1)S(1)} %collective-permute-done.28, bf16[128,896]{1,0:T(8,128)(2,1)} %collective-permute-done.26), kind=kLoop, calls=%fused_computation.3 | loop fusion | flops 458752 | bytes 688128 | tf_op jit(solution)/shard_map/broadcast_in_dim | solution.py:563
  101.4 2.3 %collective-permute-done.25 = bf16[128,896]{1,0:T(8,128)(2,1)S(1)} collective-permute-done((bf16[128,896]{1,0:T(8,128)(2,1)S(1)}, bf16[128,896]{1,0:T(8,128)(2,1)S(1)}, u32[]{:S(2)}, u32[]{:S(2)}) %collective-permute-start.25) | collective-permute-done | bytes 229408 | tf_op jit(solution)/shard_map/ppermute | solution.py:177
  (75 shorter events, 22.5 us)
Async XLA Ops:
  2.3 16.4 %collective-permute-start.3 = (bf16[144,896]{1,0:T(8,128)(2,1)}, bf16[144,896]{1,0:T(8,128)(2,1)S(1)}, u32[]{:S(2)}, u32[]{:S(2)}) collective-permute-start(bf16[144,896]{1,0:T(8,128)(2,1)} %shard_map.123.refs_5_.refs_8_), channel_id=1, source_target_pairs={{0,1},{1,3},{3,2},{2,0},{4,5},{5,7},{7,6},{6,4},{8,9},{9,11},{11,1... | collective-permute-start | bytes 774152 | tf_op jit(solution)/shard_map/ppermute | solution.py:167
  5.4 12.5 %collective-permute-start.4 = (bf16[128,896]{1,0:T(8,128)(2,1)}, bf16[128,896]{1,0:T(8,128)(2,1)S(1)}, u32[]{:S(2)}, u32[]{:S(2)}) collective-permute-start(bf16[128,896]{1,0:T(8,128)(2,1)} %bitcast.60), channel_id=1, source_target_pairs={{0,1},{1,3},{3,2},{2,0},{4,5},{5,7},{7,6},{6,4},{8,9},{9,11},{11,1... | collective-permute-start | bytes 688136 | tf_op jit(solution)/shard_map/ppermute | solution.py:167
  8.7 13.3 %copy-start.7 = (bf16[1,1,896,1024]{3,2,1,0:T(8,128)(2,1)S(1)}, bf16[1,1,896,1024]{3,2,1,0:T(8,128)(2,1)}, u32[]{:S(2)}) copy-start(bf16[1,1,896,1024]{3,2,1,0:T(8,128)(2,1)} %param.18) | copy-start | bytes 5505028
  14.3 10.5 %collective-permute-start = (bf16[3,32,1024]{2,1,0:T(8,128)(2,1)}, bf16[3,32,1024]{2,1,0:T(8,128)(2,1)S(1)}, u32[]{:S(2)}, u32[]{:S(2)}) collective-permute-start(bf16[3,32,1024]{2,1,0:T(8,128)(2,1)} %get-tuple-element.31), channel_id=1, source_target_pairs={{0,4},{4,0},{8,12},{12,8},{1,5},{5,1},{9,13},{13,9},{2,6},{6,2},{1... | collective-permute-start | bytes 589832 | tf_op jit(solution)/shard_map/ppermute | solution.py:154
  15.9 10.2 %collective-permute-start.1 = (bf16[3,32,1024]{2,1,0:T(8,128)(2,1)}, bf16[3,32,1024]{2,1,0:T(8,128)(2,1)S(1)}, u32[]{:S(2)}, u32[]{:S(2)}) collective-permute-start(bf16[3,32,1024]{2,1,0:T(8,128)(2,1)} %get-tuple-element.32), channel_id=1, source_target_pairs={{0,8},{4,12},{8,0},{12,4},{1,9},{5,13},{9,1},{13,5},{2,10},{6,14},... | collective-permute-start | bytes 589832 | tf_op jit(solution)/shard_map/ppermute | solution.py:154
  17.4 8.7 %collective-permute-start.2 = (bf16[3,32,1024]{2,1,0:T(8,128)(2,1)}, bf16[3,32,1024]{2,1,0:T(8,128)(2,1)S(1)}, u32[]{:S(2)}, u32[]{:S(2)}) collective-permute-start(bf16[3,32,1024]{2,1,0:T(8,128)(2,1)} %get-tuple-element.33), channel_id=1, source_target_pairs={{0,12},{4,8},{8,4},{12,0},{1,13},{5,9},{9,5},{13,1},{2,14},{6,10},... | collective-permute-start | bytes 589832 | tf_op jit(solution)/shard_map/ppermute | solution.py:154
  17.9 12.5 %collective-permute-start.9 = (bf16[128,896]{1,0:T(8,128)(2,1)S(1)}, bf16[128,896]{1,0:T(8,128)(2,1)S(1)}, u32[]{:S(2)}, u32[]{:S(2)}) collective-permute-start(bf16[128,896]{1,0:T(8,128)(2,1)S(1)} %collective-permute-done.4.refs_1_), channel_id=1, source_target_pairs={{0,1},{1,3},{3,2},{2,0},{4,5},{5,7},{7,6},{6,4},{8,9},{9,11},{11,1... | collective-permute-start | bytes 688136 | tf_op jit(solution)/shard_map/ppermute | solution.py:167
  18.7 12.3 %collective-permute-start.8 = (bf16[144,896]{1,0:T(8,128)(2,1)S(1)}, bf16[144,896]{1,0:T(8,128)(2,1)S(1)}, u32[]{:S(2)}, u32[]{:S(2)}) collective-permute-start(bf16[144,896]{1,0:T(8,128)(2,1)S(1)} %collective-permute-done.3.refs_0_.refs_5_.refs_8_), channel_id=1, source_target_pairs={{0,1},{1,3},{3,2},{2,0},{4,5},{5,7},{7,6},{6,4},{8,9},{9,11},{11,1... | collective-permute-start | bytes 774152 | tf_op jit(solution)/shard_map/ppermute | solution.py:167
  26.8 10.7 %collective-permute-start.5 = (bf16[5,32,1024]{2,1,0:T(8,128)(2,1)S(1)}, bf16[5,32,1024]{2,1,0:T(8,128)(2,1)S(1)}, u32[]{:S(2)}, u32[]{:S(2)}) collective-permute-start(bf16[5,32,1024]{2,1,0:T(8,128)(2,1)S(1)} %get-tuple-element.39), channel_id=1, source_target_pairs={{0,4},{4,0},{8,12},{12,8},{1,5},{5,1},{9,13},{13,9},{2,6},{6,2},{1... | collective-permute-start | bytes 983048 | tf_op jit(solution)/shard_map/ppermute | solution.py:154
  28.1 14.7 %collective-permute-start.6 = (bf16[5,32,1024]{2,1,0:T(8,128)(2,1)S(1)}, bf16[5,32,1024]{2,1,0:T(8,128)(2,1)S(1)}, u32[]{:S(2)}, u32[]{:S(2)}) collective-permute-start(bf16[5,32,1024]{2,1,0:T(8,128)(2,1)S(1)} %get-tuple-element.40), channel_id=1, source_target_pairs={{0,8},{4,12},{8,0},{12,4},{1,9},{5,13},{9,1},{13,5},{2,10},{6,14},... | collective-permute-start | bytes 983048 | tf_op jit(solution)/shard_map/ppermute | solution.py:154
  28.9 13.9 %collective-permute-start.7 = (bf16[5,32,1024]{2,1,0:T(8,128)(2,1)S(1)}, bf16[5,32,1024]{2,1,0:T(8,128)(2,1)S(1)}, u32[]{:S(2)}, u32[]{:S(2)}) collective-permute-start(bf16[5,32,1024]{2,1,0:T(8,128)(2,1)S(1)} %get-tuple-element.41), channel_id=1, source_target_pairs={{0,12},{4,8},{8,4},{12,0},{1,13},{5,9},{9,5},{13,1},{2,14},{6,10},... | collective-permute-start | bytes 983048 | tf_op jit(solution)/shard_map/ppermute | solution.py:154
  30.3 21.3 %collective-permute-start.15 = (bf16[128,896]{1,0:T(8,128)(2,1)S(1)}, bf16[128,896]{1,0:T(8,128)(2,1)S(1)}, u32[]{:S(2)}, u32[]{:S(2)}) collective-permute-start(bf16[128,896]{1,0:T(8,128)(2,1)S(1)} %collective-permute-done.9.refs_1_), channel_id=1, source_target_pairs={{0,1},{1,3},{3,2},{2,0},{4,5},{5,7},{7,6},{6,4},{8,9},{9,11},{11,1... | collective-permute-start | bytes 688136 | tf_op jit(solution)/shard_map/ppermute | solution.py:167
  32.8 14.2 %copy-start = (bf16[144,896]{1,0:T(8,128)(2,1)S(1)}, bf16[144,896]{1,0:T(8,128)(2,1)}, u32[]{:S(2)}) copy-start(bf16[144,896]{1,0:T(8,128)(2,1)} %shard_map.123.refs_5_.refs_8_) | copy-start | bytes 774148
  32.9 14.2 %copy-start.1 = (bf16[1,128,896]{2,1,0:T(8,128)(2,1)S(1)}, bf16[1,128,896]{2,1,0:T(8,128)(2,1)}, u32[]{:S(2)}) copy-start(bf16[1,128,896]{2,1,0:T(8,128)(2,1)} %param.11) | copy-start | bytes 688132
  32.9 18.7 %collective-permute-start.14 = (bf16[144,896]{1,0:T(8,128)(2,1)S(1)}, bf16[144,896]{1,0:T(8,128)(2,1)S(1)}, u32[]{:S(2)}, u32[]{:S(2)}) collective-permute-start(bf16[144,896]{1,0:T(8,128)(2,1)S(1)} %collective-permute-done.8.refs_0_.refs_5_.refs_8_), channel_id=1, source_target_pairs={{0,1},{1,3},{3,2},{2,0},{4,5},{5,7},{7,6},{6,4},{8,9},{9,11},{11,1... | collective-permute-start | bytes 774152 | tf_op jit(solution)/shard_map/ppermute | solution.py:167
  43.5 10.0 %collective-permute-start.11 = (bf16[5,32,1024]{2,1,0:T(8,128)(2,1)S(1)}, bf16[5,32,1024]{2,1,0:T(8,128)(2,1)S(1)}, u32[]{:S(2)}, u32[]{:S(2)}) collective-permute-start(bf16[5,32,1024]{2,1,0:T(8,128)(2,1)S(1)} %get-tuple-element.47), channel_id=1, source_target_pairs={{0,4},{4,0},{8,12},{12,8},{1,5},{5,1},{9,13},{13,9},{2,6},{6,2},{1... | collective-permute-start | bytes 983048 | tf_op jit(solution)/shard_map/ppermute | solution.py:154
  44.1 13.3 %collective-permute-start.12 = (bf16[5,32,1024]{2,1,0:T(8,128)(2,1)S(1)}, bf16[5,32,1024]{2,1,0:T(8,128)(2,1)S(1)}, u32[]{:S(2)}, u32[]{:S(2)}) collective-permute-start(bf16[5,32,1024]{2,1,0:T(8,128)(2,1)S(1)} %get-tuple-element.48), channel_id=1, source_target_pairs={{0,8},{4,12},{8,0},{12,4},{1,9},{5,13},{9,1},{13,5},{2,10},{6,14},... | collective-permute-start | bytes 983048 | tf_op jit(solution)/shard_map/ppermute | solution.py:154
  45.3 12.1 %collective-permute-start.13 = (bf16[5,32,1024]{2,1,0:T(8,128)(2,1)S(1)}, bf16[5,32,1024]{2,1,0:T(8,128)(2,1)S(1)}, u32[]{:S(2)}, u32[]{:S(2)}) collective-permute-start(bf16[5,32,1024]{2,1,0:T(8,128)(2,1)S(1)} %get-tuple-element.49), channel_id=1, source_target_pairs={{0,12},{4,8},{8,4},{12,0},{1,13},{5,9},{9,5},{13,1},{2,14},{6,10},... | collective-permute-start | bytes 983048 | tf_op jit(solution)/shard_map/ppermute | solution.py:154
  51.6 43.2 %collective-permute-start.26 = (bf16[128,896]{1,0:T(8,128)(2,1)}, bf16[128,896]{1,0:T(8,128)(2,1)}, u32[]{:S(2)}, u32[]{:S(2)}) collective-permute-start(bf16[128,896]{1,0:T(8,128)(2,1)} %shard_map.129.refs_5_), channel_id=1, source_target_pairs={{0,16},{16,0},{1,17},{17,1},{2,18},{18,2},{3,19},{19,3},{4,20},{20... | collective-permute-start | bytes 688136 | tf_op jit(solution)/shard_map/ppermute | solution.py:14
  59.1 7.9 %collective-permute-start.19 = (bf16[128,896]{1,0:T(8,128)(2,1)S(1)}, bf16[128,896]{1,0:T(8,128)(2,1)S(1)}, u32[]{:S(2)}, u32[]{:S(2)}) collective-permute-start(bf16[128,896]{1,0:T(8,128)(2,1)S(1)} %shard_map.132.refs_9_), channel_id=1, source_target_pairs={{0,1},{1,3},{3,2},{2,0},{4,5},{5,7},{7,6},{6,4},{8,9},{9,11},{11,1... | collective-permute-start | bytes 688136 | tf_op jit(solution)/shard_map/ppermute | solution.py:167
  59.5 9.5 %collective-permute-start.16 = (bf16[5,32,1024]{2,1,0:T(8,128)(2,1)S(1)}, bf16[5,32,1024]{2,1,0:T(8,128)(2,1)S(1)}, u32[]{:S(2)}, u32[]{:S(2)}) collective-permute-start(bf16[5,32,1024]{2,1,0:T(8,128)(2,1)S(1)} %get-tuple-element.55), channel_id=1, source_target_pairs={{0,4},{4,0},{8,12},{12,8},{1,5},{5,1},{9,13},{13,9},{2,6},{6,2},{1... | collective-permute-start | bytes 983048 | tf_op jit(solution)/shard_map/ppermute | solution.py:154
  61.4 12.0 %collective-permute-start.17 = (bf16[5,32,1024]{2,1,0:T(8,128)(2,1)S(1)}, bf16[5,32,1024]{2,1,0:T(8,128)(2,1)S(1)}, u32[]{:S(2)}, u32[]{:S(2)}) collective-permute-start(bf16[5,32,1024]{2,1,0:T(8,128)(2,1)S(1)} %get-tuple-element.56), channel_id=1, source_target_pairs={{0,8},{4,12},{8,0},{12,4},{1,9},{5,13},{9,1},{13,5},{2,10},{6,14},... | collective-permute-start | bytes 983048 | tf_op jit(solution)/shard_map/ppermute | solution.py:154
  61.6 11.7 %collective-permute-start.18 = (bf16[5,32,1024]{2,1,0:T(8,128)(2,1)S(1)}, bf16[5,32,1024]{2,1,0:T(8,128)(2,1)S(1)}, u32[]{:S(2)}, u32[]{:S(2)}) collective-permute-start(bf16[5,32,1024]{2,1,0:T(8,128)(2,1)S(1)} %get-tuple-element.57), channel_id=1, source_target_pairs={{0,12},{4,8},{8,4},{12,0},{1,13},{5,9},{9,5},{13,1},{2,14},{6,10},... | collective-permute-start | bytes 983048 | tf_op jit(solution)/shard_map/ppermute | solution.py:154
  67.0 11.6 %collective-permute-start.24 = (bf16[128,896]{1,0:T(8,128)(2,1)S(1)}, bf16[128,896]{1,0:T(8,128)(2,1)S(1)}, u32[]{:S(2)}, u32[]{:S(2)}) collective-permute-start(bf16[128,896]{1,0:T(8,128)(2,1)S(1)} %shard_map.133.refs_7_), channel_id=1, source_target_pairs={{0,1},{1,3},{3,2},{2,0},{4,5},{5,7},{7,6},{6,4},{8,9},{9,11},{11,1... | collective-permute-start | bytes 688136 | tf_op jit(solution)/shard_map/ppermute | solution.py:167
  75.0 6.5 %collective-permute-start.20 = (bf16[2,32,1024]{2,1,0:T(8,128)(2,1)S(1)}, bf16[2,32,1024]{2,1,0:T(8,128)(2,1)S(1)}, u32[]{:S(2)}, u32[]{:S(2)}) collective-permute-start(bf16[2,32,1024]{2,1,0:T(8,128)(2,1)S(1)} %shard_map.135.refs_10_.refs_0_), channel_id=1, source_target_pairs={{0,4},{4,0},{8,12},{12,8},{1,5},{5,1},{9,13},{13,9},{2,6},{6,2},{1... | collective-permute-start | bytes 393224 | tf_op jit(solution)/shard_map/ppermute | solution.py:154
  76.4 6.9 %collective-permute-start.21 = (bf16[2,32,1024]{2,1,0:T(8,128)(2,1)S(1)}, bf16[2,32,1024]{2,1,0:T(8,128)(2,1)S(1)}, u32[]{:S(2)}, u32[]{:S(2)}) collective-permute-start(bf16[2,32,1024]{2,1,0:T(8,128)(2,1)S(1)} %shard_map.135.refs_10_.refs_0_), channel_id=1, source_target_pairs={{0,8},{4,12},{8,0},{12,4},{1,9},{5,13},{9,1},{13,5},{2,10},{6,14},... | collective-permute-start | bytes 393224 | tf_op jit(solution)/shard_map/ppermute | solution.py:154
  76.9 6.3 %collective-permute-start.22 = (bf16[2,32,1024]{2,1,0:T(8,128)(2,1)S(1)}, bf16[2,32,1024]{2,1,0:T(8,128)(2,1)S(1)}, u32[]{:S(2)}, u32[]{:S(2)}) collective-permute-start(bf16[2,32,1024]{2,1,0:T(8,128)(2,1)S(1)} %shard_map.135.refs_10_.refs_0_), channel_id=1, source_target_pairs={{0,12},{4,8},{8,4},{12,0},{1,13},{5,9},{9,5},{13,1},{2,14},{6,10},... | collective-permute-start | bytes 393224 | tf_op jit(solution)/shard_map/ppermute | solution.py:154
  78.6 6.9 %collective-permute-start.23 = (bf16[128,896]{1,0:T(8,128)(2,1)S(1)}, bf16[128,896]{1,0:T(8,128)(2,1)S(1)}, u32[]{:S(2)}, u32[]{:S(2)}) collective-permute-start(bf16[128,896]{1,0:T(8,128)(2,1)S(1)} %shard_map.134.refs_4_), channel_id=1, source_target_pairs={{0,1},{1,3},{3,2},{2,0},{4,5},{5,7},{7,6},{6,4},{8,9},{9,11},{11,1... | collective-permute-start | bytes 688136 | tf_op jit(solution)/shard_map/ppermute | solution.py:167
  81.6 7.0 %collective-permute-start.27 = (bf16[128,896]{1,0:T(8,128)(2,1)S(1)}, bf16[128,896]{1,0:T(8,128)(2,1)S(1)}, u32[]{:S(2)}, u32[]{:S(2)}) collective-permute-start(bf16[128,896]{1,0:T(8,128)(2,1)S(1)} %shard_map.136.refs_7_), channel_id=1, source_target_pairs={{0,1},{1,3},{3,2},{2,0},{4,5},{5,7},{7,6},{6,4},{8,9},{9,11},{11,1... | collective-permute-start | bytes 688136 | tf_op jit(solution)/shard_map/ppermute | solution.py:167
  90.9 8.8 %collective-permute-start.28 = (bf16[128,896]{1,0:T(8,128)(2,1)S(1)}, bf16[128,896]{1,0:T(8,128)(2,1)S(1)}, u32[]{:S(2)}, u32[]{:S(2)}) collective-permute-start(bf16[128,896]{1,0:T(8,128)(2,1)S(1)} %shard_map.138), channel_id=1, source_target_pairs={{0,17},{1,19},{3,18},{2,16},{16,1},{17,3},{19,2},{18,0},{4,21},{5,... | collective-permute-start | bytes 688136 | tf_op jit(solution)/shard_map/ppermute | solution.py:177
  90.9 10.5 %collective-permute-start.10 = (bf16[128,896]{1,0:T(8,128)(2,1)S(1)}, bf16[128,896]{1,0:T(8,128)(2,1)S(1)}, u32[]{:S(2)}, u32[]{:S(2)}) collective-permute-start(bf16[128,896]{1,0:T(8,128)(2,1)S(1)} %copy-done.12), channel_id=1, source_target_pairs={{0,16},{16,0},{1,17},{17,1},{2,18},{18,2},{3,19},{19,3},{4,20},{20... | collective-permute-start | bytes 688136 | tf_op jit(solution)/shard_map/ppermute | solution.py:14
  91.8 11.9 %collective-permute-start.25 = (bf16[128,896]{1,0:T(8,128)(2,1)S(1)}, bf16[128,896]{1,0:T(8,128)(2,1)S(1)}, u32[]{:S(2)}, u32[]{:S(2)}) collective-permute-start(bf16[128,896]{1,0:T(8,128)(2,1)S(1)} %shard_map.137.refs_10_), channel_id=1, source_target_pairs={{0,17},{1,19},{3,18},{2,16},{16,1},{17,3},{19,2},{18,0},{4,21},{5,... | collective-permute-start | bytes 688136 | tf_op jit(solution)/shard_map/ppermute | solution.py:177
  (10 other events, 56.4 us)

commit v5 on v4

--- a/solution.py
+++ b/solution.py
@@ -143,7 +143,8 @@
 VMEM = pl.BlockSpec(memory_space=pltpu.VMEM)
 SMEM = pl.BlockSpec(memory_space=pltpu.SMEM)
 VMEM_BYTES = 14 << 20
-CF = 100.0
+CF = 1.0
+SUM_COST = 1e10
 WIDE_BYTES = 56 << 20
 ANY = pl.BlockSpec(memory_space=pl.ANY)
 HBM = pl.BlockSpec(memory_space=pltpu.HBM)
@@ -167,12 +168,12 @@
     return lax.ppermute(value, "dev", ring_pairs(lax.axis_size("dev"), steps))
 
 
-def along_ring_and_sections(value, shift):
+def along_ring_and_sections(value, steps, shift):
     count, sections = lax.axis_size("dev"), lax.axis_size("section")
     pairs = [
         (section * count + source, (section + shift) % sections * count + target)
         for section in range(sections)
-        for source, target in ring_pairs(count, 1)
+        for source, target in ring_pairs(count, steps)
     ]
     return lax.ppermute(value, ("section", "dev"), pairs)
 
@@ -466,6 +467,23 @@
     )
 
 
+def sum_rows(values, after):
+    def body(*refs):
+        total = sum(ref[...].astype(jnp.float32) for ref in refs[: len(values)])
+        refs[-1][...] = total
+
+    return pl.pallas_call(
+        body,
+        in_specs=[VMEM] * len(values) + [ANY] * len(after),
+        out_specs=VMEM,
+        out_shape=jax.ShapeDtypeStruct(values[0].shape, jnp.float32),
+        cost_estimate=pl.CostEstimate(
+            flops=int(SUM_COST), bytes_accessed=int(SUM_COST / 100), transcendentals=0
+        ),
+        compiler_params=pltpu.CompilerParams(vmem_limit_bytes=VMEM_BYTES),
+    )(*values, *after)
+
+
 def ring_shards(
     inputs_forward,
     routes_forward,
@@ -497,71 +515,81 @@
         tokens.append(along_ring(tokens[-1], 1))
         grads.append(along_ring(grads[-1], 1))
 
-    sent, arrived, done = [None] * (experts + 1), [None] * (experts + 1), []
-
-    def exchange(turn, own):
-        sent[turn] = own
-        arrived[turn] = [own[0]] + [
-            across(own[mask % len(own)], "node", mask) for mask in range(1, nodes)
-        ]
-
-    def first(step):
+    sent, parts, acts = [None] * experts, [None] * experts, [None] * experts
+    done = []
+
+    def exchange(own):
+        return [own[0]] + [across(own[mask % len(own)], "node", mask) for mask in range(1, nodes)]
+
+    def first(step, *after):
         if step == 0:
             sent[0] = opening_products(
                 place, inputs_forward[0], grads_backward[0], weights, nodes
             )
         else:
             sent[step] = first_products(
-                place, tokens[step], grads[step], weights, nodes, 5, done[-1:]
+                place, tokens[step], grads[step], weights, nodes, 3 if step == 1 else 5, (*done[-1:], *after)
             )
         done.append(sent[step][0])
+        if step < 2:
+            parts[step] = exchange(sent[step])
+
+    def middle(step, *after):
+        joint = 0 < step < experts - 1
+        own = activations(place, parts[step], sent[step + 1] if joint else (), (*done[-1:], *after))
+        done.append(own[0])
+        acts[step] = exchange(own)
+        if joint:
+            parts[step + 1] = acts[step]
+
+    sums, hops = [[], []], [(), ()]
+
+    def last(step, kind, *after):
+        shift = 1 - 2 * kind
+        added = (inputs_forward[0], grads_backward[0])[kind : kind + 1] if step == 0 else ()
+        if step >= 2:
+            added = hops[kind]
+        if kind == 0:
+            value = forward_results(
+                place, acts[step], weights[2], tokens[step], chosen, added, (*done[-1:], *after)
+            )
+        else:
+            value = backward_results(
+                place, acts[step], *weights[:2], stored_gate, stored_up, tokens[step], chosen, added, step, (*done[-1:], *after)
+            )
+        done.append(value)
         if step == 0:
-            exchange(0, sent[0])
-
-    def middle(step):
-        filled = sent[step + 1] if step + 1 < experts else ()
-        own = activations(place, arrived[step], filled, done[-1:])
-        done.append(own[0])
-        exchange(step + 1, own)
-
-    base, hops = [None, None], [(inputs_forward[0],), (grads_backward[0],)]
-
-    def last(step, *kinds):
-        for kind in kinds:
-            pieces, added = arrived[step + 1], hops[kind]
-            if kind == 0:
-                value = forward_results(
-                    place, pieces, weights[2], tokens[step], chosen, added, done[-1:]
-                )
-            else:
-                value = backward_results(
-                    place, pieces, *weights[:2], stored_gate, stored_up, tokens[step], chosen, added, step, done[-1:]
-                )
-            done.append(value)
-            if step == 0:
-                base[kind], hops[kind] = from_behind(value, "section", 1 - 2 * kind), ()
-            elif step < experts - 1:
-                hops[kind] = (along_ring(value, 1),)
-            else:
-                hops[kind] = (along_ring_and_sections(value, 1 - 2 * kind),)
+            sums[kind].append(from_behind(value, "section", shift))
+        elif step == 1:
+            sums[kind].append(along_ring_and_sections(value, -1, shift))
+        elif step < experts - 1:
+            hops[kind] = (along_ring(value, 1),)
+        else:
+            sums[kind].append(along_ring_and_sections(value, 1, shift))
 
     first(0)
     first(1)
-    middle(0)
-    for turn in range(1, experts - 1):
-        if turn >= 2:
-            last(turn - 2, 0, 1)
-        first(turn + 1)
-        middle(turn)
-    if experts >= 3:
-        last(experts - 3, 0, 1)
-    last(experts - 2, 0)
+    for step in range(1, experts - 1):
+        first(step + 1, *(parts[0][1:] if step == 1 else ()))
+        middle(step)
+        if step >= 2:
+            last(step - 1, 0)
+            last(step - 1, 1)
     middle(experts - 1)
-    last(experts - 2, 1)
-    last(experts - 1, 0, 1)
+    if experts > 2:
+        last(experts - 2, 0)
+        last(experts - 2, 1, *[values[0] for values in sums if values])
+    middle(0, *acts[experts - 1][1:])
+    for step in (experts - 1, 0):
+        last(step, 0)
+        last(step, 1)
+    totals = []
+    for values in sums:
+        totals.append(sum_rows(values[:-1], done[-1:]))
+        done.append(totals[-1])
     return tuple(
-        (own.astype(jnp.float32) + others[0].astype(jnp.float32)).astype(jnp.bfloat16)[None]
-        for own, others in zip(base, hops)
+        (total.astype(jnp.float32) + values[-1].astype(jnp.float32)).astype(jnp.bfloat16)[None]
+        for total, values in zip(totals, sums)
     )
 
 

time: 105 us -> 94.6 us (0.901)
  waiting for transfers between devices: 32.1 us -> 25.4 us
  starting transfers between devices: 37.3 us -> 35.7 us
    ppermute x2 -> x4, waiting for transfers between devices: 7.19 us -> 1.16 us  [along_ring_and_sections(): return lax.ppermute(value, ('section', 'dev'), pairs)]
    ppermute x15 -> x18, waiting for transfers between devices: 18.8 us -> 12.9 us  [across(): lax.ppermute(value, axis, [(source, source ^ mask) for source in range(co...]
    ppermute x10 -> x8, starting transfers between devices: 15.7 us -> 9.9 us  [along_ring(): return lax.ppermute(value, 'dev', ring_pairs(lax.axis_size('dev'), steps))]
    ppermute x15 -> x18, starting transfers between devices: 17.7 us -> 23 us  [across(): lax.ppermute(value, axis, [(source, source ^ mask) for source in range(co...]
    ppermute x10 -> x8, waiting for transfers between devices: 6.14 us -> 11.3 us  [along_ring(): return lax.ppermute(value, 'dev', ring_pairs(lax.axis_size('dev'), steps))]
    ppermute x2 -> x4, starting transfers between devices: 3.04 us -> 2.12 us  [along_ring_and_sections(): return lax.ppermute(value, ('section', 'dev'), pairs)]
  transfers between devices with their start and end apart: 29 -> 32, of which waited for: 12 -> 12; matrix products, arithmetic and copies ran while one was open for 2% -> 2% of each run, Pallas kernels for 27% -> 27%
where the time goes in v5:
time: 94.6 us; the launch traced here: 94.4 us
  starting transfers between devices  35.7 us (38%)
  Pallas kernels  28.8 us (30%)
  waiting for transfers between devices  25.4 us (27%)
  other arithmetic  2.11 us (2%)
  local copies, waits for them, and re-layouts  1.55 us (2%)
    ppermute x18, starting transfers between devices, across(): lax.ppermute(value, axis, [(source, source ^ mask) for source in range(co...  23 us
    pallas_call x15, Pallas kernels, call(): pl.pallas_call(with_after, in_specs=[SMEM] + [VMEM] * len(operands) + [AN...  21.3 us
    ppermute x18, waiting for transfers between devices, across(): lax.ppermute(value, axis, [(source, source ^ mask) for source in range(co...  12.9 us
    ppermute x8, waiting for transfers between devices, along_ring(): return lax.ppermute(value, 'dev', ring_pairs(lax.axis_size('dev'), steps))  11.3 us
    ppermute x8, starting transfers between devices, along_ring(): return lax.ppermute(value, 'dev', ring_pairs(lax.axis_size('dev'), steps))  9.9 us
    pallas_call x1, Pallas kernels, opening_products(): pl.pallas_call(body, in_specs=[SMEM] + [HBM] * 5, out_specs=[VMEM] * node...  5.65 us
    ppermute x4, starting transfers between devices, along_ring_and_sections(): return lax.ppermute(value, ('section', 'dev'), pairs)  2.12 us
  transfers between devices with their start and end apart: 32, of which 12 were waited for; matrix products, arithmetic and copies ran while one was open for 2% of the time, Pallas kernels for 27%

profile of v5, /device:TPU:0, one launch (start us, length us, event | category | flops | bytes accessed | tf_op | source)
XLA Modules:
  0.0 94.4 jit_solution(2975401303369484846)
XLA Ops:
  0.6 1.7 %shard_map.122.refs_5_.refs_8_ = bf16[144,896]{1,0:T(8,128)(2,1)} custom-call(bf16[128,896]{1,0:T(8,128)(2,1)} %bitcast.57, s32[2,128]{1,0:T(2,128)} %bitcast.63, s32[2,128]{1,0:T(2,128)} %bitcast.64, f32[2,128]{1,0:T(2,128)} %bitcast.65, f32[2,128]{1,0:T(2,128)} %bitcast.66), custom_call_target="tpu_custom_call" | custom-call | tf_op jit(solution)/shard_map/pallas_call | solution.py:307
  2.3 3.1 %collective-permute-start = (bf16[144,896]{1,0:T(8,128)(2,1)}, bf16[144,896]{1,0:T(8,128)(2,1)S(1)}, u32[]{:S(2)}, u32[]{:S(2)}) collective-permute-start(bf16[144,896]{1,0:T(8,128)(2,1)} %shard_map.122.refs_5_.refs_8_), channel_id=1, source_target_pairs={{0,1},{1,3},{3,2},{2,0},{4,5},{5,7},{7,6},{6,4},{8,9},{9,11},{11,1... | collective-permute-start | bytes 774152 | tf_op jit(solution)/shard_map/ppermute | solution.py:168
  5.4 2.6 %collective-permute-start.1 = (bf16[128,896]{1,0:T(8,128)(2,1)}, bf16[128,896]{1,0:T(8,128)(2,1)S(1)}, u32[]{:S(2)}, u32[]{:S(2)}) collective-permute-start(bf16[128,896]{1,0:T(8,128)(2,1)} %bitcast.60), channel_id=1, source_target_pairs={{0,1},{1,3},{3,2},{2,0},{4,5},{5,7},{7,6},{6,4},{8,9},{9,11},{11,1... | collective-permute-start | bytes 688136 | tf_op jit(solution)/shard_map/ppermute | solution.py:168
  8.7 5.7 %shard_map.123 = (bf16[3,32,1024]{2,1,0:T(8,128)(2,1)}, bf16[3,32,1024]{2,1,0:T(8,128)(2,1)}, bf16[3,32,1024]{2,1,0:T(8,128)(2,1)}, bf16[3,32,1024]{2,1,0:T(8,128)(2,1)}) custom-call(s32[2]{0:T(128)} %pad_add_fusion.place_ref, bf16[128,896]{1,0:T(8,128)(2,1)} %bitcast.58, bf16[896,1024]{1,0:T(8,128)(2,1)} %bitcast.33, bf16[896,1024]{1,0:T(8,128)(2,1)} %bitcast.41, ...), custom_call_target="tpu_custom_call" | custom-call | flops 704643072 | bytes 5505024 | tf_op jit(solution)/shard_map/pallas_call | solution.py:355
  14.3 1.5 %collective-permute-start.7 = (bf16[3,32,1024]{2,1,0:T(8,128)(2,1)}, bf16[3,32,1024]{2,1,0:T(8,128)(2,1)S(1)}, u32[]{:S(2)}, u32[]{:S(2)}) collective-permute-start(bf16[3,32,1024]{2,1,0:T(8,128)(2,1)} %get-tuple-element.31), channel_id=1, source_target_pairs={{0,4},{4,0},{8,12},{12,8},{1,5},{5,1},{9,13},{13,9},{2,6},{6,2},{1... | collective-permute-start | bytes 589832 | tf_op jit(solution)/shard_map/ppermute | solution.py:155
  15.9 1.5 %collective-permute-start.8 = (bf16[3,32,1024]{2,1,0:T(8,128)(2,1)}, bf16[3,32,1024]{2,1,0:T(8,128)(2,1)S(1)}, u32[]{:S(2)}, u32[]{:S(2)}) collective-permute-start(bf16[3,32,1024]{2,1,0:T(8,128)(2,1)} %get-tuple-element.32), channel_id=1, source_target_pairs={{0,8},{4,12},{8,0},{12,4},{1,9},{5,13},{9,1},{13,5},{2,10},{6,14},... | collective-permute-start | bytes 589832 | tf_op jit(solution)/shard_map/ppermute | solution.py:155
  18.3 1.5 %collective-permute-start.6 = (bf16[128,896]{1,0:T(8,128)(2,1)S(1)}, bf16[128,896]{1,0:T(8,128)(2,1)S(1)}, u32[]{:S(2)}, u32[]{:S(2)}) collective-permute-start(bf16[128,896]{1,0:T(8,128)(2,1)S(1)} %collective-permute-done.1.refs_1_), channel_id=1, source_target_pairs={{0,1},{1,3},{3,2},{2,0},{4,5},{5,7},{7,6},{6,4},{8,9},{9,11},{11,1... | collective-permute-start | bytes 688136 | tf_op jit(solution)/shard_map/ppermute | solution.py:168
  20.8 1.8 %shard_map.124 = (bf16[3,32,1024]{2,1,0:T(8,128)(2,1)S(1)}, bf16[3,32,1024]{2,1,0:T(8,128)(2,1)S(1)}, bf16[3,32,1024]{2,1,0:T(8,128)(2,1)S(1)}, bf16[3,32,1024]{2,1,0:T(8,128)(2,1)S(1)}) custom-call(s32[2]{0:T(128)S(1)} %copy-done.10, bf16[144,896]{1,0:T(8,128)(2,1)S(1)} %collective-permute-done.refs_0_.refs_5_.refs_8_, ...), custom_call_target="tpu_custom_call" | custom-call | flops 704643072 | bytes 5992448 | tf_op jit(solution)/shard_map/pallas_call | solution.py:193
  22.7 1.6 %collective-permute-start.2 = (bf16[3,32,1024]{2,1,0:T(8,128)(2,1)S(1)}, bf16[3,32,1024]{2,1,0:T(8,128)(2,1)S(1)}, u32[]{:S(2)}, u32[]{:S(2)}) collective-permute-start(bf16[3,32,1024]{2,1,0:T(8,128)(2,1)S(1)} %get-tuple-element.28), channel_id=1, source_target_pairs={{0,4},{4,0},{8,12},{12,8},{1,5},{5,1},{9,13},{13,9},{2,6},{6,2},{1... | collective-permute-start | bytes 589832 | tf_op jit(solution)/shard_map/ppermute | solution.py:155
  24.2 1.1 %collective-permute-done.8.refs_7_.refs_2_ = bf16[3,32,1024]{2,1,0:T(8,128)(2,1)S(1)} collective-permute-done((bf16[3,32,1024]{2,1,0:T(8,128)(2,1)}, bf16[3,32,1024]{2,1,0:T(8,128)(2,1)S(1)}, u32[]{:S(2)}, u32[]{:S(2)}) %collective-permute-start.8) | collective-permute-done | bytes 196640 | tf_op jit(solution)/shard_map/ppermute | solution.py:155
  25.3 2.8 %collective-permute-start.3 = (bf16[3,32,1024]{2,1,0:T(8,128)(2,1)S(1)}, bf16[3,32,1024]{2,1,0:T(8,128)(2,1)S(1)}, u32[]{:S(2)}, u32[]{:S(2)}) collective-permute-start(bf16[3,32,1024]{2,1,0:T(8,128)(2,1)S(1)} %get-tuple-element.29), channel_id=1, source_target_pairs={{0,8},{4,12},{8,0},{12,4},{1,9},{5,13},{9,1},{13,5},{2,10},{6,14},... | collective-permute-start | bytes 589832 | tf_op jit(solution)/shard_map/ppermute | solution.py:155
  29.0 1.2 %collective-permute-done.6.refs_1_ = bf16[128,896]{1,0:T(8,128)(2,1)S(1)} collective-permute-done((bf16[128,896]{1,0:T(8,128)(2,1)S(1)}, bf16[128,896]{1,0:T(8,128)(2,1)S(1)}, u32[]{:S(2)}, u32[]{:S(2)}) %collective-permute-start.6) | collective-permute-done | bytes 229408 | tf_op jit(solution)/shard_map/ppermute | solution.py:168
  30.3 1.8 %shard_map.125 = (bf16[5,32,1024]{2,1,0:T(8,128)(2,1)S(1)}, bf16[5,32,1024]{2,1,0:T(8,128)(2,1)S(1)}, bf16[5,32,1024]{2,1,0:T(8,128)(2,1)S(1)}, bf16[5,32,1024]{2,1,0:T(8,128)(2,1)S(1)}) custom-call(s32[2]{0:T(128)S(1)} %copy-done.10, bf16[144,896]{1,0:T(8,128)(2,1)S(1)} %collective-permute-done.5.refs_0_.refs_5_.refs_8_, ...), custom_call_target="tpu_custom_call" | custom-call | flops 704643072 | bytes 5992448 | tf_op jit(solution)/shard_map/pallas_call | solution.py:193
  32.1 3.2 %collective-permute-done.3.refs_2_ = bf16[3,32,1024]{2,1,0:T(8,128)(2,1)S(1)} collective-permute-done((bf16[3,32,1024]{2,1,0:T(8,128)(2,1)S(1)}, bf16[3,32,1024]{2,1,0:T(8,128)(2,1)S(1)}, u32[]{:S(2)}, u32[]{:S(2)}) %collective-permute-start.3) | collective-permute-done | bytes 196640 | tf_op jit(solution)/shard_map/ppermute | solution.py:155
  37.5 2.1 %collective-permute-start.12 = (bf16[5,32,1024]{2,1,0:T(8,128)(2,1)S(1)}, bf16[5,32,1024]{2,1,0:T(8,128)(2,1)S(1)}, u32[]{:S(2)}, u32[]{:S(2)}) collective-permute-start(bf16[5,32,1024]{2,1,0:T(8,128)(2,1)S(1)} %get-tuple-element.41), channel_id=1, source_target_pairs={{0,12},{4,8},{8,4},{12,0},{1,13},{5,9},{9,5},{13,1},{2,14},{6,10},... | collective-permute-start | bytes 983048 | tf_op jit(solution)/shard_map/ppermute | solution.py:155
  40.6 8.9 %collective-permute-done.14.refs_1_ = bf16[128,896]{1,0:T(8,128)(2,1)S(1)} collective-permute-done((bf16[128,896]{1,0:T(8,128)(2,1)S(1)}, bf16[128,896]{1,0:T(8,128)(2,1)S(1)}, u32[]{:S(2)}, u32[]{:S(2)}) %collective-permute-start.14) | collective-permute-done | bytes 229408 | tf_op jit(solution)/shard_map/ppermute | solution.py:168
  49.5 1.8 %shard_map.127 = (bf16[5,32,1024]{2,1,0:T(8,128)(2,1)S(1)}, bf16[5,32,1024]{2,1,0:T(8,128)(2,1)S(1)}, bf16[5,32,1024]{2,1,0:T(8,128)(2,1)S(1)}, bf16[5,32,1024]{2,1,0:T(8,128)(2,1)S(1)}) custom-call(s32[2]{0:T(128)S(1)} %copy-done.10, bf16[144,896]{1,0:T(8,128)(2,1)S(1)} %collective-permute-done.13.refs_0_.refs_5_.refs_8_, ...), custom_call_target="tpu_custom_call" | custom-call | flops 704643072 | bytes 5992448 | tf_op jit(solution)/shard_map/pallas_call | solution.py:193
  52.1 1.7 %collective-permute-start.16 = (bf16[5,32,1024]{2,1,0:T(8,128)(2,1)S(1)}, bf16[5,32,1024]{2,1,0:T(8,128)(2,1)S(1)}, u32[]{:S(2)}, u32[]{:S(2)}) collective-permute-start(bf16[5,32,1024]{2,1,0:T(8,128)(2,1)S(1)} %get-tuple-element.47), channel_id=1, source_target_pairs={{0,4},{4,0},{8,12},{12,8},{1,5},{5,1},{9,13},{13,9},{2,6},{6,2},{1... | collective-permute-start | bytes 983048 | tf_op jit(solution)/shard_map/ppermute | solution.py:155
  54.3 1.3 %collective-permute-start.18 = (bf16[5,32,1024]{2,1,0:T(8,128)(2,1)S(1)}, bf16[5,32,1024]{2,1,0:T(8,128)(2,1)S(1)}, u32[]{:S(2)}, u32[]{:S(2)}) collective-permute-start(bf16[5,32,1024]{2,1,0:T(8,128)(2,1)S(1)} %get-tuple-element.49), channel_id=1, source_target_pairs={{0,12},{4,8},{8,4},{12,0},{1,13},{5,9},{9,5},{13,1},{2,14},{6,10},... | collective-permute-start | bytes 983048 | tf_op jit(solution)/shard_map/ppermute | solution.py:155
  57.2 2.3 %shard_map.130.refs_4_ = bf16[128,896]{1,0:T(8,128)(2,1)S(1)} custom-call(s32[2]{0:T(128)S(1)} %copy-done.10, bf16[5,32,1024]{2,1,0:T(8,128)(2,1)S(1)} %get-tuple-element.38.refs_5_.refs_0_, bf16[5,32,1024]{2,1,0:T(8,128)(2,1)S(1)} %collective-permute-done.10.refs_1_, bf16[5,32,1024]{2,1,0:T(8,128)(2,1)S(1)} %collective-permute-done.11.refs_2_, ...), custom_call_target="tpu_custom_call" | custom-call | flops 469762048 | bytes 7335936 | tf_op jit(solution)/shard_map/pallas_call | solution.py:193
  60.4 1.1 %collective-permute-done.16.refs_1_ = bf16[5,32,1024]{2,1,0:T(8,128)(2,1)S(1)} collective-permute-done((bf16[5,32,1024]{2,1,0:T(8,128)(2,1)S(1)}, bf16[5,32,1024]{2,1,0:T(8,128)(2,1)S(1)}, u32[]{:S(2)}, u32[]{:S(2)}) %collective-permute-start.16) | collective-permute-done | bytes 327712 | tf_op jit(solution)/shard_map/ppermute | solution.py:155
  61.5 4.9 %collective-permute-done.17.refs_2_ = bf16[5,32,1024]{2,1,0:T(8,128)(2,1)S(1)} collective-permute-done((bf16[5,32,1024]{2,1,0:T(8,128)(2,1)S(1)}, bf16[5,32,1024]{2,1,0:T(8,128)(2,1)S(1)}, u32[]{:S(2)}, u32[]{:S(2)}) %collective-permute-start.17) | collective-permute-done | bytes 327712 | tf_op jit(solution)/shard_map/ppermute | solution.py:155
  68.2 1.2 %collective-permute-start.21 = (bf16[2,32,1024]{2,1,0:T(8,128)(2,1)S(1)}, bf16[2,32,1024]{2,1,0:T(8,128)(2,1)S(1)}, u32[]{:S(2)}, u32[]{:S(2)}) collective-permute-start(bf16[2,32,1024]{2,1,0:T(8,128)(2,1)S(1)} %shard_map.131.refs_6_.refs_0_), channel_id=1, source_target_pairs={{0,12},{4,8},{8,4},{12,0},{1,13},{5,9},{9,5},{13,1},{2,14},{6,10},... | collective-permute-start | bytes 393224 | tf_op jit(solution)/shard_map/ppermute | solution.py:155
  70.2 1.6 %collective-permute-start.19 = (bf16[2,32,1024]{2,1,0:T(8,128)(2,1)S(1)}, bf16[2,32,1024]{2,1,0:T(8,128)(2,1)S(1)}, u32[]{:S(2)}, u32[]{:S(2)}) collective-permute-start(bf16[2,32,1024]{2,1,0:T(8,128)(2,1)S(1)} %shard_map.131.refs_6_.refs_0_), channel_id=1, source_target_pairs={{0,4},{4,0},{8,12},{12,8},{1,5},{5,1},{9,13},{13,9},{2,6},{6,2},{1... | collective-permute-start | bytes 393224 | tf_op jit(solution)/shard_map/ppermute | solution.py:155
  71.8 2.3 %shard_map.133.refs_4_ = bf16[128,896]{1,0:T(8,128)(2,1)S(1)} custom-call(s32[2]{0:T(128)S(1)} %copy-done.10, bf16[5,32,1024]{2,1,0:T(8,128)(2,1)S(1)} %get-tuple-element.46.refs_6_.refs_0_, bf16[5,32,1024]{2,1,0:T(8,128)(2,1)S(1)} %collective-permute-done.16.refs_1_, bf16[5,32,1024]{2,1,0:T(8,128)(2,1)S(1)} %collective-permute-done.17.refs_2_, ...), custom_call_target="tpu_custom_call" | custom-call | flops 469762048 | bytes 7335936 | tf_op jit(solution)/shard_map/pallas_call | solution.py:193
  74.1 1.1 %collective-permute-start.28 = (bf16[128,896]{1,0:T(8,128)(2,1)S(1)}, bf16[128,896]{1,0:T(8,128)(2,1)S(1)}, u32[]{:S(2)}, u32[]{:S(2)}) collective-permute-start(bf16[128,896]{1,0:T(8,128)(2,1)S(1)} %shard_map.133.refs_4_), channel_id=1, source_target_pairs={{0,1},{1,3},{3,2},{2,0},{4,5},{5,7},{7,6},{6,4},{8,9},{9,11},{11,1... | collective-permute-start | bytes 688136 | tf_op jit(solution)/shard_map/ppermute | solution.py:168
  77.5 2.2 %collective-permute-start.27 = (bf16[2,32,1024]{2,1,0:T(8,128)(2,1)S(1)}, bf16[2,32,1024]{2,1,0:T(8,128)(2,1)S(1)}, u32[]{:S(2)}, u32[]{:S(2)}) collective-permute-start(bf16[2,32,1024]{2,1,0:T(8,128)(2,1)S(1)} %shard_map.134.refs_7_.refs_0_), channel_id=1, source_target_pairs={{0,12},{4,8},{8,4},{12,0},{1,13},{5,9},{9,5},{13,1},{2,14},{6,10},... | collective-permute-start | bytes 393224 | tf_op jit(solution)/shard_map/ppermute | solution.py:155
  82.1 2.3 %shard_map.136.refs_7_ = bf16[128,896]{1,0:T(8,128)(2,1)S(1)} custom-call(s32[2]{0:T(128)S(1)} %copy-done.10, bf16[2,32,1024]{2,1,0:T(8,128)(2,1)S(1)} %shard_map.131.refs_6_.refs_0_, bf16[2,32,1024]{2,1,0:T(8,128)(2,1)S(1)} %collective-permute-done.19.refs_5_.refs_1_, bf16[2,32,1024]{2,1,0:T(8,128)(2,1)S(1)} %collective-permute-done.20.refs_6_.refs_2_, ...), custom_call_target="tpu_custom_call" | custom-call | flops 469762048 | bytes 6778880 | tf_op jit(solution)/shard_map/pallas_call | solution.py:193
  84.4 1.1 %collective-permute-start.30 = (bf16[128,896]{1,0:T(8,128)(2,1)S(1)}, bf16[128,896]{1,0:T(8,128)(2,1)S(1)}, u32[]{:S(2)}, u32[]{:S(2)}) collective-permute-start(bf16[128,896]{1,0:T(8,128)(2,1)S(1)} %shard_map.136.refs_7_), channel_id=1, source_target_pairs={{0,17},{1,19},{3,18},{2,16},{16,1},{17,3},{19,2},{18,0},{4,21},{5,... | collective-permute-start | bytes 688136 | tf_op jit(solution)/shard_map/ppermute | solution.py:178
  85.5 2.1 %collective-permute-done.26.refs_2_ = bf16[2,32,1024]{2,1,0:T(8,128)(2,1)S(1)} collective-permute-done((bf16[2,32,1024]{2,1,0:T(8,128)(2,1)S(1)}, bf16[2,32,1024]{2,1,0:T(8,128)(2,1)S(1)}, u32[]{:S(2)}, u32[]{:S(2)}) %collective-permute-start.26) | collective-permute-done | bytes 131104 | tf_op jit(solution)/shard_map/ppermute | solution.py:155
  88.9 2.3 %shard_map.138.refs_2_ = bf16[128,896]{1,0:T(8,128)(2,1)S(1)} custom-call(s32[2]{0:T(128)S(1)} %copy-done.10, bf16[2,32,1024]{2,1,0:T(8,128)(2,1)S(1)} %shard_map.134.refs_7_.refs_0_, bf16[2,32,1024]{2,1,0:T(8,128)(2,1)S(1)} %collective-permute-done.25.refs_1_, bf16[2,32,1024]{2,1,0:T(8,128)(2,1)S(1)} %collective-permute-done.26.refs_2_, ...), custom_call_target="tpu_custom_call" | custom-call | flops 469762048 | bytes 6778880 | tf_op jit(solution)/shard_map/pallas_call | solution.py:193
  91.7 1.2 %collective-permute-done.30.refs_1_ = bf16[128,896]{1,0:T(8,128)(2,1)S(1)} collective-permute-done((bf16[128,896]{1,0:T(8,128)(2,1)S(1)}, bf16[128,896]{1,0:T(8,128)(2,1)S(1)}, u32[]{:S(2)}, u32[]{:S(2)}) %collective-permute-start.30) | collective-permute-done | bytes 229408 | tf_op jit(solution)/shard_map/ppermute | solution.py:178
  (78 shorter events, 20.8 us)
Async XLA Ops:
  2.3 15.5 %collective-permute-start = (bf16[144,896]{1,0:T(8,128)(2,1)}, bf16[144,896]{1,0:T(8,128)(2,1)S(1)}, u32[]{:S(2)}, u32[]{:S(2)}) collective-permute-start(bf16[144,896]{1,0:T(8,128)(2,1)} %shard_map.122.refs_5_.refs_8_), channel_id=1, source_target_pairs={{0,1},{1,3},{3,2},{2,0},{4,5},{5,7},{7,6},{6,4},{8,9},{9,11},{11,1... | collective-permute-start | bytes 774152 | tf_op jit(solution)/shard_map/ppermute | solution.py:168
  5.4 12.9 %collective-permute-start.1 = (bf16[128,896]{1,0:T(8,128)(2,1)}, bf16[128,896]{1,0:T(8,128)(2,1)S(1)}, u32[]{:S(2)}, u32[]{:S(2)}) collective-permute-start(bf16[128,896]{1,0:T(8,128)(2,1)} %bitcast.60), channel_id=1, source_target_pairs={{0,1},{1,3},{3,2},{2,0},{4,5},{5,7},{7,6},{6,4},{8,9},{9,11},{11,1... | collective-permute-start | bytes 688136 | tf_op jit(solution)/shard_map/ppermute | solution.py:168
  14.3 8.3 %collective-permute-start.7 = (bf16[3,32,1024]{2,1,0:T(8,128)(2,1)}, bf16[3,32,1024]{2,1,0:T(8,128)(2,1)S(1)}, u32[]{:S(2)}, u32[]{:S(2)}) collective-permute-start(bf16[3,32,1024]{2,1,0:T(8,128)(2,1)} %get-tuple-element.31), channel_id=1, source_target_pairs={{0,4},{4,0},{8,12},{12,8},{1,5},{5,1},{9,13},{13,9},{2,6},{6,2},{1... | collective-permute-start | bytes 589832 | tf_op jit(solution)/shard_map/ppermute | solution.py:155
  15.9 9.5 %collective-permute-start.8 = (bf16[3,32,1024]{2,1,0:T(8,128)(2,1)}, bf16[3,32,1024]{2,1,0:T(8,128)(2,1)S(1)}, u32[]{:S(2)}, u32[]{:S(2)}) collective-permute-start(bf16[3,32,1024]{2,1,0:T(8,128)(2,1)} %get-tuple-element.32), channel_id=1, source_target_pairs={{0,8},{4,12},{8,0},{12,4},{1,9},{5,13},{9,1},{13,5},{2,10},{6,14},... | collective-permute-start | bytes 589832 | tf_op jit(solution)/shard_map/ppermute | solution.py:155
  17.4 10.8 %collective-permute-start.9 = (bf16[3,32,1024]{2,1,0:T(8,128)(2,1)}, bf16[3,32,1024]{2,1,0:T(8,128)(2,1)S(1)}, u32[]{:S(2)}, u32[]{:S(2)}) collective-permute-start(bf16[3,32,1024]{2,1,0:T(8,128)(2,1)} %get-tuple-element.33), channel_id=1, source_target_pairs={{0,12},{4,8},{8,4},{12,0},{1,13},{5,9},{9,5},{13,1},{2,14},{6,10},... | collective-permute-start | bytes 589832 | tf_op jit(solution)/shard_map/ppermute | solution.py:155
  17.9 12.4 %collective-permute-start.5 = (bf16[144,896]{1,0:T(8,128)(2,1)S(1)}, bf16[144,896]{1,0:T(8,128)(2,1)S(1)}, u32[]{:S(2)}, u32[]{:S(2)}) collective-permute-start(bf16[144,896]{1,0:T(8,128)(2,1)S(1)} %collective-permute-done.refs_0_.refs_5_.refs_8_), channel_id=1, source_target_pairs={{0,1},{1,3},{3,2},{2,0},{4,5},{5,7},{7,6},{6,4},{8,9},{9,11},{11,1... | collective-permute-start | bytes 774152 | tf_op jit(solution)/shard_map/ppermute | solution.py:168
  18.3 11.9 %collective-permute-start.6 = (bf16[128,896]{1,0:T(8,128)(2,1)S(1)}, bf16[128,896]{1,0:T(8,128)(2,1)S(1)}, u32[]{:S(2)}, u32[]{:S(2)}) collective-permute-start(bf16[128,896]{1,0:T(8,128)(2,1)S(1)} %collective-permute-done.1.refs_1_), channel_id=1, source_target_pairs={{0,1},{1,3},{3,2},{2,0},{4,5},{5,7},{7,6},{6,4},{8,9},{9,11},{11,1... | collective-permute-start | bytes 688136 | tf_op jit(solution)/shard_map/ppermute | solution.py:168
  22.7 9.5 %collective-permute-start.2 = (bf16[3,32,1024]{2,1,0:T(8,128)(2,1)S(1)}, bf16[3,32,1024]{2,1,0:T(8,128)(2,1)S(1)}, u32[]{:S(2)}, u32[]{:S(2)}) collective-permute-start(bf16[3,32,1024]{2,1,0:T(8,128)(2,1)S(1)} %get-tuple-element.28), channel_id=1, source_target_pairs={{0,4},{4,0},{8,12},{12,8},{1,5},{5,1},{9,13},{13,9},{2,6},{6,2},{1... | collective-permute-start | bytes 589832 | tf_op jit(solution)/shard_map/ppermute | solution.py:155
  25.3 10.0 %collective-permute-start.3 = (bf16[3,32,1024]{2,1,0:T(8,128)(2,1)S(1)}, bf16[3,32,1024]{2,1,0:T(8,128)(2,1)S(1)}, u32[]{:S(2)}, u32[]{:S(2)}) collective-permute-start(bf16[3,32,1024]{2,1,0:T(8,128)(2,1)S(1)} %get-tuple-element.29), channel_id=1, source_target_pairs={{0,8},{4,12},{8,0},{12,4},{1,9},{5,13},{9,1},{13,5},{2,10},{6,14},... | collective-permute-start | bytes 589832 | tf_op jit(solution)/shard_map/ppermute | solution.py:155
  28.2 7.1 %collective-permute-start.4 = (bf16[3,32,1024]{2,1,0:T(8,128)(2,1)S(1)}, bf16[3,32,1024]{2,1,0:T(8,128)(2,1)S(1)}, u32[]{:S(2)}, u32[]{:S(2)}) collective-permute-start(bf16[3,32,1024]{2,1,0:T(8,128)(2,1)S(1)} %get-tuple-element.30), channel_id=1, source_target_pairs={{0,12},{4,8},{8,4},{12,0},{1,13},{5,9},{9,5},{13,1},{2,14},{6,10},... | collective-permute-start | bytes 589832 | tf_op jit(solution)/shard_map/ppermute | solution.py:155
  36.0 15.4 %collective-permute-start.10 = (bf16[5,32,1024]{2,1,0:T(8,128)(2,1)S(1)}, bf16[5,32,1024]{2,1,0:T(8,128)(2,1)S(1)}, u32[]{:S(2)}, u32[]{:S(2)}) collective-permute-start(bf16[5,32,1024]{2,1,0:T(8,128)(2,1)S(1)} %get-tuple-element.39), channel_id=1, source_target_pairs={{0,4},{4,0},{8,12},{12,8},{1,5},{5,1},{9,13},{13,9},{2,6},{6,2},{1... | collective-permute-start | bytes 983048 | tf_op jit(solution)/shard_map/ppermute | solution.py:155
  36.5 14.9 %collective-permute-start.11 = (bf16[5,32,1024]{2,1,0:T(8,128)(2,1)S(1)}, bf16[5,32,1024]{2,1,0:T(8,128)(2,1)S(1)}, u32[]{:S(2)}, u32[]{:S(2)}) collective-permute-start(bf16[5,32,1024]{2,1,0:T(8,128)(2,1)S(1)} %get-tuple-element.40), channel_id=1, source_target_pairs={{0,8},{4,12},{8,0},{12,4},{1,9},{5,13},{9,1},{13,5},{2,10},{6,14},... | collective-permute-start | bytes 983048 | tf_op jit(solution)/shard_map/ppermute | solution.py:155
  37.5 13.9 %collective-permute-start.12 = (bf16[5,32,1024]{2,1,0:T(8,128)(2,1)S(1)}, bf16[5,32,1024]{2,1,0:T(8,128)(2,1)S(1)}, u32[]{:S(2)}, u32[]{:S(2)}) collective-permute-start(bf16[5,32,1024]{2,1,0:T(8,128)(2,1)S(1)} %get-tuple-element.41), channel_id=1, source_target_pairs={{0,12},{4,8},{8,4},{12,0},{1,13},{5,9},{9,5},{13,1},{2,14},{6,10},... | collective-permute-start | bytes 983048 | tf_op jit(solution)/shard_map/ppermute | solution.py:155
  39.6 9.9 %collective-permute-start.13 = (bf16[144,896]{1,0:T(8,128)(2,1)S(1)}, bf16[144,896]{1,0:T(8,128)(2,1)S(1)}, u32[]{:S(2)}, u32[]{:S(2)}) collective-permute-start(bf16[144,896]{1,0:T(8,128)(2,1)S(1)} %collective-permute-done.5.refs_0_.refs_5_.refs_8_), channel_id=1, source_target_pairs={{0,1},{1,3},{3,2},{2,0},{4,5},{5,7},{7,6},{6,4},{8,9},{9,11},{11,1... | collective-permute-start | bytes 774152 | tf_op jit(solution)/shard_map/ppermute | solution.py:168
  40.3 9.2 %collective-permute-start.14 = (bf16[128,896]{1,0:T(8,128)(2,1)S(1)}, bf16[128,896]{1,0:T(8,128)(2,1)S(1)}, u32[]{:S(2)}, u32[]{:S(2)}) collective-permute-start(bf16[128,896]{1,0:T(8,128)(2,1)S(1)} %collective-permute-done.6.refs_1_), channel_id=1, source_target_pairs={{0,1},{1,3},{3,2},{2,0},{4,5},{5,7},{7,6},{6,4},{8,9},{9,11},{11,1... | collective-permute-start | bytes 688136 | tf_op jit(solution)/shard_map/ppermute | solution.py:168
  52.1 9.4 %collective-permute-start.16 = (bf16[5,32,1024]{2,1,0:T(8,128)(2,1)S(1)}, bf16[5,32,1024]{2,1,0:T(8,128)(2,1)S(1)}, u32[]{:S(2)}, u32[]{:S(2)}) collective-permute-start(bf16[5,32,1024]{2,1,0:T(8,128)(2,1)S(1)} %get-tuple-element.47), channel_id=1, source_target_pairs={{0,4},{4,0},{8,12},{12,8},{1,5},{5,1},{9,13},{13,9},{2,6},{6,2},{1... | collective-permute-start | bytes 983048 | tf_op jit(solution)/shard_map/ppermute | solution.py:155
  53.8 12.6 %collective-permute-start.17 = (bf16[5,32,1024]{2,1,0:T(8,128)(2,1)S(1)}, bf16[5,32,1024]{2,1,0:T(8,128)(2,1)S(1)}, u32[]{:S(2)}, u32[]{:S(2)}) collective-permute-start(bf16[5,32,1024]{2,1,0:T(8,128)(2,1)S(1)} %get-tuple-element.48), channel_id=1, source_target_pairs={{0,8},{4,12},{8,0},{12,4},{1,9},{5,13},{9,1},{13,5},{2,10},{6,14},... | collective-permute-start | bytes 983048 | tf_op jit(solution)/shard_map/ppermute | solution.py:155
  54.3 12.1 %collective-permute-start.18 = (bf16[5,32,1024]{2,1,0:T(8,128)(2,1)S(1)}, bf16[5,32,1024]{2,1,0:T(8,128)(2,1)S(1)}, u32[]{:S(2)}, u32[]{:S(2)}) collective-permute-start(bf16[5,32,1024]{2,1,0:T(8,128)(2,1)S(1)} %get-tuple-element.49), channel_id=1, source_target_pairs={{0,12},{4,8},{8,4},{12,0},{1,13},{5,9},{9,5},{13,1},{2,14},{6,10},... | collective-permute-start | bytes 983048 | tf_op jit(solution)/shard_map/ppermute | solution.py:155
  59.4 10.7 %collective-permute-start.23 = (bf16[128,896]{1,0:T(8,128)(2,1)S(1)}, bf16[128,896]{1,0:T(8,128)(2,1)S(1)}, u32[]{:S(2)}, u32[]{:S(2)}) collective-permute-start(bf16[128,896]{1,0:T(8,128)(2,1)S(1)} %shard_map.130.refs_4_), channel_id=1, source_target_pairs={{0,18},{1,16},{3,17},{2,19},{16,2},{17,0},{19,1},{18,3},{4,22},{5,... | collective-permute-start | bytes 688136 | tf_op jit(solution)/shard_map/ppermute | solution.py:178
  59.5 12.2 %collective-permute-start.15 = (bf16[128,896]{1,0:T(8,128)(2,1)S(1)}, bf16[128,896]{1,0:T(8,128)(2,1)S(1)}, u32[]{:S(2)}, u32[]{:S(2)}) collective-permute-start(bf16[128,896]{1,0:T(8,128)(2,1)S(1)} %shard_map.129.refs_9_), channel_id=1, source_target_pairs={{0,18},{1,16},{3,17},{2,19},{16,2},{17,0},{19,1},{18,3},{4,22},{5,... | collective-permute-start | bytes 688136 | tf_op jit(solution)/shard_map/ppermute | solution.py:178
  68.1 8.3 %collective-permute-start.22 = (bf16[128,896]{1,0:T(8,128)(2,1)S(1)}, bf16[128,896]{1,0:T(8,128)(2,1)S(1)}, u32[]{:S(2)}, u32[]{:S(2)}) collective-permute-start(bf16[128,896]{1,0:T(8,128)(2,1)S(1)} %shard_map.132.refs_9_), channel_id=1, source_target_pairs={{0,1},{1,3},{3,2},{2,0},{4,5},{5,7},{7,6},{6,4},{8,9},{9,11},{11,1... | collective-permute-start | bytes 688136 | tf_op jit(solution)/shard_map/ppermute | solution.py:168
  68.2 7.0 %collective-permute-start.21 = (bf16[2,32,1024]{2,1,0:T(8,128)(2,1)S(1)}, bf16[2,32,1024]{2,1,0:T(8,128)(2,1)S(1)}, u32[]{:S(2)}, u32[]{:S(2)}) collective-permute-start(bf16[2,32,1024]{2,1,0:T(8,128)(2,1)S(1)} %shard_map.131.refs_6_.refs_0_), channel_id=1, source_target_pairs={{0,12},{4,8},{8,4},{12,0},{1,13},{5,9},{9,5},{13,1},{2,14},{6,10},... | collective-permute-start | bytes 393224 | tf_op jit(solution)/shard_map/ppermute | solution.py:155
  69.4 6.1 %collective-permute-start.20 = (bf16[2,32,1024]{2,1,0:T(8,128)(2,1)S(1)}, bf16[2,32,1024]{2,1,0:T(8,128)(2,1)S(1)}, u32[]{:S(2)}, u32[]{:S(2)}) collective-permute-start(bf16[2,32,1024]{2,1,0:T(8,128)(2,1)S(1)} %shard_map.131.refs_6_.refs_0_), channel_id=1, source_target_pairs={{0,8},{4,12},{8,0},{12,4},{1,9},{5,13},{9,1},{13,5},{2,10},{6,14},... | collective-permute-start | bytes 393224 | tf_op jit(solution)/shard_map/ppermute | solution.py:155
  70.2 5.4 %collective-permute-start.19 = (bf16[2,32,1024]{2,1,0:T(8,128)(2,1)S(1)}, bf16[2,32,1024]{2,1,0:T(8,128)(2,1)S(1)}, u32[]{:S(2)}, u32[]{:S(2)}) collective-permute-start(bf16[2,32,1024]{2,1,0:T(8,128)(2,1)S(1)} %shard_map.131.refs_6_.refs_0_), channel_id=1, source_target_pairs={{0,4},{4,0},{8,12},{12,8},{1,5},{5,1},{9,13},{13,9},{2,6},{6,2},{1... | collective-permute-start | bytes 393224 | tf_op jit(solution)/shard_map/ppermute | solution.py:155
  74.1 8.1 %collective-permute-start.28 = (bf16[128,896]{1,0:T(8,128)(2,1)S(1)}, bf16[128,896]{1,0:T(8,128)(2,1)S(1)}, u32[]{:S(2)}, u32[]{:S(2)}) collective-permute-start(bf16[128,896]{1,0:T(8,128)(2,1)S(1)} %shard_map.133.refs_4_), channel_id=1, source_target_pairs={{0,1},{1,3},{3,2},{2,0},{4,5},{5,7},{7,6},{6,4},{8,9},{9,11},{11,1... | collective-permute-start | bytes 688136 | tf_op jit(solution)/shard_map/ppermute | solution.py:168
  77.4 14.2 %collective-permute-start.24 = (bf16[128,896]{1,0:T(8,128)(2,1)S(1)}, bf16[128,896]{1,0:T(8,128)(2,1)S(1)}, u32[]{:S(2)}, u32[]{:S(2)}) collective-permute-start(bf16[128,896]{1,0:T(8,128)(2,1)S(1)} %shard_map.135.refs_10_), channel_id=1, source_target_pairs={{0,17},{1,19},{3,18},{2,16},{16,1},{17,3},{19,2},{18,0},{4,21},{5,... | collective-permute-start | bytes 688136 | tf_op jit(solution)/shard_map/ppermute | solution.py:178
  77.5 8.0 %collective-permute-start.27 = (bf16[2,32,1024]{2,1,0:T(8,128)(2,1)S(1)}, bf16[2,32,1024]{2,1,0:T(8,128)(2,1)S(1)}, u32[]{:S(2)}, u32[]{:S(2)}) collective-permute-start(bf16[2,32,1024]{2,1,0:T(8,128)(2,1)S(1)} %shard_map.134.refs_7_.refs_0_), channel_id=1, source_target_pairs={{0,12},{4,8},{8,4},{12,0},{1,13},{5,9},{9,5},{13,1},{2,14},{6,10},... | collective-permute-start | bytes 393224 | tf_op jit(solution)/shard_map/ppermute | solution.py:155
  79.7 7.9 %collective-permute-start.26 = (bf16[2,32,1024]{2,1,0:T(8,128)(2,1)S(1)}, bf16[2,32,1024]{2,1,0:T(8,128)(2,1)S(1)}, u32[]{:S(2)}, u32[]{:S(2)}) collective-permute-start(bf16[2,32,1024]{2,1,0:T(8,128)(2,1)S(1)} %shard_map.134.refs_7_.refs_0_), channel_id=1, source_target_pairs={{0,8},{4,12},{8,0},{12,4},{1,9},{5,13},{9,1},{13,5},{2,10},{6,14},... | collective-permute-start | bytes 393224 | tf_op jit(solution)/shard_map/ppermute | solution.py:155
  80.5 7.2 %collective-permute-start.25 = (bf16[2,32,1024]{2,1,0:T(8,128)(2,1)S(1)}, bf16[2,32,1024]{2,1,0:T(8,128)(2,1)S(1)}, u32[]{:S(2)}, u32[]{:S(2)}) collective-permute-start(bf16[2,32,1024]{2,1,0:T(8,128)(2,1)S(1)} %shard_map.134.refs_7_.refs_0_), channel_id=1, source_target_pairs={{0,4},{4,0},{8,12},{12,8},{1,5},{5,1},{9,13},{13,9},{2,6},{6,2},{1... | collective-permute-start | bytes 393224 | tf_op jit(solution)/shard_map/ppermute | solution.py:155
  84.4 8.5 %collective-permute-start.30 = (bf16[128,896]{1,0:T(8,128)(2,1)S(1)}, bf16[128,896]{1,0:T(8,128)(2,1)S(1)}, u32[]{:S(2)}, u32[]{:S(2)}) collective-permute-start(bf16[128,896]{1,0:T(8,128)(2,1)S(1)} %shard_map.136.refs_7_), channel_id=1, source_target_pairs={{0,17},{1,19},{3,18},{2,16},{16,1},{17,3},{19,2},{18,0},{4,21},{5,... | collective-permute-start | bytes 688136 | tf_op jit(solution)/shard_map/ppermute | solution.py:178
  88.7 4.2 %collective-permute-start.29 = (bf16[128,896]{1,0:T(8,128)(2,1)S(1)}, bf16[128,896]{1,0:T(8,128)(2,1)S(1)}, u32[]{:S(2)}, u32[]{:S(2)}) collective-permute-start(bf16[128,896]{1,0:T(8,128)(2,1)S(1)} %shard_map.137.refs_10_), channel_id=1, source_target_pairs={{0,16},{16,0},{1,17},{17,1},{2,18},{18,2},{3,19},{19,3},{4,20},{20... | collective-permute-start | bytes 688136 | tf_op jit(solution)/shard_map/ppermute | solution.py:14
  91.2 2.5 %collective-permute-start.31 = (bf16[128,896]{1,0:T(8,128)(2,1)S(1)}, bf16[128,896]{1,0:T(8,128)(2,1)S(1)}, u32[]{:S(2)}, u32[]{:S(2)}) collective-permute-start(bf16[128,896]{1,0:T(8,128)(2,1)S(1)} %shard_map.138.refs_2_), channel_id=1, source_target_pairs={{0,16},{16,0},{1,17},{17,1},{2,18},{18,2},{3,19},{19,3},{4,20},{20... | collective-permute-start | bytes 688136 | tf_op jit(solution)/shard_map/ppermute | solution.py:14
  (11 other events, 81.0 us)

commit v6 on v5

--- a/solution.py
+++ b/solution.py
@@ -145,6 +145,8 @@
 VMEM_BYTES = 14 << 20
 CF = 1.0
 SUM_COST = 1e10
+SPACE_COST = 10**10
+INFO_COST = 10**6
 WIDE_BYTES = 56 << 20
 ANY = pl.BlockSpec(memory_space=pl.ANY)
 HBM = pl.BlockSpec(memory_space=pltpu.HBM)
@@ -286,33 +288,43 @@
     return copies
 
 
-def with_info(rows, routes, gates):
+def with_info(rows, routes, gates, after):
     (count, width), chosen = rows.shape, routes[0].shape[0]
     height = -(-6 * chosen // 16) * 16
     small = (*routes, *gates)
 
-    def body(*refs):
-        inputs, out, held, sems = refs[:5], refs[5], refs[6:10], refs[10]
-        targets = (out.at[pl.ds(0, count)], *held)
-        for copy in copied(inputs, targets, sems):
-            copy.wait()
-        lines = [ref[...].astype(jnp.float32) for ref in held[:2]]
-        for ref in held[2:]:
+    def body(rows_ref, *refs):
+        infos, out = refs[:4], refs[-1]
+        lines = [ref[...].astype(jnp.float32) for ref in infos[:2]]
+        for ref in infos[2:]:
             coarse = ref[...].astype(jnp.bfloat16).astype(jnp.float32)
             lines += [coarse, ref[...] - coarse]
         lines.append(jnp.zeros((height - 6 * chosen, count), jnp.float32))
+        out[0:count, :] = rows_ref[...]
         out[count:, :] = jnp.zeros((height, width), jnp.bfloat16)
         out[count:, 0:count] = jnp.concatenate(lines).astype(jnp.bfloat16)
 
     return pl.pallas_call(
         body,
-        in_specs=[HBM] * 5,
+        in_specs=[VMEM] * 5 + [ANY] * len(after),
         out_specs=VMEM,
         out_shape=jax.ShapeDtypeStruct((count + height, width), jnp.bfloat16),
-        scratch_shapes=[pltpu.VMEM(value.shape, value.dtype) for value in small]
-        + [pltpu.SemaphoreType.DMA((5,))],
-        compiler_params=pltpu.CompilerParams(vmem_limit_bytes=WIDE_BYTES),
-    )(rows, *small)
+        cost_estimate=pl.CostEstimate(flops=INFO_COST, bytes_accessed=INFO_COST // 100, transcendentals=0),
+        compiler_params=pltpu.CompilerParams(vmem_limit_bytes=4 << 20),
+    )(rows, *small, *after)
+
+
+def marker():
+    def body(out):
+        out[...] = jnp.zeros_like(out)
+
+    return pl.pallas_call(
+        body,
+        out_specs=VMEM,
+        out_shape=jax.ShapeDtypeStruct((8, 128), jnp.float32),
+        cost_estimate=pl.CostEstimate(flops=SPACE_COST, bytes_accessed=SPACE_COST // 100, transcendentals=0),
+        compiler_params=pltpu.CompilerParams(vmem_limit_bytes=1 << 20),
+    )()
 
 
 def opening_products(place, token_rows, grad_rows, weights, nodes):
@@ -432,26 +444,44 @@
     )
 
 
-def backward_results(place, pieces, w_gate, w_up, saved_gate, saved_up, info, chosen, added, block, after):
+def backward_factors(place, saved_gate, saved_up, info, chosen, count, block, after):
+    slots, hidden = saved_gate.shape
+    experts = slots // count
+
+    def body(place_ref, saved_gate_ref, saved_up_ref, info_ref, gate_out, up_out):
+        routes, _ = info_of(info_ref, count, chosen, 1)
+        select = slot_selection(place_ref[1], routes, count)
+        first = pl.multiple_of(block_behind(place_ref[1], experts, block) * count, count)
+        act_gate = matmul(select, saved_gate_ref[pl.ds(first, count), :], CONTRACT_FIRST)
+        act_up = matmul(select, saved_up_ref[pl.ds(first, count), :], CONTRACT_FIRST)
+        squash = 1.0 / (1.0 + jnp.exp(-act_gate))
+        gate_out[...] = act_up * squash * (1.0 + act_gate * (1.0 - squash))
+        up_out[...] = act_gate * squash
+
+    return call(
+        body,
+        place,
+        (saved_gate, saved_up, info),
+        after,
+        [jax.ShapeDtypeStruct((count, hidden), jnp.float32)] * 2,
+        [],
+        4 * count * count * hidden,
+    )
+
+
+def backward_results(place, pieces, w_gate, w_up, factors, info, chosen, added, after):
     nodes, (_, share, hidden), width = len(pieces), pieces[0].shape, w_gate.shape[0]
     count = share * nodes
-    experts = saved_gate.shape[0] // count
 
     def body(place_ref, *refs):
         piece_refs, refs = refs[:nodes], refs[nodes:]
-        gate_ref, up_ref, saved_gate_ref, saved_up_ref, info_ref = refs[:5]
+        gate_ref, up_ref, gate_factor, up_factor, info_ref = refs[:5]
         added_refs, (out, joined) = refs[5:-2], refs[-2:]
         join(place_ref, piece_refs, 1, joined)
-        expert = place_ref[1]
-        routes, gates = info_of(info_ref, count, chosen, 1)
-        weight = weight_column(expert, routes, gates)
-        select = slot_selection(expert, routes, count)
-        first = pl.multiple_of(block_behind(expert, experts, block) * count, count)
-        grad_gate, grad_up = backward_act(
-            joined[...].astype(jnp.float32),
-            matmul(select, saved_gate_ref[pl.ds(first, count), :], CONTRACT_FIRST),
-            matmul(select, saved_up_ref[pl.ds(first, count), :], CONTRACT_FIRST),
-        )
+        weight = weight_column(place_ref[1], *info_of(info_ref, count, chosen, 1))
+        grad_hidden = joined[...].astype(jnp.float32)
+        grad_gate = (grad_hidden * gate_factor[...]).astype(jnp.bfloat16)
+        grad_up = (grad_hidden * up_factor[...]).astype(jnp.bfloat16)
         result = matmul(grad_gate, gate_ref[...], CONTRACT_LAST)
         result += matmul(grad_up, up_ref[...], CONTRACT_LAST)
         give(out, weight, result, added_refs)
@@ -459,7 +489,7 @@
     return call(
         body,
         place,
-        (*pieces, w_gate, w_up, saved_gate, saved_up, info, *added),
+        (*pieces, w_gate, w_up, *factors, info, *added),
         after,
         jax.ShapeDtypeStruct((count, width), jnp.bfloat16),
         [pltpu.VMEM((count, hidden), jnp.bfloat16)],
@@ -508,6 +538,7 @@
             inputs_forward[0],
             (routes_forward[0].T, routes_backward[0].T),
             (gates_forward[0].T, gates_backward[0].T),
+            (marker(),),
         )
     ]
     grads = [grads_backward[0]]
@@ -515,21 +546,25 @@
         tokens.append(along_ring(tokens[-1], 1))
         grads.append(along_ring(grads[-1], 1))
 
+    count = grads_backward.shape[1]
     sent, parts, acts = [None] * experts, [None] * experts, [None] * experts
     done = []
 
     def exchange(own):
         return [own[0]] + [across(own[mask % len(own)], "node", mask) for mask in range(1, nodes)]
 
+    factors = [None] * experts
+
+    def prepare(step):
+        factors[step] = backward_factors(
+            place, stored_gate, stored_up, tokens[step], chosen, count, step, done[-1:]
+        )
+        done.append(factors[step][0])
+
     def first(step, *after):
-        if step == 0:
-            sent[0] = opening_products(
-                place, inputs_forward[0], grads_backward[0], weights, nodes
-            )
-        else:
-            sent[step] = first_products(
-                place, tokens[step], grads[step], weights, nodes, 3 if step == 1 else 5, (*done[-1:], *after)
-            )
+        sent[step] = first_products(
+            place, tokens[step], grads[step], weights, nodes, 5 if step > 1 else 3, (*done[-1:], *after)
+        )
         done.append(sent[step][0])
         if step < 2:
             parts[step] = exchange(sent[step])
@@ -555,7 +590,7 @@
             )
         else:
             value = backward_results(
-                place, acts[step], *weights[:2], stored_gate, stored_up, tokens[step], chosen, added, step, (*done[-1:], *after)
+                place, acts[step], *weights[:2], factors[step], tokens[step], chosen, added, (*done[-1:], *after)
             )
         done.append(value)
         if step == 0:
@@ -571,10 +606,13 @@
     first(1)
     for step in range(1, experts - 1):
         first(step + 1, *(parts[0][1:] if step == 1 else ()))
+        prepare(step)
         middle(step)
         if step >= 2:
             last(step - 1, 0)
             last(step - 1, 1)
+    prepare(experts - 1)
+    prepare(0)
     middle(experts - 1)
     if experts > 2:
         last(experts - 2, 0)
@@ -583,14 +621,11 @@
     for step in (experts - 1, 0):
         last(step, 0)
         last(step, 1)
-    totals = []
+    outs = []
     for values in sums:
-        totals.append(sum_rows(values[:-1], done[-1:]))
-        done.append(totals[-1])
-    return tuple(
-        (total.astype(jnp.float32) + values[-1].astype(jnp.float32)).astype(jnp.bfloat16)[None]
-        for total, values in zip(totals, sums)
-    )
+        total = sum_rows(values[:-1], (*done[-1:], *outs)) + values[-1].astype(jnp.float32)
+        outs.append(total.astype(jnp.bfloat16))
+    return tuple(out[None] for out in outs)
 
 
 def power_of_two(number):

time: 94.6 us -> 92.1 us (0.974)
  waiting for transfers between devices: 25.4 us -> 17.9 us
  starting transfers between devices: 35.7 us -> 41.6 us
  local copies, waits for them, and re-layouts: 1.55 us -> 4.57 us
  Pallas kernels: 28.8 us -> 25.9 us
  other arithmetic: 2.11 us -> 0.86 us
    pallas_call x2, Pallas kernels: 7.36 us -> 0.03 us  [the longest x1 0.03 us: with_info(): pl.pallas_call(body, in_specs=[VMEM] * 5 + [ANY] * len(after), out_specs=...]
    ppermute x8, starting transfers between devices: 9.9 us -> 14.8 us  [along_ring(): return lax.ppermute(value, 'dev', ring_pairs(lax.axis_size('dev'), steps))]
    pallas_call x15 -> x20, Pallas kernels: 21.3 us -> 25.7 us  [call(): pl.pallas_call(with_after, in_specs=[SMEM] + [VMEM] * len(operands) + [AN...]
    ppermute x18, waiting for transfers between devices: 12.9 us -> 8.96 us  [across(): lax.ppermute(value, axis, [(source, source ^ mask) for source in range(co...]
    unnamed x24 -> x28, local copies, waits for them, and re-layouts: 1.55 us -> 4.57 us
    ppermute x8, waiting for transfers between devices: 11.3 us -> 8.61 us  [along_ring(): return lax.ppermute(value, 'dev', ring_pairs(lax.axis_size('dev'), steps))]
    ppermute x4, starting transfers between devices: 2.12 us -> 3.36 us  [along_ring_and_sections(): return lax.ppermute(value, ('section', 'dev'), pairs)]
    ppermute x4, waiting for transfers between devices: 1.16 us -> 0.01 us  [along_ring_and_sections(): return lax.ppermute(value, ('section', 'dev'), pairs)]
  transfers between devices with their start and end apart: 32 -> 32, of which waited for: 12 -> 9; matrix products, arithmetic and copies ran while one was open for 2% -> 0% of each run, Pallas kernels for 27% -> 27%
where the time goes in v6:
time: 92.1 us; the launch traced here: 91.9 us
  starting transfers between devices  41.6 us (45%)
  Pallas kernels  25.9 us (28%)
  waiting for transfers between devices  17.9 us (19%)
  local copies, waits for them, and re-layouts  4.57 us (5%)
  between operations  1 us (1%)
    pallas_call x20, Pallas kernels, call(): pl.pallas_call(with_after, in_specs=[SMEM] + [VMEM] * len(operands) + [AN...  25.7 us
    ppermute x18, starting transfers between devices, across(): lax.ppermute(value, axis, [(source, source ^ mask) for source in range(co...  22.8 us
    ppermute x8, starting transfers between devices, along_ring(): return lax.ppermute(value, 'dev', ring_pairs(lax.axis_size('dev'), steps))  14.8 us
    ppermute x18, waiting for transfers between devices, across(): lax.ppermute(value, axis, [(source, source ^ mask) for source in range(co...  8.96 us
    ppermute x8, waiting for transfers between devices, along_ring(): return lax.ppermute(value, 'dev', ring_pairs(lax.axis_size('dev'), steps))  8.61 us
    unnamed x28, local copies, waits for them, and re-layouts  4.57 us
    ppermute x4, starting transfers between devices, along_ring_and_sections(): return lax.ppermute(value, ('section', 'dev'), pairs)  3.36 us
  transfers between devices with their start and end apart: 32, of which 9 were waited for; matrix products, arithmetic and copies ran while one was open for 0% of the time, Pallas kernels for 27%

profile of v6, /device:TPU:0, one launch (start us, length us, event | category | flops | bytes accessed | tf_op | source)
XLA Modules:
  0.0 91.9 jit_solution(3463022653283166258)
XLA Ops:
  1.7 3.1 %collective-permute-start = (bf16[144,896]{1,0:T(8,128)(2,1)S(1)}, bf16[144,896]{1,0:T(8,128)(2,1)S(1)}, u32[]{:S(2)}, u32[]{:S(2)}) collective-permute-start(bf16[144,896]{1,0:T(8,128)(2,1)S(1)} %shard_map.123.refs_0_.refs_2_.refs_5_.refs_8_), channel_id=1, source_target_pairs={{0,1},{1,3},{3,2},{2,0},{4,5},{5,7},{7,6},{6,4},{8,9},{9,11},{11,1... | collective-permute-start | bytes 774152 | tf_op jit(solution)/shard_map/ppermute | solution.py:170
  4.7 2.6 %collective-permute-start.1 = (bf16[128,896]{1,0:T(8,128)(2,1)S(1)}, bf16[128,896]{1,0:T(8,128)(2,1)S(1)}, u32[]{:S(2)}, u32[]{:S(2)}) collective-permute-start(bf16[128,896]{1,0:T(8,128)(2,1)S(1)} %bitcast.58), channel_id=1, source_target_pairs={{0,1},{1,3},{3,2},{2,0},{4,5},{5,7},{7,6},{6,4},{8,9},{9,11},{11,1... | collective-permute-start | bytes 688136 | tf_op jit(solution)/shard_map/ppermute | solution.py:170
  7.4 1.5 %copy-done.1 = bf16[1,1,896,1024]{3,2,1,0:T(8,128)(2,1)S(1)} copy-done((bf16[1,1,896,1024]{3,2,1,0:T(8,128)(2,1)S(1)}, bf16[1,1,896,1024]{3,2,1,0:T(8,128)(2,1)}, u32[]{:S(2)}) %copy-start.1) | copy-done | bytes 1835032
  8.9 1.5 %copy-done.3 = bf16[1,1,896,1024]{3,2,1,0:T(8,128)(2,1)S(1)} copy-done((bf16[1,1,896,1024]{3,2,1,0:T(8,128)(2,1)S(1)}, bf16[1,1,896,1024]{3,2,1,0:T(8,128)(2,1)}, u32[]{:S(2)}) %copy-start.3) | copy-done | bytes 1835032
  10.4 1.8 %shard_map.124 = (bf16[3,32,1024]{2,1,0:T(8,128)(2,1)S(1)}, bf16[3,32,1024]{2,1,0:T(8,128)(2,1)S(1)}, bf16[3,32,1024]{2,1,0:T(8,128)(2,1)S(1)}, bf16[3,32,1024]{2,1,0:T(8,128)(2,1)S(1)}) custom-call(s32[2]{0:T(128)S(1)} %pad_add_fusion.place_ref, bf16[144,896]{1,0:T(8,128)(2,1)S(1)} %shard_map.123.refs_0_.refs_2_.refs_5_.refs_8_, ...), custom_call_target="tpu_custom_call" | custom-call | flops 704643072 | bytes 5992448 | tf_op jit(solution)/shard_map/pallas_call | solution.py:195
  12.3 1.6 %collective-permute-start.7 = (bf16[3,32,1024]{2,1,0:T(8,128)(2,1)S(1)}, bf16[3,32,1024]{2,1,0:T(8,128)(2,1)S(1)}, u32[]{:S(2)}, u32[]{:S(2)}) collective-permute-start(bf16[3,32,1024]{2,1,0:T(8,128)(2,1)S(1)} %get-tuple-element.39), channel_id=1, source_target_pairs={{0,4},{4,0},{8,12},{12,8},{1,5},{5,1},{9,13},{13,9},{2,6},{6,2},{1... | collective-permute-start | bytes 589832 | tf_op jit(solution)/shard_map/ppermute | solution.py:157
  13.8 1.5 %collective-permute-start.8 = (bf16[3,32,1024]{2,1,0:T(8,128)(2,1)S(1)}, bf16[3,32,1024]{2,1,0:T(8,128)(2,1)S(1)}, u32[]{:S(2)}, u32[]{:S(2)}) collective-permute-start(bf16[3,32,1024]{2,1,0:T(8,128)(2,1)S(1)} %get-tuple-element.40), channel_id=1, source_target_pairs={{0,8},{4,12},{8,0},{12,4},{1,9},{5,13},{9,1},{13,5},{2,10},{6,14},... | collective-permute-start | bytes 589832 | tf_op jit(solution)/shard_map/ppermute | solution.py:157
  16.9 2.0 %collective-permute-start.6 = (bf16[128,896]{1,0:T(8,128)(2,1)S(1)}, bf16[128,896]{1,0:T(8,128)(2,1)S(1)}, u32[]{:S(2)}, u32[]{:S(2)}) collective-permute-start(bf16[128,896]{1,0:T(8,128)(2,1)S(1)} %collective-permute-done.1.refs_1_), channel_id=1, source_target_pairs={{0,1},{1,3},{3,2},{2,0},{4,5},{5,7},{7,6},{6,4},{8,9},{9,11},{11,1... | collective-permute-start | bytes 688136 | tf_op jit(solution)/shard_map/ppermute | solution.py:170
  18.9 1.8 %shard_map.125 = (bf16[3,32,1024]{2,1,0:T(8,128)(2,1)S(1)}, bf16[3,32,1024]{2,1,0:T(8,128)(2,1)S(1)}, bf16[3,32,1024]{2,1,0:T(8,128)(2,1)S(1)}, bf16[3,32,1024]{2,1,0:T(8,128)(2,1)S(1)}) custom-call(s32[2]{0:T(128)S(1)} %pad_add_fusion.place_ref, bf16[144,896]{1,0:T(8,128)(2,1)S(1)} %collective-permute-done.refs_0_.refs_2_.refs_5_.refs_8_, ...), custom_call_target="tpu_custom_call" | custom-call | flops 704643072 | bytes 5992448 | tf_op jit(solution)/shard_map/pallas_call | solution.py:195
  20.7 1.6 %collective-permute-start.2 = (bf16[3,32,1024]{2,1,0:T(8,128)(2,1)S(1)}, bf16[3,32,1024]{2,1,0:T(8,128)(2,1)S(1)}, u32[]{:S(2)}, u32[]{:S(2)}) collective-permute-start(bf16[3,32,1024]{2,1,0:T(8,128)(2,1)S(1)} %get-tuple-element.36), channel_id=1, source_target_pairs={{0,4},{4,0},{8,12},{12,8},{1,5},{5,1},{9,13},{13,9},{2,6},{6,2},{1... | collective-permute-start | bytes 589832 | tf_op jit(solution)/shard_map/ppermute | solution.py:157
  23.2 2.7 %collective-permute-start.3 = (bf16[3,32,1024]{2,1,0:T(8,128)(2,1)S(1)}, bf16[3,32,1024]{2,1,0:T(8,128)(2,1)S(1)}, u32[]{:S(2)}, u32[]{:S(2)}) collective-permute-start(bf16[3,32,1024]{2,1,0:T(8,128)(2,1)S(1)} %get-tuple-element.37), channel_id=1, source_target_pairs={{0,8},{4,12},{8,0},{12,4},{1,9},{5,13},{9,1},{13,5},{2,10},{6,14},... | collective-permute-start | bytes 589832 | tf_op jit(solution)/shard_map/ppermute | solution.py:157
  27.7 2.1 %collective-permute-done.6.refs_1_ = bf16[128,896]{1,0:T(8,128)(2,1)S(1)} collective-permute-done((bf16[128,896]{1,0:T(8,128)(2,1)S(1)}, bf16[128,896]{1,0:T(8,128)(2,1)S(1)}, u32[]{:S(2)}, u32[]{:S(2)}) %collective-permute-start.6) | collective-permute-done | bytes 229408 | tf_op jit(solution)/shard_map/ppermute | solution.py:170
  29.7 1.8 %shard_map.126 = (bf16[5,32,1024]{2,1,0:T(8,128)(2,1)S(1)}, bf16[5,32,1024]{2,1,0:T(8,128)(2,1)S(1)}, bf16[5,32,1024]{2,1,0:T(8,128)(2,1)S(1)}, bf16[5,32,1024]{2,1,0:T(8,128)(2,1)S(1)}) custom-call(s32[2]{0:T(128)S(1)} %pad_add_fusion.place_ref, bf16[144,896]{1,0:T(8,128)(2,1)S(1)} %collective-permute-done.5.refs_0_.refs_2_.refs_5_.refs_8_, ...), custom_call_target="tpu_custom_call" | custom-call | flops 704643072 | bytes 5992448 | tf_op jit(solution)/shard_map/pallas_call | solution.py:195
  33.7 2.2 %collective-permute-start.10 = (bf16[5,32,1024]{2,1,0:T(8,128)(2,1)S(1)}, bf16[5,32,1024]{2,1,0:T(8,128)(2,1)S(1)}, u32[]{:S(2)}, u32[]{:S(2)}) collective-permute-start(bf16[5,32,1024]{2,1,0:T(8,128)(2,1)S(1)} %get-tuple-element.48), channel_id=1, source_target_pairs={{0,4},{4,0},{8,12},{12,8},{1,5},{5,1},{9,13},{13,9},{2,6},{6,2},{1... | collective-permute-start | bytes 983048 | tf_op jit(solution)/shard_map/ppermute | solution.py:157
  35.9 1.5 %collective-permute-start.11 = (bf16[5,32,1024]{2,1,0:T(8,128)(2,1)S(1)}, bf16[5,32,1024]{2,1,0:T(8,128)(2,1)S(1)}, u32[]{:S(2)}, u32[]{:S(2)}) collective-permute-start(bf16[5,32,1024]{2,1,0:T(8,128)(2,1)S(1)} %get-tuple-element.49), channel_id=1, source_target_pairs={{0,8},{4,12},{8,0},{12,4},{1,9},{5,13},{9,1},{13,5},{2,10},{6,14},... | collective-permute-start | bytes 983048 | tf_op jit(solution)/shard_map/ppermute | solution.py:157
  38.5 5.9 %collective-permute-done.14.refs_1_ = bf16[128,896]{1,0:T(8,128)(2,1)S(1)} collective-permute-done((bf16[128,896]{1,0:T(8,128)(2,1)S(1)}, bf16[128,896]{1,0:T(8,128)(2,1)S(1)}, u32[]{:S(2)}, u32[]{:S(2)}) %collective-permute-start.14) | collective-permute-done | bytes 229408 | tf_op jit(solution)/shard_map/ppermute | solution.py:170
  44.4 1.8 %shard_map.129 = (bf16[5,32,1024]{2,1,0:T(8,128)(2,1)S(1)}, bf16[5,32,1024]{2,1,0:T(8,128)(2,1)S(1)}, bf16[5,32,1024]{2,1,0:T(8,128)(2,1)S(1)}, bf16[5,32,1024]{2,1,0:T(8,128)(2,1)S(1)}) custom-call(s32[2]{0:T(128)S(1)} %pad_add_fusion.place_ref, bf16[144,896]{1,0:T(8,128)(2,1)S(1)} %collective-permute-done.13.refs_0_.refs_2_.refs_5_.refs_8_, ...), custom_call_target="tpu_custom_call" | custom-call | flops 704643072 | bytes 5992448 | tf_op jit(solution)/shard_map/pallas_call | solution.py:195
  47.4 2.6 %collective-permute-done.11.refs_2_ = bf16[5,32,1024]{2,1,0:T(8,128)(2,1)S(1)} collective-permute-done((bf16[5,32,1024]{2,1,0:T(8,128)(2,1)S(1)}, bf16[5,32,1024]{2,1,0:T(8,128)(2,1)S(1)}, u32[]{:S(2)}, u32[]{:S(2)}) %collective-permute-start.11) | collective-permute-done | bytes 327712 | tf_op jit(solution)/shard_map/ppermute | solution.py:157
  50.8 2.3 %collective-permute-start.17 = (bf16[5,32,1024]{2,1,0:T(8,128)(2,1)S(1)}, bf16[5,32,1024]{2,1,0:T(8,128)(2,1)S(1)}, u32[]{:S(2)}, u32[]{:S(2)}) collective-permute-start(bf16[5,32,1024]{2,1,0:T(8,128)(2,1)S(1)} %get-tuple-element.58), channel_id=1, source_target_pairs={{0,8},{4,12},{8,0},{12,4},{1,9},{5,13},{9,1},{13,5},{2,10},{6,14},... | collective-permute-start | bytes 983048 | tf_op jit(solution)/shard_map/ppermute | solution.py:157
  53.1 1.2 %collective-permute-start.18 = (bf16[5,32,1024]{2,1,0:T(8,128)(2,1)S(1)}, bf16[5,32,1024]{2,1,0:T(8,128)(2,1)S(1)}, u32[]{:S(2)}, u32[]{:S(2)}) collective-permute-start(bf16[5,32,1024]{2,1,0:T(8,128)(2,1)S(1)} %get-tuple-element.59), channel_id=1, source_target_pairs={{0,12},{4,8},{8,4},{12,0},{1,13},{5,9},{9,5},{13,1},{2,14},{6,10},... | collective-permute-start | bytes 983048 | tf_op jit(solution)/shard_map/ppermute | solution.py:157
  55.2 1.8 %shard_map.133.refs_3_ = bf16[128,896]{1,0:T(8,128)(2,1)S(1)} custom-call(s32[2]{0:T(128)S(1)} %pad_add_fusion.place_ref, bf16[5,32,1024]{2,1,0:T(8,128)(2,1)S(1)} %get-tuple-element.47.refs_5_.refs_0_, bf16[5,32,1024]{2,1,0:T(8,128)(2,1)S(1)} %collective-permute-done.10.refs_1_, bf16[5,32,1024]{2,1,0:T(8,128)(2,1)S(1)} %collective-permute-done.11.refs_2_, ...), custom_call_target="tpu_custom_call" | custom-call | flops 469762048 | bytes 6287360 | tf_op jit(solution)/shard_map/pallas_call | solution.py:195
  57.1 1.8 %collective-permute-start.15 = (bf16[128,896]{1,0:T(8,128)(2,1)S(1)}, bf16[128,896]{1,0:T(8,128)(2,1)S(1)}, u32[]{:S(2)}, u32[]{:S(2)}) collective-permute-start(bf16[128,896]{1,0:T(8,128)(2,1)S(1)} %shard_map.132.refs_9_), channel_id=1, source_target_pairs={{0,18},{1,16},{3,17},{2,19},{16,2},{17,0},{19,1},{18,3},{4,22},{5,... | collective-permute-start | bytes 688136 | tf_op jit(solution)/shard_map/ppermute | solution.py:180
  61.2 1.6 %collective-permute-done.17.refs_2_ = bf16[5,32,1024]{2,1,0:T(8,128)(2,1)S(1)} collective-permute-done((bf16[5,32,1024]{2,1,0:T(8,128)(2,1)S(1)}, bf16[5,32,1024]{2,1,0:T(8,128)(2,1)S(1)}, u32[]{:S(2)}, u32[]{:S(2)}) %collective-permute-start.17) | collective-permute-done | bytes 327712 | tf_op jit(solution)/shard_map/ppermute | solution.py:157
  65.1 1.3 %collective-permute-start.21 = (bf16[2,32,1024]{2,1,0:T(8,128)(2,1)S(1)}, bf16[2,32,1024]{2,1,0:T(8,128)(2,1)S(1)}, u32[]{:S(2)}, u32[]{:S(2)}) collective-permute-start(bf16[2,32,1024]{2,1,0:T(8,128)(2,1)S(1)} %shard_map.136.refs_6_.refs_0_), channel_id=1, source_target_pairs={{0,12},{4,8},{8,4},{12,0},{1,13},{5,9},{9,5},{13,1},{2,14},{6,10},... | collective-permute-start | bytes 393224 | tf_op jit(solution)/shard_map/ppermute | solution.py:157
  66.3 1.5 %collective-permute-start.20 = (bf16[2,32,1024]{2,1,0:T(8,128)(2,1)S(1)}, bf16[2,32,1024]{2,1,0:T(8,128)(2,1)S(1)}, u32[]{:S(2)}, u32[]{:S(2)}) collective-permute-start(bf16[2,32,1024]{2,1,0:T(8,128)(2,1)S(1)} %shard_map.136.refs_6_.refs_0_), channel_id=1, source_target_pairs={{0,8},{4,12},{8,0},{12,4},{1,9},{5,13},{9,1},{13,5},{2,10},{6,14},... | collective-permute-start | bytes 393224 | tf_op jit(solution)/shard_map/ppermute | solution.py:157
  68.6 1.8 %shard_map.138.refs_4_ = bf16[128,896]{1,0:T(8,128)(2,1)S(1)} custom-call(s32[2]{0:T(128)S(1)} %pad_add_fusion.place_ref, bf16[5,32,1024]{2,1,0:T(8,128)(2,1)S(1)} %get-tuple-element.56.refs_6_.refs_0_, bf16[5,32,1024]{2,1,0:T(8,128)(2,1)S(1)} %collective-permute-done.16.refs_1_, bf16[5,32,1024]{2,1,0:T(8,128)(2,1)S(1)} %collective-permute-done.17.refs_2_, ...), custom_call_target="tpu_custom_call" | custom-call | flops 469762048 | bytes 6287360 | tf_op jit(solution)/shard_map/pallas_call | solution.py:195
  70.4 4.1 %collective-permute-start.28 = (bf16[128,896]{1,0:T(8,128)(2,1)S(1)}, bf16[128,896]{1,0:T(8,128)(2,1)S(1)}, u32[]{:S(2)}, u32[]{:S(2)}) collective-permute-start(bf16[128,896]{1,0:T(8,128)(2,1)S(1)} %shard_map.138.refs_4_), channel_id=1, source_target_pairs={{0,1},{1,3},{3,2},{2,0},{4,5},{5,7},{7,6},{6,4},{8,9},{9,11},{11,1... | collective-permute-start | bytes 688136 | tf_op jit(solution)/shard_map/ppermute | solution.py:170
  76.4 1.6 %collective-permute-start.27 = (bf16[2,32,1024]{2,1,0:T(8,128)(2,1)S(1)}, bf16[2,32,1024]{2,1,0:T(8,128)(2,1)S(1)}, u32[]{:S(2)}, u32[]{:S(2)}) collective-permute-start(bf16[2,32,1024]{2,1,0:T(8,128)(2,1)S(1)} %shard_map.139.refs_7_.refs_0_), channel_id=1, source_target_pairs={{0,12},{4,8},{8,4},{12,0},{1,13},{5,9},{9,5},{13,1},{2,14},{6,10},... | collective-permute-start | bytes 393224 | tf_op jit(solution)/shard_map/ppermute | solution.py:157
  80.0 1.8 %shard_map.141.refs_7_ = bf16[128,896]{1,0:T(8,128)(2,1)S(1)} custom-call(s32[2]{0:T(128)S(1)} %pad_add_fusion.place_ref, bf16[2,32,1024]{2,1,0:T(8,128)(2,1)S(1)} %shard_map.136.refs_6_.refs_0_, bf16[2,32,1024]{2,1,0:T(8,128)(2,1)S(1)} %collective-permute-done.19.refs_5_.refs_1_, bf16[2,32,1024]{2,1,0:T(8,128)(2,1)S(1)} %collective-permute-done.20.refs_6_.refs_2_, ...), custom_call_target="tpu_custom_call" | custom-call | flops 469762048 | bytes 5730304 | tf_op jit(solution)/shard_map/pallas_call | solution.py:195
  81.8 1.2 %collective-permute-start.30 = (bf16[128,896]{1,0:T(8,128)(2,1)S(1)}, bf16[128,896]{1,0:T(8,128)(2,1)S(1)}, u32[]{:S(2)}, u32[]{:S(2)}) collective-permute-start(bf16[128,896]{1,0:T(8,128)(2,1)S(1)} %shard_map.141.refs_7_), channel_id=1, source_target_pairs={{0,17},{1,19},{3,18},{2,16},{16,1},{17,3},{19,2},{18,0},{4,21},{5,... | collective-permute-start | bytes 688136 | tf_op jit(solution)/shard_map/ppermute | solution.py:180
  83.0 3.5 %collective-permute-done.26.refs_2_ = bf16[2,32,1024]{2,1,0:T(8,128)(2,1)S(1)} collective-permute-done((bf16[2,32,1024]{2,1,0:T(8,128)(2,1)S(1)}, bf16[2,32,1024]{2,1,0:T(8,128)(2,1)S(1)}, u32[]{:S(2)}, u32[]{:S(2)}) %collective-permute-start.26) | collective-permute-done | bytes 131104 | tf_op jit(solution)/shard_map/ppermute | solution.py:157
  87.7 1.8 %shard_map.143.refs_2_ = bf16[128,896]{1,0:T(8,128)(2,1)S(1)} custom-call(s32[2]{0:T(128)S(1)} %pad_add_fusion.place_ref, bf16[2,32,1024]{2,1,0:T(8,128)(2,1)S(1)} %shard_map.139.refs_7_.refs_0_, bf16[2,32,1024]{2,1,0:T(8,128)(2,1)S(1)} %collective-permute-done.25.refs_1_, bf16[2,32,1024]{2,1,0:T(8,128)(2,1)S(1)} %collective-permute-done.26.refs_2_, ...), custom_call_target="tpu_custom_call" | custom-call | flops 469762048 | bytes 5730304 | tf_op jit(solution)/shard_map/pallas_call | solution.py:195
  (87 shorter events, 23.9 us)
Async XLA Ops:
  1.7 14.1 %collective-permute-start = (bf16[144,896]{1,0:T(8,128)(2,1)S(1)}, bf16[144,896]{1,0:T(8,128)(2,1)S(1)}, u32[]{:S(2)}, u32[]{:S(2)}) collective-permute-start(bf16[144,896]{1,0:T(8,128)(2,1)S(1)} %shard_map.123.refs_0_.refs_2_.refs_5_.refs_8_), channel_id=1, source_target_pairs={{0,1},{1,3},{3,2},{2,0},{4,5},{5,7},{7,6},{6,4},{8,9},{9,11},{11,1... | collective-permute-start | bytes 774152 | tf_op jit(solution)/shard_map/ppermute | solution.py:170
  4.7 12.1 %collective-permute-start.1 = (bf16[128,896]{1,0:T(8,128)(2,1)S(1)}, bf16[128,896]{1,0:T(8,128)(2,1)S(1)}, u32[]{:S(2)}, u32[]{:S(2)}) collective-permute-start(bf16[128,896]{1,0:T(8,128)(2,1)S(1)} %bitcast.58), channel_id=1, source_target_pairs={{0,1},{1,3},{3,2},{2,0},{4,5},{5,7},{7,6},{6,4},{8,9},{9,11},{11,1... | collective-permute-start | bytes 688136 | tf_op jit(solution)/shard_map/ppermute | solution.py:170
  12.3 8.5 %collective-permute-start.7 = (bf16[3,32,1024]{2,1,0:T(8,128)(2,1)S(1)}, bf16[3,32,1024]{2,1,0:T(8,128)(2,1)S(1)}, u32[]{:S(2)}, u32[]{:S(2)}) collective-permute-start(bf16[3,32,1024]{2,1,0:T(8,128)(2,1)S(1)} %get-tuple-element.39), channel_id=1, source_target_pairs={{0,4},{4,0},{8,12},{12,8},{1,5},{5,1},{9,13},{13,9},{2,6},{6,2},{1... | collective-permute-start | bytes 589832 | tf_op jit(solution)/shard_map/ppermute | solution.py:157
  13.8 9.4 %collective-permute-start.8 = (bf16[3,32,1024]{2,1,0:T(8,128)(2,1)S(1)}, bf16[3,32,1024]{2,1,0:T(8,128)(2,1)S(1)}, u32[]{:S(2)}, u32[]{:S(2)}) collective-permute-start(bf16[3,32,1024]{2,1,0:T(8,128)(2,1)S(1)} %get-tuple-element.40), channel_id=1, source_target_pairs={{0,8},{4,12},{8,0},{12,4},{1,9},{5,13},{9,1},{13,5},{2,10},{6,14},... | collective-permute-start | bytes 589832 | tf_op jit(solution)/shard_map/ppermute | solution.py:157
  15.3 10.6 %collective-permute-start.9 = (bf16[3,32,1024]{2,1,0:T(8,128)(2,1)S(1)}, bf16[3,32,1024]{2,1,0:T(8,128)(2,1)S(1)}, u32[]{:S(2)}, u32[]{:S(2)}) collective-permute-start(bf16[3,32,1024]{2,1,0:T(8,128)(2,1)S(1)} %get-tuple-element.41), channel_id=1, source_target_pairs={{0,12},{4,8},{8,4},{12,0},{1,13},{5,9},{9,5},{13,1},{2,14},{6,10},... | collective-permute-start | bytes 589832 | tf_op jit(solution)/shard_map/ppermute | solution.py:157
  15.8 10.8 %collective-permute-start.5 = (bf16[144,896]{1,0:T(8,128)(2,1)S(1)}, bf16[144,896]{1,0:T(8,128)(2,1)S(1)}, u32[]{:S(2)}, u32[]{:S(2)}) collective-permute-start(bf16[144,896]{1,0:T(8,128)(2,1)S(1)} %collective-permute-done.refs_0_.refs_2_.refs_5_.refs_8_), channel_id=1, source_target_pairs={{0,1},{1,3},{3,2},{2,0},{4,5},{5,7},{7,6},{6,4},{8,9},{9,11},{11,1... | collective-permute-start | bytes 774152 | tf_op jit(solution)/shard_map/ppermute | solution.py:170
  16.9 12.9 %collective-permute-start.6 = (bf16[128,896]{1,0:T(8,128)(2,1)S(1)}, bf16[128,896]{1,0:T(8,128)(2,1)S(1)}, u32[]{:S(2)}, u32[]{:S(2)}) collective-permute-start(bf16[128,896]{1,0:T(8,128)(2,1)S(1)} %collective-permute-done.1.refs_1_), channel_id=1, source_target_pairs={{0,1},{1,3},{3,2},{2,0},{4,5},{5,7},{7,6},{6,4},{8,9},{9,11},{11,1... | collective-permute-start | bytes 688136 | tf_op jit(solution)/shard_map/ppermute | solution.py:170
  20.7 12.0 %collective-permute-start.2 = (bf16[3,32,1024]{2,1,0:T(8,128)(2,1)S(1)}, bf16[3,32,1024]{2,1,0:T(8,128)(2,1)S(1)}, u32[]{:S(2)}, u32[]{:S(2)}) collective-permute-start(bf16[3,32,1024]{2,1,0:T(8,128)(2,1)S(1)} %get-tuple-element.36), channel_id=1, source_target_pairs={{0,4},{4,0},{8,12},{12,8},{1,5},{5,1},{9,13},{13,9},{2,6},{6,2},{1... | collective-permute-start | bytes 589832 | tf_op jit(solution)/shard_map/ppermute | solution.py:157
  23.2 9.9 %collective-permute-start.3 = (bf16[3,32,1024]{2,1,0:T(8,128)(2,1)S(1)}, bf16[3,32,1024]{2,1,0:T(8,128)(2,1)S(1)}, u32[]{:S(2)}, u32[]{:S(2)}) collective-permute-start(bf16[3,32,1024]{2,1,0:T(8,128)(2,1)S(1)} %get-tuple-element.37), channel_id=1, source_target_pairs={{0,8},{4,12},{8,0},{12,4},{1,9},{5,13},{9,1},{13,5},{2,10},{6,14},... | collective-permute-start | bytes 589832 | tf_op jit(solution)/shard_map/ppermute | solution.py:157
  25.9 7.1 %collective-permute-start.4 = (bf16[3,32,1024]{2,1,0:T(8,128)(2,1)S(1)}, bf16[3,32,1024]{2,1,0:T(8,128)(2,1)S(1)}, u32[]{:S(2)}, u32[]{:S(2)}) collective-permute-start(bf16[3,32,1024]{2,1,0:T(8,128)(2,1)S(1)} %get-tuple-element.38), channel_id=1, source_target_pairs={{0,12},{4,8},{8,4},{12,0},{1,13},{5,9},{9,5},{13,1},{2,14},{6,10},... | collective-permute-start | bytes 589832 | tf_op jit(solution)/shard_map/ppermute | solution.py:157
  26.6 17.8 %collective-permute-start.13 = (bf16[144,896]{1,0:T(8,128)(2,1)S(1)}, bf16[144,896]{1,0:T(8,128)(2,1)S(1)}, u32[]{:S(2)}, u32[]{:S(2)}) collective-permute-start(bf16[144,896]{1,0:T(8,128)(2,1)S(1)} %collective-permute-done.5.refs_0_.refs_2_.refs_5_.refs_8_), channel_id=1, source_target_pairs={{0,1},{1,3},{3,2},{2,0},{4,5},{5,7},{7,6},{6,4},{8,9},{9,11},{11,1... | collective-permute-start | bytes 774152 | tf_op jit(solution)/shard_map/ppermute | solution.py:170
  33.7 13.6 %collective-permute-start.10 = (bf16[5,32,1024]{2,1,0:T(8,128)(2,1)S(1)}, bf16[5,32,1024]{2,1,0:T(8,128)(2,1)S(1)}, u32[]{:S(2)}, u32[]{:S(2)}) collective-permute-start(bf16[5,32,1024]{2,1,0:T(8,128)(2,1)S(1)} %get-tuple-element.48), channel_id=1, source_target_pairs={{0,4},{4,0},{8,12},{12,8},{1,5},{5,1},{9,13},{13,9},{2,6},{6,2},{1... | collective-permute-start | bytes 983048 | tf_op jit(solution)/shard_map/ppermute | solution.py:157
  35.9 14.1 %collective-permute-start.11 = (bf16[5,32,1024]{2,1,0:T(8,128)(2,1)S(1)}, bf16[5,32,1024]{2,1,0:T(8,128)(2,1)S(1)}, u32[]{:S(2)}, u32[]{:S(2)}) collective-permute-start(bf16[5,32,1024]{2,1,0:T(8,128)(2,1)S(1)} %get-tuple-element.49), channel_id=1, source_target_pairs={{0,8},{4,12},{8,0},{12,4},{1,9},{5,13},{9,1},{13,5},{2,10},{6,14},... | collective-permute-start | bytes 983048 | tf_op jit(solution)/shard_map/ppermute | solution.py:157
  37.5 12.6 %collective-permute-start.12 = (bf16[5,32,1024]{2,1,0:T(8,128)(2,1)S(1)}, bf16[5,32,1024]{2,1,0:T(8,128)(2,1)S(1)}, u32[]{:S(2)}, u32[]{:S(2)}) collective-permute-start(bf16[5,32,1024]{2,1,0:T(8,128)(2,1)S(1)} %get-tuple-element.50), channel_id=1, source_target_pairs={{0,12},{4,8},{8,4},{12,0},{1,13},{5,9},{9,5},{13,1},{2,14},{6,10},... | collective-permute-start | bytes 983048 | tf_op jit(solution)/shard_map/ppermute | solution.py:157
  37.5 6.9 %collective-permute-start.14 = (bf16[128,896]{1,0:T(8,128)(2,1)S(1)}, bf16[128,896]{1,0:T(8,128)(2,1)S(1)}, u32[]{:S(2)}, u32[]{:S(2)}) collective-permute-start(bf16[128,896]{1,0:T(8,128)(2,1)S(1)} %collective-permute-done.6.refs_1_), channel_id=1, source_target_pairs={{0,1},{1,3},{3,2},{2,0},{4,5},{5,7},{7,6},{6,4},{8,9},{9,11},{11,1... | collective-permute-start | bytes 688136 | tf_op jit(solution)/shard_map/ppermute | solution.py:170
  50.7 10.5 %collective-permute-start.16 = (bf16[5,32,1024]{2,1,0:T(8,128)(2,1)S(1)}, bf16[5,32,1024]{2,1,0:T(8,128)(2,1)S(1)}, u32[]{:S(2)}, u32[]{:S(2)}) collective-permute-start(bf16[5,32,1024]{2,1,0:T(8,128)(2,1)S(1)} %get-tuple-element.57), channel_id=1, source_target_pairs={{0,4},{4,0},{8,12},{12,8},{1,5},{5,1},{9,13},{13,9},{2,6},{6,2},{1... | collective-permute-start | bytes 983048 | tf_op jit(solution)/shard_map/ppermute | solution.py:157
  50.8 12.0 %collective-permute-start.17 = (bf16[5,32,1024]{2,1,0:T(8,128)(2,1)S(1)}, bf16[5,32,1024]{2,1,0:T(8,128)(2,1)S(1)}, u32[]{:S(2)}, u32[]{:S(2)}) collective-permute-start(bf16[5,32,1024]{2,1,0:T(8,128)(2,1)S(1)} %get-tuple-element.58), channel_id=1, source_target_pairs={{0,8},{4,12},{8,0},{12,4},{1,9},{5,13},{9,1},{13,5},{2,10},{6,14},... | collective-permute-start | bytes 983048 | tf_op jit(solution)/shard_map/ppermute | solution.py:157
  53.1 9.8 %collective-permute-start.18 = (bf16[5,32,1024]{2,1,0:T(8,128)(2,1)S(1)}, bf16[5,32,1024]{2,1,0:T(8,128)(2,1)S(1)}, u32[]{:S(2)}, u32[]{:S(2)}) collective-permute-start(bf16[5,32,1024]{2,1,0:T(8,128)(2,1)S(1)} %get-tuple-element.59), channel_id=1, source_target_pairs={{0,12},{4,8},{8,4},{12,0},{1,13},{5,9},{9,5},{13,1},{2,14},{6,10},... | collective-permute-start | bytes 983048 | tf_op jit(solution)/shard_map/ppermute | solution.py:157
  57.1 10.7 %collective-permute-start.23 = (bf16[128,896]{1,0:T(8,128)(2,1)S(1)}, bf16[128,896]{1,0:T(8,128)(2,1)S(1)}, u32[]{:S(2)}, u32[]{:S(2)}) collective-permute-start(bf16[128,896]{1,0:T(8,128)(2,1)S(1)} %shard_map.133.refs_3_), channel_id=1, source_target_pairs={{0,18},{1,16},{3,17},{2,19},{16,2},{17,0},{19,1},{18,3},{4,22},{5,... | collective-permute-start | bytes 688136 | tf_op jit(solution)/shard_map/ppermute | solution.py:180
  57.1 11.4 %collective-permute-start.15 = (bf16[128,896]{1,0:T(8,128)(2,1)S(1)}, bf16[128,896]{1,0:T(8,128)(2,1)S(1)}, u32[]{:S(2)}, u32[]{:S(2)}) collective-permute-start(bf16[128,896]{1,0:T(8,128)(2,1)S(1)} %shard_map.132.refs_9_), channel_id=1, source_target_pairs={{0,18},{1,16},{3,17},{2,19},{16,2},{17,0},{19,1},{18,3},{4,22},{5,... | collective-permute-start | bytes 688136 | tf_op jit(solution)/shard_map/ppermute | solution.py:180
  64.5 10.6 %collective-permute-start.22 = (bf16[128,896]{1,0:T(8,128)(2,1)S(1)}, bf16[128,896]{1,0:T(8,128)(2,1)S(1)}, u32[]{:S(2)}, u32[]{:S(2)}) collective-permute-start(bf16[128,896]{1,0:T(8,128)(2,1)S(1)} %shard_map.137.refs_9_), channel_id=1, source_target_pairs={{0,1},{1,3},{3,2},{2,0},{4,5},{5,7},{7,6},{6,4},{8,9},{9,11},{11,1... | collective-permute-start | bytes 688136 | tf_op jit(solution)/shard_map/ppermute | solution.py:170
  65.1 9.4 %collective-permute-start.21 = (bf16[2,32,1024]{2,1,0:T(8,128)(2,1)S(1)}, bf16[2,32,1024]{2,1,0:T(8,128)(2,1)S(1)}, u32[]{:S(2)}, u32[]{:S(2)}) collective-permute-start(bf16[2,32,1024]{2,1,0:T(8,128)(2,1)S(1)} %shard_map.136.refs_6_.refs_0_), channel_id=1, source_target_pairs={{0,12},{4,8},{8,4},{12,0},{1,13},{5,9},{9,5},{13,1},{2,14},{6,10},... | collective-permute-start | bytes 393224 | tf_op jit(solution)/shard_map/ppermute | solution.py:157
  66.3 8.1 %collective-permute-start.20 = (bf16[2,32,1024]{2,1,0:T(8,128)(2,1)S(1)}, bf16[2,32,1024]{2,1,0:T(8,128)(2,1)S(1)}, u32[]{:S(2)}, u32[]{:S(2)}) collective-permute-start(bf16[2,32,1024]{2,1,0:T(8,128)(2,1)S(1)} %shard_map.136.refs_6_.refs_0_), channel_id=1, source_target_pairs={{0,8},{4,12},{8,0},{12,4},{1,9},{5,13},{9,1},{13,5},{2,10},{6,14},... | collective-permute-start | bytes 393224 | tf_op jit(solution)/shard_map/ppermute | solution.py:157
  67.8 6.7 %collective-permute-start.19 = (bf16[2,32,1024]{2,1,0:T(8,128)(2,1)S(1)}, bf16[2,32,1024]{2,1,0:T(8,128)(2,1)S(1)}, u32[]{:S(2)}, u32[]{:S(2)}) collective-permute-start(bf16[2,32,1024]{2,1,0:T(8,128)(2,1)S(1)} %shard_map.136.refs_6_.refs_0_), channel_id=1, source_target_pairs={{0,4},{4,0},{8,12},{12,8},{1,5},{5,1},{9,13},{13,9},{2,6},{6,2},{1... | collective-permute-start | bytes 393224 | tf_op jit(solution)/shard_map/ppermute | solution.py:157
  70.4 9.6 %collective-permute-start.28 = (bf16[128,896]{1,0:T(8,128)(2,1)S(1)}, bf16[128,896]{1,0:T(8,128)(2,1)S(1)}, u32[]{:S(2)}, u32[]{:S(2)}) collective-permute-start(bf16[128,896]{1,0:T(8,128)(2,1)S(1)} %shard_map.138.refs_4_), channel_id=1, source_target_pairs={{0,1},{1,3},{3,2},{2,0},{4,5},{5,7},{7,6},{6,4},{8,9},{9,11},{11,1... | collective-permute-start | bytes 688136 | tf_op jit(solution)/shard_map/ppermute | solution.py:170
  76.2 13.8 %collective-permute-start.24 = (bf16[128,896]{1,0:T(8,128)(2,1)S(1)}, bf16[128,896]{1,0:T(8,128)(2,1)S(1)}, u32[]{:S(2)}, u32[]{:S(2)}) collective-permute-start(bf16[128,896]{1,0:T(8,128)(2,1)S(1)} %shard_map.140.refs_10_), channel_id=1, source_target_pairs={{0,17},{1,19},{3,18},{2,16},{16,1},{17,3},{19,2},{18,0},{4,21},{5,... | collective-permute-start | bytes 688136 | tf_op jit(solution)/shard_map/ppermute | solution.py:180
  76.4 6.6 %collective-permute-start.27 = (bf16[2,32,1024]{2,1,0:T(8,128)(2,1)S(1)}, bf16[2,32,1024]{2,1,0:T(8,128)(2,1)S(1)}, u32[]{:S(2)}, u32[]{:S(2)}) collective-permute-start(bf16[2,32,1024]{2,1,0:T(8,128)(2,1)S(1)} %shard_map.139.refs_7_.refs_0_), channel_id=1, source_target_pairs={{0,12},{4,8},{8,4},{12,0},{1,13},{5,9},{9,5},{13,1},{2,14},{6,10},... | collective-permute-start | bytes 393224 | tf_op jit(solution)/shard_map/ppermute | solution.py:157
  78.0 8.5 %collective-permute-start.26 = (bf16[2,32,1024]{2,1,0:T(8,128)(2,1)S(1)}, bf16[2,32,1024]{2,1,0:T(8,128)(2,1)S(1)}, u32[]{:S(2)}, u32[]{:S(2)}) collective-permute-start(bf16[2,32,1024]{2,1,0:T(8,128)(2,1)S(1)} %shard_map.139.refs_7_.refs_0_), channel_id=1, source_target_pairs={{0,8},{4,12},{8,0},{12,4},{1,9},{5,13},{9,1},{13,5},{2,10},{6,14},... | collective-permute-start | bytes 393224 | tf_op jit(solution)/shard_map/ppermute | solution.py:157
  79.1 7.4 %collective-permute-start.25 = (bf16[2,32,1024]{2,1,0:T(8,128)(2,1)S(1)}, bf16[2,32,1024]{2,1,0:T(8,128)(2,1)S(1)}, u32[]{:S(2)}, u32[]{:S(2)}) collective-permute-start(bf16[2,32,1024]{2,1,0:T(8,128)(2,1)S(1)} %shard_map.139.refs_7_.refs_0_), channel_id=1, source_target_pairs={{0,4},{4,0},{8,12},{12,8},{1,5},{5,1},{9,13},{13,9},{2,6},{6,2},{1... | collective-permute-start | bytes 393224 | tf_op jit(solution)/shard_map/ppermute | solution.py:157
  81.8 8.3 %collective-permute-start.30 = (bf16[128,896]{1,0:T(8,128)(2,1)S(1)}, bf16[128,896]{1,0:T(8,128)(2,1)S(1)}, u32[]{:S(2)}, u32[]{:S(2)}) collective-permute-start(bf16[128,896]{1,0:T(8,128)(2,1)S(1)} %shard_map.141.refs_7_), channel_id=1, source_target_pairs={{0,17},{1,19},{3,18},{2,16},{16,1},{17,3},{19,2},{18,0},{4,21},{5,... | collective-permute-start | bytes 688136 | tf_op jit(solution)/shard_map/ppermute | solution.py:180
  87.5 2.5 %collective-permute-start.29 = (bf16[128,896]{1,0:T(8,128)(2,1)S(1)}, bf16[128,896]{1,0:T(8,128)(2,1)S(1)}, u32[]{:S(2)}, u32[]{:S(2)}) collective-permute-start(bf16[128,896]{1,0:T(8,128)(2,1)S(1)} %shard_map.142.refs_10_), channel_id=1, source_target_pairs={{0,16},{16,0},{1,17},{17,1},{2,18},{18,2},{3,19},{19,3},{4,20},{20... | collective-permute-start | bytes 688136 | tf_op jit(solution)/shard_map/ppermute | solution.py:14
  89.6 1.6 %collective-permute-start.31 = (bf16[128,896]{1,0:T(8,128)(2,1)S(1)}, bf16[128,896]{1,0:T(8,128)(2,1)S(1)}, u32[]{:S(2)}, u32[]{:S(2)}) collective-permute-start(bf16[128,896]{1,0:T(8,128)(2,1)S(1)} %shard_map.143.refs_2_), channel_id=1, source_target_pairs={{0,16},{16,0},{1,17},{17,1},{2,18},{18,2},{3,19},{19,3},{4,20},{20... | collective-permute-start | bytes 688136 | tf_op jit(solution)/shard_map/ppermute | solution.py:14
  (14 other events, 42.0 us)

commit v7 on v6

--- a/solution.py
+++ b/solution.py
@@ -216,7 +216,7 @@
 
 
 def first_products(place, token_rows, grad_rows, weights, nodes, planes, after):
-    (count, width), hidden = grad_rows.shape, weights[0].shape[1]
+    (count, width), hidden = token_rows.shape, weights[0].shape[1]
     share = count // nodes
 
     def body(place_ref, token_ref, grad_ref, gate_ref, up_ref, down_ref, *refs):
@@ -243,39 +243,50 @@
     )
 
 
-def activations(place, pieces, filled, after):
+def activations(place, pieces, filled, after, extra=()):
     nodes, (_, share, hidden) = len(pieces), pieces[0].shape
 
     def body(place_ref, *refs):
-        piece_refs, outs = refs[:nodes], refs[nodes + len(filled) :]
+        piece_refs, extra_refs = refs[:nodes], refs[nodes + len(filled) :][: len(extra)]
+        outs = refs[nodes + len(filled) + len(extra) :]
         gate, up, grad = (
             sum(ref[index].astype(jnp.float32) for ref in piece_refs) for index in range(3)
         )
         act = (gate / (1.0 + jnp.exp(-gate)) * up).astype(jnp.bfloat16)
         grad = grad.astype(jnp.bfloat16)
         for out in outs:
-            planes = out.shape[0]
-            out[planes - 2] = act
-            out[planes - 1] = grad
+            start = 3 if filled else 0
+            out[start] = act
+            out[start + 1] = grad
+            for index, ref in enumerate(extra_refs):
+                out[start + 2 + index] = ref[1]
 
     shapes = [jax.ShapeDtypeStruct(array.shape, array.dtype) for array in filled]
     return call(
         body,
         place,
-        (*pieces, *filled),
+        (*pieces, *filled, *extra),
         after,
-        shapes or [jax.ShapeDtypeStruct((2, share, hidden), jnp.bfloat16)],
+        shapes or [jax.ShapeDtypeStruct((2 + len(extra), share, hidden), jnp.bfloat16)],
         [],
         16 * share * hidden,
         {nodes + index: index for index in range(len(filled))},
     )
 
 
+def first_plane(place, planes, after):
+    def body(place_ref, planes_ref, out):
+        out[0] = planes_ref[0]
+
+    shape = (1, *planes.shape[1:])
+    return call(body, place, (planes,), after, jax.ShapeDtypeStruct(shape, planes.dtype), [], 0)
+
+
 def join(place_ref, piece_refs, index, joined):
-    planes, rows, _ = piece_refs[0].shape
+    rows = piece_refs[0].shape[1]
     for mask, ref in enumerate(piece_refs):
         first = pl.multiple_of((place_ref[0] ^ mask) * rows, rows)
-        joined[pl.ds(first, rows), :] = ref[planes - 2 + index]
+        joined[pl.ds(first, rows), :] = ref[index]
 
 
 def copied(sources, targets, sems):
@@ -422,14 +433,14 @@
     out[...] = total.astype(jnp.bfloat16)
 
 
-def forward_results(place, pieces, w_down, info, chosen, added, after):
+def forward_results(place, pieces, plane, w_down, info, chosen, added, after):
     nodes, (_, share, hidden), width = len(pieces), pieces[0].shape, w_down.shape[1]
     count = share * nodes
 
     def body(place_ref, *refs):
         piece_refs, refs = refs[:nodes], refs[nodes:]
         (down_ref, info_ref), added_refs, (out, joined) = refs[:2], refs[2:-2], refs[-2:]
-        join(place_ref, piece_refs, 0, joined)
+        join(place_ref, piece_refs, plane, joined)
         weight = weight_column(place_ref[1], *info_of(info_ref, count, chosen, 0))
         give(out, weight, matmul(joined[...], down_ref[...]), added_refs)
 
@@ -469,7 +480,7 @@
     )
 
 
-def backward_results(place, pieces, w_gate, w_up, factors, info, chosen, added, after):
+def backward_results(place, pieces, plane, w_gate, w_up, factors, info, chosen, added, after):
     nodes, (_, share, hidden), width = len(pieces), pieces[0].shape, w_gate.shape[0]
     count = share * nodes
 
@@ -477,7 +488,7 @@
         piece_refs, refs = refs[:nodes], refs[nodes:]
         gate_ref, up_ref, gate_factor, up_factor, info_ref = refs[:5]
         added_refs, (out, joined) = refs[5:-2], refs[-2:]
-        join(place_ref, piece_refs, 1, joined)
+        join(place_ref, piece_refs, plane, joined)
         weight = weight_column(place_ref[1], *info_of(info_ref, count, chosen, 1))
         grad_hidden = joined[...].astype(jnp.float32)
         grad_gate = (grad_hidden * gate_factor[...]).astype(jnp.bfloat16)
@@ -533,21 +544,22 @@
     stored_gate, stored_up = saved_gate[0, 0], saved_up[0, 0]
 
     chosen = routes_forward.shape[2]
-    tokens = [
+    tokens = [inputs_forward[0]]
+    grads = [
         with_info(
-            inputs_forward[0],
+            grads_backward[0],
             (routes_forward[0].T, routes_backward[0].T),
             (gates_forward[0].T, gates_backward[0].T),
             (marker(),),
         )
     ]
-    grads = [grads_backward[0]]
     for _ in range(1, experts):
         tokens.append(along_ring(tokens[-1], 1))
         grads.append(along_ring(grads[-1], 1))
 
     count = grads_backward.shape[1]
-    sent, parts, acts = [None] * experts, [None] * experts, [None] * experts
+    sent, parts = [None] * experts, [None] * experts
+    acts = [None] * experts, [None] * experts
     done = []
 
     def exchange(own):
@@ -557,7 +569,7 @@
 
     def prepare(step):
         factors[step] = backward_factors(
-            place, stored_gate, stored_up, tokens[step], chosen, count, step, done[-1:]
+            place, stored_gate, stored_up, grads[step], chosen, count, step, done[-1:]
         )
         done.append(factors[step][0])
 
@@ -571,13 +583,18 @@
 
     def middle(step, *after):
         joint = 0 < step < experts - 1
-        own = activations(place, parts[step], sent[step + 1] if joint else (), (*done[-1:], *after))
+        filled, extra = (sent[step + 1], ()) if joint else ((), (own_acts,))
+        own = activations(place, parts[step], filled, (*done[-1:], *after), extra)
         done.append(own[0])
-        acts[step] = exchange(own)
+        arrived = exchange(own)
+        plane = 3 if joint else 0
+        acts[0][step], acts[1][step] = (arrived, plane), (arrived, plane + 1)
         if joint:
-            parts[step + 1] = acts[step]
-
-    sums, hops = [[], []], [(), ()]
+            parts[step + 1] = arrived
+        else:
+            acts[1][0] = (arrived, plane + 2)
+
+    sums, hops, base = [[], []], [(), ()], [None, None]
 
     def last(step, kind, *after):
         shift = 1 - 2 * kind
@@ -586,15 +603,15 @@
             added = hops[kind]
         if kind == 0:
             value = forward_results(
-                place, acts[step], weights[2], tokens[step], chosen, added, (*done[-1:], *after)
+                place, *acts[0][step], weights[2], grads[step], chosen, added, (*done[-1:], *after)
             )
         else:
             value = backward_results(
-                place, acts[step], *weights[:2], factors[step], tokens[step], chosen, added, (*done[-1:], *after)
+                place, *acts[1][step], *weights[:2], factors[step], grads[step], chosen, added, (*done[-1:], *after)
             )
         done.append(value)
         if step == 0:
-            sums[kind].append(from_behind(value, "section", shift))
+            base[kind] = from_behind(value, "section", shift)
         elif step == 1:
             sums[kind].append(along_ring_and_sections(value, -1, shift))
         elif step < experts - 1:
@@ -604,8 +621,10 @@
 
     first(0)
     first(1)
+    own_acts = activations(place, parts[0], (), done[-1:])[0]
+    done.append(own_acts)
     for step in range(1, experts - 1):
-        first(step + 1, *(parts[0][1:] if step == 1 else ()))
+        first(step + 1)
         prepare(step)
         middle(step)
         if step >= 2:
@@ -617,13 +636,16 @@
     if experts > 2:
         last(experts - 2, 0)
         last(experts - 2, 1, *[values[0] for values in sums if values])
-    middle(0, *acts[experts - 1][1:])
-    for step in (experts - 1, 0):
-        last(step, 0)
-        last(step, 1)
+    last(experts - 1, 0)
+    own_plane = first_plane(place, own_acts, (*done[-1:], *acts[0][experts - 1][0][1:]))
+    done.append(own_plane)
+    acts[0][0] = (exchange([own_plane]), 0)
+    last(experts - 1, 1)
+    last(0, 1)
+    last(0, 0)
     outs = []
-    for values in sums:
-        total = sum_rows(values[:-1], (*done[-1:], *outs)) + values[-1].astype(jnp.float32)
+    for values, own in zip(sums, base):
+        total = sum_rows(values, (*done[-1:], *outs)) + own.astype(jnp.float32)
         outs.append(total.astype(jnp.bfloat16))
     return tuple(out[None] for out in outs)
 

time: 92.1 us -> 91.3 us (level)
  waiting for transfers between devices: 17.9 us -> 14.4 us
  starting transfers between devices: 41.6 us -> 43.9 us
    ppermute x18, waiting for transfers between devices: 8.96 us -> 5.78 us  [across(): lax.ppermute(value, axis, [(source, source ^ mask) for source in range(co...]
    ppermute x4, starting transfers between devices: 3.36 us -> 4.77 us  [along_ring_and_sections(): return lax.ppermute(value, ('section', 'dev'), pairs)]
    ppermute x8, waiting for transfers between devices: 8.61 us -> 7.21 us  [along_ring(): return lax.ppermute(value, 'dev', ring_pairs(lax.axis_size('dev'), steps))]
    ppermute x2, waiting for transfers between devices: 0.36 us -> 1.4 us  [from_behind(): return lax.ppermute(value, axis, pairs)]
    pallas_call x20 -> x21, Pallas kernels: 25.7 us -> 26.3 us  [call(): pl.pallas_call(with_after, in_specs=[SMEM] + [VMEM] * len(operands) + [AN...]
  transfers between devices with their start and end apart: 32 -> 32, of which waited for: 9 -> 9; matrix products, arithmetic and copies ran while one was open for 0% -> 0% of each run, Pallas kernels for 27% -> 28%
where the time goes in v7:
time: 91.3 us; the launch traced here: 91.1 us
  starting transfers between devices  43.9 us (48%)
  Pallas kernels  26.4 us (29%)
  waiting for transfers between devices  14.4 us (16%)
  local copies, waits for them, and re-layouts  4.55 us (5%)
  between operations  1.02 us (1%)
    pallas_call x21, Pallas kernels, call(): pl.pallas_call(with_after, in_specs=[SMEM] + [VMEM] * len(operands) + [AN...  26.3 us
    ppermute x18, starting transfers between devices, across(): lax.ppermute(value, axis, [(source, source ^ mask) for source in range(co...  22.7 us
    ppermute x8, starting transfers between devices, along_ring(): return lax.ppermute(value, 'dev', ring_pairs(lax.axis_size('dev'), steps))  15.1 us
    ppermute x8, waiting for transfers between devices, along_ring(): return lax.ppermute(value, 'dev', ring_pairs(lax.axis_size('dev'), steps))  7.21 us
    ppermute x18, waiting for transfers between devices, across(): lax.ppermute(value, axis, [(source, source ^ mask) for source in range(co...  5.78 us
    ppermute x4, starting transfers between devices, along_ring_and_sections(): return lax.ppermute(value, ('section', 'dev'), pairs)  4.77 us
    unnamed x28, local copies, waits for them, and re-layouts  4.55 us
  transfers between devices with their start and end apart: 32, of which 9 were waited for; matrix products, arithmetic and copies ran while one was open for 0% of the time, Pallas kernels for 28%

profile of v7, /device:TPU:0, one launch (start us, length us, event | category | flops | bytes accessed | tf_op | source)
XLA Modules:
  0.0 91.1 jit_solution(10645059664749951181)
XLA Ops:
  1.6 3.1 %collective-permute-start.1 = (bf16[144,896]{1,0:T(8,128)(2,1)S(1)}, bf16[144,896]{1,0:T(8,128)(2,1)S(1)}, u32[]{:S(2)}, u32[]{:S(2)}) collective-permute-start(bf16[144,896]{1,0:T(8,128)(2,1)S(1)} %shard_map.123.refs_1_.refs_2_.refs_8_.refs_5_), channel_id=1, source_target_pairs={{0,1},{1,3},{3,2},{2,0},{4,5},{5,7},{7,6},{6,4},{8,9},{9,11},{11,1... | collective-permute-start | bytes 774152 | tf_op jit(solution)/shard_map/ppermute | solution.py:170
  4.7 2.6 %collective-permute-start = (bf16[128,896]{1,0:T(8,128)(2,1)S(1)}, bf16[128,896]{1,0:T(8,128)(2,1)S(1)}, u32[]{:S(2)}, u32[]{:S(2)}) collective-permute-start(bf16[128,896]{1,0:T(8,128)(2,1)S(1)} %bitcast.58), channel_id=1, source_target_pairs={{0,1},{1,3},{3,2},{2,0},{4,5},{5,7},{7,6},{6,4},{8,9},{9,11},{11,1... | collective-permute-start | bytes 688136 | tf_op jit(solution)/shard_map/ppermute | solution.py:170
  7.4 1.5 %copy-done.1 = bf16[1,1,896,1024]{3,2,1,0:T(8,128)(2,1)S(1)} copy-done((bf16[1,1,896,1024]{3,2,1,0:T(8,128)(2,1)S(1)}, bf16[1,1,896,1024]{3,2,1,0:T(8,128)(2,1)}, u32[]{:S(2)}) %copy-start.1) | copy-done | bytes 1835032
  8.9 1.5 %copy-done.3 = bf16[1,1,896,1024]{3,2,1,0:T(8,128)(2,1)S(1)} copy-done((bf16[1,1,896,1024]{3,2,1,0:T(8,128)(2,1)S(1)}, bf16[1,1,896,1024]{3,2,1,0:T(8,128)(2,1)}, u32[]{:S(2)}) %copy-start.3) | copy-done | bytes 1835032
  10.4 1.8 %shard_map.124 = (bf16[3,32,1024]{2,1,0:T(8,128)(2,1)S(1)}, bf16[3,32,1024]{2,1,0:T(8,128)(2,1)S(1)}, bf16[3,32,1024]{2,1,0:T(8,128)(2,1)S(1)}, bf16[3,32,1024]{2,1,0:T(8,128)(2,1)S(1)}) custom-call(s32[2]{0:T(128)S(1)} %pad_add_fusion.place_ref, bf16[128,896]{1,0:T(8,128)(2,1)S(1)} %bitcast.59, ...), custom_call_target="tpu_custom_call" | custom-call | flops 704643072 | bytes 5992448 | tf_op jit(solution)/shard_map/pallas_call | solution.py:195
  12.2 1.6 %collective-permute-start.7 = (bf16[3,32,1024]{2,1,0:T(8,128)(2,1)S(1)}, bf16[3,32,1024]{2,1,0:T(8,128)(2,1)S(1)}, u32[]{:S(2)}, u32[]{:S(2)}) collective-permute-start(bf16[3,32,1024]{2,1,0:T(8,128)(2,1)S(1)} %get-tuple-element.39), channel_id=1, source_target_pairs={{0,4},{4,0},{8,12},{12,8},{1,5},{5,1},{9,13},{13,9},{2,6},{6,2},{1... | collective-permute-start | bytes 589832 | tf_op jit(solution)/shard_map/ppermute | solution.py:157
  13.8 1.5 %collective-permute-start.8 = (bf16[3,32,1024]{2,1,0:T(8,128)(2,1)S(1)}, bf16[3,32,1024]{2,1,0:T(8,128)(2,1)S(1)}, u32[]{:S(2)}, u32[]{:S(2)}) collective-permute-start(bf16[3,32,1024]{2,1,0:T(8,128)(2,1)S(1)} %get-tuple-element.40), channel_id=1, source_target_pairs={{0,8},{4,12},{8,0},{12,4},{1,9},{5,13},{9,1},{13,5},{2,10},{6,14},... | collective-permute-start | bytes 589832 | tf_op jit(solution)/shard_map/ppermute | solution.py:157
  16.9 2.0 %collective-permute-start.5 = (bf16[128,896]{1,0:T(8,128)(2,1)S(1)}, bf16[128,896]{1,0:T(8,128)(2,1)S(1)}, u32[]{:S(2)}, u32[]{:S(2)}) collective-permute-start(bf16[128,896]{1,0:T(8,128)(2,1)S(1)} %collective-permute-done.refs_0_), channel_id=1, source_target_pairs={{0,1},{1,3},{3,2},{2,0},{4,5},{5,7},{7,6},{6,4},{8,9},{9,11},{11,1... | collective-permute-start | bytes 688136 | tf_op jit(solution)/shard_map/ppermute | solution.py:170
  18.8 1.8 %shard_map.125 = (bf16[3,32,1024]{2,1,0:T(8,128)(2,1)S(1)}, bf16[3,32,1024]{2,1,0:T(8,128)(2,1)S(1)}, bf16[3,32,1024]{2,1,0:T(8,128)(2,1)S(1)}, bf16[3,32,1024]{2,1,0:T(8,128)(2,1)S(1)}) custom-call(s32[2]{0:T(128)S(1)} %pad_add_fusion.place_ref, bf16[128,896]{1,0:T(8,128)(2,1)S(1)} %collective-permute-done.refs_0_, ...), custom_call_target="tpu_custom_call" | custom-call | flops 704643072 | bytes 5992448 | tf_op jit(solution)/shard_map/pallas_call | solution.py:195
  20.7 1.6 %collective-permute-start.2 = (bf16[3,32,1024]{2,1,0:T(8,128)(2,1)S(1)}, bf16[3,32,1024]{2,1,0:T(8,128)(2,1)S(1)}, u32[]{:S(2)}, u32[]{:S(2)}) collective-permute-start(bf16[3,32,1024]{2,1,0:T(8,128)(2,1)S(1)} %get-tuple-element.36), channel_id=1, source_target_pairs={{0,4},{4,0},{8,12},{12,8},{1,5},{5,1},{9,13},{13,9},{2,6},{6,2},{1... | collective-permute-start | bytes 589832 | tf_op jit(solution)/shard_map/ppermute | solution.py:157
  23.2 2.7 %collective-permute-start.3 = (bf16[3,32,1024]{2,1,0:T(8,128)(2,1)S(1)}, bf16[3,32,1024]{2,1,0:T(8,128)(2,1)S(1)}, u32[]{:S(2)}, u32[]{:S(2)}) collective-permute-start(bf16[3,32,1024]{2,1,0:T(8,128)(2,1)S(1)} %get-tuple-element.37), channel_id=1, source_target_pairs={{0,8},{4,12},{8,0},{12,4},{1,9},{5,13},{9,1},{13,5},{2,10},{6,14},... | collective-permute-start | bytes 589832 | tf_op jit(solution)/shard_map/ppermute | solution.py:157
  28.9 1.8 %shard_map.127 = (bf16[5,32,1024]{2,1,0:T(8,128)(2,1)S(1)}, bf16[5,32,1024]{2,1,0:T(8,128)(2,1)S(1)}, bf16[5,32,1024]{2,1,0:T(8,128)(2,1)S(1)}, bf16[5,32,1024]{2,1,0:T(8,128)(2,1)S(1)}) custom-call(s32[2]{0:T(128)S(1)} %pad_add_fusion.place_ref, bf16[128,896]{1,0:T(8,128)(2,1)S(1)} %collective-permute-done.5.refs_0_, ...), custom_call_target="tpu_custom_call" | custom-call | flops 704643072 | bytes 5992448 | tf_op jit(solution)/shard_map/pallas_call | solution.py:195
  33.7 1.4 %collective-permute-start.10 = (bf16[5,32,1024]{2,1,0:T(8,128)(2,1)S(1)}, bf16[5,32,1024]{2,1,0:T(8,128)(2,1)S(1)}, u32[]{:S(2)}, u32[]{:S(2)}) collective-permute-start(bf16[5,32,1024]{2,1,0:T(8,128)(2,1)S(1)} %get-tuple-element.48), channel_id=1, source_target_pairs={{0,4},{4,0},{8,12},{12,8},{1,5},{5,1},{9,13},{13,9},{2,6},{6,2},{1... | collective-permute-start | bytes 983048 | tf_op jit(solution)/shard_map/ppermute | solution.py:157
  35.1 1.5 %collective-permute-start.11 = (bf16[5,32,1024]{2,1,0:T(8,128)(2,1)S(1)}, bf16[5,32,1024]{2,1,0:T(8,128)(2,1)S(1)}, u32[]{:S(2)}, u32[]{:S(2)}) collective-permute-start(bf16[5,32,1024]{2,1,0:T(8,128)(2,1)S(1)} %get-tuple-element.49), channel_id=1, source_target_pairs={{0,8},{4,12},{8,0},{12,4},{1,9},{5,13},{9,1},{13,5},{2,10},{6,14},... | collective-permute-start | bytes 983048 | tf_op jit(solution)/shard_map/ppermute | solution.py:157
  38.5 5.7 %collective-permute-done.13.refs_0_ = bf16[128,896]{1,0:T(8,128)(2,1)S(1)} collective-permute-done((bf16[128,896]{1,0:T(8,128)(2,1)S(1)}, bf16[128,896]{1,0:T(8,128)(2,1)S(1)}, u32[]{:S(2)}, u32[]{:S(2)}) %collective-permute-start.13) | collective-permute-done | bytes 229408 | tf_op jit(solution)/shard_map/ppermute | solution.py:170
  44.2 1.8 %shard_map.130 = (bf16[5,32,1024]{2,1,0:T(8,128)(2,1)S(1)}, bf16[5,32,1024]{2,1,0:T(8,128)(2,1)S(1)}, bf16[5,32,1024]{2,1,0:T(8,128)(2,1)S(1)}, bf16[5,32,1024]{2,1,0:T(8,128)(2,1)S(1)}) custom-call(s32[2]{0:T(128)S(1)} %pad_add_fusion.place_ref, bf16[128,896]{1,0:T(8,128)(2,1)S(1)} %collective-permute-done.13.refs_0_, ...), custom_call_target="tpu_custom_call" | custom-call | flops 704643072 | bytes 5992448 | tf_op jit(solution)/shard_map/pallas_call | solution.py:195
  47.2 2.1 %collective-permute-done.11.refs_2_ = bf16[5,32,1024]{2,1,0:T(8,128)(2,1)S(1)} collective-permute-done((bf16[5,32,1024]{2,1,0:T(8,128)(2,1)S(1)}, bf16[5,32,1024]{2,1,0:T(8,128)(2,1)S(1)}, u32[]{:S(2)}, u32[]{:S(2)}) %collective-permute-start.11) | collective-permute-done | bytes 327712 | tf_op jit(solution)/shard_map/ppermute | solution.py:157
  50.1 2.5 %collective-permute-start.17 = (bf16[5,32,1024]{2,1,0:T(8,128)(2,1)S(1)}, bf16[5,32,1024]{2,1,0:T(8,128)(2,1)S(1)}, u32[]{:S(2)}, u32[]{:S(2)}) collective-permute-start(bf16[5,32,1024]{2,1,0:T(8,128)(2,1)S(1)} %get-tuple-element.58), channel_id=1, source_target_pairs={{0,8},{4,12},{8,0},{12,4},{1,9},{5,13},{9,1},{13,5},{2,10},{6,14},... | collective-permute-start | bytes 983048 | tf_op jit(solution)/shard_map/ppermute | solution.py:157
  54.5 1.8 %shard_map.134.refs_3_ = bf16[128,896]{1,0:T(8,128)(2,1)S(1)} custom-call(s32[2]{0:T(128)S(1)} %pad_add_fusion.place_ref, bf16[5,32,1024]{2,1,0:T(8,128)(2,1)S(1)} %get-tuple-element.47.refs_5_.refs_0_, bf16[5,32,1024]{2,1,0:T(8,128)(2,1)S(1)} %collective-permute-done.10.refs_1_, bf16[5,32,1024]{2,1,0:T(8,128)(2,1)S(1)} %collective-permute-done.11.refs_2_, ...), custom_call_target="tpu_custom_call" | custom-call | flops 469762048 | bytes 6287360 | tf_op jit(solution)/shard_map/pallas_call | solution.py:195
  56.4 2.5 %collective-permute-start.15 = (bf16[128,896]{1,0:T(8,128)(2,1)S(1)}, bf16[128,896]{1,0:T(8,128)(2,1)S(1)}, u32[]{:S(2)}, u32[]{:S(2)}) collective-permute-start(bf16[128,896]{1,0:T(8,128)(2,1)S(1)} %shard_map.133.refs_9_), channel_id=1, source_target_pairs={{0,18},{1,16},{3,17},{2,19},{16,2},{17,0},{19,1},{18,3},{4,22},{5,... | collective-permute-start | bytes 688136 | tf_op jit(solution)/shard_map/ppermute | solution.py:180
  61.2 1.6 %collective-permute-done.17.refs_2_ = bf16[5,32,1024]{2,1,0:T(8,128)(2,1)S(1)} collective-permute-done((bf16[5,32,1024]{2,1,0:T(8,128)(2,1)S(1)}, bf16[5,32,1024]{2,1,0:T(8,128)(2,1)S(1)}, u32[]{:S(2)}, u32[]{:S(2)}) %collective-permute-start.17) | collective-permute-done | bytes 327712 | tf_op jit(solution)/shard_map/ppermute | solution.py:157
  65.0 1.4 %collective-permute-start.21 = (bf16[3,32,1024]{2,1,0:T(8,128)(2,1)S(1)}, bf16[3,32,1024]{2,1,0:T(8,128)(2,1)S(1)}, u32[]{:S(2)}, u32[]{:S(2)}) collective-permute-start(bf16[3,32,1024]{2,1,0:T(8,128)(2,1)S(1)} %shard_map.137.refs_6_.refs_0_), channel_id=1, source_target_pairs={{0,12},{4,8},{8,4},{12,0},{1,13},{5,9},{9,5},{13,1},{2,14},{6,10},... | collective-permute-start | bytes 589832 | tf_op jit(solution)/shard_map/ppermute | solution.py:157
  66.4 1.3 %collective-permute-start.20 = (bf16[3,32,1024]{2,1,0:T(8,128)(2,1)S(1)}, bf16[3,32,1024]{2,1,0:T(8,128)(2,1)S(1)}, u32[]{:S(2)}, u32[]{:S(2)}) collective-permute-start(bf16[3,32,1024]{2,1,0:T(8,128)(2,1)S(1)} %shard_map.137.refs_6_.refs_0_), channel_id=1, source_target_pairs={{0,8},{4,12},{8,0},{12,4},{1,9},{5,13},{9,1},{13,5},{2,10},{6,14},... | collective-permute-start | bytes 589832 | tf_op jit(solution)/shard_map/ppermute | solution.py:157
  68.5 1.8 %shard_map.139.refs_7_ = bf16[128,896]{1,0:T(8,128)(2,1)S(1)} custom-call(s32[2]{0:T(128)S(1)} %pad_add_fusion.place_ref, bf16[5,32,1024]{2,1,0:T(8,128)(2,1)S(1)} %get-tuple-element.56.refs_6_.refs_0_, bf16[5,32,1024]{2,1,0:T(8,128)(2,1)S(1)} %collective-permute-done.16.refs_1_, bf16[5,32,1024]{2,1,0:T(8,128)(2,1)S(1)} %collective-permute-done.17.refs_2_, ...), custom_call_target="tpu_custom_call" | custom-call | flops 469762048 | bytes 6287360 | tf_op jit(solution)/shard_map/pallas_call | solution.py:195
  70.3 4.1 %collective-permute-start.28 = (bf16[128,896]{1,0:T(8,128)(2,1)S(1)}, bf16[128,896]{1,0:T(8,128)(2,1)S(1)}, u32[]{:S(2)}, u32[]{:S(2)}) collective-permute-start(bf16[128,896]{1,0:T(8,128)(2,1)S(1)} %shard_map.139.refs_7_), channel_id=1, source_target_pairs={{0,1},{1,3},{3,2},{2,0},{4,5},{5,7},{7,6},{6,4},{8,9},{9,11},{11,1... | collective-permute-start | bytes 688136 | tf_op jit(solution)/shard_map/ppermute | solution.py:170
  76.6 1.3 %collective-permute-start.27 = (bf16[1,32,1024]{2,1,0:T(8,128)(2,1)S(1)}, bf16[1,32,1024]{2,1,0:T(8,128)(2,1)S(1)}, u32[]{:S(2)}, u32[]{:S(2)}) collective-permute-start(bf16[1,32,1024]{2,1,0:T(8,128)(2,1)S(1)} %shard_map.141.refs_10_.refs_0_), channel_id=1, source_target_pairs={{0,12},{4,8},{8,4},{12,0},{1,13},{5,9},{9,5},{13,1},{2,14},{6,10},... | collective-permute-start | bytes 196616 | tf_op jit(solution)/shard_map/ppermute | solution.py:157
  78.0 1.7 %collective-permute-start.26 = (bf16[1,32,1024]{2,1,0:T(8,128)(2,1)S(1)}, bf16[1,32,1024]{2,1,0:T(8,128)(2,1)S(1)}, u32[]{:S(2)}, u32[]{:S(2)}) collective-permute-start(bf16[1,32,1024]{2,1,0:T(8,128)(2,1)S(1)} %shard_map.141.refs_10_.refs_0_), channel_id=1, source_target_pairs={{0,8},{4,12},{8,0},{12,4},{1,9},{5,13},{9,1},{13,5},{2,10},{6,14},... | collective-permute-start | bytes 196616 | tf_op jit(solution)/shard_map/ppermute | solution.py:157
  80.2 1.8 %shard_map.142.refs_10_ = bf16[128,896]{1,0:T(8,128)(2,1)S(1)} custom-call(s32[2]{0:T(128)S(1)} %pad_add_fusion.place_ref, bf16[3,32,1024]{2,1,0:T(8,128)(2,1)S(1)} %shard_map.137.refs_6_.refs_0_, bf16[3,32,1024]{2,1,0:T(8,128)(2,1)S(1)} %collective-permute-done.19.refs_1_.refs_2_, bf16[3,32,1024]{2,1,0:T(8,128)(2,1)S(1)} %collective-permute-done.20.refs_2_.refs_3_, ...), custom_call_target="tpu_custom_call" | custom-call | flops 469762048 | bytes 5992448 | tf_op jit(solution)/shard_map/pallas_call | solution.py:195
  82.0 2.0 %collective-permute-start.30 = (bf16[128,896]{1,0:T(8,128)(2,1)S(1)}, bf16[128,896]{1,0:T(8,128)(2,1)S(1)}, u32[]{:S(2)}, u32[]{:S(2)}) collective-permute-start(bf16[128,896]{1,0:T(8,128)(2,1)S(1)} %shard_map.142.refs_10_), channel_id=1, source_target_pairs={{0,17},{1,19},{3,18},{2,16},{16,1},{17,3},{19,2},{18,0},{4,21},{5,... | collective-permute-start | bytes 688136 | tf_op jit(solution)/shard_map/ppermute | solution.py:180
  84.0 1.8 %shard_map.143.refs_7_ = bf16[128,896]{1,0:T(8,128)(2,1)S(1)} custom-call(s32[2]{0:T(128)S(1)} %pad_add_fusion.place_ref, bf16[3,32,1024]{2,1,0:T(8,128)(2,1)S(1)} %shard_map.137.refs_6_.refs_0_, bf16[3,32,1024]{2,1,0:T(8,128)(2,1)S(1)} %collective-permute-done.19.refs_1_.refs_2_, bf16[3,32,1024]{2,1,0:T(8,128)(2,1)S(1)} %collective-permute-done.20.refs_2_.refs_3_, ...), custom_call_target="tpu_custom_call" | custom-call | flops 469762048 | bytes 5992448 | tf_op jit(solution)/shard_map/pallas_call | solution.py:195
  85.8 1.2 %collective-permute-start.31 = (bf16[128,896]{1,0:T(8,128)(2,1)S(1)}, bf16[128,896]{1,0:T(8,128)(2,1)S(1)}, u32[]{:S(2)}, u32[]{:S(2)}) collective-permute-start(bf16[128,896]{1,0:T(8,128)(2,1)S(1)} %shard_map.143.refs_7_), channel_id=1, source_target_pairs={{0,16},{16,0},{1,17},{17,1},{2,18},{18,2},{3,19},{19,3},{4,20},{20... | collective-permute-start | bytes 688136 | tf_op jit(solution)/shard_map/ppermute | solution.py:14
  88.2 1.4 %collective-permute-done.29 = bf16[128,896]{1,0:T(8,128)(2,1)S(1)} collective-permute-done((bf16[128,896]{1,0:T(8,128)(2,1)S(1)}, bf16[128,896]{1,0:T(8,128)(2,1)S(1)}, u32[]{:S(2)}, u32[]{:S(2)}) %collective-permute-start.29) | collective-permute-done | bytes 229408 | tf_op jit(solution)/shard_map/ppermute | solution.py:14
  (88 shorter events, 25.5 us)
Async XLA Ops:
  1.6 14.1 %collective-permute-start.1 = (bf16[144,896]{1,0:T(8,128)(2,1)S(1)}, bf16[144,896]{1,0:T(8,128)(2,1)S(1)}, u32[]{:S(2)}, u32[]{:S(2)}) collective-permute-start(bf16[144,896]{1,0:T(8,128)(2,1)S(1)} %shard_map.123.refs_1_.refs_2_.refs_8_.refs_5_), channel_id=1, source_target_pairs={{0,1},{1,3},{3,2},{2,0},{4,5},{5,7},{7,6},{6,4},{8,9},{9,11},{11,1... | collective-permute-start | bytes 774152 | tf_op jit(solution)/shard_map/ppermute | solution.py:170
  4.7 12.1 %collective-permute-start = (bf16[128,896]{1,0:T(8,128)(2,1)S(1)}, bf16[128,896]{1,0:T(8,128)(2,1)S(1)}, u32[]{:S(2)}, u32[]{:S(2)}) collective-permute-start(bf16[128,896]{1,0:T(8,128)(2,1)S(1)} %bitcast.58), channel_id=1, source_target_pairs={{0,1},{1,3},{3,2},{2,0},{4,5},{5,7},{7,6},{6,4},{8,9},{9,11},{11,1... | collective-permute-start | bytes 688136 | tf_op jit(solution)/shard_map/ppermute | solution.py:170
  12.2 8.5 %collective-permute-start.7 = (bf16[3,32,1024]{2,1,0:T(8,128)(2,1)S(1)}, bf16[3,32,1024]{2,1,0:T(8,128)(2,1)S(1)}, u32[]{:S(2)}, u32[]{:S(2)}) collective-permute-start(bf16[3,32,1024]{2,1,0:T(8,128)(2,1)S(1)} %get-tuple-element.39), channel_id=1, source_target_pairs={{0,4},{4,0},{8,12},{12,8},{1,5},{5,1},{9,13},{13,9},{2,6},{6,2},{1... | collective-permute-start | bytes 589832 | tf_op jit(solution)/shard_map/ppermute | solution.py:157
  13.8 9.4 %collective-permute-start.8 = (bf16[3,32,1024]{2,1,0:T(8,128)(2,1)S(1)}, bf16[3,32,1024]{2,1,0:T(8,128)(2,1)S(1)}, u32[]{:S(2)}, u32[]{:S(2)}) collective-permute-start(bf16[3,32,1024]{2,1,0:T(8,128)(2,1)S(1)} %get-tuple-element.40), channel_id=1, source_target_pairs={{0,8},{4,12},{8,0},{12,4},{1,9},{5,13},{9,1},{13,5},{2,10},{6,14},... | collective-permute-start | bytes 589832 | tf_op jit(solution)/shard_map/ppermute | solution.py:157
  15.3 10.6 %collective-permute-start.9 = (bf16[3,32,1024]{2,1,0:T(8,128)(2,1)S(1)}, bf16[3,32,1024]{2,1,0:T(8,128)(2,1)S(1)}, u32[]{:S(2)}, u32[]{:S(2)}) collective-permute-start(bf16[3,32,1024]{2,1,0:T(8,128)(2,1)S(1)} %get-tuple-element.41), channel_id=1, source_target_pairs={{0,12},{4,8},{8,4},{12,0},{1,13},{5,9},{9,5},{13,1},{2,14},{6,10},... | collective-permute-start | bytes 589832 | tf_op jit(solution)/shard_map/ppermute | solution.py:157
  15.8 11.5 %collective-permute-start.6 = (bf16[144,896]{1,0:T(8,128)(2,1)S(1)}, bf16[144,896]{1,0:T(8,128)(2,1)S(1)}, u32[]{:S(2)}, u32[]{:S(2)}) collective-permute-start(bf16[144,896]{1,0:T(8,128)(2,1)S(1)} %collective-permute-done.1.refs_1_.refs_2_.refs_5_.refs_8_), channel_id=1, source_target_pairs={{0,1},{1,3},{3,2},{2,0},{4,5},{5,7},{7,6},{6,4},{8,9},{9,11},{11,1... | collective-permute-start | bytes 774152 | tf_op jit(solution)/shard_map/ppermute | solution.py:170
  16.9 12.1 %collective-permute-start.5 = (bf16[128,896]{1,0:T(8,128)(2,1)S(1)}, bf16[128,896]{1,0:T(8,128)(2,1)S(1)}, u32[]{:S(2)}, u32[]{:S(2)}) collective-permute-start(bf16[128,896]{1,0:T(8,128)(2,1)S(1)} %collective-permute-done.refs_0_), channel_id=1, source_target_pairs={{0,1},{1,3},{3,2},{2,0},{4,5},{5,7},{7,6},{6,4},{8,9},{9,11},{11,1... | collective-permute-start | bytes 688136 | tf_op jit(solution)/shard_map/ppermute | solution.py:170
  20.7 11.2 %collective-permute-start.2 = (bf16[3,32,1024]{2,1,0:T(8,128)(2,1)S(1)}, bf16[3,32,1024]{2,1,0:T(8,128)(2,1)S(1)}, u32[]{:S(2)}, u32[]{:S(2)}) collective-permute-start(bf16[3,32,1024]{2,1,0:T(8,128)(2,1)S(1)} %get-tuple-element.36), channel_id=1, source_target_pairs={{0,4},{4,0},{8,12},{12,8},{1,5},{5,1},{9,13},{13,9},{2,6},{6,2},{1... | collective-permute-start | bytes 589832 | tf_op jit(solution)/shard_map/ppermute | solution.py:157
  23.2 9.8 %collective-permute-start.3 = (bf16[3,32,1024]{2,1,0:T(8,128)(2,1)S(1)}, bf16[3,32,1024]{2,1,0:T(8,128)(2,1)S(1)}, u32[]{:S(2)}, u32[]{:S(2)}) collective-permute-start(bf16[3,32,1024]{2,1,0:T(8,128)(2,1)S(1)} %get-tuple-element.37), channel_id=1, source_target_pairs={{0,8},{4,12},{8,0},{12,4},{1,9},{5,13},{9,1},{13,5},{2,10},{6,14},... | collective-permute-start | bytes 589832 | tf_op jit(solution)/shard_map/ppermute | solution.py:157
  25.9 7.1 %collective-permute-start.4 = (bf16[3,32,1024]{2,1,0:T(8,128)(2,1)S(1)}, bf16[3,32,1024]{2,1,0:T(8,128)(2,1)S(1)}, u32[]{:S(2)}, u32[]{:S(2)}) collective-permute-start(bf16[3,32,1024]{2,1,0:T(8,128)(2,1)S(1)} %get-tuple-element.38), channel_id=1, source_target_pairs={{0,12},{4,8},{8,4},{12,0},{1,13},{5,9},{9,5},{13,1},{2,14},{6,10},... | collective-permute-start | bytes 589832 | tf_op jit(solution)/shard_map/ppermute | solution.py:157
  27.3 16.9 %collective-permute-start.14 = (bf16[144,896]{1,0:T(8,128)(2,1)S(1)}, bf16[144,896]{1,0:T(8,128)(2,1)S(1)}, u32[]{:S(2)}, u32[]{:S(2)}) collective-permute-start(bf16[144,896]{1,0:T(8,128)(2,1)S(1)} %collective-permute-done.6.refs_1_.refs_2_.refs_5_.refs_8_), channel_id=1, source_target_pairs={{0,1},{1,3},{3,2},{2,0},{4,5},{5,7},{7,6},{6,4},{8,9},{9,11},{11,1... | collective-permute-start | bytes 774152 | tf_op jit(solution)/shard_map/ppermute | solution.py:170
  33.7 13.4 %collective-permute-start.10 = (bf16[5,32,1024]{2,1,0:T(8,128)(2,1)S(1)}, bf16[5,32,1024]{2,1,0:T(8,128)(2,1)S(1)}, u32[]{:S(2)}, u32[]{:S(2)}) collective-permute-start(bf16[5,32,1024]{2,1,0:T(8,128)(2,1)S(1)} %get-tuple-element.48), channel_id=1, source_target_pairs={{0,4},{4,0},{8,12},{12,8},{1,5},{5,1},{9,13},{13,9},{2,6},{6,2},{1... | collective-permute-start | bytes 983048 | tf_op jit(solution)/shard_map/ppermute | solution.py:157
  35.1 14.2 %collective-permute-start.11 = (bf16[5,32,1024]{2,1,0:T(8,128)(2,1)S(1)}, bf16[5,32,1024]{2,1,0:T(8,128)(2,1)S(1)}, u32[]{:S(2)}, u32[]{:S(2)}) collective-permute-start(bf16[5,32,1024]{2,1,0:T(8,128)(2,1)S(1)} %get-tuple-element.49), channel_id=1, source_target_pairs={{0,8},{4,12},{8,0},{12,4},{1,9},{5,13},{9,1},{13,5},{2,10},{6,14},... | collective-permute-start | bytes 983048 | tf_op jit(solution)/shard_map/ppermute | solution.py:157
  36.7 12.6 %collective-permute-start.12 = (bf16[5,32,1024]{2,1,0:T(8,128)(2,1)S(1)}, bf16[5,32,1024]{2,1,0:T(8,128)(2,1)S(1)}, u32[]{:S(2)}, u32[]{:S(2)}) collective-permute-start(bf16[5,32,1024]{2,1,0:T(8,128)(2,1)S(1)} %get-tuple-element.50), channel_id=1, source_target_pairs={{0,12},{4,8},{8,4},{12,0},{1,13},{5,9},{9,5},{13,1},{2,14},{6,10},... | collective-permute-start | bytes 983048 | tf_op jit(solution)/shard_map/ppermute | solution.py:157
  37.3 6.9 %collective-permute-start.13 = (bf16[128,896]{1,0:T(8,128)(2,1)S(1)}, bf16[128,896]{1,0:T(8,128)(2,1)S(1)}, u32[]{:S(2)}, u32[]{:S(2)}) collective-permute-start(bf16[128,896]{1,0:T(8,128)(2,1)S(1)} %collective-permute-done.5.refs_0_), channel_id=1, source_target_pairs={{0,1},{1,3},{3,2},{2,0},{4,5},{5,7},{7,6},{6,4},{8,9},{9,11},{11,1... | collective-permute-start | bytes 688136 | tf_op jit(solution)/shard_map/ppermute | solution.py:170
  50.0 11.2 %collective-permute-start.16 = (bf16[5,32,1024]{2,1,0:T(8,128)(2,1)S(1)}, bf16[5,32,1024]{2,1,0:T(8,128)(2,1)S(1)}, u32[]{:S(2)}, u32[]{:S(2)}) collective-permute-start(bf16[5,32,1024]{2,1,0:T(8,128)(2,1)S(1)} %get-tuple-element.57), channel_id=1, source_target_pairs={{0,4},{4,0},{8,12},{12,8},{1,5},{5,1},{9,13},{13,9},{2,6},{6,2},{1... | collective-permute-start | bytes 983048 | tf_op jit(solution)/shard_map/ppermute | solution.py:157
  50.1 12.7 %collective-permute-start.17 = (bf16[5,32,1024]{2,1,0:T(8,128)(2,1)S(1)}, bf16[5,32,1024]{2,1,0:T(8,128)(2,1)S(1)}, u32[]{:S(2)}, u32[]{:S(2)}) collective-permute-start(bf16[5,32,1024]{2,1,0:T(8,128)(2,1)S(1)} %get-tuple-element.58), channel_id=1, source_target_pairs={{0,8},{4,12},{8,0},{12,4},{1,9},{5,13},{9,1},{13,5},{2,10},{6,14},... | collective-permute-start | bytes 983048 | tf_op jit(solution)/shard_map/ppermute | solution.py:157
  52.6 10.2 %collective-permute-start.18 = (bf16[5,32,1024]{2,1,0:T(8,128)(2,1)S(1)}, bf16[5,32,1024]{2,1,0:T(8,128)(2,1)S(1)}, u32[]{:S(2)}, u32[]{:S(2)}) collective-permute-start(bf16[5,32,1024]{2,1,0:T(8,128)(2,1)S(1)} %get-tuple-element.59), channel_id=1, source_target_pairs={{0,12},{4,8},{8,4},{12,0},{1,13},{5,9},{9,5},{13,1},{2,14},{6,10},... | collective-permute-start | bytes 983048 | tf_op jit(solution)/shard_map/ppermute | solution.py:157
  56.4 11.4 %collective-permute-start.23 = (bf16[128,896]{1,0:T(8,128)(2,1)S(1)}, bf16[128,896]{1,0:T(8,128)(2,1)S(1)}, u32[]{:S(2)}, u32[]{:S(2)}) collective-permute-start(bf16[128,896]{1,0:T(8,128)(2,1)S(1)} %shard_map.134.refs_3_), channel_id=1, source_target_pairs={{0,18},{1,16},{3,17},{2,19},{16,2},{17,0},{19,1},{18,3},{4,22},{5,... | collective-permute-start | bytes 688136 | tf_op jit(solution)/shard_map/ppermute | solution.py:180
  56.4 12.1 %collective-permute-start.15 = (bf16[128,896]{1,0:T(8,128)(2,1)S(1)}, bf16[128,896]{1,0:T(8,128)(2,1)S(1)}, u32[]{:S(2)}, u32[]{:S(2)}) collective-permute-start(bf16[128,896]{1,0:T(8,128)(2,1)S(1)} %shard_map.133.refs_9_), channel_id=1, source_target_pairs={{0,18},{1,16},{3,17},{2,19},{16,2},{17,0},{19,1},{18,3},{4,22},{5,... | collective-permute-start | bytes 688136 | tf_op jit(solution)/shard_map/ppermute | solution.py:180
  64.5 10.3 %collective-permute-start.22 = (bf16[128,896]{1,0:T(8,128)(2,1)S(1)}, bf16[128,896]{1,0:T(8,128)(2,1)S(1)}, u32[]{:S(2)}, u32[]{:S(2)}) collective-permute-start(bf16[128,896]{1,0:T(8,128)(2,1)S(1)} %shard_map.138.refs_9_), channel_id=1, source_target_pairs={{0,1},{1,3},{3,2},{2,0},{4,5},{5,7},{7,6},{6,4},{8,9},{9,11},{11,1... | collective-permute-start | bytes 688136 | tf_op jit(solution)/shard_map/ppermute | solution.py:170
  65.0 9.5 %collective-permute-start.21 = (bf16[3,32,1024]{2,1,0:T(8,128)(2,1)S(1)}, bf16[3,32,1024]{2,1,0:T(8,128)(2,1)S(1)}, u32[]{:S(2)}, u32[]{:S(2)}) collective-permute-start(bf16[3,32,1024]{2,1,0:T(8,128)(2,1)S(1)} %shard_map.137.refs_6_.refs_0_), channel_id=1, source_target_pairs={{0,12},{4,8},{8,4},{12,0},{1,13},{5,9},{9,5},{13,1},{2,14},{6,10},... | collective-permute-start | bytes 589832 | tf_op jit(solution)/shard_map/ppermute | solution.py:157
  66.4 8.1 %collective-permute-start.20 = (bf16[3,32,1024]{2,1,0:T(8,128)(2,1)S(1)}, bf16[3,32,1024]{2,1,0:T(8,128)(2,1)S(1)}, u32[]{:S(2)}, u32[]{:S(2)}) collective-permute-start(bf16[3,32,1024]{2,1,0:T(8,128)(2,1)S(1)} %shard_map.137.refs_6_.refs_0_), channel_id=1, source_target_pairs={{0,8},{4,12},{8,0},{12,4},{1,9},{5,13},{9,1},{13,5},{2,10},{6,14},... | collective-permute-start | bytes 589832 | tf_op jit(solution)/shard_map/ppermute | solution.py:157
  67.8 6.7 %collective-permute-start.19 = (bf16[3,32,1024]{2,1,0:T(8,128)(2,1)S(1)}, bf16[3,32,1024]{2,1,0:T(8,128)(2,1)S(1)}, u32[]{:S(2)}, u32[]{:S(2)}) collective-permute-start(bf16[3,32,1024]{2,1,0:T(8,128)(2,1)S(1)} %shard_map.137.refs_6_.refs_0_), channel_id=1, source_target_pairs={{0,4},{4,0},{8,12},{12,8},{1,5},{5,1},{9,13},{13,9},{2,6},{6,2},{1... | collective-permute-start | bytes 589832 | tf_op jit(solution)/shard_map/ppermute | solution.py:157
  70.3 9.8 %collective-permute-start.28 = (bf16[128,896]{1,0:T(8,128)(2,1)S(1)}, bf16[128,896]{1,0:T(8,128)(2,1)S(1)}, u32[]{:S(2)}, u32[]{:S(2)}) collective-permute-start(bf16[128,896]{1,0:T(8,128)(2,1)S(1)} %shard_map.139.refs_7_), channel_id=1, source_target_pairs={{0,1},{1,3},{3,2},{2,0},{4,5},{5,7},{7,6},{6,4},{8,9},{9,11},{11,1... | collective-permute-start | bytes 688136 | tf_op jit(solution)/shard_map/ppermute | solution.py:170
  75.8 12.3 %collective-permute-start.24 = (bf16[128,896]{1,0:T(8,128)(2,1)S(1)}, bf16[128,896]{1,0:T(8,128)(2,1)S(1)}, u32[]{:S(2)}, u32[]{:S(2)}) collective-permute-start(bf16[128,896]{1,0:T(8,128)(2,1)S(1)} %shard_map.140.refs_1_), channel_id=1, source_target_pairs={{0,17},{1,19},{3,18},{2,16},{16,1},{17,3},{19,2},{18,0},{4,21},{5,... | collective-permute-start | bytes 688136 | tf_op jit(solution)/shard_map/ppermute | solution.py:180
  76.6 9.2 %collective-permute-start.27 = (bf16[1,32,1024]{2,1,0:T(8,128)(2,1)S(1)}, bf16[1,32,1024]{2,1,0:T(8,128)(2,1)S(1)}, u32[]{:S(2)}, u32[]{:S(2)}) collective-permute-start(bf16[1,32,1024]{2,1,0:T(8,128)(2,1)S(1)} %shard_map.141.refs_10_.refs_0_), channel_id=1, source_target_pairs={{0,12},{4,8},{8,4},{12,0},{1,13},{5,9},{9,5},{13,1},{2,14},{6,10},... | collective-permute-start | bytes 196616 | tf_op jit(solution)/shard_map/ppermute | solution.py:157
  78.0 9.1 %collective-permute-start.26 = (bf16[1,32,1024]{2,1,0:T(8,128)(2,1)S(1)}, bf16[1,32,1024]{2,1,0:T(8,128)(2,1)S(1)}, u32[]{:S(2)}, u32[]{:S(2)}) collective-permute-start(bf16[1,32,1024]{2,1,0:T(8,128)(2,1)S(1)} %shard_map.141.refs_10_.refs_0_), channel_id=1, source_target_pairs={{0,8},{4,12},{8,0},{12,4},{1,9},{5,13},{9,1},{13,5},{2,10},{6,14},... | collective-permute-start | bytes 196616 | tf_op jit(solution)/shard_map/ppermute | solution.py:157
  79.6 7.4 %collective-permute-start.25 = (bf16[1,32,1024]{2,1,0:T(8,128)(2,1)S(1)}, bf16[1,32,1024]{2,1,0:T(8,128)(2,1)S(1)}, u32[]{:S(2)}, u32[]{:S(2)}) collective-permute-start(bf16[1,32,1024]{2,1,0:T(8,128)(2,1)S(1)} %shard_map.141.refs_10_.refs_0_), channel_id=1, source_target_pairs={{0,4},{4,0},{8,12},{12,8},{1,5},{5,1},{9,13},{13,9},{2,6},{6,2},{1... | collective-permute-start | bytes 196616 | tf_op jit(solution)/shard_map/ppermute | solution.py:157
  82.0 7.7 %collective-permute-start.30 = (bf16[128,896]{1,0:T(8,128)(2,1)S(1)}, bf16[128,896]{1,0:T(8,128)(2,1)S(1)}, u32[]{:S(2)}, u32[]{:S(2)}) collective-permute-start(bf16[128,896]{1,0:T(8,128)(2,1)S(1)} %shard_map.142.refs_10_), channel_id=1, source_target_pairs={{0,17},{1,19},{3,18},{2,16},{16,1},{17,3},{19,2},{18,0},{4,21},{5,... | collective-permute-start | bytes 688136 | tf_op jit(solution)/shard_map/ppermute | solution.py:180
  85.8 4.6 %collective-permute-start.31 = (bf16[128,896]{1,0:T(8,128)(2,1)S(1)}, bf16[128,896]{1,0:T(8,128)(2,1)S(1)}, u32[]{:S(2)}, u32[]{:S(2)}) collective-permute-start(bf16[128,896]{1,0:T(8,128)(2,1)S(1)} %shard_map.143.refs_7_), channel_id=1, source_target_pairs={{0,16},{16,0},{1,17},{17,1},{2,18},{18,2},{3,19},{19,3},{4,20},{20... | collective-permute-start | bytes 688136 | tf_op jit(solution)/shard_map/ppermute | solution.py:14
  88.1 1.6 %collective-permute-start.29 = (bf16[128,896]{1,0:T(8,128)(2,1)S(1)}, bf16[128,896]{1,0:T(8,128)(2,1)S(1)}, u32[]{:S(2)}, u32[]{:S(2)}) collective-permute-start(bf16[128,896]{1,0:T(8,128)(2,1)S(1)} %shard_map.144.refs_2_), channel_id=1, source_target_pairs={{0,16},{16,0},{1,17},{17,1},{2,18},{18,2},{3,19},{19,3},{4,20},{20... | collective-permute-start | bytes 688136 | tf_op jit(solution)/shard_map/ppermute | solution.py:14
  (14 other events, 46.4 us)

commit v8 on v7

--- a/solution.py
+++ b/solution.py
@@ -139,11 +139,13 @@
 
 
 CONTRACT_LAST = (((1,), (1,)), ((), ()))
+PLAIN = (((1,), (0,)), ((), ()))
 CONTRACT_FIRST = (((0,), (0,)), ((), ()))
 VMEM = pl.BlockSpec(memory_space=pltpu.VMEM)
 SMEM = pl.BlockSpec(memory_space=pltpu.SMEM)
 VMEM_BYTES = 14 << 20
 CF = 1.0
+TURN_DOWN = True
 SUM_COST = 1e10
 SPACE_COST = 10**10
 INFO_COST = 10**6
@@ -215,7 +217,7 @@
         sorted_rows[mask * rows : (mask + 1) * rows, :] = rows_ref[pl.ds(first, rows), :]
 
 
-def first_products(place, token_rows, grad_rows, weights, nodes, planes, after):
+def first_products(place, token_rows, grad_rows, weights, dims, nodes, planes, after):
     (count, width), hidden = token_rows.shape, weights[0].shape[1]
     share = count // nodes
 
@@ -226,7 +228,7 @@
         parts = (
             matmul(sorted_tokens[...], gate_ref[...]),
             matmul(sorted_tokens[...], up_ref[...]),
-            matmul(sorted_grads[...], down_ref[...], CONTRACT_LAST),
+            matmul(sorted_grads[...], down_ref[...], dims),
         )
         for index, part in enumerate(parts):
             for mask in range(nodes):
@@ -241,6 +243,14 @@
         [pltpu.VMEM((count, width), jnp.bfloat16)] * 2,
         6 * count * width * hidden,
     )
+
+
+def transposed(place, weight, after):
+    def body(place_ref, weight_ref, out):
+        out[...] = weight_ref[...].T
+
+    shape = jax.ShapeDtypeStruct(weight.shape[::-1], weight.dtype)
+    return call(body, place, (weight,), after, shape, [], 0)
 
 
 def activations(place, pieces, filled, after, extra=()):
@@ -481,7 +491,7 @@
 
 
 def backward_results(place, pieces, plane, w_gate, w_up, factors, info, chosen, added, after):
-    nodes, (_, share, hidden), width = len(pieces), pieces[0].shape, w_gate.shape[0]
+    nodes, (_, share, hidden), width = len(pieces), pieces[0].shape, w_gate.shape[1]
     count = share * nodes
 
     def body(place_ref, *refs):
@@ -493,8 +503,8 @@
         grad_hidden = joined[...].astype(jnp.float32)
         grad_gate = (grad_hidden * gate_factor[...]).astype(jnp.bfloat16)
         grad_up = (grad_hidden * up_factor[...]).astype(jnp.bfloat16)
-        result = matmul(grad_gate, gate_ref[...], CONTRACT_LAST)
-        result += matmul(grad_up, up_ref[...], CONTRACT_LAST)
+        result = matmul(grad_gate, gate_ref[...])
+        result += matmul(grad_up, up_ref[...])
         give(out, weight, result, added_refs)
 
     return call(
@@ -563,7 +573,8 @@
     done = []
 
     def exchange(own):
-        return [own[0]] + [across(own[mask % len(own)], "node", mask) for mask in range(1, nodes)]
+        arrived = [across(own[mask % len(own)], "node", mask) for mask in range(nodes - 1, 0, -1)]
+        return [own[0]] + arrived[::-1]
 
     factors = [None] * experts
 
@@ -573,9 +584,17 @@
         )
         done.append(factors[step][0])
 
+    first_weights = [weights, CONTRACT_LAST]
+    turned = [None, None]
+
+    def turn(index):
+        value = transposed(place, weights[index], done[-1:])
+        done.append(value)
+        return value
+
     def first(step, *after):
         sent[step] = first_products(
-            place, tokens[step], grads[step], weights, nodes, 5 if step > 1 else 3, (*done[-1:], *after)
+            place, tokens[step], grads[step], first_weights[0], first_weights[1], nodes, 5 if step > 1 else 3, (*done[-1:], *after)
         )
         done.append(sent[step][0])
         if step < 2:
@@ -607,7 +626,7 @@
             )
         else:
             value = backward_results(
-                place, *acts[1][step], *weights[:2], factors[step], grads[step], chosen, added, (*done[-1:], *after)
+                place, *acts[1][step], *turned, factors[step], grads[step], chosen, added, (*done[-1:], *after)
             )
         done.append(value)
         if step == 0:
@@ -620,10 +639,14 @@
             sums[kind].append(along_ring_and_sections(value, 1, shift))
 
     first(0)
+    if TURN_DOWN:
+        first_weights[:] = (*weights[:2], turn(2)), PLAIN
     first(1)
     own_acts = activations(place, parts[0], (), done[-1:])[0]
     done.append(own_acts)
     for step in range(1, experts - 1):
+        if step == experts - 2:
+            turned[:] = turn(0), turn(1)
         first(step + 1)
         prepare(step)
         middle(step)
@@ -641,11 +664,11 @@
     done.append(own_plane)
     acts[0][0] = (exchange([own_plane]), 0)
     last(experts - 1, 1)
+    last(0, 0)
     last(0, 1)
-    last(0, 0)
     outs = []
     for values, own in zip(sums, base):
-        total = sum_rows(values, (*done[-1:], *outs)) + own.astype(jnp.float32)
+        total = sum(value.astype(jnp.float32) for value in (sum_rows(values[-1:], (*done[-1:], *outs)), *values[:-1], own))
         outs.append(total.astype(jnp.bfloat16))
     return tuple(out[None] for out in outs)
 

time: 91.3 us -> 90.2 us (0.988)
  waiting for transfers between devices: 14.4 us -> 7.7 us
  starting transfers between devices: 43.9 us -> 48.3 us
    ppermute x8, waiting for transfers between devices: 7.21 us -> 1.95 us  [along_ring(): return lax.ppermute(value, 'dev', ring_pairs(lax.axis_size('dev'), steps))]
    ppermute x8, starting transfers between devices: 15.1 us -> 19.9 us  [along_ring(): return lax.ppermute(value, 'dev', ring_pairs(lax.axis_size('dev'), steps))]
    ppermute x18, waiting for transfers between devices: 5.78 us -> 4.09 us  [across(): lax.ppermute(value, axis, [(source, source ^ mask) for source in range(co...]
    ppermute x4, waiting for transfers between devices: 0.01 us -> 1.66 us  [along_ring_and_sections(): return lax.ppermute(value, ('section', 'dev'), pairs)]
    ppermute x2, waiting for transfers between devices: 1.4 us -> 0.01 us  [from_behind(): return lax.ppermute(value, axis, pairs)]
    ppermute x18, starting transfers between devices: 22.7 us -> 21.3 us  [across(): lax.ppermute(value, axis, [(source, source ^ mask) for source in range(co...]
    ppermute x4, starting transfers between devices: 4.77 us -> 5.9 us  [along_ring_and_sections(): return lax.ppermute(value, ('section', 'dev'), pairs)]
    pallas_call x21 -> x24, Pallas kernels: 26.3 us -> 26.6 us  [call(): pl.pallas_call(with_after, in_specs=[SMEM] + [VMEM] * len(operands) + [AN...]
  transfers between devices with their start and end apart: 32 -> 32, of which waited for: 9 -> 8; matrix products, arithmetic and copies ran while one was open for 0% -> 0% of each run, Pallas kernels for 28% -> 29%
where the time goes in v8:
time: 90.2 us; the launch traced here: 89.3 us
  starting transfers between devices  48.3 us (54%)
  Pallas kernels  26.6 us (29%)
  waiting for transfers between devices  7.7 us (9%)
  local copies, waits for them, and re-layouts  4.76 us (5%)
  between operations  1.05 us (1%)
  other arithmetic  0.92 us (1%)
    pallas_call x24, Pallas kernels, call(): pl.pallas_call(with_after, in_specs=[SMEM] + [VMEM] * len(operands) + [AN...  26.6 us
    ppermute x18, starting transfers between devices, across(): lax.ppermute(value, axis, [(source, source ^ mask) for source in range(co...  21.3 us
    ppermute x8, starting transfers between devices, along_ring(): return lax.ppermute(value, 'dev', ring_pairs(lax.axis_size('dev'), steps))  19.9 us
    ppermute x4, starting transfers between devices, along_ring_and_sections(): return lax.ppermute(value, ('section', 'dev'), pairs)  5.9 us
    unnamed x28, local copies, waits for them, and re-layouts  4.76 us
    ppermute x18, waiting for transfers between devices, across(): lax.ppermute(value, axis, [(source, source ^ mask) for source in range(co...  4.09 us
    ppermute x8, waiting for transfers between devices, along_ring(): return lax.ppermute(value, 'dev', ring_pairs(lax.axis_size('dev'), steps))  1.95 us
  transfers between devices with their start and end apart: 32, of which 8 were waited for; matrix products, arithmetic and copies ran while one was open for 0% of the time, Pallas kernels for 29%

profile of v8, /device:TPU:0, one launch (start us, length us, event | category | flops | bytes accessed | tf_op | source)
XLA Modules:
  0.0 89.3 jit_solution(6310914867143674583)
XLA Ops:
  1.6 3.1 %collective-permute-start.1 = (bf16[144,896]{1,0:T(8,128)(2,1)S(1)}, bf16[144,896]{1,0:T(8,128)(2,1)S(1)}, u32[]{:S(2)}, u32[]{:S(2)}) collective-permute-start(bf16[144,896]{1,0:T(8,128)(2,1)S(1)} %shard_map.123.refs_1_.refs_2_.refs_5_.refs_8_), channel_id=1, source_target_pairs={{0,1},{1,3},{3,2},{2,0},{4,5},{5,7},{7,6},{6,4},{8,9},{9,11},{11,1... | collective-permute-start | bytes 774152 | tf_op jit(solution)/shard_map/ppermute | solution.py:172
  4.7 2.6 %collective-permute-start = (bf16[128,896]{1,0:T(8,128)(2,1)S(1)}, bf16[128,896]{1,0:T(8,128)(2,1)S(1)}, u32[]{:S(2)}, u32[]{:S(2)}) collective-permute-start(bf16[128,896]{1,0:T(8,128)(2,1)S(1)} %bitcast.50), channel_id=1, source_target_pairs={{0,1},{1,3},{3,2},{2,0},{4,5},{5,7},{7,6},{6,4},{8,9},{9,11},{11,1... | collective-permute-start | bytes 688136 | tf_op jit(solution)/shard_map/ppermute | solution.py:172
  7.4 1.5 %copy-done.1 = bf16[1,1,896,1024]{3,2,1,0:T(8,128)(2,1)S(1)} copy-done((bf16[1,1,896,1024]{3,2,1,0:T(8,128)(2,1)S(1)}, bf16[1,1,896,1024]{3,2,1,0:T(8,128)(2,1)}, u32[]{:S(2)}) %copy-start.1) | copy-done | bytes 1835032
  8.9 1.5 %copy-done.3 = bf16[1,1,896,1024]{3,2,1,0:T(8,128)(2,1)S(1)} copy-done((bf16[1,1,896,1024]{3,2,1,0:T(8,128)(2,1)S(1)}, bf16[1,1,896,1024]{3,2,1,0:T(8,128)(2,1)}, u32[]{:S(2)}) %copy-start.3) | copy-done | bytes 1835032
  10.4 1.8 %shard_map.124 = (bf16[3,32,1024]{2,1,0:T(8,128)(2,1)S(1)}, bf16[3,32,1024]{2,1,0:T(8,128)(2,1)S(1)}, bf16[3,32,1024]{2,1,0:T(8,128)(2,1)S(1)}, bf16[3,32,1024]{2,1,0:T(8,128)(2,1)S(1)}) custom-call(s32[2]{0:T(128)S(1)} %pad_add_fusion.place_ref, bf16[128,896]{1,0:T(8,128)(2,1)S(1)} %bitcast.51, ...), custom_call_target="tpu_custom_call" | custom-call | flops 704643072 | bytes 5992448 | tf_op jit(solution)/shard_map/pallas_call | solution.py:197
  12.2 1.6 %collective-permute-start.7 = (bf16[3,32,1024]{2,1,0:T(8,128)(2,1)S(1)}, bf16[3,32,1024]{2,1,0:T(8,128)(2,1)S(1)}, u32[]{:S(2)}, u32[]{:S(2)}) collective-permute-start(bf16[3,32,1024]{2,1,0:T(8,128)(2,1)S(1)} %get-tuple-element.39), channel_id=1, source_target_pairs={{0,4},{4,0},{8,12},{12,8},{1,5},{5,1},{9,13},{13,9},{2,6},{6,2},{1... | collective-permute-start | bytes 589832 | tf_op jit(solution)/shard_map/ppermute | solution.py:159
  13.8 1.5 %collective-permute-start.8 = (bf16[3,32,1024]{2,1,0:T(8,128)(2,1)S(1)}, bf16[3,32,1024]{2,1,0:T(8,128)(2,1)S(1)}, u32[]{:S(2)}, u32[]{:S(2)}) collective-permute-start(bf16[3,32,1024]{2,1,0:T(8,128)(2,1)S(1)} %get-tuple-element.40), channel_id=1, source_target_pairs={{0,8},{4,12},{8,0},{12,4},{1,9},{5,13},{9,1},{13,5},{2,10},{6,14},... | collective-permute-start | bytes 589832 | tf_op jit(solution)/shard_map/ppermute | solution.py:159
  16.9 2.0 %collective-permute-start.5 = (bf16[128,896]{1,0:T(8,128)(2,1)S(1)}, bf16[128,896]{1,0:T(8,128)(2,1)S(1)}, u32[]{:S(2)}, u32[]{:S(2)}) collective-permute-start(bf16[128,896]{1,0:T(8,128)(2,1)S(1)} %collective-permute-done.refs_0_), channel_id=1, source_target_pairs={{0,1},{1,3},{3,2},{2,0},{4,5},{5,7},{7,6},{6,4},{8,9},{9,11},{11,1... | collective-permute-start | bytes 688136 | tf_op jit(solution)/shard_map/ppermute | solution.py:172
  20.3 1.6 %shard_map.126 = (bf16[3,32,1024]{2,1,0:T(8,128)(2,1)S(1)}, bf16[3,32,1024]{2,1,0:T(8,128)(2,1)S(1)}, bf16[3,32,1024]{2,1,0:T(8,128)(2,1)S(1)}, bf16[3,32,1024]{2,1,0:T(8,128)(2,1)S(1)}) custom-call(s32[2]{0:T(128)S(1)} %pad_add_fusion.place_ref, bf16[128,896]{1,0:T(8,128)(2,1)S(1)} %collective-permute-done.refs_0_, ...), custom_call_target="tpu_custom_call" | custom-call | flops 704643072 | bytes 5992448 | tf_op jit(solution)/shard_map/pallas_call | solution.py:197
  21.9 1.5 %collective-permute-start.2 = (bf16[3,32,1024]{2,1,0:T(8,128)(2,1)S(1)}, bf16[3,32,1024]{2,1,0:T(8,128)(2,1)S(1)}, u32[]{:S(2)}, u32[]{:S(2)}) collective-permute-start(bf16[3,32,1024]{2,1,0:T(8,128)(2,1)S(1)} %get-tuple-element.36), channel_id=1, source_target_pairs={{0,4},{4,0},{8,12},{12,8},{1,5},{5,1},{9,13},{13,9},{2,6},{6,2},{1... | collective-permute-start | bytes 589832 | tf_op jit(solution)/shard_map/ppermute | solution.py:159
  23.6 2.1 %collective-permute-start.3 = (bf16[3,32,1024]{2,1,0:T(8,128)(2,1)S(1)}, bf16[3,32,1024]{2,1,0:T(8,128)(2,1)S(1)}, u32[]{:S(2)}, u32[]{:S(2)}) collective-permute-start(bf16[3,32,1024]{2,1,0:T(8,128)(2,1)S(1)} %get-tuple-element.37), channel_id=1, source_target_pairs={{0,8},{4,12},{8,0},{12,4},{1,9},{5,13},{9,1},{13,5},{2,10},{6,14},... | collective-permute-start | bytes 589832 | tf_op jit(solution)/shard_map/ppermute | solution.py:159
  26.4 3.2 %collective-permute-start.14 = (bf16[144,896]{1,0:T(8,128)(2,1)S(1)}, bf16[144,896]{1,0:T(8,128)(2,1)S(1)}, u32[]{:S(2)}, u32[]{:S(2)}) collective-permute-start(bf16[144,896]{1,0:T(8,128)(2,1)S(1)} %collective-permute-done.6.refs_1_.refs_2_.refs_5_.refs_8_), channel_id=1, source_target_pairs={{0,1},{1,3},{3,2},{2,0},{4,5},{5,7},{7,6},{6,4},{8,9},{9,11},{11,1... | collective-permute-start | bytes 774152 | tf_op jit(solution)/shard_map/ppermute | solution.py:172
  29.6 1.5 %shard_map.128 = (bf16[5,32,1024]{2,1,0:T(8,128)(2,1)S(1)}, bf16[5,32,1024]{2,1,0:T(8,128)(2,1)S(1)}, bf16[5,32,1024]{2,1,0:T(8,128)(2,1)S(1)}, bf16[5,32,1024]{2,1,0:T(8,128)(2,1)S(1)}) custom-call(s32[2]{0:T(128)S(1)} %pad_add_fusion.place_ref, bf16[128,896]{1,0:T(8,128)(2,1)S(1)} %collective-permute-done.5.refs_0_, ...), custom_call_target="tpu_custom_call" | custom-call | flops 704643072 | bytes 5992448 | tf_op jit(solution)/shard_map/pallas_call | solution.py:197
  33.1 1.7 %collective-permute-start.10 = (bf16[5,32,1024]{2,1,0:T(8,128)(2,1)S(1)}, bf16[5,32,1024]{2,1,0:T(8,128)(2,1)S(1)}, u32[]{:S(2)}, u32[]{:S(2)}) collective-permute-start(bf16[5,32,1024]{2,1,0:T(8,128)(2,1)S(1)} %get-tuple-element.48), channel_id=1, source_target_pairs={{0,4},{4,0},{8,12},{12,8},{1,5},{5,1},{9,13},{13,9},{2,6},{6,2},{1... | collective-permute-start | bytes 983048 | tf_op jit(solution)/shard_map/ppermute | solution.py:159
  34.8 1.5 %collective-permute-start.11 = (bf16[5,32,1024]{2,1,0:T(8,128)(2,1)S(1)}, bf16[5,32,1024]{2,1,0:T(8,128)(2,1)S(1)}, u32[]{:S(2)}, u32[]{:S(2)}) collective-permute-start(bf16[5,32,1024]{2,1,0:T(8,128)(2,1)S(1)} %get-tuple-element.49), channel_id=1, source_target_pairs={{0,8},{4,12},{8,0},{12,4},{1,9},{5,13},{9,1},{13,5},{2,10},{6,14},... | collective-permute-start | bytes 983048 | tf_op jit(solution)/shard_map/ppermute | solution.py:159
  36.6 3.0 %collective-permute-start.13 = (bf16[128,896]{1,0:T(8,128)(2,1)S(1)}, bf16[128,896]{1,0:T(8,128)(2,1)S(1)}, u32[]{:S(2)}, u32[]{:S(2)}) collective-permute-start(bf16[128,896]{1,0:T(8,128)(2,1)S(1)} %collective-permute-done.5.refs_0_), channel_id=1, source_target_pairs={{0,1},{1,3},{3,2},{2,0},{4,5},{5,7},{7,6},{6,4},{8,9},{9,11},{11,1... | collective-permute-start | bytes 688136 | tf_op jit(solution)/shard_map/ppermute | solution.py:172
  42.2 1.3 %collective-permute-done.13.refs_0_ = bf16[128,896]{1,0:T(8,128)(2,1)S(1)} collective-permute-done((bf16[128,896]{1,0:T(8,128)(2,1)S(1)}, bf16[128,896]{1,0:T(8,128)(2,1)S(1)}, u32[]{:S(2)}, u32[]{:S(2)}) %collective-permute-start.13) | collective-permute-done | bytes 229408 | tf_op jit(solution)/shard_map/ppermute | solution.py:172
  43.5 1.6 %shard_map.133 = (bf16[5,32,1024]{2,1,0:T(8,128)(2,1)S(1)}, bf16[5,32,1024]{2,1,0:T(8,128)(2,1)S(1)}, bf16[5,32,1024]{2,1,0:T(8,128)(2,1)S(1)}, bf16[5,32,1024]{2,1,0:T(8,128)(2,1)S(1)}) custom-call(s32[2]{0:T(128)S(1)} %pad_add_fusion.place_ref, bf16[128,896]{1,0:T(8,128)(2,1)S(1)} %collective-permute-done.13.refs_0_, ...), custom_call_target="tpu_custom_call" | custom-call | flops 704643072 | bytes 5992448 | tf_op jit(solution)/shard_map/pallas_call | solution.py:197
  46.2 1.7 %collective-permute-done.11.refs_2_ = bf16[5,32,1024]{2,1,0:T(8,128)(2,1)S(1)} collective-permute-done((bf16[5,32,1024]{2,1,0:T(8,128)(2,1)S(1)}, bf16[5,32,1024]{2,1,0:T(8,128)(2,1)S(1)}, u32[]{:S(2)}, u32[]{:S(2)}) %collective-permute-start.11) | collective-permute-done | bytes 327712 | tf_op jit(solution)/shard_map/ppermute | solution.py:159
  48.6 1.4 %collective-permute-start.15 = (bf16[5,32,1024]{2,1,0:T(8,128)(2,1)S(1)}, bf16[5,32,1024]{2,1,0:T(8,128)(2,1)S(1)}, u32[]{:S(2)}, u32[]{:S(2)}) collective-permute-start(bf16[5,32,1024]{2,1,0:T(8,128)(2,1)S(1)} %get-tuple-element.57), channel_id=1, source_target_pairs={{0,4},{4,0},{8,12},{12,8},{1,5},{5,1},{9,13},{13,9},{2,6},{6,2},{1... | collective-permute-start | bytes 983048 | tf_op jit(solution)/shard_map/ppermute | solution.py:159
  53.1 1.3 %shard_map.137.refs_3_ = bf16[128,896]{1,0:T(8,128)(2,1)S(1)} custom-call(s32[2]{0:T(128)S(1)} %pad_add_fusion.place_ref, bf16[5,32,1024]{2,1,0:T(8,128)(2,1)S(1)} %get-tuple-element.47.refs_1_.refs_0_, bf16[5,32,1024]{2,1,0:T(8,128)(2,1)S(1)} %collective-permute-done.10.refs_1_, bf16[5,32,1024]{2,1,0:T(8,128)(2,1)S(1)} %collective-permute-done.11.refs_2_, ...), custom_call_target="tpu_custom_call" | custom-call | flops 469762048 | bytes 6287360 | tf_op jit(solution)/shard_map/pallas_call | solution.py:197
  54.5 3.6 %collective-permute-start.22 = (bf16[128,896]{1,0:T(8,128)(2,1)S(1)}, bf16[128,896]{1,0:T(8,128)(2,1)S(1)}, u32[]{:S(2)}, u32[]{:S(2)}) collective-permute-start(bf16[128,896]{1,0:T(8,128)(2,1)S(1)} %shard_map.136.refs_9_), channel_id=1, source_target_pairs={{0,18},{1,16},{3,17},{2,19},{16,2},{17,0},{19,1},{18,3},{4,22},{5,... | collective-permute-start | bytes 688136 | tf_op jit(solution)/shard_map/ppermute | solution.py:182
  60.3 1.4 %collective-permute-done.16.refs_2_ = bf16[5,32,1024]{2,1,0:T(8,128)(2,1)S(1)} collective-permute-done((bf16[5,32,1024]{2,1,0:T(8,128)(2,1)S(1)}, bf16[5,32,1024]{2,1,0:T(8,128)(2,1)S(1)}, u32[]{:S(2)}, u32[]{:S(2)}) %collective-permute-start.16) | collective-permute-done | bytes 327712 | tf_op jit(solution)/shard_map/ppermute | solution.py:159
  63.4 2.1 %collective-permute-start.21 = (bf16[128,896]{1,0:T(8,128)(2,1)S(1)}, bf16[128,896]{1,0:T(8,128)(2,1)S(1)}, u32[]{:S(2)}, u32[]{:S(2)}) collective-permute-start(bf16[128,896]{1,0:T(8,128)(2,1)S(1)} %shard_map.141.refs_9_), channel_id=1, source_target_pairs={{0,1},{1,3},{3,2},{2,0},{4,5},{5,7},{7,6},{6,4},{8,9},{9,11},{11,1... | collective-permute-start | bytes 688136 | tf_op jit(solution)/shard_map/ppermute | solution.py:172
  65.5 2.0 %collective-permute-start.20 = (bf16[3,32,1024]{2,1,0:T(8,128)(2,1)S(1)}, bf16[3,32,1024]{2,1,0:T(8,128)(2,1)S(1)}, u32[]{:S(2)}, u32[]{:S(2)}) collective-permute-start(bf16[3,32,1024]{2,1,0:T(8,128)(2,1)S(1)} %shard_map.140.refs_6_.refs_0_), channel_id=1, source_target_pairs={{0,12},{4,8},{8,4},{12,0},{1,13},{5,9},{9,5},{13,1},{2,14},{6,10},... | collective-permute-start | bytes 589832 | tf_op jit(solution)/shard_map/ppermute | solution.py:159
  69.0 1.3 %shard_map.142.refs_7_ = bf16[128,896]{1,0:T(8,128)(2,1)S(1)} custom-call(s32[2]{0:T(128)S(1)} %pad_add_fusion.place_ref, bf16[5,32,1024]{2,1,0:T(8,128)(2,1)S(1)} %get-tuple-element.56.refs_6_.refs_0_, bf16[5,32,1024]{2,1,0:T(8,128)(2,1)S(1)} %collective-permute-done.15.refs_1_, bf16[5,32,1024]{2,1,0:T(8,128)(2,1)S(1)} %collective-permute-done.16.refs_2_, ...), custom_call_target="tpu_custom_call" | custom-call | flops 469762048 | bytes 6287360 | tf_op jit(solution)/shard_map/pallas_call | solution.py:197
  70.3 3.5 %collective-permute-start.28 = (bf16[128,896]{1,0:T(8,128)(2,1)S(1)}, bf16[128,896]{1,0:T(8,128)(2,1)S(1)}, u32[]{:S(2)}, u32[]{:S(2)}) collective-permute-start(bf16[128,896]{1,0:T(8,128)(2,1)S(1)} %shard_map.142.refs_7_), channel_id=1, source_target_pairs={{0,1},{1,3},{3,2},{2,0},{4,5},{5,7},{7,6},{6,4},{8,9},{9,11},{11,1... | collective-permute-start | bytes 688136 | tf_op jit(solution)/shard_map/ppermute | solution.py:172
  75.9 2.1 %collective-permute-start.27 = (bf16[1,32,1024]{2,1,0:T(8,128)(2,1)S(1)}, bf16[1,32,1024]{2,1,0:T(8,128)(2,1)S(1)}, u32[]{:S(2)}, u32[]{:S(2)}) collective-permute-start(bf16[1,32,1024]{2,1,0:T(8,128)(2,1)S(1)} %shard_map.144.refs_10_.refs_0_), channel_id=1, source_target_pairs={{0,12},{4,8},{8,4},{12,0},{1,13},{5,9},{9,5},{13,1},{2,14},{6,10},... | collective-permute-start | bytes 196616 | tf_op jit(solution)/shard_map/ppermute | solution.py:159
  79.5 1.3 %shard_map.145.refs_7_ = bf16[128,896]{1,0:T(8,128)(2,1)S(1)} custom-call(s32[2]{0:T(128)S(1)} %pad_add_fusion.place_ref, bf16[3,32,1024]{2,1,0:T(8,128)(2,1)S(1)} %shard_map.140.refs_6_.refs_0_, bf16[3,32,1024]{2,1,0:T(8,128)(2,1)S(1)} %collective-permute-done.18.refs_1_.refs_2_, bf16[3,32,1024]{2,1,0:T(8,128)(2,1)S(1)} %collective-permute-done.19.refs_2_.refs_3_, ...), custom_call_target="tpu_custom_call" | custom-call | flops 469762048 | bytes 5992448 | tf_op jit(solution)/shard_map/pallas_call | solution.py:197
  80.8 2.2 %collective-permute-start.30 = (bf16[128,896]{1,0:T(8,128)(2,1)S(1)}, bf16[128,896]{1,0:T(8,128)(2,1)S(1)}, u32[]{:S(2)}, u32[]{:S(2)}) collective-permute-start(bf16[128,896]{1,0:T(8,128)(2,1)S(1)} %shard_map.145.refs_7_), channel_id=1, source_target_pairs={{0,17},{1,19},{3,18},{2,16},{16,1},{17,3},{19,2},{18,0},{4,21},{5,... | collective-permute-start | bytes 688136 | tf_op jit(solution)/shard_map/ppermute | solution.py:182
  85.3 1.3 %shard_map.147.refs_1_ = bf16[128,896]{1,0:T(8,128)(2,1)S(1)} custom-call(s32[2]{0:T(128)S(1)} %pad_add_fusion.place_ref, bf16[3,32,1024]{2,1,0:T(8,128)(2,1)S(1)} %shard_map.140.refs_6_.refs_0_, bf16[3,32,1024]{2,1,0:T(8,128)(2,1)S(1)} %collective-permute-done.18.refs_1_.refs_2_, bf16[3,32,1024]{2,1,0:T(8,128)(2,1)S(1)} %collective-permute-done.19.refs_2_.refs_3_, ...), custom_call_target="tpu_custom_call" | custom-call | flops 469762048 | bytes 5992448 | tf_op jit(solution)/shard_map/pallas_call | solution.py:197
  86.9 1.7 %collective-permute-done.30.refs_0_ = bf16[128,896]{1,0:T(8,128)(2,1)S(1)} collective-permute-done((bf16[128,896]{1,0:T(8,128)(2,1)S(1)}, bf16[128,896]{1,0:T(8,128)(2,1)S(1)}, u32[]{:S(2)}, u32[]{:S(2)}) %collective-permute-start.30) | collective-permute-done | bytes 229408 | tf_op jit(solution)/shard_map/ppermute | solution.py:182
  (91 shorter events, 26.9 us)
Async XLA Ops:
  1.6 14.1 %collective-permute-start.1 = (bf16[144,896]{1,0:T(8,128)(2,1)S(1)}, bf16[144,896]{1,0:T(8,128)(2,1)S(1)}, u32[]{:S(2)}, u32[]{:S(2)}) collective-permute-start(bf16[144,896]{1,0:T(8,128)(2,1)S(1)} %shard_map.123.refs_1_.refs_2_.refs_5_.refs_8_), channel_id=1, source_target_pairs={{0,1},{1,3},{3,2},{2,0},{4,5},{5,7},{7,6},{6,4},{8,9},{9,11},{11,1... | collective-permute-start | bytes 774152 | tf_op jit(solution)/shard_map/ppermute | solution.py:172
  4.7 12.1 %collective-permute-start = (bf16[128,896]{1,0:T(8,128)(2,1)S(1)}, bf16[128,896]{1,0:T(8,128)(2,1)S(1)}, u32[]{:S(2)}, u32[]{:S(2)}) collective-permute-start(bf16[128,896]{1,0:T(8,128)(2,1)S(1)} %bitcast.50), channel_id=1, source_target_pairs={{0,1},{1,3},{3,2},{2,0},{4,5},{5,7},{7,6},{6,4},{8,9},{9,11},{11,1... | collective-permute-start | bytes 688136 | tf_op jit(solution)/shard_map/ppermute | solution.py:172
  12.2 9.7 %collective-permute-start.7 = (bf16[3,32,1024]{2,1,0:T(8,128)(2,1)S(1)}, bf16[3,32,1024]{2,1,0:T(8,128)(2,1)S(1)}, u32[]{:S(2)}, u32[]{:S(2)}) collective-permute-start(bf16[3,32,1024]{2,1,0:T(8,128)(2,1)S(1)} %get-tuple-element.39), channel_id=1, source_target_pairs={{0,4},{4,0},{8,12},{12,8},{1,5},{5,1},{9,13},{13,9},{2,6},{6,2},{1... | collective-permute-start | bytes 589832 | tf_op jit(solution)/shard_map/ppermute | solution.py:159
  13.8 9.8 %collective-permute-start.8 = (bf16[3,32,1024]{2,1,0:T(8,128)(2,1)S(1)}, bf16[3,32,1024]{2,1,0:T(8,128)(2,1)S(1)}, u32[]{:S(2)}, u32[]{:S(2)}) collective-permute-start(bf16[3,32,1024]{2,1,0:T(8,128)(2,1)S(1)} %get-tuple-element.40), channel_id=1, source_target_pairs={{0,8},{4,12},{8,0},{12,4},{1,9},{5,13},{9,1},{13,5},{2,10},{6,14},... | collective-permute-start | bytes 589832 | tf_op jit(solution)/shard_map/ppermute | solution.py:159
  15.3 10.4 %collective-permute-start.9 = (bf16[3,32,1024]{2,1,0:T(8,128)(2,1)S(1)}, bf16[3,32,1024]{2,1,0:T(8,128)(2,1)S(1)}, u32[]{:S(2)}, u32[]{:S(2)}) collective-permute-start(bf16[3,32,1024]{2,1,0:T(8,128)(2,1)S(1)} %get-tuple-element.41), channel_id=1, source_target_pairs={{0,12},{4,8},{8,4},{12,0},{1,13},{5,9},{9,5},{13,1},{2,14},{6,10},... | collective-permute-start | bytes 589832 | tf_op jit(solution)/shard_map/ppermute | solution.py:159
  15.8 10.7 %collective-permute-start.6 = (bf16[144,896]{1,0:T(8,128)(2,1)S(1)}, bf16[144,896]{1,0:T(8,128)(2,1)S(1)}, u32[]{:S(2)}, u32[]{:S(2)}) collective-permute-start(bf16[144,896]{1,0:T(8,128)(2,1)S(1)} %collective-permute-done.1.refs_1_.refs_2_.refs_5_.refs_8_), channel_id=1, source_target_pairs={{0,1},{1,3},{3,2},{2,0},{4,5},{5,7},{7,6},{6,4},{8,9},{9,11},{11,1... | collective-permute-start | bytes 774152 | tf_op jit(solution)/shard_map/ppermute | solution.py:172
  16.9 12.8 %collective-permute-start.5 = (bf16[128,896]{1,0:T(8,128)(2,1)S(1)}, bf16[128,896]{1,0:T(8,128)(2,1)S(1)}, u32[]{:S(2)}, u32[]{:S(2)}) collective-permute-start(bf16[128,896]{1,0:T(8,128)(2,1)S(1)} %collective-permute-done.refs_0_), channel_id=1, source_target_pairs={{0,1},{1,3},{3,2},{2,0},{4,5},{5,7},{7,6},{6,4},{8,9},{9,11},{11,1... | collective-permute-start | bytes 688136 | tf_op jit(solution)/shard_map/ppermute | solution.py:172
  21.9 10.4 %collective-permute-start.2 = (bf16[3,32,1024]{2,1,0:T(8,128)(2,1)S(1)}, bf16[3,32,1024]{2,1,0:T(8,128)(2,1)S(1)}, u32[]{:S(2)}, u32[]{:S(2)}) collective-permute-start(bf16[3,32,1024]{2,1,0:T(8,128)(2,1)S(1)} %get-tuple-element.36), channel_id=1, source_target_pairs={{0,4},{4,0},{8,12},{12,8},{1,5},{5,1},{9,13},{13,9},{2,6},{6,2},{1... | collective-permute-start | bytes 589832 | tf_op jit(solution)/shard_map/ppermute | solution.py:159
  23.6 8.7 %collective-permute-start.3 = (bf16[3,32,1024]{2,1,0:T(8,128)(2,1)S(1)}, bf16[3,32,1024]{2,1,0:T(8,128)(2,1)S(1)}, u32[]{:S(2)}, u32[]{:S(2)}) collective-permute-start(bf16[3,32,1024]{2,1,0:T(8,128)(2,1)S(1)} %get-tuple-element.37), channel_id=1, source_target_pairs={{0,8},{4,12},{8,0},{12,4},{1,9},{5,13},{9,1},{13,5},{2,10},{6,14},... | collective-permute-start | bytes 589832 | tf_op jit(solution)/shard_map/ppermute | solution.py:159
  25.7 6.6 %collective-permute-start.4 = (bf16[3,32,1024]{2,1,0:T(8,128)(2,1)S(1)}, bf16[3,32,1024]{2,1,0:T(8,128)(2,1)S(1)}, u32[]{:S(2)}, u32[]{:S(2)}) collective-permute-start(bf16[3,32,1024]{2,1,0:T(8,128)(2,1)S(1)} %get-tuple-element.38), channel_id=1, source_target_pairs={{0,12},{4,8},{8,4},{12,0},{1,13},{5,9},{9,5},{13,1},{2,14},{6,10},... | collective-permute-start | bytes 589832 | tf_op jit(solution)/shard_map/ppermute | solution.py:159
  26.4 17.1 %collective-permute-start.14 = (bf16[144,896]{1,0:T(8,128)(2,1)S(1)}, bf16[144,896]{1,0:T(8,128)(2,1)S(1)}, u32[]{:S(2)}, u32[]{:S(2)}) collective-permute-start(bf16[144,896]{1,0:T(8,128)(2,1)S(1)} %collective-permute-done.6.refs_1_.refs_2_.refs_5_.refs_8_), channel_id=1, source_target_pairs={{0,1},{1,3},{3,2},{2,0},{4,5},{5,7},{7,6},{6,4},{8,9},{9,11},{11,1... | collective-permute-start | bytes 774152 | tf_op jit(solution)/shard_map/ppermute | solution.py:172
  33.1 13.2 %collective-permute-start.10 = (bf16[5,32,1024]{2,1,0:T(8,128)(2,1)S(1)}, bf16[5,32,1024]{2,1,0:T(8,128)(2,1)S(1)}, u32[]{:S(2)}, u32[]{:S(2)}) collective-permute-start(bf16[5,32,1024]{2,1,0:T(8,128)(2,1)S(1)} %get-tuple-element.48), channel_id=1, source_target_pairs={{0,4},{4,0},{8,12},{12,8},{1,5},{5,1},{9,13},{13,9},{2,6},{6,2},{1... | collective-permute-start | bytes 983048 | tf_op jit(solution)/shard_map/ppermute | solution.py:159
  34.8 13.1 %collective-permute-start.11 = (bf16[5,32,1024]{2,1,0:T(8,128)(2,1)S(1)}, bf16[5,32,1024]{2,1,0:T(8,128)(2,1)S(1)}, u32[]{:S(2)}, u32[]{:S(2)}) collective-permute-start(bf16[5,32,1024]{2,1,0:T(8,128)(2,1)S(1)} %get-tuple-element.49), channel_id=1, source_target_pairs={{0,8},{4,12},{8,0},{12,4},{1,9},{5,13},{9,1},{13,5},{2,10},{6,14},... | collective-permute-start | bytes 983048 | tf_op jit(solution)/shard_map/ppermute | solution.py:159
  36.3 11.6 %collective-permute-start.12 = (bf16[5,32,1024]{2,1,0:T(8,128)(2,1)S(1)}, bf16[5,32,1024]{2,1,0:T(8,128)(2,1)S(1)}, u32[]{:S(2)}, u32[]{:S(2)}) collective-permute-start(bf16[5,32,1024]{2,1,0:T(8,128)(2,1)S(1)} %get-tuple-element.50), channel_id=1, source_target_pairs={{0,12},{4,8},{8,4},{12,0},{1,13},{5,9},{9,5},{13,1},{2,14},{6,10},... | collective-permute-start | bytes 983048 | tf_op jit(solution)/shard_map/ppermute | solution.py:159
  36.6 6.9 %collective-permute-start.13 = (bf16[128,896]{1,0:T(8,128)(2,1)S(1)}, bf16[128,896]{1,0:T(8,128)(2,1)S(1)}, u32[]{:S(2)}, u32[]{:S(2)}) collective-permute-start(bf16[128,896]{1,0:T(8,128)(2,1)S(1)} %collective-permute-done.5.refs_0_), channel_id=1, source_target_pairs={{0,1},{1,3},{3,2},{2,0},{4,5},{5,7},{7,6},{6,4},{8,9},{9,11},{11,1... | collective-permute-start | bytes 688136 | tf_op jit(solution)/shard_map/ppermute | solution.py:172
  48.6 11.7 %collective-permute-start.15 = (bf16[5,32,1024]{2,1,0:T(8,128)(2,1)S(1)}, bf16[5,32,1024]{2,1,0:T(8,128)(2,1)S(1)}, u32[]{:S(2)}, u32[]{:S(2)}) collective-permute-start(bf16[5,32,1024]{2,1,0:T(8,128)(2,1)S(1)} %get-tuple-element.57), channel_id=1, source_target_pairs={{0,4},{4,0},{8,12},{12,8},{1,5},{5,1},{9,13},{13,9},{2,6},{6,2},{1... | collective-permute-start | bytes 983048 | tf_op jit(solution)/shard_map/ppermute | solution.py:159
  50.0 11.7 %collective-permute-start.16 = (bf16[5,32,1024]{2,1,0:T(8,128)(2,1)S(1)}, bf16[5,32,1024]{2,1,0:T(8,128)(2,1)S(1)}, u32[]{:S(2)}, u32[]{:S(2)}) collective-permute-start(bf16[5,32,1024]{2,1,0:T(8,128)(2,1)S(1)} %get-tuple-element.58), channel_id=1, source_target_pairs={{0,8},{4,12},{8,0},{12,4},{1,9},{5,13},{9,1},{13,5},{2,10},{6,14},... | collective-permute-start | bytes 983048 | tf_op jit(solution)/shard_map/ppermute | solution.py:159
  51.0 10.8 %collective-permute-start.17 = (bf16[5,32,1024]{2,1,0:T(8,128)(2,1)S(1)}, bf16[5,32,1024]{2,1,0:T(8,128)(2,1)S(1)}, u32[]{:S(2)}, u32[]{:S(2)}) collective-permute-start(bf16[5,32,1024]{2,1,0:T(8,128)(2,1)S(1)} %get-tuple-element.59), channel_id=1, source_target_pairs={{0,12},{4,8},{8,4},{12,0},{1,13},{5,9},{9,5},{13,1},{2,14},{6,10},... | collective-permute-start | bytes 983048 | tf_op jit(solution)/shard_map/ppermute | solution.py:159
  54.4 13.8 %collective-permute-start.23 = (bf16[128,896]{1,0:T(8,128)(2,1)S(1)}, bf16[128,896]{1,0:T(8,128)(2,1)S(1)}, u32[]{:S(2)}, u32[]{:S(2)}) collective-permute-start(bf16[128,896]{1,0:T(8,128)(2,1)S(1)} %shard_map.137.refs_3_), channel_id=1, source_target_pairs={{0,18},{1,16},{3,17},{2,19},{16,2},{17,0},{19,1},{18,3},{4,22},{5,... | collective-permute-start | bytes 688136 | tf_op jit(solution)/shard_map/ppermute | solution.py:182
  54.5 14.6 %collective-permute-start.22 = (bf16[128,896]{1,0:T(8,128)(2,1)S(1)}, bf16[128,896]{1,0:T(8,128)(2,1)S(1)}, u32[]{:S(2)}, u32[]{:S(2)}) collective-permute-start(bf16[128,896]{1,0:T(8,128)(2,1)S(1)} %shard_map.136.refs_9_), channel_id=1, source_target_pairs={{0,18},{1,16},{3,17},{2,19},{16,2},{17,0},{19,1},{18,3},{4,22},{5,... | collective-permute-start | bytes 688136 | tf_op jit(solution)/shard_map/ppermute | solution.py:182
  63.4 10.9 %collective-permute-start.21 = (bf16[128,896]{1,0:T(8,128)(2,1)S(1)}, bf16[128,896]{1,0:T(8,128)(2,1)S(1)}, u32[]{:S(2)}, u32[]{:S(2)}) collective-permute-start(bf16[128,896]{1,0:T(8,128)(2,1)S(1)} %shard_map.141.refs_9_), channel_id=1, source_target_pairs={{0,1},{1,3},{3,2},{2,0},{4,5},{5,7},{7,6},{6,4},{8,9},{9,11},{11,1... | collective-permute-start | bytes 688136 | tf_op jit(solution)/shard_map/ppermute | solution.py:172
  65.5 8.3 %collective-permute-start.20 = (bf16[3,32,1024]{2,1,0:T(8,128)(2,1)S(1)}, bf16[3,32,1024]{2,1,0:T(8,128)(2,1)S(1)}, u32[]{:S(2)}, u32[]{:S(2)}) collective-permute-start(bf16[3,32,1024]{2,1,0:T(8,128)(2,1)S(1)} %shard_map.140.refs_6_.refs_0_), channel_id=1, source_target_pairs={{0,12},{4,8},{8,4},{12,0},{1,13},{5,9},{9,5},{13,1},{2,14},{6,10},... | collective-permute-start | bytes 589832 | tf_op jit(solution)/shard_map/ppermute | solution.py:159
  67.6 6.6 %collective-permute-start.19 = (bf16[3,32,1024]{2,1,0:T(8,128)(2,1)S(1)}, bf16[3,32,1024]{2,1,0:T(8,128)(2,1)S(1)}, u32[]{:S(2)}, u32[]{:S(2)}) collective-permute-start(bf16[3,32,1024]{2,1,0:T(8,128)(2,1)S(1)} %shard_map.140.refs_6_.refs_0_), channel_id=1, source_target_pairs={{0,8},{4,12},{8,0},{12,4},{1,9},{5,13},{9,1},{13,5},{2,10},{6,14},... | collective-permute-start | bytes 589832 | tf_op jit(solution)/shard_map/ppermute | solution.py:159
  68.2 6.1 %collective-permute-start.18 = (bf16[3,32,1024]{2,1,0:T(8,128)(2,1)S(1)}, bf16[3,32,1024]{2,1,0:T(8,128)(2,1)S(1)}, u32[]{:S(2)}, u32[]{:S(2)}) collective-permute-start(bf16[3,32,1024]{2,1,0:T(8,128)(2,1)S(1)} %shard_map.140.refs_6_.refs_0_), channel_id=1, source_target_pairs={{0,4},{4,0},{8,12},{12,8},{1,5},{5,1},{9,13},{13,9},{2,6},{6,2},{1... | collective-permute-start | bytes 589832 | tf_op jit(solution)/shard_map/ppermute | solution.py:159
  70.3 9.1 %collective-permute-start.28 = (bf16[128,896]{1,0:T(8,128)(2,1)S(1)}, bf16[128,896]{1,0:T(8,128)(2,1)S(1)}, u32[]{:S(2)}, u32[]{:S(2)}) collective-permute-start(bf16[128,896]{1,0:T(8,128)(2,1)S(1)} %shard_map.142.refs_7_), channel_id=1, source_target_pairs={{0,1},{1,3},{3,2},{2,0},{4,5},{5,7},{7,6},{6,4},{8,9},{9,11},{11,1... | collective-permute-start | bytes 688136 | tf_op jit(solution)/shard_map/ppermute | solution.py:172
  75.3 11.4 %collective-permute-start.24 = (bf16[128,896]{1,0:T(8,128)(2,1)S(1)}, bf16[128,896]{1,0:T(8,128)(2,1)S(1)}, u32[]{:S(2)}, u32[]{:S(2)}) collective-permute-start(bf16[128,896]{1,0:T(8,128)(2,1)S(1)} %shard_map.143.refs_1_), channel_id=1, source_target_pairs={{0,17},{1,19},{3,18},{2,16},{16,1},{17,3},{19,2},{18,0},{4,21},{5,... | collective-permute-start | bytes 688136 | tf_op jit(solution)/shard_map/ppermute | solution.py:182
  75.9 7.0 %collective-permute-start.27 = (bf16[1,32,1024]{2,1,0:T(8,128)(2,1)S(1)}, bf16[1,32,1024]{2,1,0:T(8,128)(2,1)S(1)}, u32[]{:S(2)}, u32[]{:S(2)}) collective-permute-start(bf16[1,32,1024]{2,1,0:T(8,128)(2,1)S(1)} %shard_map.144.refs_10_.refs_0_), channel_id=1, source_target_pairs={{0,12},{4,8},{8,4},{12,0},{1,13},{5,9},{9,5},{13,1},{2,14},{6,10},... | collective-permute-start | bytes 196616 | tf_op jit(solution)/shard_map/ppermute | solution.py:159
  78.0 5.0 %collective-permute-start.26 = (bf16[1,32,1024]{2,1,0:T(8,128)(2,1)S(1)}, bf16[1,32,1024]{2,1,0:T(8,128)(2,1)S(1)}, u32[]{:S(2)}, u32[]{:S(2)}) collective-permute-start(bf16[1,32,1024]{2,1,0:T(8,128)(2,1)S(1)} %shard_map.144.refs_10_.refs_0_), channel_id=1, source_target_pairs={{0,8},{4,12},{8,0},{12,4},{1,9},{5,13},{9,1},{13,5},{2,10},{6,14},... | collective-permute-start | bytes 196616 | tf_op jit(solution)/shard_map/ppermute | solution.py:159
  78.6 4.7 %collective-permute-start.25 = (bf16[1,32,1024]{2,1,0:T(8,128)(2,1)S(1)}, bf16[1,32,1024]{2,1,0:T(8,128)(2,1)S(1)}, u32[]{:S(2)}, u32[]{:S(2)}) collective-permute-start(bf16[1,32,1024]{2,1,0:T(8,128)(2,1)S(1)} %shard_map.144.refs_10_.refs_0_), channel_id=1, source_target_pairs={{0,4},{4,0},{8,12},{12,8},{1,5},{5,1},{9,13},{13,9},{2,6},{6,2},{1... | collective-permute-start | bytes 196616 | tf_op jit(solution)/shard_map/ppermute | solution.py:159
  80.8 7.8 %collective-permute-start.30 = (bf16[128,896]{1,0:T(8,128)(2,1)S(1)}, bf16[128,896]{1,0:T(8,128)(2,1)S(1)}, u32[]{:S(2)}, u32[]{:S(2)}) collective-permute-start(bf16[128,896]{1,0:T(8,128)(2,1)S(1)} %shard_map.145.refs_7_), channel_id=1, source_target_pairs={{0,17},{1,19},{3,18},{2,16},{16,1},{17,3},{19,2},{18,0},{4,21},{5,... | collective-permute-start | bytes 688136 | tf_op jit(solution)/shard_map/ppermute | solution.py:182
  84.3 2.5 %collective-permute-start.29 = (bf16[128,896]{1,0:T(8,128)(2,1)S(1)}, bf16[128,896]{1,0:T(8,128)(2,1)S(1)}, u32[]{:S(2)}, u32[]{:S(2)}) collective-permute-start(bf16[128,896]{1,0:T(8,128)(2,1)S(1)} %shard_map.146.refs_10_), channel_id=1, source_target_pairs={{0,16},{16,0},{1,17},{17,1},{2,18},{18,2},{3,19},{19,3},{4,20},{20... | collective-permute-start | bytes 688136 | tf_op jit(solution)/shard_map/ppermute | solution.py:14
  86.6 1.9 %collective-permute-start.31 = (bf16[128,896]{1,0:T(8,128)(2,1)S(1)}, bf16[128,896]{1,0:T(8,128)(2,1)S(1)}, u32[]{:S(2)}, u32[]{:S(2)}) collective-permute-start(bf16[128,896]{1,0:T(8,128)(2,1)S(1)} %shard_map.147.refs_1_), channel_id=1, source_target_pairs={{0,16},{16,0},{1,17},{17,1},{2,18},{18,2},{3,19},{19,3},{4,20},{20... | collective-permute-start | bytes 688136 | tf_op jit(solution)/shard_map/ppermute | solution.py:14
  (14 other events, 32.1 us)

commit v9 on v8

--- a/solution.py
+++ b/solution.py
@@ -144,14 +144,10 @@
 VMEM = pl.BlockSpec(memory_space=pltpu.VMEM)
 SMEM = pl.BlockSpec(memory_space=pltpu.SMEM)
 VMEM_BYTES = 14 << 20
-CF = 1.0
-TURN_DOWN = True
 SUM_COST = 1e10
 SPACE_COST = 10**10
 INFO_COST = 10**6
-WIDE_BYTES = 56 << 20
 ANY = pl.BlockSpec(memory_space=pl.ANY)
-HBM = pl.BlockSpec(memory_space=pltpu.HBM)
 
 
 def across(value, axis, mask):
@@ -201,7 +197,7 @@
         scratch_shapes=scratch,
         out_shape=out_shape,
         input_output_aliases={index + 1: out for index, out in aliases.items()},
-        cost_estimate=pl.CostEstimate(flops=int(CF * flops), bytes_accessed=int(CF * touched), transcendentals=0),
+        cost_estimate=pl.CostEstimate(flops=flops, bytes_accessed=touched, transcendentals=0),
         compiler_params=pltpu.CompilerParams(vmem_limit_bytes=VMEM_BYTES),
     )(place, *operands, *after)
 
@@ -299,16 +295,6 @@
         joined[pl.ds(first, rows), :] = ref[index]
 
 
-def copied(sources, targets, sems):
-    copies = [
-        pltpu.make_async_copy(source, target, sems.at[index])
-        for index, (source, target) in enumerate(zip(sources, targets))
-    ]
-    for copy in copies:
-        copy.start()
-    return copies
-
-
 def with_info(rows, routes, gates, after):
     (count, width), chosen = rows.shape, routes[0].shape[0]
     height = -(-6 * chosen // 16) * 16
@@ -346,59 +332,6 @@
         cost_estimate=pl.CostEstimate(flops=SPACE_COST, bytes_accessed=SPACE_COST // 100, transcendentals=0),
         compiler_params=pltpu.CompilerParams(vmem_limit_bytes=1 << 20),
     )()
-
-
-def opening_products(place, token_rows, grad_rows, weights, nodes):
-    (count, width), hidden = grad_rows.shape, weights[0].shape[1]
-    share = count // nodes
-    operands = (token_rows, weights[0], weights[1], grad_rows, weights[2])
-    cuts = 4
-
-    def body(place_ref, *refs):
-        inputs, pieces, held = refs[:5], refs[5 : 5 + nodes], refs[5 + nodes : 10 + nodes]
-        sorted_rows, sems = refs[10 + nodes :]
-
-        def pieces_of(ref):
-            rows = ref.shape[0] // cuts
-            return [ref.at[pl.ds(cut * rows, rows)] for cut in range(cuts)]
-
-        parts = [
-            copied(pieces_of(source), pieces_of(target), sems.at[index])
-            for index, (source, target) in enumerate(zip(inputs, held))
-        ]
-
-        def wait(index):
-            for copy in parts[index]:
-                copy.wait()
-
-        def give(index, part):
-            for mask in range(nodes):
-                pieces[mask][index] = part[mask * share : (mask + 1) * share].astype(jnp.bfloat16)
-
-        wait(0)
-        by_owner(place_ref, held[0], sorted_rows, nodes)
-        for index in (0, 1):
-            wait(index + 1)
-            give(index, matmul(sorted_rows[...], held[index + 1][...]))
-        wait(3)
-        by_owner(place_ref, held[3], sorted_rows, nodes)
-        wait(4)
-        give(2, matmul(sorted_rows[...], held[4][...], CONTRACT_LAST))
-
-    return pl.pallas_call(
-        body,
-        in_specs=[SMEM] + [HBM] * 5,
-        out_specs=[VMEM] * nodes,
-        out_shape=[jax.ShapeDtypeStruct((3, share, hidden), jnp.bfloat16)] * nodes,
-        scratch_shapes=[pltpu.VMEM(value.shape, value.dtype) for value in operands]
-        + [pltpu.VMEM((count, width), jnp.bfloat16), pltpu.SemaphoreType.DMA((5, cuts))],
-        cost_estimate=pl.CostEstimate(
-            flops=int(CF * 6 * count * width * hidden),
-            bytes_accessed=int(CF * 6 * width * hidden),
-            transcendentals=0,
-        ),
-        compiler_params=pltpu.CompilerParams(vmem_limit_bytes=WIDE_BYTES),
-    )(place, *operands)
 
 
 def info_of(ref, count, chosen, which):
@@ -639,8 +572,7 @@
             sums[kind].append(along_ring_and_sections(value, 1, shift))
 
     first(0)
-    if TURN_DOWN:
-        first_weights[:] = (*weights[:2], turn(2)), PLAIN
+    first_weights[:] = (*weights[:2], turn(2)), PLAIN
     first(1)
     own_acts = activations(place, parts[0], (), done[-1:])[0]
     done.append(own_acts)
@@ -680,7 +612,8 @@
 def shards(*args):
     experts, nodes = lax.axis_size("dev"), lax.axis_size("node")
     tokens, capacity = args[0].shape[1], args[9].shape[2] // experts
-    if capacity == tokens and experts > 1 and power_of_two(nodes) and tokens % (16 * nodes) == 0:
+    fits = tokens <= args[0].shape[2]
+    if fits and capacity == tokens and experts > 1 and power_of_two(nodes) and tokens % (16 * nodes) == 0:
         return ring_shards(*args)
     return shards_by_slots(*args)
 

time: 90.2 us -> 90.2 us (level)
  no operation moved by 1% of the time
where the time goes in v9:
time: 90.2 us; the launch traced here: 89.3 us
  starting transfers between devices  48.3 us (54%)
  Pallas kernels  26.6 us (29%)
  waiting for transfers between devices  7.7 us (9%)
  local copies, waits for them, and re-layouts  4.76 us (5%)
  between operations  1.05 us (1%)
  other arithmetic  0.92 us (1%)
    pallas_call x24, Pallas kernels, call(): pl.pallas_call(with_after, in_specs=[SMEM] + [VMEM] * len(operands) + [AN...  26.6 us
    ppermute x18, starting transfers between devices, across(): lax.ppermute(value, axis, [(source, source ^ mask) for source in range(co...  21.3 us
    ppermute x8, starting transfers between devices, along_ring(): return lax.ppermute(value, 'dev', ring_pairs(lax.axis_size('dev'), steps))  19.9 us
    ppermute x4, starting transfers between devices, along_ring_and_sections(): return lax.ppermute(value, ('section', 'dev'), pairs)  5.9 us
    unnamed x28, local copies, waits for them, and re-layouts  4.76 us
    ppermute x18, waiting for transfers between devices, across(): lax.ppermute(value, axis, [(source, source ^ mask) for source in range(co...  4.09 us
    ppermute x8, waiting for transfers between devices, along_ring(): return lax.ppermute(value, 'dev', ring_pairs(lax.axis_size('dev'), steps))  1.95 us
  transfers between devices with their start and end apart: 32, of which 8 were waited for; matrix products, arithmetic and copies ran while one was open for 0% of the time, Pallas kernels for 29%

profile of v9, /device:TPU:0, one launch (start us, length us, event | category | flops | bytes accessed | tf_op | source)
XLA Modules:
  0.0 89.3 jit_solution(6310914867143674583)
XLA Ops:
  1.6 3.1 %collective-permute-start.1 = (bf16[144,896]{1,0:T(8,128)(2,1)S(1)}, bf16[144,896]{1,0:T(8,128)(2,1)S(1)}, u32[]{:S(2)}, u32[]{:S(2)}) collective-permute-start(bf16[144,896]{1,0:T(8,128)(2,1)S(1)} %shard_map.123.refs_1_.refs_2_.refs_5_.refs_8_), channel_id=1, source_target_pairs={{0,1},{1,3},{3,2},{2,0},{4,5},{5,7},{7,6},{6,4},{8,9},{9,11},{11,1... | collective-permute-start | bytes 774152 | tf_op jit(solution)/shard_map/ppermute | solution.py:168
  4.7 2.6 %collective-permute-start = (bf16[128,896]{1,0:T(8,128)(2,1)S(1)}, bf16[128,896]{1,0:T(8,128)(2,1)S(1)}, u32[]{:S(2)}, u32[]{:S(2)}) collective-permute-start(bf16[128,896]{1,0:T(8,128)(2,1)S(1)} %bitcast.50), channel_id=1, source_target_pairs={{0,1},{1,3},{3,2},{2,0},{4,5},{5,7},{7,6},{6,4},{8,9},{9,11},{11,1... | collective-permute-start | bytes 688136 | tf_op jit(solution)/shard_map/ppermute | solution.py:168
  7.4 1.5 %copy-done.1 = bf16[1,1,896,1024]{3,2,1,0:T(8,128)(2,1)S(1)} copy-done((bf16[1,1,896,1024]{3,2,1,0:T(8,128)(2,1)S(1)}, bf16[1,1,896,1024]{3,2,1,0:T(8,128)(2,1)}, u32[]{:S(2)}) %copy-start.1) | copy-done | bytes 1835032
  8.9 1.5 %copy-done.3 = bf16[1,1,896,1024]{3,2,1,0:T(8,128)(2,1)S(1)} copy-done((bf16[1,1,896,1024]{3,2,1,0:T(8,128)(2,1)S(1)}, bf16[1,1,896,1024]{3,2,1,0:T(8,128)(2,1)}, u32[]{:S(2)}) %copy-start.3) | copy-done | bytes 1835032
  10.4 1.8 %shard_map.124 = (bf16[3,32,1024]{2,1,0:T(8,128)(2,1)S(1)}, bf16[3,32,1024]{2,1,0:T(8,128)(2,1)S(1)}, bf16[3,32,1024]{2,1,0:T(8,128)(2,1)S(1)}, bf16[3,32,1024]{2,1,0:T(8,128)(2,1)S(1)}) custom-call(s32[2]{0:T(128)S(1)} %pad_add_fusion.place_ref, bf16[128,896]{1,0:T(8,128)(2,1)S(1)} %bitcast.51, ...), custom_call_target="tpu_custom_call" | custom-call | flops 704643072 | bytes 5992448 | tf_op jit(solution)/shard_map/pallas_call | solution.py:193
  12.2 1.6 %collective-permute-start.7 = (bf16[3,32,1024]{2,1,0:T(8,128)(2,1)S(1)}, bf16[3,32,1024]{2,1,0:T(8,128)(2,1)S(1)}, u32[]{:S(2)}, u32[]{:S(2)}) collective-permute-start(bf16[3,32,1024]{2,1,0:T(8,128)(2,1)S(1)} %get-tuple-element.39), channel_id=1, source_target_pairs={{0,4},{4,0},{8,12},{12,8},{1,5},{5,1},{9,13},{13,9},{2,6},{6,2},{1... | collective-permute-start | bytes 589832 | tf_op jit(solution)/shard_map/ppermute | solution.py:155
  13.8 1.5 %collective-permute-start.8 = (bf16[3,32,1024]{2,1,0:T(8,128)(2,1)S(1)}, bf16[3,32,1024]{2,1,0:T(8,128)(2,1)S(1)}, u32[]{:S(2)}, u32[]{:S(2)}) collective-permute-start(bf16[3,32,1024]{2,1,0:T(8,128)(2,1)S(1)} %get-tuple-element.40), channel_id=1, source_target_pairs={{0,8},{4,12},{8,0},{12,4},{1,9},{5,13},{9,1},{13,5},{2,10},{6,14},... | collective-permute-start | bytes 589832 | tf_op jit(solution)/shard_map/ppermute | solution.py:155
  16.9 2.0 %collective-permute-start.5 = (bf16[128,896]{1,0:T(8,128)(2,1)S(1)}, bf16[128,896]{1,0:T(8,128)(2,1)S(1)}, u32[]{:S(2)}, u32[]{:S(2)}) collective-permute-start(bf16[128,896]{1,0:T(8,128)(2,1)S(1)} %collective-permute-done.refs_0_), channel_id=1, source_target_pairs={{0,1},{1,3},{3,2},{2,0},{4,5},{5,7},{7,6},{6,4},{8,9},{9,11},{11,1... | collective-permute-start | bytes 688136 | tf_op jit(solution)/shard_map/ppermute | solution.py:168
  20.3 1.6 %shard_map.126 = (bf16[3,32,1024]{2,1,0:T(8,128)(2,1)S(1)}, bf16[3,32,1024]{2,1,0:T(8,128)(2,1)S(1)}, bf16[3,32,1024]{2,1,0:T(8,128)(2,1)S(1)}, bf16[3,32,1024]{2,1,0:T(8,128)(2,1)S(1)}) custom-call(s32[2]{0:T(128)S(1)} %pad_add_fusion.place_ref, bf16[128,896]{1,0:T(8,128)(2,1)S(1)} %collective-permute-done.refs_0_, ...), custom_call_target="tpu_custom_call" | custom-call | flops 704643072 | bytes 5992448 | tf_op jit(solution)/shard_map/pallas_call | solution.py:193
  21.9 1.5 %collective-permute-start.2 = (bf16[3,32,1024]{2,1,0:T(8,128)(2,1)S(1)}, bf16[3,32,1024]{2,1,0:T(8,128)(2,1)S(1)}, u32[]{:S(2)}, u32[]{:S(2)}) collective-permute-start(bf16[3,32,1024]{2,1,0:T(8,128)(2,1)S(1)} %get-tuple-element.36), channel_id=1, source_target_pairs={{0,4},{4,0},{8,12},{12,8},{1,5},{5,1},{9,13},{13,9},{2,6},{6,2},{1... | collective-permute-start | bytes 589832 | tf_op jit(solution)/shard_map/ppermute | solution.py:155
  23.6 2.1 %collective-permute-start.3 = (bf16[3,32,1024]{2,1,0:T(8,128)(2,1)S(1)}, bf16[3,32,1024]{2,1,0:T(8,128)(2,1)S(1)}, u32[]{:S(2)}, u32[]{:S(2)}) collective-permute-start(bf16[3,32,1024]{2,1,0:T(8,128)(2,1)S(1)} %get-tuple-element.37), channel_id=1, source_target_pairs={{0,8},{4,12},{8,0},{12,4},{1,9},{5,13},{9,1},{13,5},{2,10},{6,14},... | collective-permute-start | bytes 589832 | tf_op jit(solution)/shard_map/ppermute | solution.py:155
  26.4 3.2 %collective-permute-start.14 = (bf16[144,896]{1,0:T(8,128)(2,1)S(1)}, bf16[144,896]{1,0:T(8,128)(2,1)S(1)}, u32[]{:S(2)}, u32[]{:S(2)}) collective-permute-start(bf16[144,896]{1,0:T(8,128)(2,1)S(1)} %collective-permute-done.6.refs_1_.refs_2_.refs_5_.refs_8_), channel_id=1, source_target_pairs={{0,1},{1,3},{3,2},{2,0},{4,5},{5,7},{7,6},{6,4},{8,9},{9,11},{11,1... | collective-permute-start | bytes 774152 | tf_op jit(solution)/shard_map/ppermute | solution.py:168
  29.6 1.5 %shard_map.128 = (bf16[5,32,1024]{2,1,0:T(8,128)(2,1)S(1)}, bf16[5,32,1024]{2,1,0:T(8,128)(2,1)S(1)}, bf16[5,32,1024]{2,1,0:T(8,128)(2,1)S(1)}, bf16[5,32,1024]{2,1,0:T(8,128)(2,1)S(1)}) custom-call(s32[2]{0:T(128)S(1)} %pad_add_fusion.place_ref, bf16[128,896]{1,0:T(8,128)(2,1)S(1)} %collective-permute-done.5.refs_0_, ...), custom_call_target="tpu_custom_call" | custom-call | flops 704643072 | bytes 5992448 | tf_op jit(solution)/shard_map/pallas_call | solution.py:193
  33.1 1.7 %collective-permute-start.10 = (bf16[5,32,1024]{2,1,0:T(8,128)(2,1)S(1)}, bf16[5,32,1024]{2,1,0:T(8,128)(2,1)S(1)}, u32[]{:S(2)}, u32[]{:S(2)}) collective-permute-start(bf16[5,32,1024]{2,1,0:T(8,128)(2,1)S(1)} %get-tuple-element.48), channel_id=1, source_target_pairs={{0,4},{4,0},{8,12},{12,8},{1,5},{5,1},{9,13},{13,9},{2,6},{6,2},{1... | collective-permute-start | bytes 983048 | tf_op jit(solution)/shard_map/ppermute | solution.py:155
  34.8 1.5 %collective-permute-start.11 = (bf16[5,32,1024]{2,1,0:T(8,128)(2,1)S(1)}, bf16[5,32,1024]{2,1,0:T(8,128)(2,1)S(1)}, u32[]{:S(2)}, u32[]{:S(2)}) collective-permute-start(bf16[5,32,1024]{2,1,0:T(8,128)(2,1)S(1)} %get-tuple-element.49), channel_id=1, source_target_pairs={{0,8},{4,12},{8,0},{12,4},{1,9},{5,13},{9,1},{13,5},{2,10},{6,14},... | collective-permute-start | bytes 983048 | tf_op jit(solution)/shard_map/ppermute | solution.py:155
  36.6 3.0 %collective-permute-start.13 = (bf16[128,896]{1,0:T(8,128)(2,1)S(1)}, bf16[128,896]{1,0:T(8,128)(2,1)S(1)}, u32[]{:S(2)}, u32[]{:S(2)}) collective-permute-start(bf16[128,896]{1,0:T(8,128)(2,1)S(1)} %collective-permute-done.5.refs_0_), channel_id=1, source_target_pairs={{0,1},{1,3},{3,2},{2,0},{4,5},{5,7},{7,6},{6,4},{8,9},{9,11},{11,1... | collective-permute-start | bytes 688136 | tf_op jit(solution)/shard_map/ppermute | solution.py:168
  42.2 1.3 %collective-permute-done.13.refs_0_ = bf16[128,896]{1,0:T(8,128)(2,1)S(1)} collective-permute-done((bf16[128,896]{1,0:T(8,128)(2,1)S(1)}, bf16[128,896]{1,0:T(8,128)(2,1)S(1)}, u32[]{:S(2)}, u32[]{:S(2)}) %collective-permute-start.13) | collective-permute-done | bytes 229408 | tf_op jit(solution)/shard_map/ppermute | solution.py:168
  43.5 1.6 %shard_map.133 = (bf16[5,32,1024]{2,1,0:T(8,128)(2,1)S(1)}, bf16[5,32,1024]{2,1,0:T(8,128)(2,1)S(1)}, bf16[5,32,1024]{2,1,0:T(8,128)(2,1)S(1)}, bf16[5,32,1024]{2,1,0:T(8,128)(2,1)S(1)}) custom-call(s32[2]{0:T(128)S(1)} %pad_add_fusion.place_ref, bf16[128,896]{1,0:T(8,128)(2,1)S(1)} %collective-permute-done.13.refs_0_, ...), custom_call_target="tpu_custom_call" | custom-call | flops 704643072 | bytes 5992448 | tf_op jit(solution)/shard_map/pallas_call | solution.py:193
  46.2 1.7 %collective-permute-done.11.refs_2_ = bf16[5,32,1024]{2,1,0:T(8,128)(2,1)S(1)} collective-permute-done((bf16[5,32,1024]{2,1,0:T(8,128)(2,1)S(1)}, bf16[5,32,1024]{2,1,0:T(8,128)(2,1)S(1)}, u32[]{:S(2)}, u32[]{:S(2)}) %collective-permute-start.11) | collective-permute-done | bytes 327712 | tf_op jit(solution)/shard_map/ppermute | solution.py:155
  48.6 1.4 %collective-permute-start.15 = (bf16[5,32,1024]{2,1,0:T(8,128)(2,1)S(1)}, bf16[5,32,1024]{2,1,0:T(8,128)(2,1)S(1)}, u32[]{:S(2)}, u32[]{:S(2)}) collective-permute-start(bf16[5,32,1024]{2,1,0:T(8,128)(2,1)S(1)} %get-tuple-element.57), channel_id=1, source_target_pairs={{0,4},{4,0},{8,12},{12,8},{1,5},{5,1},{9,13},{13,9},{2,6},{6,2},{1... | collective-permute-start | bytes 983048 | tf_op jit(solution)/shard_map/ppermute | solution.py:155
  53.1 1.3 %shard_map.137.refs_3_ = bf16[128,896]{1,0:T(8,128)(2,1)S(1)} custom-call(s32[2]{0:T(128)S(1)} %pad_add_fusion.place_ref, bf16[5,32,1024]{2,1,0:T(8,128)(2,1)S(1)} %get-tuple-element.47.refs_1_.refs_0_, bf16[5,32,1024]{2,1,0:T(8,128)(2,1)S(1)} %collective-permute-done.10.refs_1_, bf16[5,32,1024]{2,1,0:T(8,128)(2,1)S(1)} %collective-permute-done.11.refs_2_, ...), custom_call_target="tpu_custom_call" | custom-call | flops 469762048 | bytes 6287360 | tf_op jit(solution)/shard_map/pallas_call | solution.py:193
  54.5 3.6 %collective-permute-start.22 = (bf16[128,896]{1,0:T(8,128)(2,1)S(1)}, bf16[128,896]{1,0:T(8,128)(2,1)S(1)}, u32[]{:S(2)}, u32[]{:S(2)}) collective-permute-start(bf16[128,896]{1,0:T(8,128)(2,1)S(1)} %shard_map.136.refs_9_), channel_id=1, source_target_pairs={{0,18},{1,16},{3,17},{2,19},{16,2},{17,0},{19,1},{18,3},{4,22},{5,... | collective-permute-start | bytes 688136 | tf_op jit(solution)/shard_map/ppermute | solution.py:178
  60.3 1.4 %collective-permute-done.16.refs_2_ = bf16[5,32,1024]{2,1,0:T(8,128)(2,1)S(1)} collective-permute-done((bf16[5,32,1024]{2,1,0:T(8,128)(2,1)S(1)}, bf16[5,32,1024]{2,1,0:T(8,128)(2,1)S(1)}, u32[]{:S(2)}, u32[]{:S(2)}) %collective-permute-start.16) | collective-permute-done | bytes 327712 | tf_op jit(solution)/shard_map/ppermute | solution.py:155
  63.4 2.1 %collective-permute-start.21 = (bf16[128,896]{1,0:T(8,128)(2,1)S(1)}, bf16[128,896]{1,0:T(8,128)(2,1)S(1)}, u32[]{:S(2)}, u32[]{:S(2)}) collective-permute-start(bf16[128,896]{1,0:T(8,128)(2,1)S(1)} %shard_map.141.refs_9_), channel_id=1, source_target_pairs={{0,1},{1,3},{3,2},{2,0},{4,5},{5,7},{7,6},{6,4},{8,9},{9,11},{11,1... | collective-permute-start | bytes 688136 | tf_op jit(solution)/shard_map/ppermute | solution.py:168
  65.5 2.0 %collective-permute-start.20 = (bf16[3,32,1024]{2,1,0:T(8,128)(2,1)S(1)}, bf16[3,32,1024]{2,1,0:T(8,128)(2,1)S(1)}, u32[]{:S(2)}, u32[]{:S(2)}) collective-permute-start(bf16[3,32,1024]{2,1,0:T(8,128)(2,1)S(1)} %shard_map.140.refs_6_.refs_0_), channel_id=1, source_target_pairs={{0,12},{4,8},{8,4},{12,0},{1,13},{5,9},{9,5},{13,1},{2,14},{6,10},... | collective-permute-start | bytes 589832 | tf_op jit(solution)/shard_map/ppermute | solution.py:155
  69.0 1.3 %shard_map.142.refs_7_ = bf16[128,896]{1,0:T(8,128)(2,1)S(1)} custom-call(s32[2]{0:T(128)S(1)} %pad_add_fusion.place_ref, bf16[5,32,1024]{2,1,0:T(8,128)(2,1)S(1)} %get-tuple-element.56.refs_6_.refs_0_, bf16[5,32,1024]{2,1,0:T(8,128)(2,1)S(1)} %collective-permute-done.15.refs_1_, bf16[5,32,1024]{2,1,0:T(8,128)(2,1)S(1)} %collective-permute-done.16.refs_2_, ...), custom_call_target="tpu_custom_call" | custom-call | flops 469762048 | bytes 6287360 | tf_op jit(solution)/shard_map/pallas_call | solution.py:193
  70.3 3.5 %collective-permute-start.28 = (bf16[128,896]{1,0:T(8,128)(2,1)S(1)}, bf16[128,896]{1,0:T(8,128)(2,1)S(1)}, u32[]{:S(2)}, u32[]{:S(2)}) collective-permute-start(bf16[128,896]{1,0:T(8,128)(2,1)S(1)} %shard_map.142.refs_7_), channel_id=1, source_target_pairs={{0,1},{1,3},{3,2},{2,0},{4,5},{5,7},{7,6},{6,4},{8,9},{9,11},{11,1... | collective-permute-start | bytes 688136 | tf_op jit(solution)/shard_map/ppermute | solution.py:168
  75.9 2.1 %collective-permute-start.27 = (bf16[1,32,1024]{2,1,0:T(8,128)(2,1)S(1)}, bf16[1,32,1024]{2,1,0:T(8,128)(2,1)S(1)}, u32[]{:S(2)}, u32[]{:S(2)}) collective-permute-start(bf16[1,32,1024]{2,1,0:T(8,128)(2,1)S(1)} %shard_map.144.refs_10_.refs_0_), channel_id=1, source_target_pairs={{0,12},{4,8},{8,4},{12,0},{1,13},{5,9},{9,5},{13,1},{2,14},{6,10},... | collective-permute-start | bytes 196616 | tf_op jit(solution)/shard_map/ppermute | solution.py:155
  79.5 1.3 %shard_map.145.refs_7_ = bf16[128,896]{1,0:T(8,128)(2,1)S(1)} custom-call(s32[2]{0:T(128)S(1)} %pad_add_fusion.place_ref, bf16[3,32,1024]{2,1,0:T(8,128)(2,1)S(1)} %shard_map.140.refs_6_.refs_0_, bf16[3,32,1024]{2,1,0:T(8,128)(2,1)S(1)} %collective-permute-done.18.refs_1_.refs_2_, bf16[3,32,1024]{2,1,0:T(8,128)(2,1)S(1)} %collective-permute-done.19.refs_2_.refs_3_, ...), custom_call_target="tpu_custom_call" | custom-call | flops 469762048 | bytes 5992448 | tf_op jit(solution)/shard_map/pallas_call | solution.py:193
  80.8 2.2 %collective-permute-start.30 = (bf16[128,896]{1,0:T(8,128)(2,1)S(1)}, bf16[128,896]{1,0:T(8,128)(2,1)S(1)}, u32[]{:S(2)}, u32[]{:S(2)}) collective-permute-start(bf16[128,896]{1,0:T(8,128)(2,1)S(1)} %shard_map.145.refs_7_), channel_id=1, source_target_pairs={{0,17},{1,19},{3,18},{2,16},{16,1},{17,3},{19,2},{18,0},{4,21},{5,... | collective-permute-start | bytes 688136 | tf_op jit(solution)/shard_map/ppermute | solution.py:178
  85.3 1.3 %shard_map.147.refs_1_ = bf16[128,896]{1,0:T(8,128)(2,1)S(1)} custom-call(s32[2]{0:T(128)S(1)} %pad_add_fusion.place_ref, bf16[3,32,1024]{2,1,0:T(8,128)(2,1)S(1)} %shard_map.140.refs_6_.refs_0_, bf16[3,32,1024]{2,1,0:T(8,128)(2,1)S(1)} %collective-permute-done.18.refs_1_.refs_2_, bf16[3,32,1024]{2,1,0:T(8,128)(2,1)S(1)} %collective-permute-done.19.refs_2_.refs_3_, ...), custom_call_target="tpu_custom_call" | custom-call | flops 469762048 | bytes 5992448 | tf_op jit(solution)/shard_map/pallas_call | solution.py:193
  86.9 1.7 %collective-permute-done.30.refs_0_ = bf16[128,896]{1,0:T(8,128)(2,1)S(1)} collective-permute-done((bf16[128,896]{1,0:T(8,128)(2,1)S(1)}, bf16[128,896]{1,0:T(8,128)(2,1)S(1)}, u32[]{:S(2)}, u32[]{:S(2)}) %collective-permute-start.30) | collective-permute-done | bytes 229408 | tf_op jit(solution)/shard_map/ppermute | solution.py:178
  (91 shorter events, 26.9 us)
Async XLA Ops:
  1.6 14.1 %collective-permute-start.1 = (bf16[144,896]{1,0:T(8,128)(2,1)S(1)}, bf16[144,896]{1,0:T(8,128)(2,1)S(1)}, u32[]{:S(2)}, u32[]{:S(2)}) collective-permute-start(bf16[144,896]{1,0:T(8,128)(2,1)S(1)} %shard_map.123.refs_1_.refs_2_.refs_5_.refs_8_), channel_id=1, source_target_pairs={{0,1},{1,3},{3,2},{2,0},{4,5},{5,7},{7,6},{6,4},{8,9},{9,11},{11,1... | collective-permute-start | bytes 774152 | tf_op jit(solution)/shard_map/ppermute | solution.py:168
  4.7 12.1 %collective-permute-start = (bf16[128,896]{1,0:T(8,128)(2,1)S(1)}, bf16[128,896]{1,0:T(8,128)(2,1)S(1)}, u32[]{:S(2)}, u32[]{:S(2)}) collective-permute-start(bf16[128,896]{1,0:T(8,128)(2,1)S(1)} %bitcast.50), channel_id=1, source_target_pairs={{0,1},{1,3},{3,2},{2,0},{4,5},{5,7},{7,6},{6,4},{8,9},{9,11},{11,1... | collective-permute-start | bytes 688136 | tf_op jit(solution)/shard_map/ppermute | solution.py:168
  12.2 9.7 %collective-permute-start.7 = (bf16[3,32,1024]{2,1,0:T(8,128)(2,1)S(1)}, bf16[3,32,1024]{2,1,0:T(8,128)(2,1)S(1)}, u32[]{:S(2)}, u32[]{:S(2)}) collective-permute-start(bf16[3,32,1024]{2,1,0:T(8,128)(2,1)S(1)} %get-tuple-element.39), channel_id=1, source_target_pairs={{0,4},{4,0},{8,12},{12,8},{1,5},{5,1},{9,13},{13,9},{2,6},{6,2},{1... | collective-permute-start | bytes 589832 | tf_op jit(solution)/shard_map/ppermute | solution.py:155
  13.8 9.8 %collective-permute-start.8 = (bf16[3,32,1024]{2,1,0:T(8,128)(2,1)S(1)}, bf16[3,32,1024]{2,1,0:T(8,128)(2,1)S(1)}, u32[]{:S(2)}, u32[]{:S(2)}) collective-permute-start(bf16[3,32,1024]{2,1,0:T(8,128)(2,1)S(1)} %get-tuple-element.40), channel_id=1, source_target_pairs={{0,8},{4,12},{8,0},{12,4},{1,9},{5,13},{9,1},{13,5},{2,10},{6,14},... | collective-permute-start | bytes 589832 | tf_op jit(solution)/shard_map/ppermute | solution.py:155
  15.3 10.4 %collective-permute-start.9 = (bf16[3,32,1024]{2,1,0:T(8,128)(2,1)S(1)}, bf16[3,32,1024]{2,1,0:T(8,128)(2,1)S(1)}, u32[]{:S(2)}, u32[]{:S(2)}) collective-permute-start(bf16[3,32,1024]{2,1,0:T(8,128)(2,1)S(1)} %get-tuple-element.41), channel_id=1, source_target_pairs={{0,12},{4,8},{8,4},{12,0},{1,13},{5,9},{9,5},{13,1},{2,14},{6,10},... | collective-permute-start | bytes 589832 | tf_op jit(solution)/shard_map/ppermute | solution.py:155
  15.8 10.7 %collective-permute-start.6 = (bf16[144,896]{1,0:T(8,128)(2,1)S(1)}, bf16[144,896]{1,0:T(8,128)(2,1)S(1)}, u32[]{:S(2)}, u32[]{:S(2)}) collective-permute-start(bf16[144,896]{1,0:T(8,128)(2,1)S(1)} %collective-permute-done.1.refs_1_.refs_2_.refs_5_.refs_8_), channel_id=1, source_target_pairs={{0,1},{1,3},{3,2},{2,0},{4,5},{5,7},{7,6},{6,4},{8,9},{9,11},{11,1... | collective-permute-start | bytes 774152 | tf_op jit(solution)/shard_map/ppermute | solution.py:168
  16.9 12.8 %collective-permute-start.5 = (bf16[128,896]{1,0:T(8,128)(2,1)S(1)}, bf16[128,896]{1,0:T(8,128)(2,1)S(1)}, u32[]{:S(2)}, u32[]{:S(2)}) collective-permute-start(bf16[128,896]{1,0:T(8,128)(2,1)S(1)} %collective-permute-done.refs_0_), channel_id=1, source_target_pairs={{0,1},{1,3},{3,2},{2,0},{4,5},{5,7},{7,6},{6,4},{8,9},{9,11},{11,1... | collective-permute-start | bytes 688136 | tf_op jit(solution)/shard_map/ppermute | solution.py:168
  21.9 10.4 %collective-permute-start.2 = (bf16[3,32,1024]{2,1,0:T(8,128)(2,1)S(1)}, bf16[3,32,1024]{2,1,0:T(8,128)(2,1)S(1)}, u32[]{:S(2)}, u32[]{:S(2)}) collective-permute-start(bf16[3,32,1024]{2,1,0:T(8,128)(2,1)S(1)} %get-tuple-element.36), channel_id=1, source_target_pairs={{0,4},{4,0},{8,12},{12,8},{1,5},{5,1},{9,13},{13,9},{2,6},{6,2},{1... | collective-permute-start | bytes 589832 | tf_op jit(solution)/shard_map/ppermute | solution.py:155
  23.6 8.7 %collective-permute-start.3 = (bf16[3,32,1024]{2,1,0:T(8,128)(2,1)S(1)}, bf16[3,32,1024]{2,1,0:T(8,128)(2,1)S(1)}, u32[]{:S(2)}, u32[]{:S(2)}) collective-permute-start(bf16[3,32,1024]{2,1,0:T(8,128)(2,1)S(1)} %get-tuple-element.37), channel_id=1, source_target_pairs={{0,8},{4,12},{8,0},{12,4},{1,9},{5,13},{9,1},{13,5},{2,10},{6,14},... | collective-permute-start | bytes 589832 | tf_op jit(solution)/shard_map/ppermute | solution.py:155
  25.7 6.6 %collective-permute-start.4 = (bf16[3,32,1024]{2,1,0:T(8,128)(2,1)S(1)}, bf16[3,32,1024]{2,1,0:T(8,128)(2,1)S(1)}, u32[]{:S(2)}, u32[]{:S(2)}) collective-permute-start(bf16[3,32,1024]{2,1,0:T(8,128)(2,1)S(1)} %get-tuple-element.38), channel_id=1, source_target_pairs={{0,12},{4,8},{8,4},{12,0},{1,13},{5,9},{9,5},{13,1},{2,14},{6,10},... | collective-permute-start | bytes 589832 | tf_op jit(solution)/shard_map/ppermute | solution.py:155
  26.4 17.1 %collective-permute-start.14 = (bf16[144,896]{1,0:T(8,128)(2,1)S(1)}, bf16[144,896]{1,0:T(8,128)(2,1)S(1)}, u32[]{:S(2)}, u32[]{:S(2)}) collective-permute-start(bf16[144,896]{1,0:T(8,128)(2,1)S(1)} %collective-permute-done.6.refs_1_.refs_2_.refs_5_.refs_8_), channel_id=1, source_target_pairs={{0,1},{1,3},{3,2},{2,0},{4,5},{5,7},{7,6},{6,4},{8,9},{9,11},{11,1... | collective-permute-start | bytes 774152 | tf_op jit(solution)/shard_map/ppermute | solution.py:168
  33.1 13.2 %collective-permute-start.10 = (bf16[5,32,1024]{2,1,0:T(8,128)(2,1)S(1)}, bf16[5,32,1024]{2,1,0:T(8,128)(2,1)S(1)}, u32[]{:S(2)}, u32[]{:S(2)}) collective-permute-start(bf16[5,32,1024]{2,1,0:T(8,128)(2,1)S(1)} %get-tuple-element.48), channel_id=1, source_target_pairs={{0,4},{4,0},{8,12},{12,8},{1,5},{5,1},{9,13},{13,9},{2,6},{6,2},{1... | collective-permute-start | bytes 983048 | tf_op jit(solution)/shard_map/ppermute | solution.py:155
  34.8 13.1 %collective-permute-start.11 = (bf16[5,32,1024]{2,1,0:T(8,128)(2,1)S(1)}, bf16[5,32,1024]{2,1,0:T(8,128)(2,1)S(1)}, u32[]{:S(2)}, u32[]{:S(2)}) collective-permute-start(bf16[5,32,1024]{2,1,0:T(8,128)(2,1)S(1)} %get-tuple-element.49), channel_id=1, source_target_pairs={{0,8},{4,12},{8,0},{12,4},{1,9},{5,13},{9,1},{13,5},{2,10},{6,14},... | collective-permute-start | bytes 983048 | tf_op jit(solution)/shard_map/ppermute | solution.py:155
  36.3 11.6 %collective-permute-start.12 = (bf16[5,32,1024]{2,1,0:T(8,128)(2,1)S(1)}, bf16[5,32,1024]{2,1,0:T(8,128)(2,1)S(1)}, u32[]{:S(2)}, u32[]{:S(2)}) collective-permute-start(bf16[5,32,1024]{2,1,0:T(8,128)(2,1)S(1)} %get-tuple-element.50), channel_id=1, source_target_pairs={{0,12},{4,8},{8,4},{12,0},{1,13},{5,9},{9,5},{13,1},{2,14},{6,10},... | collective-permute-start | bytes 983048 | tf_op jit(solution)/shard_map/ppermute | solution.py:155
  36.6 6.9 %collective-permute-start.13 = (bf16[128,896]{1,0:T(8,128)(2,1)S(1)}, bf16[128,896]{1,0:T(8,128)(2,1)S(1)}, u32[]{:S(2)}, u32[]{:S(2)}) collective-permute-start(bf16[128,896]{1,0:T(8,128)(2,1)S(1)} %collective-permute-done.5.refs_0_), channel_id=1, source_target_pairs={{0,1},{1,3},{3,2},{2,0},{4,5},{5,7},{7,6},{6,4},{8,9},{9,11},{11,1... | collective-permute-start | bytes 688136 | tf_op jit(solution)/shard_map/ppermute | solution.py:168
  48.6 11.7 %collective-permute-start.15 = (bf16[5,32,1024]{2,1,0:T(8,128)(2,1)S(1)}, bf16[5,32,1024]{2,1,0:T(8,128)(2,1)S(1)}, u32[]{:S(2)}, u32[]{:S(2)}) collective-permute-start(bf16[5,32,1024]{2,1,0:T(8,128)(2,1)S(1)} %get-tuple-element.57), channel_id=1, source_target_pairs={{0,4},{4,0},{8,12},{12,8},{1,5},{5,1},{9,13},{13,9},{2,6},{6,2},{1... | collective-permute-start | bytes 983048 | tf_op jit(solution)/shard_map/ppermute | solution.py:155
  50.0 11.7 %collective-permute-start.16 = (bf16[5,32,1024]{2,1,0:T(8,128)(2,1)S(1)}, bf16[5,32,1024]{2,1,0:T(8,128)(2,1)S(1)}, u32[]{:S(2)}, u32[]{:S(2)}) collective-permute-start(bf16[5,32,1024]{2,1,0:T(8,128)(2,1)S(1)} %get-tuple-element.58), channel_id=1, source_target_pairs={{0,8},{4,12},{8,0},{12,4},{1,9},{5,13},{9,1},{13,5},{2,10},{6,14},... | collective-permute-start | bytes 983048 | tf_op jit(solution)/shard_map/ppermute | solution.py:155
  51.0 10.8 %collective-permute-start.17 = (bf16[5,32,1024]{2,1,0:T(8,128)(2,1)S(1)}, bf16[5,32,1024]{2,1,0:T(8,128)(2,1)S(1)}, u32[]{:S(2)}, u32[]{:S(2)}) collective-permute-start(bf16[5,32,1024]{2,1,0:T(8,128)(2,1)S(1)} %get-tuple-element.59), channel_id=1, source_target_pairs={{0,12},{4,8},{8,4},{12,0},{1,13},{5,9},{9,5},{13,1},{2,14},{6,10},... | collective-permute-start | bytes 983048 | tf_op jit(solution)/shard_map/ppermute | solution.py:155
  54.4 13.8 %collective-permute-start.23 = (bf16[128,896]{1,0:T(8,128)(2,1)S(1)}, bf16[128,896]{1,0:T(8,128)(2,1)S(1)}, u32[]{:S(2)}, u32[]{:S(2)}) collective-permute-start(bf16[128,896]{1,0:T(8,128)(2,1)S(1)} %shard_map.137.refs_3_), channel_id=1, source_target_pairs={{0,18},{1,16},{3,17},{2,19},{16,2},{17,0},{19,1},{18,3},{4,22},{5,... | collective-permute-start | bytes 688136 | tf_op jit(solution)/shard_map/ppermute | solution.py:178
  54.5 14.6 %collective-permute-start.22 = (bf16[128,896]{1,0:T(8,128)(2,1)S(1)}, bf16[128,896]{1,0:T(8,128)(2,1)S(1)}, u32[]{:S(2)}, u32[]{:S(2)}) collective-permute-start(bf16[128,896]{1,0:T(8,128)(2,1)S(1)} %shard_map.136.refs_9_), channel_id=1, source_target_pairs={{0,18},{1,16},{3,17},{2,19},{16,2},{17,0},{19,1},{18,3},{4,22},{5,... | collective-permute-start | bytes 688136 | tf_op jit(solution)/shard_map/ppermute | solution.py:178
  63.4 10.9 %collective-permute-start.21 = (bf16[128,896]{1,0:T(8,128)(2,1)S(1)}, bf16[128,896]{1,0:T(8,128)(2,1)S(1)}, u32[]{:S(2)}, u32[]{:S(2)}) collective-permute-start(bf16[128,896]{1,0:T(8,128)(2,1)S(1)} %shard_map.141.refs_9_), channel_id=1, source_target_pairs={{0,1},{1,3},{3,2},{2,0},{4,5},{5,7},{7,6},{6,4},{8,9},{9,11},{11,1... | collective-permute-start | bytes 688136 | tf_op jit(solution)/shard_map/ppermute | solution.py:168
  65.5 8.3 %collective-permute-start.20 = (bf16[3,32,1024]{2,1,0:T(8,128)(2,1)S(1)}, bf16[3,32,1024]{2,1,0:T(8,128)(2,1)S(1)}, u32[]{:S(2)}, u32[]{:S(2)}) collective-permute-start(bf16[3,32,1024]{2,1,0:T(8,128)(2,1)S(1)} %shard_map.140.refs_6_.refs_0_), channel_id=1, source_target_pairs={{0,12},{4,8},{8,4},{12,0},{1,13},{5,9},{9,5},{13,1},{2,14},{6,10},... | collective-permute-start | bytes 589832 | tf_op jit(solution)/shard_map/ppermute | solution.py:155
  67.6 6.6 %collective-permute-start.19 = (bf16[3,32,1024]{2,1,0:T(8,128)(2,1)S(1)}, bf16[3,32,1024]{2,1,0:T(8,128)(2,1)S(1)}, u32[]{:S(2)}, u32[]{:S(2)}) collective-permute-start(bf16[3,32,1024]{2,1,0:T(8,128)(2,1)S(1)} %shard_map.140.refs_6_.refs_0_), channel_id=1, source_target_pairs={{0,8},{4,12},{8,0},{12,4},{1,9},{5,13},{9,1},{13,5},{2,10},{6,14},... | collective-permute-start | bytes 589832 | tf_op jit(solution)/shard_map/ppermute | solution.py:155
  68.2 6.1 %collective-permute-start.18 = (bf16[3,32,1024]{2,1,0:T(8,128)(2,1)S(1)}, bf16[3,32,1024]{2,1,0:T(8,128)(2,1)S(1)}, u32[]{:S(2)}, u32[]{:S(2)}) collective-permute-start(bf16[3,32,1024]{2,1,0:T(8,128)(2,1)S(1)} %shard_map.140.refs_6_.refs_0_), channel_id=1, source_target_pairs={{0,4},{4,0},{8,12},{12,8},{1,5},{5,1},{9,13},{13,9},{2,6},{6,2},{1... | collective-permute-start | bytes 589832 | tf_op jit(solution)/shard_map/ppermute | solution.py:155
  70.3 9.1 %collective-permute-start.28 = (bf16[128,896]{1,0:T(8,128)(2,1)S(1)}, bf16[128,896]{1,0:T(8,128)(2,1)S(1)}, u32[]{:S(2)}, u32[]{:S(2)}) collective-permute-start(bf16[128,896]{1,0:T(8,128)(2,1)S(1)} %shard_map.142.refs_7_), channel_id=1, source_target_pairs={{0,1},{1,3},{3,2},{2,0},{4,5},{5,7},{7,6},{6,4},{8,9},{9,11},{11,1... | collective-permute-start | bytes 688136 | tf_op jit(solution)/shard_map/ppermute | solution.py:168
  75.3 11.4 %collective-permute-start.24 = (bf16[128,896]{1,0:T(8,128)(2,1)S(1)}, bf16[128,896]{1,0:T(8,128)(2,1)S(1)}, u32[]{:S(2)}, u32[]{:S(2)}) collective-permute-start(bf16[128,896]{1,0:T(8,128)(2,1)S(1)} %shard_map.143.refs_1_), channel_id=1, source_target_pairs={{0,17},{1,19},{3,18},{2,16},{16,1},{17,3},{19,2},{18,0},{4,21},{5,... | collective-permute-start | bytes 688136 | tf_op jit(solution)/shard_map/ppermute | solution.py:178
  75.9 7.0 %collective-permute-start.27 = (bf16[1,32,1024]{2,1,0:T(8,128)(2,1)S(1)}, bf16[1,32,1024]{2,1,0:T(8,128)(2,1)S(1)}, u32[]{:S(2)}, u32[]{:S(2)}) collective-permute-start(bf16[1,32,1024]{2,1,0:T(8,128)(2,1)S(1)} %shard_map.144.refs_10_.refs_0_), channel_id=1, source_target_pairs={{0,12},{4,8},{8,4},{12,0},{1,13},{5,9},{9,5},{13,1},{2,14},{6,10},... | collective-permute-start | bytes 196616 | tf_op jit(solution)/shard_map/ppermute | solution.py:155
  78.0 5.0 %collective-permute-start.26 = (bf16[1,32,1024]{2,1,0:T(8,128)(2,1)S(1)}, bf16[1,32,1024]{2,1,0:T(8,128)(2,1)S(1)}, u32[]{:S(2)}, u32[]{:S(2)}) collective-permute-start(bf16[1,32,1024]{2,1,0:T(8,128)(2,1)S(1)} %shard_map.144.refs_10_.refs_0_), channel_id=1, source_target_pairs={{0,8},{4,12},{8,0},{12,4},{1,9},{5,13},{9,1},{13,5},{2,10},{6,14},... | collective-permute-start | bytes 196616 | tf_op jit(solution)/shard_map/ppermute | solution.py:155
  78.6 4.7 %collective-permute-start.25 = (bf16[1,32,1024]{2,1,0:T(8,128)(2,1)S(1)}, bf16[1,32,1024]{2,1,0:T(8,128)(2,1)S(1)}, u32[]{:S(2)}, u32[]{:S(2)}) collective-permute-start(bf16[1,32,1024]{2,1,0:T(8,128)(2,1)S(1)} %shard_map.144.refs_10_.refs_0_), channel_id=1, source_target_pairs={{0,4},{4,0},{8,12},{12,8},{1,5},{5,1},{9,13},{13,9},{2,6},{6,2},{1... | collective-permute-start | bytes 196616 | tf_op jit(solution)/shard_map/ppermute | solution.py:155
  80.8 7.8 %collective-permute-start.30 = (bf16[128,896]{1,0:T(8,128)(2,1)S(1)}, bf16[128,896]{1,0:T(8,128)(2,1)S(1)}, u32[]{:S(2)}, u32[]{:S(2)}) collective-permute-start(bf16[128,896]{1,0:T(8,128)(2,1)S(1)} %shard_map.145.refs_7_), channel_id=1, source_target_pairs={{0,17},{1,19},{3,18},{2,16},{16,1},{17,3},{19,2},{18,0},{4,21},{5,... | collective-permute-start | bytes 688136 | tf_op jit(solution)/shard_map/ppermute | solution.py:178
  84.3 2.5 %collective-permute-start.29 = (bf16[128,896]{1,0:T(8,128)(2,1)S(1)}, bf16[128,896]{1,0:T(8,128)(2,1)S(1)}, u32[]{:S(2)}, u32[]{:S(2)}) collective-permute-start(bf16[128,896]{1,0:T(8,128)(2,1)S(1)} %shard_map.146.refs_10_), channel_id=1, source_target_pairs={{0,16},{16,0},{1,17},{17,1},{2,18},{18,2},{3,19},{19,3},{4,20},{20... | collective-permute-start | bytes 688136 | tf_op jit(solution)/shard_map/ppermute | solution.py:14
  86.6 1.9 %collective-permute-start.31 = (bf16[128,896]{1,0:T(8,128)(2,1)S(1)}, bf16[128,896]{1,0:T(8,128)(2,1)S(1)}, u32[]{:S(2)}, u32[]{:S(2)}) collective-permute-start(bf16[128,896]{1,0:T(8,128)(2,1)S(1)} %shard_map.147.refs_1_), channel_id=1, source_target_pairs={{0,16},{16,0},{1,17},{17,1},{2,18},{18,2},{3,19},{19,3},{4,20},{20... | collective-permute-start | bytes 688136 | tf_op jit(solution)/shard_map/ppermute | solution.py:14
  (14 other events, 32.1 us)

commit v10 on v8

--- a/solution.py
+++ b/solution.py
@@ -645,10 +645,10 @@
     own_acts = activations(place, parts[0], (), done[-1:])[0]
     done.append(own_acts)
     for step in range(1, experts - 1):
+        first(step + 1)
+        prepare(step)
         if step == experts - 2:
             turned[:] = turn(0), turn(1)
-        first(step + 1)
-        prepare(step)
         middle(step)
         if step >= 2:
             last(step - 1, 0)
@@ -664,8 +664,8 @@
     done.append(own_plane)
     acts[0][0] = (exchange([own_plane]), 0)
     last(experts - 1, 1)
+    last(0, 1)
     last(0, 0)
-    last(0, 1)
     outs = []
     for values, own in zip(sums, base):
         total = sum(value.astype(jnp.float32) for value in (sum_rows(values[-1:], (*done[-1:], *outs)), *values[:-1], own))

time: 90.2 us -> 90.2 us (level)
    ppermute x8, waiting for transfers between devices: 1.95 us -> 4.54 us  [along_ring(): return lax.ppermute(value, 'dev', ring_pairs(lax.axis_size('dev'), steps))]
    ppermute x18, waiting for transfers between devices: 4.09 us -> 1.96 us  [across(): lax.ppermute(value, axis, [(source, source ^ mask) for source in range(co...]
    ppermute x2, waiting for transfers between devices: 0.01 us -> 1.42 us  [from_behind(): return lax.ppermute(value, axis, pairs)]
    ppermute x4, waiting for transfers between devices: 1.66 us -> 0.39 us  [along_ring_and_sections(): return lax.ppermute(value, ('section', 'dev'), pairs)]
  transfers between devices with their start and end apart: 32 -> 32, of which waited for: 8 -> 7; matrix products, arithmetic and copies ran while one was open for 0% -> 0% of each run, Pallas kernels for 29% -> 29%
where the time goes in v10:
time: 90.2 us; the launch traced here: 89.6 us
  starting transfers between devices  48.1 us (53%)
  Pallas kernels  26.7 us (30%)
  waiting for transfers between devices  8.3 us (9%)
  local copies, waits for them, and re-layouts  4.59 us (5%)
  between operations  1.05 us (1%)
  other arithmetic  0.91 us (1%)
    pallas_call x24, Pallas kernels, call(): pl.pallas_call(with_after, in_specs=[SMEM] + [VMEM] * len(operands) + [AN...  26.6 us
    ppermute x18, starting transfers between devices, across(): lax.ppermute(value, axis, [(source, source ^ mask) for source in range(co...  21.3 us
    ppermute x8, starting transfers between devices, along_ring(): return lax.ppermute(value, 'dev', ring_pairs(lax.axis_size('dev'), steps))  19.9 us
    ppermute x4, starting transfers between devices, along_ring_and_sections(): return lax.ppermute(value, ('section', 'dev'), pairs)  5.47 us
    unnamed x28, local copies, waits for them, and re-layouts  4.59 us
    ppermute x8, waiting for transfers between devices, along_ring(): return lax.ppermute(value, 'dev', ring_pairs(lax.axis_size('dev'), steps))  4.54 us
    ppermute x18, waiting for transfers between devices, across(): lax.ppermute(value, axis, [(source, source ^ mask) for source in range(co...  1.96 us
  transfers between devices with their start and end apart: 32, of which 7 were waited for; matrix products, arithmetic and copies ran while one was open for 0% of the time, Pallas kernels for 29%

profile of v10, /device:TPU:0, one launch (start us, length us, event | category | flops | bytes accessed | tf_op | source)
XLA Modules:
  0.0 89.6 jit_solution(7601602172804898484)
XLA Ops:
  1.6 3.1 %collective-permute-start.1 = (bf16[144,896]{1,0:T(8,128)(2,1)S(1)}, bf16[144,896]{1,0:T(8,128)(2,1)S(1)}, u32[]{:S(2)}, u32[]{:S(2)}) collective-permute-start(bf16[144,896]{1,0:T(8,128)(2,1)S(1)} %shard_map.123.refs_1_.refs_2_.refs_8_.refs_5_), channel_id=1, source_target_pairs={{0,1},{1,3},{3,2},{2,0},{4,5},{5,7},{7,6},{6,4},{8,9},{9,11},{11,1... | collective-permute-start | bytes 774152 | tf_op jit(solution)/shard_map/ppermute | solution.py:172
  4.7 2.6 %collective-permute-start = (bf16[128,896]{1,0:T(8,128)(2,1)S(1)}, bf16[128,896]{1,0:T(8,128)(2,1)S(1)}, u32[]{:S(2)}, u32[]{:S(2)}) collective-permute-start(bf16[128,896]{1,0:T(8,128)(2,1)S(1)} %bitcast.50), channel_id=1, source_target_pairs={{0,1},{1,3},{3,2},{2,0},{4,5},{5,7},{7,6},{6,4},{8,9},{9,11},{11,1... | collective-permute-start | bytes 688136 | tf_op jit(solution)/shard_map/ppermute | solution.py:172
  7.4 1.5 %copy-done.1 = bf16[1,1,896,1024]{3,2,1,0:T(8,128)(2,1)S(1)} copy-done((bf16[1,1,896,1024]{3,2,1,0:T(8,128)(2,1)S(1)}, bf16[1,1,896,1024]{3,2,1,0:T(8,128)(2,1)}, u32[]{:S(2)}) %copy-start.1) | copy-done | bytes 1835032
  8.9 1.5 %copy-done.3 = bf16[1,1,896,1024]{3,2,1,0:T(8,128)(2,1)S(1)} copy-done((bf16[1,1,896,1024]{3,2,1,0:T(8,128)(2,1)S(1)}, bf16[1,1,896,1024]{3,2,1,0:T(8,128)(2,1)}, u32[]{:S(2)}) %copy-start.3) | copy-done | bytes 1835032
  10.4 1.8 %shard_map.124 = (bf16[3,32,1024]{2,1,0:T(8,128)(2,1)S(1)}, bf16[3,32,1024]{2,1,0:T(8,128)(2,1)S(1)}, bf16[3,32,1024]{2,1,0:T(8,128)(2,1)S(1)}, bf16[3,32,1024]{2,1,0:T(8,128)(2,1)S(1)}) custom-call(s32[2]{0:T(128)S(1)} %pad_add_fusion.place_ref, bf16[128,896]{1,0:T(8,128)(2,1)S(1)} %bitcast.51, ...), custom_call_target="tpu_custom_call" | custom-call | flops 704643072 | bytes 5992448 | tf_op jit(solution)/shard_map/pallas_call | solution.py:197
  12.2 1.6 %collective-permute-start.7 = (bf16[3,32,1024]{2,1,0:T(8,128)(2,1)S(1)}, bf16[3,32,1024]{2,1,0:T(8,128)(2,1)S(1)}, u32[]{:S(2)}, u32[]{:S(2)}) collective-permute-start(bf16[3,32,1024]{2,1,0:T(8,128)(2,1)S(1)} %get-tuple-element.39), channel_id=1, source_target_pairs={{0,4},{4,0},{8,12},{12,8},{1,5},{5,1},{9,13},{13,9},{2,6},{6,2},{1... | collective-permute-start | bytes 589832 | tf_op jit(solution)/shard_map/ppermute | solution.py:159
  13.8 1.5 %collective-permute-start.8 = (bf16[3,32,1024]{2,1,0:T(8,128)(2,1)S(1)}, bf16[3,32,1024]{2,1,0:T(8,128)(2,1)S(1)}, u32[]{:S(2)}, u32[]{:S(2)}) collective-permute-start(bf16[3,32,1024]{2,1,0:T(8,128)(2,1)S(1)} %get-tuple-element.40), channel_id=1, source_target_pairs={{0,8},{4,12},{8,0},{12,4},{1,9},{5,13},{9,1},{13,5},{2,10},{6,14},... | collective-permute-start | bytes 589832 | tf_op jit(solution)/shard_map/ppermute | solution.py:159
  16.9 2.0 %collective-permute-start.5 = (bf16[128,896]{1,0:T(8,128)(2,1)S(1)}, bf16[128,896]{1,0:T(8,128)(2,1)S(1)}, u32[]{:S(2)}, u32[]{:S(2)}) collective-permute-start(bf16[128,896]{1,0:T(8,128)(2,1)S(1)} %collective-permute-done.refs_0_), channel_id=1, source_target_pairs={{0,1},{1,3},{3,2},{2,0},{4,5},{5,7},{7,6},{6,4},{8,9},{9,11},{11,1... | collective-permute-start | bytes 688136 | tf_op jit(solution)/shard_map/ppermute | solution.py:172
  20.3 1.6 %shard_map.126 = (bf16[3,32,1024]{2,1,0:T(8,128)(2,1)S(1)}, bf16[3,32,1024]{2,1,0:T(8,128)(2,1)S(1)}, bf16[3,32,1024]{2,1,0:T(8,128)(2,1)S(1)}, bf16[3,32,1024]{2,1,0:T(8,128)(2,1)S(1)}) custom-call(s32[2]{0:T(128)S(1)} %pad_add_fusion.place_ref, bf16[128,896]{1,0:T(8,128)(2,1)S(1)} %collective-permute-done.refs_0_, ...), custom_call_target="tpu_custom_call" | custom-call | flops 704643072 | bytes 5992448 | tf_op jit(solution)/shard_map/pallas_call | solution.py:197
  21.9 1.5 %collective-permute-start.2 = (bf16[3,32,1024]{2,1,0:T(8,128)(2,1)S(1)}, bf16[3,32,1024]{2,1,0:T(8,128)(2,1)S(1)}, u32[]{:S(2)}, u32[]{:S(2)}) collective-permute-start(bf16[3,32,1024]{2,1,0:T(8,128)(2,1)S(1)} %get-tuple-element.36), channel_id=1, source_target_pairs={{0,4},{4,0},{8,12},{12,8},{1,5},{5,1},{9,13},{13,9},{2,6},{6,2},{1... | collective-permute-start | bytes 589832 | tf_op jit(solution)/shard_map/ppermute | solution.py:159
  23.6 2.1 %collective-permute-start.3 = (bf16[3,32,1024]{2,1,0:T(8,128)(2,1)S(1)}, bf16[3,32,1024]{2,1,0:T(8,128)(2,1)S(1)}, u32[]{:S(2)}, u32[]{:S(2)}) collective-permute-start(bf16[3,32,1024]{2,1,0:T(8,128)(2,1)S(1)} %get-tuple-element.37), channel_id=1, source_target_pairs={{0,8},{4,12},{8,0},{12,4},{1,9},{5,13},{9,1},{13,5},{2,10},{6,14},... | collective-permute-start | bytes 589832 | tf_op jit(solution)/shard_map/ppermute | solution.py:159
  26.4 3.2 %collective-permute-start.14 = (bf16[144,896]{1,0:T(8,128)(2,1)S(1)}, bf16[144,896]{1,0:T(8,128)(2,1)S(1)}, u32[]{:S(2)}, u32[]{:S(2)}) collective-permute-start(bf16[144,896]{1,0:T(8,128)(2,1)S(1)} %collective-permute-done.6.refs_1_.refs_2_.refs_5_.refs_8_), channel_id=1, source_target_pairs={{0,1},{1,3},{3,2},{2,0},{4,5},{5,7},{7,6},{6,4},{8,9},{9,11},{11,1... | collective-permute-start | bytes 774152 | tf_op jit(solution)/shard_map/ppermute | solution.py:172
  29.6 1.5 %shard_map.128 = (bf16[5,32,1024]{2,1,0:T(8,128)(2,1)S(1)}, bf16[5,32,1024]{2,1,0:T(8,128)(2,1)S(1)}, bf16[5,32,1024]{2,1,0:T(8,128)(2,1)S(1)}, bf16[5,32,1024]{2,1,0:T(8,128)(2,1)S(1)}) custom-call(s32[2]{0:T(128)S(1)} %pad_add_fusion.place_ref, bf16[128,896]{1,0:T(8,128)(2,1)S(1)} %collective-permute-done.5.refs_0_, ...), custom_call_target="tpu_custom_call" | custom-call | flops 704643072 | bytes 5992448 | tf_op jit(solution)/shard_map/pallas_call | solution.py:197
  33.1 1.7 %collective-permute-start.10 = (bf16[5,32,1024]{2,1,0:T(8,128)(2,1)S(1)}, bf16[5,32,1024]{2,1,0:T(8,128)(2,1)S(1)}, u32[]{:S(2)}, u32[]{:S(2)}) collective-permute-start(bf16[5,32,1024]{2,1,0:T(8,128)(2,1)S(1)} %get-tuple-element.48), channel_id=1, source_target_pairs={{0,4},{4,0},{8,12},{12,8},{1,5},{5,1},{9,13},{13,9},{2,6},{6,2},{1... | collective-permute-start | bytes 983048 | tf_op jit(solution)/shard_map/ppermute | solution.py:159
  34.8 1.5 %collective-permute-start.11 = (bf16[5,32,1024]{2,1,0:T(8,128)(2,1)S(1)}, bf16[5,32,1024]{2,1,0:T(8,128)(2,1)S(1)}, u32[]{:S(2)}, u32[]{:S(2)}) collective-permute-start(bf16[5,32,1024]{2,1,0:T(8,128)(2,1)S(1)} %get-tuple-element.49), channel_id=1, source_target_pairs={{0,8},{4,12},{8,0},{12,4},{1,9},{5,13},{9,1},{13,5},{2,10},{6,14},... | collective-permute-start | bytes 983048 | tf_op jit(solution)/shard_map/ppermute | solution.py:159
  36.6 3.0 %collective-permute-start.13 = (bf16[128,896]{1,0:T(8,128)(2,1)S(1)}, bf16[128,896]{1,0:T(8,128)(2,1)S(1)}, u32[]{:S(2)}, u32[]{:S(2)}) collective-permute-start(bf16[128,896]{1,0:T(8,128)(2,1)S(1)} %collective-permute-done.5.refs_0_), channel_id=1, source_target_pairs={{0,1},{1,3},{3,2},{2,0},{4,5},{5,7},{7,6},{6,4},{8,9},{9,11},{11,1... | collective-permute-start | bytes 688136 | tf_op jit(solution)/shard_map/ppermute | solution.py:172
  39.7 3.9 %collective-permute-done.13.refs_0_ = bf16[128,896]{1,0:T(8,128)(2,1)S(1)} collective-permute-done((bf16[128,896]{1,0:T(8,128)(2,1)S(1)}, bf16[128,896]{1,0:T(8,128)(2,1)S(1)}, u32[]{:S(2)}, u32[]{:S(2)}) %collective-permute-start.13) | collective-permute-done | bytes 229408 | tf_op jit(solution)/shard_map/ppermute | solution.py:172
  43.5 1.5 %shard_map.131 = (bf16[5,32,1024]{2,1,0:T(8,128)(2,1)S(1)}, bf16[5,32,1024]{2,1,0:T(8,128)(2,1)S(1)}, bf16[5,32,1024]{2,1,0:T(8,128)(2,1)S(1)}, bf16[5,32,1024]{2,1,0:T(8,128)(2,1)S(1)}) custom-call(s32[2]{0:T(128)S(1)} %pad_add_fusion.place_ref, bf16[128,896]{1,0:T(8,128)(2,1)S(1)} %collective-permute-done.13.refs_0_, ...), custom_call_target="tpu_custom_call" | custom-call | flops 704643072 | bytes 5992448 | tf_op jit(solution)/shard_map/pallas_call | solution.py:197
  49.1 1.7 %collective-permute-start.15 = (bf16[5,32,1024]{2,1,0:T(8,128)(2,1)S(1)}, bf16[5,32,1024]{2,1,0:T(8,128)(2,1)S(1)}, u32[]{:S(2)}, u32[]{:S(2)}) collective-permute-start(bf16[5,32,1024]{2,1,0:T(8,128)(2,1)S(1)} %get-tuple-element.57), channel_id=1, source_target_pairs={{0,4},{4,0},{8,12},{12,8},{1,5},{5,1},{9,13},{13,9},{2,6},{6,2},{1... | collective-permute-start | bytes 983048 | tf_op jit(solution)/shard_map/ppermute | solution.py:159
  50.8 1.5 %collective-permute-start.16 = (bf16[5,32,1024]{2,1,0:T(8,128)(2,1)S(1)}, bf16[5,32,1024]{2,1,0:T(8,128)(2,1)S(1)}, u32[]{:S(2)}, u32[]{:S(2)}) collective-permute-start(bf16[5,32,1024]{2,1,0:T(8,128)(2,1)S(1)} %get-tuple-element.58), channel_id=1, source_target_pairs={{0,8},{4,12},{8,0},{12,4},{1,9},{5,13},{9,1},{13,5},{2,10},{6,14},... | collective-permute-start | bytes 983048 | tf_op jit(solution)/shard_map/ppermute | solution.py:159
  53.6 1.3 %shard_map.137.refs_3_ = bf16[128,896]{1,0:T(8,128)(2,1)S(1)} custom-call(s32[2]{0:T(128)S(1)} %pad_add_fusion.place_ref, bf16[5,32,1024]{2,1,0:T(8,128)(2,1)S(1)} %get-tuple-element.47.refs_5_.refs_0_, bf16[5,32,1024]{2,1,0:T(8,128)(2,1)S(1)} %collective-permute-done.10.refs_1_, bf16[5,32,1024]{2,1,0:T(8,128)(2,1)S(1)} %collective-permute-done.11.refs_2_, ...), custom_call_target="tpu_custom_call" | custom-call | flops 469762048 | bytes 6287360 | tf_op jit(solution)/shard_map/pallas_call | solution.py:197
  55.0 3.1 %collective-permute-start.22 = (bf16[128,896]{1,0:T(8,128)(2,1)S(1)}, bf16[128,896]{1,0:T(8,128)(2,1)S(1)}, u32[]{:S(2)}, u32[]{:S(2)}) collective-permute-start(bf16[128,896]{1,0:T(8,128)(2,1)S(1)} %shard_map.136.refs_9_), channel_id=1, source_target_pairs={{0,18},{1,16},{3,17},{2,19},{16,2},{17,0},{19,1},{18,3},{4,22},{5,... | collective-permute-start | bytes 688136 | tf_op jit(solution)/shard_map/ppermute | solution.py:182
  60.4 1.3 %collective-permute-done.16.refs_2_ = bf16[5,32,1024]{2,1,0:T(8,128)(2,1)S(1)} collective-permute-done((bf16[5,32,1024]{2,1,0:T(8,128)(2,1)S(1)}, bf16[5,32,1024]{2,1,0:T(8,128)(2,1)S(1)}, u32[]{:S(2)}, u32[]{:S(2)}) %collective-permute-start.16) | collective-permute-done | bytes 327712 | tf_op jit(solution)/shard_map/ppermute | solution.py:159
  63.4 2.1 %collective-permute-start.21 = (bf16[128,896]{1,0:T(8,128)(2,1)S(1)}, bf16[128,896]{1,0:T(8,128)(2,1)S(1)}, u32[]{:S(2)}, u32[]{:S(2)}) collective-permute-start(bf16[128,896]{1,0:T(8,128)(2,1)S(1)} %shard_map.141.refs_9_), channel_id=1, source_target_pairs={{0,1},{1,3},{3,2},{2,0},{4,5},{5,7},{7,6},{6,4},{8,9},{9,11},{11,1... | collective-permute-start | bytes 688136 | tf_op jit(solution)/shard_map/ppermute | solution.py:172
  65.5 1.7 %collective-permute-start.20 = (bf16[3,32,1024]{2,1,0:T(8,128)(2,1)S(1)}, bf16[3,32,1024]{2,1,0:T(8,128)(2,1)S(1)}, u32[]{:S(2)}, u32[]{:S(2)}) collective-permute-start(bf16[3,32,1024]{2,1,0:T(8,128)(2,1)S(1)} %shard_map.140.refs_6_.refs_0_), channel_id=1, source_target_pairs={{0,12},{4,8},{8,4},{12,0},{1,13},{5,9},{9,5},{13,1},{2,14},{6,10},... | collective-permute-start | bytes 589832 | tf_op jit(solution)/shard_map/ppermute | solution.py:159
  69.0 1.3 %shard_map.142.refs_7_ = bf16[128,896]{1,0:T(8,128)(2,1)S(1)} custom-call(s32[2]{0:T(128)S(1)} %pad_add_fusion.place_ref, bf16[5,32,1024]{2,1,0:T(8,128)(2,1)S(1)} %get-tuple-element.56.refs_6_.refs_0_, bf16[5,32,1024]{2,1,0:T(8,128)(2,1)S(1)} %collective-permute-done.15.refs_1_, bf16[5,32,1024]{2,1,0:T(8,128)(2,1)S(1)} %collective-permute-done.16.refs_2_, ...), custom_call_target="tpu_custom_call" | custom-call | flops 469762048 | bytes 6287360 | tf_op jit(solution)/shard_map/pallas_call | solution.py:197
  70.4 3.5 %collective-permute-start.28 = (bf16[128,896]{1,0:T(8,128)(2,1)S(1)}, bf16[128,896]{1,0:T(8,128)(2,1)S(1)}, u32[]{:S(2)}, u32[]{:S(2)}) collective-permute-start(bf16[128,896]{1,0:T(8,128)(2,1)S(1)} %shard_map.142.refs_7_), channel_id=1, source_target_pairs={{0,1},{1,3},{3,2},{2,0},{4,5},{5,7},{7,6},{6,4},{8,9},{9,11},{11,1... | collective-permute-start | bytes 688136 | tf_op jit(solution)/shard_map/ppermute | solution.py:172
  75.9 2.1 %collective-permute-start.27 = (bf16[1,32,1024]{2,1,0:T(8,128)(2,1)S(1)}, bf16[1,32,1024]{2,1,0:T(8,128)(2,1)S(1)}, u32[]{:S(2)}, u32[]{:S(2)}) collective-permute-start(bf16[1,32,1024]{2,1,0:T(8,128)(2,1)S(1)} %shard_map.144.refs_10_.refs_0_), channel_id=1, source_target_pairs={{0,12},{4,8},{8,4},{12,0},{1,13},{5,9},{9,5},{13,1},{2,14},{6,10},... | collective-permute-start | bytes 196616 | tf_op jit(solution)/shard_map/ppermute | solution.py:159
  79.4 1.3 %shard_map.145.refs_10_ = bf16[128,896]{1,0:T(8,128)(2,1)S(1)} custom-call(s32[2]{0:T(128)S(1)} %pad_add_fusion.place_ref, bf16[3,32,1024]{2,1,0:T(8,128)(2,1)S(1)} %shard_map.140.refs_6_.refs_0_, bf16[3,32,1024]{2,1,0:T(8,128)(2,1)S(1)} %collective-permute-done.18.refs_1_.refs_2_, bf16[3,32,1024]{2,1,0:T(8,128)(2,1)S(1)} %collective-permute-done.19.refs_2_.refs_3_, ...), custom_call_target="tpu_custom_call" | custom-call | flops 469762048 | bytes 5992448 | tf_op jit(solution)/shard_map/pallas_call | solution.py:197
  80.7 2.2 %collective-permute-start.30 = (bf16[128,896]{1,0:T(8,128)(2,1)S(1)}, bf16[128,896]{1,0:T(8,128)(2,1)S(1)}, u32[]{:S(2)}, u32[]{:S(2)}) collective-permute-start(bf16[128,896]{1,0:T(8,128)(2,1)S(1)} %shard_map.145.refs_10_), channel_id=1, source_target_pairs={{0,17},{1,19},{3,18},{2,16},{16,1},{17,3},{19,2},{18,0},{4,21},{5,... | collective-permute-start | bytes 688136 | tf_op jit(solution)/shard_map/ppermute | solution.py:182
  83.0 1.3 %shard_map.146.refs_7_ = bf16[128,896]{1,0:T(8,128)(2,1)S(1)} custom-call(s32[2]{0:T(128)S(1)} %pad_add_fusion.place_ref, bf16[3,32,1024]{2,1,0:T(8,128)(2,1)S(1)} %shard_map.140.refs_6_.refs_0_, bf16[3,32,1024]{2,1,0:T(8,128)(2,1)S(1)} %collective-permute-done.18.refs_1_.refs_2_, bf16[3,32,1024]{2,1,0:T(8,128)(2,1)S(1)} %collective-permute-done.19.refs_2_.refs_3_, ...), custom_call_target="tpu_custom_call" | custom-call | flops 469762048 | bytes 5992448 | tf_op jit(solution)/shard_map/pallas_call | solution.py:197
  86.7 1.4 %collective-permute-done.29 = bf16[128,896]{1,0:T(8,128)(2,1)S(1)} collective-permute-done((bf16[128,896]{1,0:T(8,128)(2,1)S(1)}, bf16[128,896]{1,0:T(8,128)(2,1)S(1)}, u32[]{:S(2)}, u32[]{:S(2)}) %collective-permute-start.29) | collective-permute-done | bytes 229408 | tf_op jit(solution)/shard_map/ppermute | solution.py:14
  (91 shorter events, 25.4 us)
Async XLA Ops:
  1.6 14.1 %collective-permute-start.1 = (bf16[144,896]{1,0:T(8,128)(2,1)S(1)}, bf16[144,896]{1,0:T(8,128)(2,1)S(1)}, u32[]{:S(2)}, u32[]{:S(2)}) collective-permute-start(bf16[144,896]{1,0:T(8,128)(2,1)S(1)} %shard_map.123.refs_1_.refs_2_.refs_8_.refs_5_), channel_id=1, source_target_pairs={{0,1},{1,3},{3,2},{2,0},{4,5},{5,7},{7,6},{6,4},{8,9},{9,11},{11,1... | collective-permute-start | bytes 774152 | tf_op jit(solution)/shard_map/ppermute | solution.py:172
  4.7 12.1 %collective-permute-start = (bf16[128,896]{1,0:T(8,128)(2,1)S(1)}, bf16[128,896]{1,0:T(8,128)(2,1)S(1)}, u32[]{:S(2)}, u32[]{:S(2)}) collective-permute-start(bf16[128,896]{1,0:T(8,128)(2,1)S(1)} %bitcast.50), channel_id=1, source_target_pairs={{0,1},{1,3},{3,2},{2,0},{4,5},{5,7},{7,6},{6,4},{8,9},{9,11},{11,1... | collective-permute-start | bytes 688136 | tf_op jit(solution)/shard_map/ppermute | solution.py:172
  12.2 9.7 %collective-permute-start.7 = (bf16[3,32,1024]{2,1,0:T(8,128)(2,1)S(1)}, bf16[3,32,1024]{2,1,0:T(8,128)(2,1)S(1)}, u32[]{:S(2)}, u32[]{:S(2)}) collective-permute-start(bf16[3,32,1024]{2,1,0:T(8,128)(2,1)S(1)} %get-tuple-element.39), channel_id=1, source_target_pairs={{0,4},{4,0},{8,12},{12,8},{1,5},{5,1},{9,13},{13,9},{2,6},{6,2},{1... | collective-permute-start | bytes 589832 | tf_op jit(solution)/shard_map/ppermute | solution.py:159
  13.8 9.8 %collective-permute-start.8 = (bf16[3,32,1024]{2,1,0:T(8,128)(2,1)S(1)}, bf16[3,32,1024]{2,1,0:T(8,128)(2,1)S(1)}, u32[]{:S(2)}, u32[]{:S(2)}) collective-permute-start(bf16[3,32,1024]{2,1,0:T(8,128)(2,1)S(1)} %get-tuple-element.40), channel_id=1, source_target_pairs={{0,8},{4,12},{8,0},{12,4},{1,9},{5,13},{9,1},{13,5},{2,10},{6,14},... | collective-permute-start | bytes 589832 | tf_op jit(solution)/shard_map/ppermute | solution.py:159
  15.3 10.4 %collective-permute-start.9 = (bf16[3,32,1024]{2,1,0:T(8,128)(2,1)S(1)}, bf16[3,32,1024]{2,1,0:T(8,128)(2,1)S(1)}, u32[]{:S(2)}, u32[]{:S(2)}) collective-permute-start(bf16[3,32,1024]{2,1,0:T(8,128)(2,1)S(1)} %get-tuple-element.41), channel_id=1, source_target_pairs={{0,12},{4,8},{8,4},{12,0},{1,13},{5,9},{9,5},{13,1},{2,14},{6,10},... | collective-permute-start | bytes 589832 | tf_op jit(solution)/shard_map/ppermute | solution.py:159
  15.8 10.7 %collective-permute-start.6 = (bf16[144,896]{1,0:T(8,128)(2,1)S(1)}, bf16[144,896]{1,0:T(8,128)(2,1)S(1)}, u32[]{:S(2)}, u32[]{:S(2)}) collective-permute-start(bf16[144,896]{1,0:T(8,128)(2,1)S(1)} %collective-permute-done.1.refs_1_.refs_2_.refs_5_.refs_8_), channel_id=1, source_target_pairs={{0,1},{1,3},{3,2},{2,0},{4,5},{5,7},{7,6},{6,4},{8,9},{9,11},{11,1... | collective-permute-start | bytes 774152 | tf_op jit(solution)/shard_map/ppermute | solution.py:172
  16.9 12.8 %collective-permute-start.5 = (bf16[128,896]{1,0:T(8,128)(2,1)S(1)}, bf16[128,896]{1,0:T(8,128)(2,1)S(1)}, u32[]{:S(2)}, u32[]{:S(2)}) collective-permute-start(bf16[128,896]{1,0:T(8,128)(2,1)S(1)} %collective-permute-done.refs_0_), channel_id=1, source_target_pairs={{0,1},{1,3},{3,2},{2,0},{4,5},{5,7},{7,6},{6,4},{8,9},{9,11},{11,1... | collective-permute-start | bytes 688136 | tf_op jit(solution)/shard_map/ppermute | solution.py:172
  21.9 10.4 %collective-permute-start.2 = (bf16[3,32,1024]{2,1,0:T(8,128)(2,1)S(1)}, bf16[3,32,1024]{2,1,0:T(8,128)(2,1)S(1)}, u32[]{:S(2)}, u32[]{:S(2)}) collective-permute-start(bf16[3,32,1024]{2,1,0:T(8,128)(2,1)S(1)} %get-tuple-element.36), channel_id=1, source_target_pairs={{0,4},{4,0},{8,12},{12,8},{1,5},{5,1},{9,13},{13,9},{2,6},{6,2},{1... | collective-permute-start | bytes 589832 | tf_op jit(solution)/shard_map/ppermute | solution.py:159
  23.6 8.7 %collective-permute-start.3 = (bf16[3,32,1024]{2,1,0:T(8,128)(2,1)S(1)}, bf16[3,32,1024]{2,1,0:T(8,128)(2,1)S(1)}, u32[]{:S(2)}, u32[]{:S(2)}) collective-permute-start(bf16[3,32,1024]{2,1,0:T(8,128)(2,1)S(1)} %get-tuple-element.37), channel_id=1, source_target_pairs={{0,8},{4,12},{8,0},{12,4},{1,9},{5,13},{9,1},{13,5},{2,10},{6,14},... | collective-permute-start | bytes 589832 | tf_op jit(solution)/shard_map/ppermute | solution.py:159
  25.7 6.6 %collective-permute-start.4 = (bf16[3,32,1024]{2,1,0:T(8,128)(2,1)S(1)}, bf16[3,32,1024]{2,1,0:T(8,128)(2,1)S(1)}, u32[]{:S(2)}, u32[]{:S(2)}) collective-permute-start(bf16[3,32,1024]{2,1,0:T(8,128)(2,1)S(1)} %get-tuple-element.38), channel_id=1, source_target_pairs={{0,12},{4,8},{8,4},{12,0},{1,13},{5,9},{9,5},{13,1},{2,14},{6,10},... | collective-permute-start | bytes 589832 | tf_op jit(solution)/shard_map/ppermute | solution.py:159
  26.4 17.1 %collective-permute-start.14 = (bf16[144,896]{1,0:T(8,128)(2,1)S(1)}, bf16[144,896]{1,0:T(8,128)(2,1)S(1)}, u32[]{:S(2)}, u32[]{:S(2)}) collective-permute-start(bf16[144,896]{1,0:T(8,128)(2,1)S(1)} %collective-permute-done.6.refs_1_.refs_2_.refs_5_.refs_8_), channel_id=1, source_target_pairs={{0,1},{1,3},{3,2},{2,0},{4,5},{5,7},{7,6},{6,4},{8,9},{9,11},{11,1... | collective-permute-start | bytes 774152 | tf_op jit(solution)/shard_map/ppermute | solution.py:172
  33.1 15.3 %collective-permute-start.10 = (bf16[5,32,1024]{2,1,0:T(8,128)(2,1)S(1)}, bf16[5,32,1024]{2,1,0:T(8,128)(2,1)S(1)}, u32[]{:S(2)}, u32[]{:S(2)}) collective-permute-start(bf16[5,32,1024]{2,1,0:T(8,128)(2,1)S(1)} %get-tuple-element.48), channel_id=1, source_target_pairs={{0,4},{4,0},{8,12},{12,8},{1,5},{5,1},{9,13},{13,9},{2,6},{6,2},{1... | collective-permute-start | bytes 983048 | tf_op jit(solution)/shard_map/ppermute | solution.py:159
  34.8 13.6 %collective-permute-start.11 = (bf16[5,32,1024]{2,1,0:T(8,128)(2,1)S(1)}, bf16[5,32,1024]{2,1,0:T(8,128)(2,1)S(1)}, u32[]{:S(2)}, u32[]{:S(2)}) collective-permute-start(bf16[5,32,1024]{2,1,0:T(8,128)(2,1)S(1)} %get-tuple-element.49), channel_id=1, source_target_pairs={{0,8},{4,12},{8,0},{12,4},{1,9},{5,13},{9,1},{13,5},{2,10},{6,14},... | collective-permute-start | bytes 983048 | tf_op jit(solution)/shard_map/ppermute | solution.py:159
  36.3 12.1 %collective-permute-start.12 = (bf16[5,32,1024]{2,1,0:T(8,128)(2,1)S(1)}, bf16[5,32,1024]{2,1,0:T(8,128)(2,1)S(1)}, u32[]{:S(2)}, u32[]{:S(2)}) collective-permute-start(bf16[5,32,1024]{2,1,0:T(8,128)(2,1)S(1)} %get-tuple-element.50), channel_id=1, source_target_pairs={{0,12},{4,8},{8,4},{12,0},{1,13},{5,9},{9,5},{13,1},{2,14},{6,10},... | collective-permute-start | bytes 983048 | tf_op jit(solution)/shard_map/ppermute | solution.py:159
  36.6 6.9 %collective-permute-start.13 = (bf16[128,896]{1,0:T(8,128)(2,1)S(1)}, bf16[128,896]{1,0:T(8,128)(2,1)S(1)}, u32[]{:S(2)}, u32[]{:S(2)}) collective-permute-start(bf16[128,896]{1,0:T(8,128)(2,1)S(1)} %collective-permute-done.5.refs_0_), channel_id=1, source_target_pairs={{0,1},{1,3},{3,2},{2,0},{4,5},{5,7},{7,6},{6,4},{8,9},{9,11},{11,1... | collective-permute-start | bytes 688136 | tf_op jit(solution)/shard_map/ppermute | solution.py:172
  49.1 11.3 %collective-permute-start.15 = (bf16[5,32,1024]{2,1,0:T(8,128)(2,1)S(1)}, bf16[5,32,1024]{2,1,0:T(8,128)(2,1)S(1)}, u32[]{:S(2)}, u32[]{:S(2)}) collective-permute-start(bf16[5,32,1024]{2,1,0:T(8,128)(2,1)S(1)} %get-tuple-element.57), channel_id=1, source_target_pairs={{0,4},{4,0},{8,12},{12,8},{1,5},{5,1},{9,13},{13,9},{2,6},{6,2},{1... | collective-permute-start | bytes 983048 | tf_op jit(solution)/shard_map/ppermute | solution.py:159
  50.8 10.9 %collective-permute-start.16 = (bf16[5,32,1024]{2,1,0:T(8,128)(2,1)S(1)}, bf16[5,32,1024]{2,1,0:T(8,128)(2,1)S(1)}, u32[]{:S(2)}, u32[]{:S(2)}) collective-permute-start(bf16[5,32,1024]{2,1,0:T(8,128)(2,1)S(1)} %get-tuple-element.58), channel_id=1, source_target_pairs={{0,8},{4,12},{8,0},{12,4},{1,9},{5,13},{9,1},{13,5},{2,10},{6,14},... | collective-permute-start | bytes 983048 | tf_op jit(solution)/shard_map/ppermute | solution.py:159
  52.3 9.4 %collective-permute-start.17 = (bf16[5,32,1024]{2,1,0:T(8,128)(2,1)S(1)}, bf16[5,32,1024]{2,1,0:T(8,128)(2,1)S(1)}, u32[]{:S(2)}, u32[]{:S(2)}) collective-permute-start(bf16[5,32,1024]{2,1,0:T(8,128)(2,1)S(1)} %get-tuple-element.59), channel_id=1, source_target_pairs={{0,12},{4,8},{8,4},{12,0},{1,13},{5,9},{9,5},{13,1},{2,14},{6,10},... | collective-permute-start | bytes 983048 | tf_op jit(solution)/shard_map/ppermute | solution.py:159
  55.0 13.2 %collective-permute-start.23 = (bf16[128,896]{1,0:T(8,128)(2,1)S(1)}, bf16[128,896]{1,0:T(8,128)(2,1)S(1)}, u32[]{:S(2)}, u32[]{:S(2)}) collective-permute-start(bf16[128,896]{1,0:T(8,128)(2,1)S(1)} %shard_map.137.refs_3_), channel_id=1, source_target_pairs={{0,18},{1,16},{3,17},{2,19},{16,2},{17,0},{19,1},{18,3},{4,22},{5,... | collective-permute-start | bytes 688136 | tf_op jit(solution)/shard_map/ppermute | solution.py:182
  55.0 14.0 %collective-permute-start.22 = (bf16[128,896]{1,0:T(8,128)(2,1)S(1)}, bf16[128,896]{1,0:T(8,128)(2,1)S(1)}, u32[]{:S(2)}, u32[]{:S(2)}) collective-permute-start(bf16[128,896]{1,0:T(8,128)(2,1)S(1)} %shard_map.136.refs_9_), channel_id=1, source_target_pairs={{0,18},{1,16},{3,17},{2,19},{16,2},{17,0},{19,1},{18,3},{4,22},{5,... | collective-permute-start | bytes 688136 | tf_op jit(solution)/shard_map/ppermute | solution.py:182
  63.4 10.8 %collective-permute-start.21 = (bf16[128,896]{1,0:T(8,128)(2,1)S(1)}, bf16[128,896]{1,0:T(8,128)(2,1)S(1)}, u32[]{:S(2)}, u32[]{:S(2)}) collective-permute-start(bf16[128,896]{1,0:T(8,128)(2,1)S(1)} %shard_map.141.refs_9_), channel_id=1, source_target_pairs={{0,1},{1,3},{3,2},{2,0},{4,5},{5,7},{7,6},{6,4},{8,9},{9,11},{11,1... | collective-permute-start | bytes 688136 | tf_op jit(solution)/shard_map/ppermute | solution.py:172
  65.5 8.3 %collective-permute-start.20 = (bf16[3,32,1024]{2,1,0:T(8,128)(2,1)S(1)}, bf16[3,32,1024]{2,1,0:T(8,128)(2,1)S(1)}, u32[]{:S(2)}, u32[]{:S(2)}) collective-permute-start(bf16[3,32,1024]{2,1,0:T(8,128)(2,1)S(1)} %shard_map.140.refs_6_.refs_0_), channel_id=1, source_target_pairs={{0,12},{4,8},{8,4},{12,0},{1,13},{5,9},{9,5},{13,1},{2,14},{6,10},... | collective-permute-start | bytes 589832 | tf_op jit(solution)/shard_map/ppermute | solution.py:159
  67.3 7.0 %collective-permute-start.19 = (bf16[3,32,1024]{2,1,0:T(8,128)(2,1)S(1)}, bf16[3,32,1024]{2,1,0:T(8,128)(2,1)S(1)}, u32[]{:S(2)}, u32[]{:S(2)}) collective-permute-start(bf16[3,32,1024]{2,1,0:T(8,128)(2,1)S(1)} %shard_map.140.refs_6_.refs_0_), channel_id=1, source_target_pairs={{0,8},{4,12},{8,0},{12,4},{1,9},{5,13},{9,1},{13,5},{2,10},{6,14},... | collective-permute-start | bytes 589832 | tf_op jit(solution)/shard_map/ppermute | solution.py:159
  68.2 6.0 %collective-permute-start.18 = (bf16[3,32,1024]{2,1,0:T(8,128)(2,1)S(1)}, bf16[3,32,1024]{2,1,0:T(8,128)(2,1)S(1)}, u32[]{:S(2)}, u32[]{:S(2)}) collective-permute-start(bf16[3,32,1024]{2,1,0:T(8,128)(2,1)S(1)} %shard_map.140.refs_6_.refs_0_), channel_id=1, source_target_pairs={{0,4},{4,0},{8,12},{12,8},{1,5},{5,1},{9,13},{13,9},{2,6},{6,2},{1... | collective-permute-start | bytes 589832 | tf_op jit(solution)/shard_map/ppermute | solution.py:159
  70.4 9.1 %collective-permute-start.28 = (bf16[128,896]{1,0:T(8,128)(2,1)S(1)}, bf16[128,896]{1,0:T(8,128)(2,1)S(1)}, u32[]{:S(2)}, u32[]{:S(2)}) collective-permute-start(bf16[128,896]{1,0:T(8,128)(2,1)S(1)} %shard_map.142.refs_7_), channel_id=1, source_target_pairs={{0,1},{1,3},{3,2},{2,0},{4,5},{5,7},{7,6},{6,4},{8,9},{9,11},{11,1... | collective-permute-start | bytes 688136 | tf_op jit(solution)/shard_map/ppermute | solution.py:172
  75.3 11.4 %collective-permute-start.24 = (bf16[128,896]{1,0:T(8,128)(2,1)S(1)}, bf16[128,896]{1,0:T(8,128)(2,1)S(1)}, u32[]{:S(2)}, u32[]{:S(2)}) collective-permute-start(bf16[128,896]{1,0:T(8,128)(2,1)S(1)} %shard_map.143.refs_1_), channel_id=1, source_target_pairs={{0,17},{1,19},{3,18},{2,16},{16,1},{17,3},{19,2},{18,0},{4,21},{5,... | collective-permute-start | bytes 688136 | tf_op jit(solution)/shard_map/ppermute | solution.py:182
  75.9 8.4 %collective-permute-start.27 = (bf16[1,32,1024]{2,1,0:T(8,128)(2,1)S(1)}, bf16[1,32,1024]{2,1,0:T(8,128)(2,1)S(1)}, u32[]{:S(2)}, u32[]{:S(2)}) collective-permute-start(bf16[1,32,1024]{2,1,0:T(8,128)(2,1)S(1)} %shard_map.144.refs_10_.refs_0_), channel_id=1, source_target_pairs={{0,12},{4,8},{8,4},{12,0},{1,13},{5,9},{9,5},{13,1},{2,14},{6,10},... | collective-permute-start | bytes 196616 | tf_op jit(solution)/shard_map/ppermute | solution.py:159
  78.0 7.6 %collective-permute-start.26 = (bf16[1,32,1024]{2,1,0:T(8,128)(2,1)S(1)}, bf16[1,32,1024]{2,1,0:T(8,128)(2,1)S(1)}, u32[]{:S(2)}, u32[]{:S(2)}) collective-permute-start(bf16[1,32,1024]{2,1,0:T(8,128)(2,1)S(1)} %shard_map.144.refs_10_.refs_0_), channel_id=1, source_target_pairs={{0,8},{4,12},{8,0},{12,4},{1,9},{5,13},{9,1},{13,5},{2,10},{6,14},... | collective-permute-start | bytes 196616 | tf_op jit(solution)/shard_map/ppermute | solution.py:159
  78.6 6.9 %collective-permute-start.25 = (bf16[1,32,1024]{2,1,0:T(8,128)(2,1)S(1)}, bf16[1,32,1024]{2,1,0:T(8,128)(2,1)S(1)}, u32[]{:S(2)}, u32[]{:S(2)}) collective-permute-start(bf16[1,32,1024]{2,1,0:T(8,128)(2,1)S(1)} %shard_map.144.refs_10_.refs_0_), channel_id=1, source_target_pairs={{0,4},{4,0},{8,12},{12,8},{1,5},{5,1},{9,13},{13,9},{2,6},{6,2},{1... | collective-permute-start | bytes 196616 | tf_op jit(solution)/shard_map/ppermute | solution.py:159
  80.7 7.8 %collective-permute-start.30 = (bf16[128,896]{1,0:T(8,128)(2,1)S(1)}, bf16[128,896]{1,0:T(8,128)(2,1)S(1)}, u32[]{:S(2)}, u32[]{:S(2)}) collective-permute-start(bf16[128,896]{1,0:T(8,128)(2,1)S(1)} %shard_map.145.refs_10_), channel_id=1, source_target_pairs={{0,17},{1,19},{3,18},{2,16},{16,1},{17,3},{19,2},{18,0},{4,21},{5,... | collective-permute-start | bytes 688136 | tf_op jit(solution)/shard_map/ppermute | solution.py:182
  84.3 4.6 %collective-permute-start.31 = (bf16[128,896]{1,0:T(8,128)(2,1)S(1)}, bf16[128,896]{1,0:T(8,128)(2,1)S(1)}, u32[]{:S(2)}, u32[]{:S(2)}) collective-permute-start(bf16[128,896]{1,0:T(8,128)(2,1)S(1)} %shard_map.146.refs_7_), channel_id=1, source_target_pairs={{0,16},{16,0},{1,17},{17,1},{2,18},{18,2},{3,19},{19,3},{4,20},{20... | collective-permute-start | bytes 688136 | tf_op jit(solution)/shard_map/ppermute | solution.py:14
  86.5 1.6 %collective-permute-start.29 = (bf16[128,896]{1,0:T(8,128)(2,1)S(1)}, bf16[128,896]{1,0:T(8,128)(2,1)S(1)}, u32[]{:S(2)}, u32[]{:S(2)}) collective-permute-start(bf16[128,896]{1,0:T(8,128)(2,1)S(1)} %shard_map.147.refs_1_), channel_id=1, source_target_pairs={{0,16},{16,0},{1,17},{17,1},{2,18},{18,2},{3,19},{19,3},{4,20},{20... | collective-permute-start | bytes 688136 | tf_op jit(solution)/shard_map/ppermute | solution.py:14
  (14 other events, 40.8 us)

commit v11 on v8

--- a/solution.py
+++ b/solution.py
@@ -639,9 +639,8 @@
             sums[kind].append(along_ring_and_sections(value, 1, shift))
 
     first(0)
-    if TURN_DOWN:
-        first_weights[:] = (*weights[:2], turn(2)), PLAIN
     first(1)
+    first_weights[:] = (*weights[:2], turn(2)), PLAIN
     own_acts = activations(place, parts[0], (), done[-1:])[0]
     done.append(own_acts)
     for step in range(1, experts - 1):

time: 90.2 us -> 90.2 us (level)
  waiting for transfers between devices: 7.7 us -> 12.5 us
  starting transfers between devices: 48.3 us -> 43.9 us
    ppermute x8, starting transfers between devices: 19.9 us -> 14.8 us  [along_ring(): return lax.ppermute(value, 'dev', ring_pairs(lax.axis_size('dev'), steps))]
    ppermute x8, waiting for transfers between devices: 1.95 us -> 4.42 us  [along_ring(): return lax.ppermute(value, 'dev', ring_pairs(lax.axis_size('dev'), steps))]
    ppermute x18, waiting for transfers between devices: 4.09 us -> 6.4 us  [across(): lax.ppermute(value, axis, [(source, source ^ mask) for source in range(co...]
    ppermute x18, starting transfers between devices: 21.3 us -> 22.7 us  [across(): lax.ppermute(value, axis, [(source, source ^ mask) for source in range(co...]
  transfers between devices with their start and end apart: 32 -> 32, of which waited for: 8 -> 9; matrix products, arithmetic and copies ran while one was open for 0% -> 0% of each run, Pallas kernels for 29% -> 29%
where the time goes in v11:
time: 90.2 us; the launch traced here: 89.3 us
  starting transfers between devices  43.9 us (49%)
  Pallas kernels  27 us (30%)
  waiting for transfers between devices  12.5 us (14%)
  local copies, waits for them, and re-layouts  3.94 us (4%)
  between operations  1.05 us (1%)
  other arithmetic  0.92 us (1%)
    pallas_call x24, Pallas kernels, call(): pl.pallas_call(with_after, in_specs=[SMEM] + [VMEM] * len(operands) + [AN...  26.9 us
    ppermute x18, starting transfers between devices, across(): lax.ppermute(value, axis, [(source, source ^ mask) for source in range(co...  22.7 us
    ppermute x8, starting transfers between devices, along_ring(): return lax.ppermute(value, 'dev', ring_pairs(lax.axis_size('dev'), steps))  14.8 us
    ppermute x18, waiting for transfers between devices, across(): lax.ppermute(value, axis, [(source, source ^ mask) for source in range(co...  6.4 us
    ppermute x4, starting transfers between devices, along_ring_and_sections(): return lax.ppermute(value, ('section', 'dev'), pairs)  5.31 us
    ppermute x8, waiting for transfers between devices, along_ring(): return lax.ppermute(value, 'dev', ring_pairs(lax.axis_size('dev'), steps))  4.42 us
    unnamed x28, local copies, waits for them, and re-layouts  3.94 us
  transfers between devices with their start and end apart: 32, of which 9 were waited for; matrix products, arithmetic and copies ran while one was open for 0% of the time, Pallas kernels for 29%

profile of v11, /device:TPU:0, one launch (start us, length us, event | category | flops | bytes accessed | tf_op | source)
XLA Modules:
  0.0 89.3 jit_solution(17793018049777464412)
XLA Ops:
  1.6 3.1 %collective-permute-start.1 = (bf16[144,896]{1,0:T(8,128)(2,1)S(1)}, bf16[144,896]{1,0:T(8,128)(2,1)S(1)}, u32[]{:S(2)}, u32[]{:S(2)}) collective-permute-start(bf16[144,896]{1,0:T(8,128)(2,1)S(1)} %shard_map.123.refs_1_.refs_2_.refs_5_.refs_8_), channel_id=1, source_target_pairs={{0,1},{1,3},{3,2},{2,0},{4,5},{5,7},{7,6},{6,4},{8,9},{9,11},{11,1... | collective-permute-start | bytes 774152 | tf_op jit(solution)/shard_map/ppermute | solution.py:172
  4.7 2.6 %collective-permute-start = (bf16[128,896]{1,0:T(8,128)(2,1)S(1)}, bf16[128,896]{1,0:T(8,128)(2,1)S(1)}, u32[]{:S(2)}, u32[]{:S(2)}) collective-permute-start(bf16[128,896]{1,0:T(8,128)(2,1)S(1)} %bitcast.51), channel_id=1, source_target_pairs={{0,1},{1,3},{3,2},{2,0},{4,5},{5,7},{7,6},{6,4},{8,9},{9,11},{11,1... | collective-permute-start | bytes 688136 | tf_op jit(solution)/shard_map/ppermute | solution.py:172
  7.4 1.5 %copy-done.1 = bf16[1,1,896,1024]{3,2,1,0:T(8,128)(2,1)S(1)} copy-done((bf16[1,1,896,1024]{3,2,1,0:T(8,128)(2,1)S(1)}, bf16[1,1,896,1024]{3,2,1,0:T(8,128)(2,1)}, u32[]{:S(2)}) %copy-start.1) | copy-done | bytes 1835032
  8.9 1.5 %copy-done.3 = bf16[1,1,896,1024]{3,2,1,0:T(8,128)(2,1)S(1)} copy-done((bf16[1,1,896,1024]{3,2,1,0:T(8,128)(2,1)S(1)}, bf16[1,1,896,1024]{3,2,1,0:T(8,128)(2,1)}, u32[]{:S(2)}) %copy-start.3) | copy-done | bytes 1835032
  10.4 1.8 %shard_map.124 = (bf16[3,32,1024]{2,1,0:T(8,128)(2,1)S(1)}, bf16[3,32,1024]{2,1,0:T(8,128)(2,1)S(1)}, bf16[3,32,1024]{2,1,0:T(8,128)(2,1)S(1)}, bf16[3,32,1024]{2,1,0:T(8,128)(2,1)S(1)}) custom-call(s32[2]{0:T(128)S(1)} %pad_add_fusion.place_ref, bf16[128,896]{1,0:T(8,128)(2,1)S(1)} %bitcast.52, ...), custom_call_target="tpu_custom_call" | custom-call | flops 704643072 | bytes 5992448 | tf_op jit(solution)/shard_map/pallas_call | solution.py:197
  12.2 1.6 %collective-permute-start.7 = (bf16[3,32,1024]{2,1,0:T(8,128)(2,1)S(1)}, bf16[3,32,1024]{2,1,0:T(8,128)(2,1)S(1)}, u32[]{:S(2)}, u32[]{:S(2)}) collective-permute-start(bf16[3,32,1024]{2,1,0:T(8,128)(2,1)S(1)} %get-tuple-element.39), channel_id=1, source_target_pairs={{0,4},{4,0},{8,12},{12,8},{1,5},{5,1},{9,13},{13,9},{2,6},{6,2},{1... | collective-permute-start | bytes 589832 | tf_op jit(solution)/shard_map/ppermute | solution.py:159
  13.8 1.5 %collective-permute-start.8 = (bf16[3,32,1024]{2,1,0:T(8,128)(2,1)S(1)}, bf16[3,32,1024]{2,1,0:T(8,128)(2,1)S(1)}, u32[]{:S(2)}, u32[]{:S(2)}) collective-permute-start(bf16[3,32,1024]{2,1,0:T(8,128)(2,1)S(1)} %get-tuple-element.40), channel_id=1, source_target_pairs={{0,8},{4,12},{8,0},{12,4},{1,9},{5,13},{9,1},{13,5},{2,10},{6,14},... | collective-permute-start | bytes 589832 | tf_op jit(solution)/shard_map/ppermute | solution.py:159
  16.9 2.0 %collective-permute-start.5 = (bf16[128,896]{1,0:T(8,128)(2,1)S(1)}, bf16[128,896]{1,0:T(8,128)(2,1)S(1)}, u32[]{:S(2)}, u32[]{:S(2)}) collective-permute-start(bf16[128,896]{1,0:T(8,128)(2,1)S(1)} %collective-permute-done.refs_0_), channel_id=1, source_target_pairs={{0,1},{1,3},{3,2},{2,0},{4,5},{5,7},{7,6},{6,4},{8,9},{9,11},{11,1... | collective-permute-start | bytes 688136 | tf_op jit(solution)/shard_map/ppermute | solution.py:172
  18.8 1.8 %shard_map.125 = (bf16[3,32,1024]{2,1,0:T(8,128)(2,1)S(1)}, bf16[3,32,1024]{2,1,0:T(8,128)(2,1)S(1)}, bf16[3,32,1024]{2,1,0:T(8,128)(2,1)S(1)}, bf16[3,32,1024]{2,1,0:T(8,128)(2,1)S(1)}) custom-call(s32[2]{0:T(128)S(1)} %pad_add_fusion.place_ref, bf16[128,896]{1,0:T(8,128)(2,1)S(1)} %collective-permute-done.refs_0_, ...), custom_call_target="tpu_custom_call" | custom-call | flops 704643072 | bytes 5992448 | tf_op jit(solution)/shard_map/pallas_call | solution.py:197
  20.7 1.6 %collective-permute-start.2 = (bf16[3,32,1024]{2,1,0:T(8,128)(2,1)S(1)}, bf16[3,32,1024]{2,1,0:T(8,128)(2,1)S(1)}, u32[]{:S(2)}, u32[]{:S(2)}) collective-permute-start(bf16[3,32,1024]{2,1,0:T(8,128)(2,1)S(1)} %get-tuple-element.36), channel_id=1, source_target_pairs={{0,4},{4,0},{8,12},{12,8},{1,5},{5,1},{9,13},{13,9},{2,6},{6,2},{1... | collective-permute-start | bytes 589832 | tf_op jit(solution)/shard_map/ppermute | solution.py:159
  23.2 2.7 %collective-permute-start.3 = (bf16[3,32,1024]{2,1,0:T(8,128)(2,1)S(1)}, bf16[3,32,1024]{2,1,0:T(8,128)(2,1)S(1)}, u32[]{:S(2)}, u32[]{:S(2)}) collective-permute-start(bf16[3,32,1024]{2,1,0:T(8,128)(2,1)S(1)} %get-tuple-element.37), channel_id=1, source_target_pairs={{0,8},{4,12},{8,0},{12,4},{1,9},{5,13},{9,1},{13,5},{2,10},{6,14},... | collective-permute-start | bytes 589832 | tf_op jit(solution)/shard_map/ppermute | solution.py:159
  29.5 1.6 %shard_map.128 = (bf16[5,32,1024]{2,1,0:T(8,128)(2,1)S(1)}, bf16[5,32,1024]{2,1,0:T(8,128)(2,1)S(1)}, bf16[5,32,1024]{2,1,0:T(8,128)(2,1)S(1)}, bf16[5,32,1024]{2,1,0:T(8,128)(2,1)S(1)}) custom-call(s32[2]{0:T(128)S(1)} %pad_add_fusion.place_ref, bf16[128,896]{1,0:T(8,128)(2,1)S(1)} %collective-permute-done.5.refs_0_, ...), custom_call_target="tpu_custom_call" | custom-call | flops 704643072 | bytes 5992448 | tf_op jit(solution)/shard_map/pallas_call | solution.py:197
  34.5 1.5 %collective-permute-start.11 = (bf16[5,32,1024]{2,1,0:T(8,128)(2,1)S(1)}, bf16[5,32,1024]{2,1,0:T(8,128)(2,1)S(1)}, u32[]{:S(2)}, u32[]{:S(2)}) collective-permute-start(bf16[5,32,1024]{2,1,0:T(8,128)(2,1)S(1)} %get-tuple-element.49), channel_id=1, source_target_pairs={{0,8},{4,12},{8,0},{12,4},{1,9},{5,13},{9,1},{13,5},{2,10},{6,14},... | collective-permute-start | bytes 983048 | tf_op jit(solution)/shard_map/ppermute | solution.py:159
  36.0 1.2 %collective-permute-start.12 = (bf16[5,32,1024]{2,1,0:T(8,128)(2,1)S(1)}, bf16[5,32,1024]{2,1,0:T(8,128)(2,1)S(1)}, u32[]{:S(2)}, u32[]{:S(2)}) collective-permute-start(bf16[5,32,1024]{2,1,0:T(8,128)(2,1)S(1)} %get-tuple-element.50), channel_id=1, source_target_pairs={{0,12},{4,8},{8,4},{12,0},{1,13},{5,9},{9,5},{13,1},{2,14},{6,10},... | collective-permute-start | bytes 983048 | tf_op jit(solution)/shard_map/ppermute | solution.py:159
  37.3 1.2 %collective-permute-start.13 = (bf16[128,896]{1,0:T(8,128)(2,1)S(1)}, bf16[128,896]{1,0:T(8,128)(2,1)S(1)}, u32[]{:S(2)}, u32[]{:S(2)}) collective-permute-start(bf16[128,896]{1,0:T(8,128)(2,1)S(1)} %collective-permute-done.5.refs_0_), channel_id=1, source_target_pairs={{0,1},{1,3},{3,2},{2,0},{4,5},{5,7},{7,6},{6,4},{8,9},{9,11},{11,1... | collective-permute-start | bytes 688136 | tf_op jit(solution)/shard_map/ppermute | solution.py:172
  40.6 3.6 %collective-permute-done.13.refs_0_ = bf16[128,896]{1,0:T(8,128)(2,1)S(1)} collective-permute-done((bf16[128,896]{1,0:T(8,128)(2,1)S(1)}, bf16[128,896]{1,0:T(8,128)(2,1)S(1)}, u32[]{:S(2)}, u32[]{:S(2)}) %collective-permute-start.13) | collective-permute-done | bytes 229408 | tf_op jit(solution)/shard_map/ppermute | solution.py:172
  44.2 1.5 %shard_map.133 = (bf16[5,32,1024]{2,1,0:T(8,128)(2,1)S(1)}, bf16[5,32,1024]{2,1,0:T(8,128)(2,1)S(1)}, bf16[5,32,1024]{2,1,0:T(8,128)(2,1)S(1)}, bf16[5,32,1024]{2,1,0:T(8,128)(2,1)S(1)}) custom-call(s32[2]{0:T(128)S(1)} %pad_add_fusion.place_ref, bf16[128,896]{1,0:T(8,128)(2,1)S(1)} %collective-permute-done.13.refs_0_, ...), custom_call_target="tpu_custom_call" | custom-call | flops 704643072 | bytes 5992448 | tf_op jit(solution)/shard_map/pallas_call | solution.py:197
  46.9 1.9 %collective-permute-done.11.refs_2_ = bf16[5,32,1024]{2,1,0:T(8,128)(2,1)S(1)} collective-permute-done((bf16[5,32,1024]{2,1,0:T(8,128)(2,1)S(1)}, bf16[5,32,1024]{2,1,0:T(8,128)(2,1)S(1)}, u32[]{:S(2)}, u32[]{:S(2)}) %collective-permute-start.11) | collective-permute-done | bytes 327712 | tf_op jit(solution)/shard_map/ppermute | solution.py:159
  49.9 2.2 %collective-permute-start.16 = (bf16[5,32,1024]{2,1,0:T(8,128)(2,1)S(1)}, bf16[5,32,1024]{2,1,0:T(8,128)(2,1)S(1)}, u32[]{:S(2)}, u32[]{:S(2)}) collective-permute-start(bf16[5,32,1024]{2,1,0:T(8,128)(2,1)S(1)} %get-tuple-element.58), channel_id=1, source_target_pairs={{0,8},{4,12},{8,0},{12,4},{1,9},{5,13},{9,1},{13,5},{2,10},{6,14},... | collective-permute-start | bytes 983048 | tf_op jit(solution)/shard_map/ppermute | solution.py:159
  54.0 1.3 %shard_map.137.refs_3_ = bf16[128,896]{1,0:T(8,128)(2,1)S(1)} custom-call(s32[2]{0:T(128)S(1)} %pad_add_fusion.place_ref, bf16[5,32,1024]{2,1,0:T(8,128)(2,1)S(1)} %get-tuple-element.47.refs_1_.refs_0_, bf16[5,32,1024]{2,1,0:T(8,128)(2,1)S(1)} %collective-permute-done.10.refs_1_, bf16[5,32,1024]{2,1,0:T(8,128)(2,1)S(1)} %collective-permute-done.11.refs_2_, ...), custom_call_target="tpu_custom_call" | custom-call | flops 469762048 | bytes 6287360 | tf_op jit(solution)/shard_map/pallas_call | solution.py:197
  55.4 2.8 %collective-permute-start.22 = (bf16[128,896]{1,0:T(8,128)(2,1)S(1)}, bf16[128,896]{1,0:T(8,128)(2,1)S(1)}, u32[]{:S(2)}, u32[]{:S(2)}) collective-permute-start(bf16[128,896]{1,0:T(8,128)(2,1)S(1)} %shard_map.136.refs_9_), channel_id=1, source_target_pairs={{0,18},{1,16},{3,17},{2,19},{16,2},{17,0},{19,1},{18,3},{4,22},{5,... | collective-permute-start | bytes 688136 | tf_op jit(solution)/shard_map/ppermute | solution.py:182
  60.4 2.4 %collective-permute-done.16.refs_2_ = bf16[5,32,1024]{2,1,0:T(8,128)(2,1)S(1)} collective-permute-done((bf16[5,32,1024]{2,1,0:T(8,128)(2,1)S(1)}, bf16[5,32,1024]{2,1,0:T(8,128)(2,1)S(1)}, u32[]{:S(2)}, u32[]{:S(2)}) %collective-permute-start.16) | collective-permute-done | bytes 327712 | tf_op jit(solution)/shard_map/ppermute | solution.py:159
  64.6 1.8 %collective-permute-start.20 = (bf16[3,32,1024]{2,1,0:T(8,128)(2,1)S(1)}, bf16[3,32,1024]{2,1,0:T(8,128)(2,1)S(1)}, u32[]{:S(2)}, u32[]{:S(2)}) collective-permute-start(bf16[3,32,1024]{2,1,0:T(8,128)(2,1)S(1)} %shard_map.140.refs_6_.refs_0_), channel_id=1, source_target_pairs={{0,12},{4,8},{8,4},{12,0},{1,13},{5,9},{9,5},{13,1},{2,14},{6,10},... | collective-permute-start | bytes 589832 | tf_op jit(solution)/shard_map/ppermute | solution.py:159
  66.4 1.2 %collective-permute-start.19 = (bf16[3,32,1024]{2,1,0:T(8,128)(2,1)S(1)}, bf16[3,32,1024]{2,1,0:T(8,128)(2,1)S(1)}, u32[]{:S(2)}, u32[]{:S(2)}) collective-permute-start(bf16[3,32,1024]{2,1,0:T(8,128)(2,1)S(1)} %shard_map.140.refs_6_.refs_0_), channel_id=1, source_target_pairs={{0,8},{4,12},{8,0},{12,4},{1,9},{5,13},{9,1},{13,5},{2,10},{6,14},... | collective-permute-start | bytes 589832 | tf_op jit(solution)/shard_map/ppermute | solution.py:159
  68.1 1.3 %shard_map.142.refs_7_ = bf16[128,896]{1,0:T(8,128)(2,1)S(1)} custom-call(s32[2]{0:T(128)S(1)} %pad_add_fusion.place_ref, bf16[5,32,1024]{2,1,0:T(8,128)(2,1)S(1)} %get-tuple-element.56.refs_6_.refs_0_, bf16[5,32,1024]{2,1,0:T(8,128)(2,1)S(1)} %collective-permute-done.15.refs_1_, bf16[5,32,1024]{2,1,0:T(8,128)(2,1)S(1)} %collective-permute-done.16.refs_2_, ...), custom_call_target="tpu_custom_call" | custom-call | flops 469762048 | bytes 6287360 | tf_op jit(solution)/shard_map/pallas_call | solution.py:197
  69.5 4.4 %collective-permute-start.28 = (bf16[128,896]{1,0:T(8,128)(2,1)S(1)}, bf16[128,896]{1,0:T(8,128)(2,1)S(1)}, u32[]{:S(2)}, u32[]{:S(2)}) collective-permute-start(bf16[128,896]{1,0:T(8,128)(2,1)S(1)} %shard_map.142.refs_7_), channel_id=1, source_target_pairs={{0,1},{1,3},{3,2},{2,0},{4,5},{5,7},{7,6},{6,4},{8,9},{9,11},{11,1... | collective-permute-start | bytes 688136 | tf_op jit(solution)/shard_map/ppermute | solution.py:172
  75.7 1.8 %collective-permute-start.27 = (bf16[1,32,1024]{2,1,0:T(8,128)(2,1)S(1)}, bf16[1,32,1024]{2,1,0:T(8,128)(2,1)S(1)}, u32[]{:S(2)}, u32[]{:S(2)}) collective-permute-start(bf16[1,32,1024]{2,1,0:T(8,128)(2,1)S(1)} %shard_map.144.refs_10_.refs_0_), channel_id=1, source_target_pairs={{0,12},{4,8},{8,4},{12,0},{1,13},{5,9},{9,5},{13,1},{2,14},{6,10},... | collective-permute-start | bytes 196616 | tf_op jit(solution)/shard_map/ppermute | solution.py:159
  77.4 1.2 %collective-permute-start.26 = (bf16[1,32,1024]{2,1,0:T(8,128)(2,1)S(1)}, bf16[1,32,1024]{2,1,0:T(8,128)(2,1)S(1)}, u32[]{:S(2)}, u32[]{:S(2)}) collective-permute-start(bf16[1,32,1024]{2,1,0:T(8,128)(2,1)S(1)} %shard_map.144.refs_10_.refs_0_), channel_id=1, source_target_pairs={{0,8},{4,12},{8,0},{12,4},{1,9},{5,13},{9,1},{13,5},{2,10},{6,14},... | collective-permute-start | bytes 196616 | tf_op jit(solution)/shard_map/ppermute | solution.py:159
  79.2 1.3 %shard_map.145.refs_7_ = bf16[128,896]{1,0:T(8,128)(2,1)S(1)} custom-call(s32[2]{0:T(128)S(1)} %pad_add_fusion.place_ref, bf16[3,32,1024]{2,1,0:T(8,128)(2,1)S(1)} %shard_map.140.refs_6_.refs_0_, bf16[3,32,1024]{2,1,0:T(8,128)(2,1)S(1)} %collective-permute-done.18.refs_1_.refs_2_, bf16[3,32,1024]{2,1,0:T(8,128)(2,1)S(1)} %collective-permute-done.19.refs_2_.refs_3_, ...), custom_call_target="tpu_custom_call" | custom-call | flops 469762048 | bytes 5992448 | tf_op jit(solution)/shard_map/pallas_call | solution.py:197
  80.5 2.4 %collective-permute-start.30 = (bf16[128,896]{1,0:T(8,128)(2,1)S(1)}, bf16[128,896]{1,0:T(8,128)(2,1)S(1)}, u32[]{:S(2)}, u32[]{:S(2)}) collective-permute-start(bf16[128,896]{1,0:T(8,128)(2,1)S(1)} %shard_map.145.refs_7_), channel_id=1, source_target_pairs={{0,17},{1,19},{3,18},{2,16},{16,1},{17,3},{19,2},{18,0},{4,21},{5,... | collective-permute-start | bytes 688136 | tf_op jit(solution)/shard_map/ppermute | solution.py:182
  85.2 1.3 %shard_map.147.refs_1_ = bf16[128,896]{1,0:T(8,128)(2,1)S(1)} custom-call(s32[2]{0:T(128)S(1)} %pad_add_fusion.place_ref, bf16[3,32,1024]{2,1,0:T(8,128)(2,1)S(1)} %shard_map.140.refs_6_.refs_0_, bf16[3,32,1024]{2,1,0:T(8,128)(2,1)S(1)} %collective-permute-done.18.refs_1_.refs_2_, bf16[3,32,1024]{2,1,0:T(8,128)(2,1)S(1)} %collective-permute-done.19.refs_2_.refs_3_, ...), custom_call_target="tpu_custom_call" | custom-call | flops 469762048 | bytes 5992448 | tf_op jit(solution)/shard_map/pallas_call | solution.py:197
  86.8 1.7 %collective-permute-done.30.refs_0_ = bf16[128,896]{1,0:T(8,128)(2,1)S(1)} collective-permute-done((bf16[128,896]{1,0:T(8,128)(2,1)S(1)}, bf16[128,896]{1,0:T(8,128)(2,1)S(1)}, u32[]{:S(2)}, u32[]{:S(2)}) %collective-permute-start.30) | collective-permute-done | bytes 229408 | tf_op jit(solution)/shard_map/ppermute | solution.py:182
  (91 shorter events, 27.0 us)
Async XLA Ops:
  1.6 14.1 %collective-permute-start.1 = (bf16[144,896]{1,0:T(8,128)(2,1)S(1)}, bf16[144,896]{1,0:T(8,128)(2,1)S(1)}, u32[]{:S(2)}, u32[]{:S(2)}) collective-permute-start(bf16[144,896]{1,0:T(8,128)(2,1)S(1)} %shard_map.123.refs_1_.refs_2_.refs_5_.refs_8_), channel_id=1, source_target_pairs={{0,1},{1,3},{3,2},{2,0},{4,5},{5,7},{7,6},{6,4},{8,9},{9,11},{11,1... | collective-permute-start | bytes 774152 | tf_op jit(solution)/shard_map/ppermute | solution.py:172
  4.7 12.1 %collective-permute-start = (bf16[128,896]{1,0:T(8,128)(2,1)S(1)}, bf16[128,896]{1,0:T(8,128)(2,1)S(1)}, u32[]{:S(2)}, u32[]{:S(2)}) collective-permute-start(bf16[128,896]{1,0:T(8,128)(2,1)S(1)} %bitcast.51), channel_id=1, source_target_pairs={{0,1},{1,3},{3,2},{2,0},{4,5},{5,7},{7,6},{6,4},{8,9},{9,11},{11,1... | collective-permute-start | bytes 688136 | tf_op jit(solution)/shard_map/ppermute | solution.py:172
  12.2 8.5 %collective-permute-start.7 = (bf16[3,32,1024]{2,1,0:T(8,128)(2,1)S(1)}, bf16[3,32,1024]{2,1,0:T(8,128)(2,1)S(1)}, u32[]{:S(2)}, u32[]{:S(2)}) collective-permute-start(bf16[3,32,1024]{2,1,0:T(8,128)(2,1)S(1)} %get-tuple-element.39), channel_id=1, source_target_pairs={{0,4},{4,0},{8,12},{12,8},{1,5},{5,1},{9,13},{13,9},{2,6},{6,2},{1... | collective-permute-start | bytes 589832 | tf_op jit(solution)/shard_map/ppermute | solution.py:159
  13.8 9.4 %collective-permute-start.8 = (bf16[3,32,1024]{2,1,0:T(8,128)(2,1)S(1)}, bf16[3,32,1024]{2,1,0:T(8,128)(2,1)S(1)}, u32[]{:S(2)}, u32[]{:S(2)}) collective-permute-start(bf16[3,32,1024]{2,1,0:T(8,128)(2,1)S(1)} %get-tuple-element.40), channel_id=1, source_target_pairs={{0,8},{4,12},{8,0},{12,4},{1,9},{5,13},{9,1},{13,5},{2,10},{6,14},... | collective-permute-start | bytes 589832 | tf_op jit(solution)/shard_map/ppermute | solution.py:159
  15.3 10.6 %collective-permute-start.9 = (bf16[3,32,1024]{2,1,0:T(8,128)(2,1)S(1)}, bf16[3,32,1024]{2,1,0:T(8,128)(2,1)S(1)}, u32[]{:S(2)}, u32[]{:S(2)}) collective-permute-start(bf16[3,32,1024]{2,1,0:T(8,128)(2,1)S(1)} %get-tuple-element.41), channel_id=1, source_target_pairs={{0,12},{4,8},{8,4},{12,0},{1,13},{5,9},{9,5},{13,1},{2,14},{6,10},... | collective-permute-start | bytes 589832 | tf_op jit(solution)/shard_map/ppermute | solution.py:159
  15.8 12.6 %collective-permute-start.6 = (bf16[144,896]{1,0:T(8,128)(2,1)S(1)}, bf16[144,896]{1,0:T(8,128)(2,1)S(1)}, u32[]{:S(2)}, u32[]{:S(2)}) collective-permute-start(bf16[144,896]{1,0:T(8,128)(2,1)S(1)} %collective-permute-done.1.refs_1_.refs_2_.refs_5_.refs_8_), channel_id=1, source_target_pairs={{0,1},{1,3},{3,2},{2,0},{4,5},{5,7},{7,6},{6,4},{8,9},{9,11},{11,1... | collective-permute-start | bytes 774152 | tf_op jit(solution)/shard_map/ppermute | solution.py:172
  16.9 12.7 %collective-permute-start.5 = (bf16[128,896]{1,0:T(8,128)(2,1)S(1)}, bf16[128,896]{1,0:T(8,128)(2,1)S(1)}, u32[]{:S(2)}, u32[]{:S(2)}) collective-permute-start(bf16[128,896]{1,0:T(8,128)(2,1)S(1)} %collective-permute-done.refs_0_), channel_id=1, source_target_pairs={{0,1},{1,3},{3,2},{2,0},{4,5},{5,7},{7,6},{6,4},{8,9},{9,11},{11,1... | collective-permute-start | bytes 688136 | tf_op jit(solution)/shard_map/ppermute | solution.py:172
  20.7 11.5 %collective-permute-start.2 = (bf16[3,32,1024]{2,1,0:T(8,128)(2,1)S(1)}, bf16[3,32,1024]{2,1,0:T(8,128)(2,1)S(1)}, u32[]{:S(2)}, u32[]{:S(2)}) collective-permute-start(bf16[3,32,1024]{2,1,0:T(8,128)(2,1)S(1)} %get-tuple-element.36), channel_id=1, source_target_pairs={{0,4},{4,0},{8,12},{12,8},{1,5},{5,1},{9,13},{13,9},{2,6},{6,2},{1... | collective-permute-start | bytes 589832 | tf_op jit(solution)/shard_map/ppermute | solution.py:159
  23.2 9.8 %collective-permute-start.3 = (bf16[3,32,1024]{2,1,0:T(8,128)(2,1)S(1)}, bf16[3,32,1024]{2,1,0:T(8,128)(2,1)S(1)}, u32[]{:S(2)}, u32[]{:S(2)}) collective-permute-start(bf16[3,32,1024]{2,1,0:T(8,128)(2,1)S(1)} %get-tuple-element.37), channel_id=1, source_target_pairs={{0,8},{4,12},{8,0},{12,4},{1,9},{5,13},{9,1},{13,5},{2,10},{6,14},... | collective-permute-start | bytes 589832 | tf_op jit(solution)/shard_map/ppermute | solution.py:159
  25.9 7.1 %collective-permute-start.4 = (bf16[3,32,1024]{2,1,0:T(8,128)(2,1)S(1)}, bf16[3,32,1024]{2,1,0:T(8,128)(2,1)S(1)}, u32[]{:S(2)}, u32[]{:S(2)}) collective-permute-start(bf16[3,32,1024]{2,1,0:T(8,128)(2,1)S(1)} %get-tuple-element.38), channel_id=1, source_target_pairs={{0,12},{4,8},{8,4},{12,0},{1,13},{5,9},{9,5},{13,1},{2,14},{6,10},... | collective-permute-start | bytes 589832 | tf_op jit(solution)/shard_map/ppermute | solution.py:159
  28.4 15.8 %collective-permute-start.14 = (bf16[144,896]{1,0:T(8,128)(2,1)S(1)}, bf16[144,896]{1,0:T(8,128)(2,1)S(1)}, u32[]{:S(2)}, u32[]{:S(2)}) collective-permute-start(bf16[144,896]{1,0:T(8,128)(2,1)S(1)} %collective-permute-done.6.refs_1_.refs_2_.refs_5_.refs_8_), channel_id=1, source_target_pairs={{0,1},{1,3},{3,2},{2,0},{4,5},{5,7},{7,6},{6,4},{8,9},{9,11},{11,1... | collective-permute-start | bytes 774152 | tf_op jit(solution)/shard_map/ppermute | solution.py:172
  33.7 13.2 %collective-permute-start.10 = (bf16[5,32,1024]{2,1,0:T(8,128)(2,1)S(1)}, bf16[5,32,1024]{2,1,0:T(8,128)(2,1)S(1)}, u32[]{:S(2)}, u32[]{:S(2)}) collective-permute-start(bf16[5,32,1024]{2,1,0:T(8,128)(2,1)S(1)} %get-tuple-element.48), channel_id=1, source_target_pairs={{0,4},{4,0},{8,12},{12,8},{1,5},{5,1},{9,13},{13,9},{2,6},{6,2},{1... | collective-permute-start | bytes 983048 | tf_op jit(solution)/shard_map/ppermute | solution.py:159
  34.5 14.3 %collective-permute-start.11 = (bf16[5,32,1024]{2,1,0:T(8,128)(2,1)S(1)}, bf16[5,32,1024]{2,1,0:T(8,128)(2,1)S(1)}, u32[]{:S(2)}, u32[]{:S(2)}) collective-permute-start(bf16[5,32,1024]{2,1,0:T(8,128)(2,1)S(1)} %get-tuple-element.49), channel_id=1, source_target_pairs={{0,8},{4,12},{8,0},{12,4},{1,9},{5,13},{9,1},{13,5},{2,10},{6,14},... | collective-permute-start | bytes 983048 | tf_op jit(solution)/shard_map/ppermute | solution.py:159
  36.0 12.7 %collective-permute-start.12 = (bf16[5,32,1024]{2,1,0:T(8,128)(2,1)S(1)}, bf16[5,32,1024]{2,1,0:T(8,128)(2,1)S(1)}, u32[]{:S(2)}, u32[]{:S(2)}) collective-permute-start(bf16[5,32,1024]{2,1,0:T(8,128)(2,1)S(1)} %get-tuple-element.50), channel_id=1, source_target_pairs={{0,12},{4,8},{8,4},{12,0},{1,13},{5,9},{9,5},{13,1},{2,14},{6,10},... | collective-permute-start | bytes 983048 | tf_op jit(solution)/shard_map/ppermute | solution.py:159
  37.3 6.9 %collective-permute-start.13 = (bf16[128,896]{1,0:T(8,128)(2,1)S(1)}, bf16[128,896]{1,0:T(8,128)(2,1)S(1)}, u32[]{:S(2)}, u32[]{:S(2)}) collective-permute-start(bf16[128,896]{1,0:T(8,128)(2,1)S(1)} %collective-permute-done.5.refs_0_), channel_id=1, source_target_pairs={{0,1},{1,3},{3,2},{2,0},{4,5},{5,7},{7,6},{6,4},{8,9},{9,11},{11,1... | collective-permute-start | bytes 688136 | tf_op jit(solution)/shard_map/ppermute | solution.py:172
  49.4 11.0 %collective-permute-start.15 = (bf16[5,32,1024]{2,1,0:T(8,128)(2,1)S(1)}, bf16[5,32,1024]{2,1,0:T(8,128)(2,1)S(1)}, u32[]{:S(2)}, u32[]{:S(2)}) collective-permute-start(bf16[5,32,1024]{2,1,0:T(8,128)(2,1)S(1)} %get-tuple-element.57), channel_id=1, source_target_pairs={{0,4},{4,0},{8,12},{12,8},{1,5},{5,1},{9,13},{13,9},{2,6},{6,2},{1... | collective-permute-start | bytes 983048 | tf_op jit(solution)/shard_map/ppermute | solution.py:159
  49.9 13.0 %collective-permute-start.16 = (bf16[5,32,1024]{2,1,0:T(8,128)(2,1)S(1)}, bf16[5,32,1024]{2,1,0:T(8,128)(2,1)S(1)}, u32[]{:S(2)}, u32[]{:S(2)}) collective-permute-start(bf16[5,32,1024]{2,1,0:T(8,128)(2,1)S(1)} %get-tuple-element.58), channel_id=1, source_target_pairs={{0,8},{4,12},{8,0},{12,4},{1,9},{5,13},{9,1},{13,5},{2,10},{6,14},... | collective-permute-start | bytes 983048 | tf_op jit(solution)/shard_map/ppermute | solution.py:159
  52.0 10.8 %collective-permute-start.17 = (bf16[5,32,1024]{2,1,0:T(8,128)(2,1)S(1)}, bf16[5,32,1024]{2,1,0:T(8,128)(2,1)S(1)}, u32[]{:S(2)}, u32[]{:S(2)}) collective-permute-start(bf16[5,32,1024]{2,1,0:T(8,128)(2,1)S(1)} %get-tuple-element.59), channel_id=1, source_target_pairs={{0,12},{4,8},{8,4},{12,0},{1,13},{5,9},{9,5},{13,1},{2,14},{6,10},... | collective-permute-start | bytes 983048 | tf_op jit(solution)/shard_map/ppermute | solution.py:159
  55.3 12.2 %collective-permute-start.23 = (bf16[128,896]{1,0:T(8,128)(2,1)S(1)}, bf16[128,896]{1,0:T(8,128)(2,1)S(1)}, u32[]{:S(2)}, u32[]{:S(2)}) collective-permute-start(bf16[128,896]{1,0:T(8,128)(2,1)S(1)} %shard_map.137.refs_3_), channel_id=1, source_target_pairs={{0,18},{1,16},{3,17},{2,19},{16,2},{17,0},{19,1},{18,3},{4,22},{5,... | collective-permute-start | bytes 688136 | tf_op jit(solution)/shard_map/ppermute | solution.py:182
  55.4 12.8 %collective-permute-start.22 = (bf16[128,896]{1,0:T(8,128)(2,1)S(1)}, bf16[128,896]{1,0:T(8,128)(2,1)S(1)}, u32[]{:S(2)}, u32[]{:S(2)}) collective-permute-start(bf16[128,896]{1,0:T(8,128)(2,1)S(1)} %shard_map.136.refs_9_), channel_id=1, source_target_pairs={{0,18},{1,16},{3,17},{2,19},{16,2},{17,0},{19,1},{18,3},{4,22},{5,... | collective-permute-start | bytes 688136 | tf_op jit(solution)/shard_map/ppermute | solution.py:182
  64.5 9.5 %collective-permute-start.21 = (bf16[128,896]{1,0:T(8,128)(2,1)S(1)}, bf16[128,896]{1,0:T(8,128)(2,1)S(1)}, u32[]{:S(2)}, u32[]{:S(2)}) collective-permute-start(bf16[128,896]{1,0:T(8,128)(2,1)S(1)} %shard_map.141.refs_9_), channel_id=1, source_target_pairs={{0,1},{1,3},{3,2},{2,0},{4,5},{5,7},{7,6},{6,4},{8,9},{9,11},{11,1... | collective-permute-start | bytes 688136 | tf_op jit(solution)/shard_map/ppermute | solution.py:172
  64.6 9.2 %collective-permute-start.20 = (bf16[3,32,1024]{2,1,0:T(8,128)(2,1)S(1)}, bf16[3,32,1024]{2,1,0:T(8,128)(2,1)S(1)}, u32[]{:S(2)}, u32[]{:S(2)}) collective-permute-start(bf16[3,32,1024]{2,1,0:T(8,128)(2,1)S(1)} %shard_map.140.refs_6_.refs_0_), channel_id=1, source_target_pairs={{0,12},{4,8},{8,4},{12,0},{1,13},{5,9},{9,5},{13,1},{2,14},{6,10},... | collective-permute-start | bytes 589832 | tf_op jit(solution)/shard_map/ppermute | solution.py:159
  66.4 7.4 %collective-permute-start.19 = (bf16[3,32,1024]{2,1,0:T(8,128)(2,1)S(1)}, bf16[3,32,1024]{2,1,0:T(8,128)(2,1)S(1)}, u32[]{:S(2)}, u32[]{:S(2)}) collective-permute-start(bf16[3,32,1024]{2,1,0:T(8,128)(2,1)S(1)} %shard_map.140.refs_6_.refs_0_), channel_id=1, source_target_pairs={{0,8},{4,12},{8,0},{12,4},{1,9},{5,13},{9,1},{13,5},{2,10},{6,14},... | collective-permute-start | bytes 589832 | tf_op jit(solution)/shard_map/ppermute | solution.py:159
  67.6 6.3 %collective-permute-start.18 = (bf16[3,32,1024]{2,1,0:T(8,128)(2,1)S(1)}, bf16[3,32,1024]{2,1,0:T(8,128)(2,1)S(1)}, u32[]{:S(2)}, u32[]{:S(2)}) collective-permute-start(bf16[3,32,1024]{2,1,0:T(8,128)(2,1)S(1)} %shard_map.140.refs_6_.refs_0_), channel_id=1, source_target_pairs={{0,4},{4,0},{8,12},{12,8},{1,5},{5,1},{9,13},{13,9},{2,6},{6,2},{1... | collective-permute-start | bytes 589832 | tf_op jit(solution)/shard_map/ppermute | solution.py:159
  69.5 9.8 %collective-permute-start.28 = (bf16[128,896]{1,0:T(8,128)(2,1)S(1)}, bf16[128,896]{1,0:T(8,128)(2,1)S(1)}, u32[]{:S(2)}, u32[]{:S(2)}) collective-permute-start(bf16[128,896]{1,0:T(8,128)(2,1)S(1)} %shard_map.142.refs_7_), channel_id=1, source_target_pairs={{0,1},{1,3},{3,2},{2,0},{4,5},{5,7},{7,6},{6,4},{8,9},{9,11},{11,1... | collective-permute-start | bytes 688136 | tf_op jit(solution)/shard_map/ppermute | solution.py:172
  75.0 11.6 %collective-permute-start.24 = (bf16[128,896]{1,0:T(8,128)(2,1)S(1)}, bf16[128,896]{1,0:T(8,128)(2,1)S(1)}, u32[]{:S(2)}, u32[]{:S(2)}) collective-permute-start(bf16[128,896]{1,0:T(8,128)(2,1)S(1)} %shard_map.143.refs_1_), channel_id=1, source_target_pairs={{0,17},{1,19},{3,18},{2,16},{16,1},{17,3},{19,2},{18,0},{4,21},{5,... | collective-permute-start | bytes 688136 | tf_op jit(solution)/shard_map/ppermute | solution.py:182
  75.7 7.3 %collective-permute-start.27 = (bf16[1,32,1024]{2,1,0:T(8,128)(2,1)S(1)}, bf16[1,32,1024]{2,1,0:T(8,128)(2,1)S(1)}, u32[]{:S(2)}, u32[]{:S(2)}) collective-permute-start(bf16[1,32,1024]{2,1,0:T(8,128)(2,1)S(1)} %shard_map.144.refs_10_.refs_0_), channel_id=1, source_target_pairs={{0,12},{4,8},{8,4},{12,0},{1,13},{5,9},{9,5},{13,1},{2,14},{6,10},... | collective-permute-start | bytes 196616 | tf_op jit(solution)/shard_map/ppermute | solution.py:159
  77.4 5.5 %collective-permute-start.26 = (bf16[1,32,1024]{2,1,0:T(8,128)(2,1)S(1)}, bf16[1,32,1024]{2,1,0:T(8,128)(2,1)S(1)}, u32[]{:S(2)}, u32[]{:S(2)}) collective-permute-start(bf16[1,32,1024]{2,1,0:T(8,128)(2,1)S(1)} %shard_map.144.refs_10_.refs_0_), channel_id=1, source_target_pairs={{0,8},{4,12},{8,0},{12,4},{1,9},{5,13},{9,1},{13,5},{2,10},{6,14},... | collective-permute-start | bytes 196616 | tf_op jit(solution)/shard_map/ppermute | solution.py:159
  78.6 4.6 %collective-permute-start.25 = (bf16[1,32,1024]{2,1,0:T(8,128)(2,1)S(1)}, bf16[1,32,1024]{2,1,0:T(8,128)(2,1)S(1)}, u32[]{:S(2)}, u32[]{:S(2)}) collective-permute-start(bf16[1,32,1024]{2,1,0:T(8,128)(2,1)S(1)} %shard_map.144.refs_10_.refs_0_), channel_id=1, source_target_pairs={{0,4},{4,0},{8,12},{12,8},{1,5},{5,1},{9,13},{13,9},{2,6},{6,2},{1... | collective-permute-start | bytes 196616 | tf_op jit(solution)/shard_map/ppermute | solution.py:159
  80.5 8.0 %collective-permute-start.30 = (bf16[128,896]{1,0:T(8,128)(2,1)S(1)}, bf16[128,896]{1,0:T(8,128)(2,1)S(1)}, u32[]{:S(2)}, u32[]{:S(2)}) collective-permute-start(bf16[128,896]{1,0:T(8,128)(2,1)S(1)} %shard_map.145.refs_7_), channel_id=1, source_target_pairs={{0,17},{1,19},{3,18},{2,16},{16,1},{17,3},{19,2},{18,0},{4,21},{5,... | collective-permute-start | bytes 688136 | tf_op jit(solution)/shard_map/ppermute | solution.py:182
  84.3 2.4 %collective-permute-start.29 = (bf16[128,896]{1,0:T(8,128)(2,1)S(1)}, bf16[128,896]{1,0:T(8,128)(2,1)S(1)}, u32[]{:S(2)}, u32[]{:S(2)}) collective-permute-start(bf16[128,896]{1,0:T(8,128)(2,1)S(1)} %shard_map.146.refs_10_), channel_id=1, source_target_pairs={{0,16},{16,0},{1,17},{17,1},{2,18},{18,2},{3,19},{19,3},{4,20},{20... | collective-permute-start | bytes 688136 | tf_op jit(solution)/shard_map/ppermute | solution.py:14
  86.6 2.0 %collective-permute-start.31 = (bf16[128,896]{1,0:T(8,128)(2,1)S(1)}, bf16[128,896]{1,0:T(8,128)(2,1)S(1)}, u32[]{:S(2)}, u32[]{:S(2)}) collective-permute-start(bf16[128,896]{1,0:T(8,128)(2,1)S(1)} %shard_map.147.refs_1_), channel_id=1, source_target_pairs={{0,16},{16,0},{1,17},{17,1},{2,18},{18,2},{3,19},{19,3},{4,20},{20... | collective-permute-start | bytes 688136 | tf_op jit(solution)/shard_map/ppermute | solution.py:14
  (14 other events, 35.4 us)
